TPU v7x, 128 devices: a whole 4x4x4 slice. The times are simulated.
128 devices in a mesh: stream: 4 (over x_lo, core), blk: 4 (over z), uly: 8 (over y, x_hi).
Axes of the slice: x: 4 (x_hi: 2, x_lo: 2; x = x_hi * 2 + x_lo), y: 4, z: 4, core: 2. Of those that a mesh axis runs over, the one named last changes fastest.
Arguments:
- tokens: bfloat16 [4, 4096, 2048], P('stream', ('blk', 'uly')), may hold values from -6 to 6
- document_starts: int32 [4, 8], P('stream'), may hold values from 0 to 4095, as said below
- document_adapter: int32 [4, 8], P('stream'), may hold values from 0 to 7
- layernorm_gain: float32 [2, 2048], replicated, may hold values from 0.1 to 1.9
- layernorm_bias: float32 [2, 2048], replicated, may hold values from -4 to 4
- projection_weight: bfloat16 [2048, 3, 2048], P(('stream', 'blk', 'uly')), may hold values from -0.125 to 0.125
- output_weight: bfloat16 [2048, 2048], P(('stream', 'blk', 'uly')), may hold values from -1 to 1
- up_weight: bfloat16 [2048, 8192], P(('stream', 'blk', 'uly')), may hold values from -0.125 to 0.125
- down_weight: bfloat16 [8192, 2048], P(('stream', 'blk', 'uly')), may hold values from -0.0625 to 0.0625
- projection_bias: float32 [4, 2048], replicated, may hold values from -4 to 4
- upper_bias: float32 [8192], replicated, may hold values from -6 to 6
- attention_down_maps: bfloat16 [4, 2048, 128], replicated, may hold values from -0.125 to 0.125
- attention_up_maps: bfloat16 [4, 128, 2048], replicated, may hold values from -0.75 to 0.75
- upper_down_maps: bfloat16 [2048, 128], replicated, may hold values from -0.125 to 0.125
- upper_up_maps: bfloat16 [128, 8192], replicated, may hold values from -0.75 to 0.75
- lower_down_maps: bfloat16 [8192, 128], replicated, may hold values from -0.0625 to 0.0625
- lower_up_maps: bfloat16 [128, 2048], replicated, may hold values from -0.75 to 0.75
- cotangent: bfloat16 [4, 4096, 2048], P('stream', ('blk', 'uly')), may hold values from -6 to 6
Outputs:
- mixed: bfloat16 [4, 4096, 2048], P('stream', ('blk', 'uly'))
- input_grad: bfloat16 [4, 4096, 2048], P('stream', ('blk', 'uly'))
- grad_a_attn: float32 [4, 2048, 128], replicated
- grad_b_attn: float32 [4, 128, 2048], replicated
- grad_a_up: float32 [2048, 128], replicated
- grad_b_up: float32 [128, 8192], replicated
- grad_a_down: float32 [8192, 128], replicated
- grad_b_down: float32 [128, 2048], replicated
Inputs may be any that keep to these rules, and one draw needn't show every extreme that they name: `document_starts`: each row starts with 0 and rises strictly; document d of a stream runs from its start to the next start, or to 4096.
All inputs are finite; a program needn't handle non-finite values.
Results may differ from a plain program's by a relative error of at most 0.015.
Values may be sent and summed in bfloat16 or wider, within the bound.
A program may use at most 384 MiB of HBM per device.

v0:
```python
import jax
import jax.numpy as jnp
from jax import lax
from jax.sharding import PartitionSpec as P

HEADS = 16
ADAPTER_RANK = 16


def layer_norm(values, gain, shift):
    center = values - jnp.mean(values, axis=-1, keepdims=True)
    spread = jnp.mean(center * center, axis=-1, keepdims=True)
    return center * lax.rsqrt(spread + 1e-05) * gain + shift


def segment_of(starts, positions):
    return jnp.sum((starts[None, :] <= positions[:, None]).astype(jnp.int32), axis=1) - 1


def simple_product(left, right):
    return jnp.dot(left, right, preferred_element_type=jnp.float32)


def product_right_transposed(left, right):
    return lax.dot_general(
        left, right, (((1,), (1,)), ((), ())), preferred_element_type=jnp.float32
    )


def dot_left_t(left, right):
    return lax.dot_general(
        left, right, (((0,), (0,)), ((), ())), preferred_element_type=jnp.float32
    )


def exact_gelu(values):
    return jax.nn.gelu(values, approximate=False)


def per_device(
    tokens,
    document_starts,
    document_adapter,
    layernorm_gain,
    layernorm_bias,
    projection_weight,
    output_weight,
    up_weight,
    down_weight,
    projection_bias,
    upper_bias,
    attention_down_maps,
    attention_up_maps,
    upper_down_maps,
    upper_up_maps,
    lower_down_maps,
    lower_up_maps,
    cotangent,
):
    local_rows = tokens.shape[1]
    width = tokens.shape[2]
    head_size = width // HEADS
    uly_count = lax.axis_size("uly")
    heads_here = HEADS // uly_count
    query_rows = local_rows * uly_count
    scale = head_size ** (-0.5)
    starts = document_starts[0]
    chosen = document_adapter[0]
    first_row = (lax.axis_index("blk") * uly_count + lax.axis_index("uly")) * local_rows
    local_pos = first_row + jnp.arange(local_rows, dtype=jnp.int32)
    local_seg = segment_of(starts, local_pos)
    doc_ids = jnp.arange(starts.shape[0], dtype=jnp.int32)
    token_adapter = jnp.sum(
        jnp.where(local_seg[:, None] == doc_ids[None, :], chosen[None, :], 0), axis=1
    )
    column_adapter_index = jnp.arange(upper_down_maps.shape[1], dtype=jnp.int32) // ADAPTER_RANK
    document_mask = (token_adapter[:, None] == column_adapter_index[None, :]).astype(jnp.float32)
    query_pos = lax.axis_index("blk") * query_rows + jnp.arange(query_rows, dtype=jnp.int32)
    query_seg = segment_of(starts, query_pos)

    def masked_scores(queries, keys_piece):
        count = keys_piece.shape[0]
        key_pos = jnp.arange(count, dtype=jnp.int32)
        key_seg = segment_of(starts, key_pos)
        allowed = (key_pos[None, :] <= query_pos[:, None]) & (
            key_seg[None, :] == query_seg[:, None]
        )
        raw = jnp.einsum("qhd,khd->hqk", queries, keys_piece, preferred_element_type=jnp.float32)
        return (jnp.where(allowed[None], raw * scale, -1000000000.0), allowed)

    inputs = tokens[0].astype(jnp.float32)
    attn_full, output_projection_total = (
        lax.all_gather(projection_weight, ("stream", "blk", "uly"), axis=0, tiled=True),
        lax.all_gather(output_weight, ("stream", "blk", "uly"), axis=0, tiled=True),
    )
    normed_one, norm_one_back = jax.vjp(
        lambda values: layer_norm(values, layernorm_gain[0], layernorm_bias[0]), inputs
    )
    first_norm_input = normed_one.astype(jnp.bfloat16)
    adapter_projection_delta = (
        jnp.einsum(
            "zl,xlr->xzr",
            first_norm_input,
            attention_down_maps[:3],
            preferred_element_type=jnp.float32,
        )
        * document_mask[None]
    ).astype(jnp.bfloat16)
    bias_rows = jnp.stack(
        [projection_bias[0], jnp.zeros_like(projection_bias[0]), projection_bias[1]]
    )
    projected = (
        jnp.einsum("td,dpe->pte", first_norm_input, attn_full, preferred_element_type=jnp.float32)
        + bias_rows[:, None, :]
        + jnp.einsum(
            "moa,maz->moz",
            adapter_projection_delta,
            attention_up_maps[:3],
            preferred_element_type=jnp.float32,
        )
    )
    projected_low = projected.astype(jnp.bfloat16).reshape(3, local_rows, HEADS, head_size)
    by_heads = lax.all_to_all(projected_low, "uly", split_axis=2, concat_axis=1, tiled=True)
    queries = by_heads[0]
    keys = by_heads[1]
    values_heads = by_heads[2]
    run_max = jnp.full((heads_here, query_rows), -1e30, jnp.float32)
    scores, allowed = masked_scores(queries, lax.all_gather(keys, "blk", axis=0, tiled=True))
    new_max = jnp.maximum(run_max, jnp.max(scores, axis=-1))
    weights = jnp.where(allowed[None], jnp.exp(scores - new_max[..., None]), 0.0)
    run_sum = jnp.sum(weights, axis=-1)
    log_total = new_max + jnp.log(run_sum)
    keys_piece = lax.all_gather(keys, "blk", axis=0, tiled=True)
    values_piece = lax.all_gather(values_heads, "blk", axis=0, tiled=True)
    scores, allowed = masked_scores(queries, keys_piece)
    probs_low = jnp.exp(scores - log_total[..., None]).astype(jnp.bfloat16)
    attended = jnp.einsum(
        "hqk,khd->qhd", probs_low, values_piece, preferred_element_type=jnp.float32
    )
    attended_low = attended.astype(jnp.bfloat16)
    back_rows = lax.all_to_all(attended_low, "uly", split_axis=0, concat_axis=1, tiled=True)
    heads_merged = back_rows.reshape(local_rows, width)
    adapter_output_delta = (
        simple_product(heads_merged, attention_down_maps[3]) * document_mask
    ).astype(jnp.bfloat16)
    residual_stream = (
        inputs
        + simple_product(heads_merged, output_projection_total)
        + projection_bias[2]
        + simple_product(adapter_output_delta, attention_up_maps[3])
    )
    normed_two, norm_two_back = jax.vjp(
        lambda values: layer_norm(values, layernorm_gain[1], layernorm_bias[1]), residual_stream
    )
    second_norm_input = normed_two.astype(jnp.bfloat16)
    up_projection_total, down_projection_total = (
        lax.all_gather(up_weight, ("stream", "blk", "uly"), axis=0, tiled=True),
        lax.all_gather(down_weight, ("stream", "blk", "uly"), axis=0, tiled=True),
    )
    adapter_up_delta = (simple_product(second_norm_input, upper_down_maps) * document_mask).astype(
        jnp.bfloat16
    )
    preactivation = (
        simple_product(second_norm_input, up_projection_total)
        + upper_bias
        + simple_product(adapter_up_delta, upper_up_maps)
    )
    activated, gelu_back = jax.vjp(exact_gelu, preactivation)
    activation_reduced = activated.astype(jnp.bfloat16)
    adapter_down_delta = (
        simple_product(activation_reduced, lower_down_maps) * document_mask
    ).astype(jnp.bfloat16)
    output = (
        residual_stream
        + simple_product(activation_reduced, down_projection_total)
        + projection_bias[3]
        + simple_product(adapter_down_delta, lower_up_maps)
    )
    output_gradient = cotangent[0]
    up_projection_total, down_projection_total = (
        lax.all_gather(up_weight, ("stream", "blk", "uly"), axis=0, tiled=True),
        lax.all_gather(down_weight, ("stream", "blk", "uly"), axis=0, tiled=True),
    )
    grad_b_down = dot_left_t(adapter_down_delta, output_gradient)
    adapter_down_gradient = (
        product_right_transposed(output_gradient, lower_up_maps) * document_mask
    ).astype(jnp.bfloat16)
    grad_a_down = dot_left_t(activation_reduced, adapter_down_gradient)
    activation_gradient = product_right_transposed(
        output_gradient, down_projection_total
    ) + product_right_transposed(adapter_down_gradient, lower_down_maps)
    preactivation_gradient = gelu_back(activation_gradient)[0].astype(jnp.bfloat16)
    grad_b_up = dot_left_t(adapter_up_delta, preactivation_gradient)
    adapter_up_gradient = (
        product_right_transposed(preactivation_gradient, upper_up_maps) * document_mask
    ).astype(jnp.bfloat16)
    grad_a_up = dot_left_t(second_norm_input, adapter_up_gradient)
    second_norm_gradient = product_right_transposed(
        preactivation_gradient, up_projection_total
    ) + product_right_transposed(adapter_up_gradient, upper_down_maps)
    grad_residual = output_gradient.astype(jnp.float32) + norm_two_back(second_norm_gradient)[0]
    branch_gradient = grad_residual.astype(jnp.bfloat16)
    grad_b_out = dot_left_t(adapter_output_delta, branch_gradient)
    adapter_output_gradient = (
        product_right_transposed(branch_gradient, attention_up_maps[3]) * document_mask
    ).astype(jnp.bfloat16)
    grad_a_out = dot_left_t(heads_merged, adapter_output_gradient)
    attn_full, output_projection_total = (
        lax.all_gather(projection_weight, ("stream", "blk", "uly"), axis=0, tiled=True),
        lax.all_gather(output_weight, ("stream", "blk", "uly"), axis=0, tiled=True),
    )
    merged_gradient = product_right_transposed(
        branch_gradient, output_projection_total
    ) + product_right_transposed(adapter_output_gradient, attention_down_maps[3])
    grad_rows = merged_gradient.astype(jnp.bfloat16).reshape(local_rows, HEADS, head_size)
    grad_heads = lax.all_to_all(grad_rows, "uly", split_axis=1, concat_axis=0, tiled=True)
    row_dot = jnp.transpose(jnp.sum(grad_heads.astype(jnp.float32) * attended, axis=-1))
    keys_piece = lax.all_gather(keys, "blk", axis=0, tiled=True)
    values_piece = lax.all_gather(values_heads, "blk", axis=0, tiled=True)
    count = keys_piece.shape[0]
    scores, allowed = masked_scores(queries, keys_piece)
    probs = jnp.exp(scores - log_total[..., None])
    probs_low = probs.astype(jnp.bfloat16)
    grad_probs = jnp.einsum(
        "qhd,khd->hqk", grad_heads, values_piece, preferred_element_type=jnp.float32
    )
    grad_scores = (scale * probs * (grad_probs - row_dot[..., None])).astype(jnp.bfloat16)
    grad_query = jnp.einsum(
        "hqk,khd->qhd", grad_scores, keys_piece, preferred_element_type=jnp.float32
    )
    key_part = jnp.einsum("hqk,qhd->khd", grad_scores, queries, preferred_element_type=jnp.float32)
    value_part = jnp.einsum(
        "hqk,qhd->khd", probs_low, grad_heads, preferred_element_type=jnp.float32
    )
    grad_keys = key_part
    grad_values = value_part
    grad_query, grad_keys, grad_values = (grad_query, grad_keys, grad_values)
    key_sum, value_sum = (
        lax.psum_scatter(
            grad_keys.astype(jnp.bfloat16), "blk", scatter_dimension=0, tiled=True
        ).astype(jnp.float32),
        lax.psum_scatter(
            grad_values.astype(jnp.bfloat16), "blk", scatter_dimension=0, tiled=True
        ).astype(jnp.float32),
    )
    grad_stack = jnp.stack([grad_query, key_sum, value_sum]).astype(jnp.bfloat16)
    grad_tokens = lax.all_to_all(grad_stack, "uly", split_axis=1, concat_axis=2, tiled=True)
    projection_gradient = grad_tokens.reshape(3, local_rows, width)
    grad_b_qkv = jnp.einsum(
        "ptc,pte->pce",
        adapter_projection_delta,
        projection_gradient,
        preferred_element_type=jnp.float32,
    )
    adapter_projection_gradient = (
        jnp.einsum(
            "yuv,yrv->yur",
            projection_gradient,
            attention_up_maps[:3],
            preferred_element_type=jnp.float32,
        )
        * document_mask[None]
    ).astype(jnp.bfloat16)
    grad_a_qkv = jnp.einsum(
        "td,ptc->pdc",
        first_norm_input,
        adapter_projection_gradient,
        preferred_element_type=jnp.float32,
    )
    grad_first = jnp.einsum(
        "pte,dpe->td", projection_gradient, attn_full, preferred_element_type=jnp.float32
    ) + jnp.einsum(
        "kfr,kor->fo",
        adapter_projection_gradient,
        attention_down_maps[:3],
        preferred_element_type=jnp.float32,
    )
    input_grad = grad_residual + norm_one_back(grad_first)[0]
    grad_a_attn = jnp.concatenate([grad_a_qkv, grad_a_out[None]], axis=0)
    grad_b_attn = jnp.concatenate([grad_b_qkv, grad_b_out[None]], axis=0)
    totals = lax.psum(
        (grad_a_attn, grad_b_attn, grad_a_up, grad_b_up, grad_a_down, grad_b_down),
        ("stream", "blk", "uly"),
    )
    return (
        output.astype(jnp.bfloat16)[None],
        input_grad.astype(jnp.bfloat16)[None],
        totals[0],
        totals[1],
        totals[2],
        totals[3],
        totals[4],
        totals[5],
    )


def solution(mesh):
    in_specs = (
        P("stream", ("blk", "uly"), None),
        P("stream", None),
        P("stream", None),
        P(),
        P(),
        P(("stream", "blk", "uly"), None, None),
        P(("stream", "blk", "uly"), None),
        P(("stream", "blk", "uly"), None),
        P(("stream", "blk", "uly"), None),
        P(),
        P(),
        P(),
        P(),
        P(),
        P(),
        P(),
        P(),
        P("stream", ("blk", "uly"), None),
    )
    out_specs = (
        P("stream", ("blk", "uly"), None),
        P("stream", ("blk", "uly"), None),
        P(),
        P(),
        P(),
        P(),
        P(),
        P(),
    )
    return jax.shard_map(
        per_device, mesh=mesh, in_specs=in_specs, out_specs=out_specs, check_vma=False
    )
```

profile of v0, /device:TPU:1, one launch (start us, length us, event | category | flops | bytes accessed | tf_op | source)
XLA Modules:
  0.0 1922.7 jit_solution(11763520848308916220)
XLA Ops:
  16.7 335.4 %all-gather.7.cloned.1.call-done = bf16[2048,3,2048]{2,0,1:T(8,128)(2,1)} async-done(((bf16[16,3,2048]{2,0,1:T(8,128)(2,1)}), bf16[2048,3,2048]{2,0,1:T(8,128)(2,1)}) %all-gather.7.cloned.1.call-update) | async-done | bytes 25165840 | tf_op jit(solution)/shard_map/all_gather | solution.py:93
  352.1 10.3 fusion.81
  363.5 28.5 %all_to_all.63 = bf16[3,128,16,128]{3,1,0,2:T(8,128)(2,1)S(1)} all-to-all(bf16[3,128,16,128]{3,1,0,2:T(8,128)(2,1)S(1)} %bitcast.207), channel_id=1, replica_groups=mesh['stream'=4,'blk'=4,'uly'=8] {'uly'}, dimensions={2} | all-to-all | bytes 3145728 | tf_op jit(solution)/shard_map/all_to_all | solution.py:123
  402.9 19.3 %all-gather.11.cloned.1.call-done = bf16[4096,2,128]{2,0,1:T(8,128)(2,1)} async-done(((bf16[1024,2,128]{2,0,1:T(8,128)(2,1)}), bf16[4096,2,128]{2,0,1:T(8,128)(2,1)}) %all-gather.11.cloned.1.call-update) | async-done | bytes 2097168 | tf_op jit(solution)/shard_map/all_gather | solution.py:133
  422.2 17.4 fusion.1
  439.6 16.5 select_reduce_fusion
  456.1 16.3 fusion.91
  482.2 10.2 all-to-all-done.1
  497.9 270.5 %all-gather.13.cloned.1.call-done = bf16[2048,2048]{1,0:T(8,128)(2,1)} async-done(((bf16[16,2048]{1,0:T(8,128)(2,1)}), bf16[2048,2048]{1,0:T(8,128)(2,1)}) %all-gather.13.cloned.1.call-update) | async-done | bytes 8388624 | tf_op jit(solution)/shard_map/all_gather | solution.py:94
  777.1 344.7 %all-gather.15.cloned.1.call-done = bf16[2048,8192]{1,0:T(8,128)(2,1)} async-done(((bf16[16,8192]{1,0:T(8,128)(2,1)}), bf16[2048,8192]{1,0:T(8,128)(2,1)}) %all-gather.15.cloned.1.call-update) | async-done | bytes 33554448 | tf_op jit(solution)/shard_map/all_gather | solution.py:157
  1121.8 13.3 convolution_add_fusion.2
  1135.1 11.2 multiply_convert_fusion.1
  1146.2 326.5 %all-gather.17.cloned.1.call-done = bf16[8192,2048]{1,0:T(8,128)(2,1)} async-done(((bf16[64,2048]{1,0:T(8,128)(2,1)}), bf16[8192,2048]{1,0:T(8,128)(2,1)}) %all-gather.17.cloned.1.call-update) | async-done | bytes 33554448 | tf_op jit(solution)/shard_map/all_gather | solution.py:158
  1472.7 17.6 fusion.66
  1496.9 16.4 fusion.93
  1523.9 17.5 all_to_all.64
  1543.7 17.4 fusion.4
  1562.5 23.8 %multiply_convert_fusion = bf16[2,1024,4096]{2,1,0:T(8,128)(2,1)} fusion(f32[2,1024,4096]{2,1,0:T(8,128)} %get-tuple-element.70, f32[2,1024]{1,0:T(2,128)S(1)} %bitcast.229, f32[2,1024]{1,0:T(2,128)S(1)} %log_add_fusion, pred[1024,4096]{1,0:T(8,128)(4,1)} %fusion.2, bf16[1024,2,128]{0,2,1:T(8,128)(2,1)S(1)} %all_to_all.55, ...), kind=kOutput, calls=%fused_computation | convolution fusion | flops 2206203904 | bytes 57163776 | tf_op jit(solution)/shard_map/qhd,khd->hqk/dot_general | solution.py:224
  1598.8 12.5 fusion.33
  1611.3 12.5 reduce-scatter.3.cloned.1.call-done
  1649.0 10.7 all-to-all-done.3
  1676.6 14.9 fusion.15
  1694.3 15.0 fusion.59
  1714.0 184.0 %all-reduce.3.cloned.1.call-done = (f32[4,2048,128]{1,2,0:T(8,128)}, f32[4,128,2048]{2,1,0:T(8,128)}, f32[2048,128]{1,0:T(8,128)}, f32[128,8192]{1,0:T(8,128)}, f32[8192,128]{1,0:T(8,128)}, /*index=5*/f32[128,2048]{1,0:T(8,128)}) async-done(((f32[4,2048,128]{1,2,0:T(8,128)}, f32[4,128,2048]{2,1,0:T(8,128)}, f32[2048,128]{1,0:T(8,128)}, f32[128,8192]{1,0:T(8,128)}, f32[8192,128]{1,0:T(8,128)}, ...) | async-done | bytes 18874384 | tf_op jit(solution)/shard_map/psum | solution.py:281
  (204 shorter events, 145.7 us)
Async XLA Ops:
  7.2 1127.9 %copy-start = (bf16[128,8192]{1,0:T(8,128)(2,1)S(1)}, bf16[128,8192]{1,0:T(8,128)(2,1)}, u32[]{:S(2)}) copy-start(bf16[128,8192]{1,0:T(8,128)(2,1)} %param.32) | copy-start | bytes 6291460
  7.2 344.9 %copy-start.2 = (bf16[1,128,2048]{2,1,0:T(8,128)(2,1)S(1)}, bf16[1,128,2048]{2,1,0:T(8,128)(2,1)}, u32[]{:S(2)}) copy-start(bf16[1,128,2048]{2,1,0:T(8,128)(2,1)} %param.18) | copy-start | bytes 1572868
  7.2 344.8 %all-gather.7.cloned.1.call-start = ((), (), s32[]{:S(2)}) async-start(), calls=%async_computation.6 | async-start | bytes 25362432 | tf_op jit(solution)/shard_map/all_gather | solution.py:93
  7.9 414.2 %all-gather.11.cloned.1.call-start = ((), (), s32[]{:S(2)}) async-start(), calls=%async_computation.8 | async-start | bytes 2621440 | tf_op jit(solution)/shard_map/all_gather | solution.py:133
  10.8 351.6 %copy-start.42 = (f32[128]{0:T(128)}, f32[128]{0:T(128)S(1)}, u32[]{:S(2)}) copy-start(f32[128]{0:T(128)S(1)} %broadcast_multiply_fusion.1) | copy-start | bytes 1540
  12.1 350.2 %copy-start.47 = (f32[128]{0:T(128)}, f32[128]{0:T(128)S(1)}, u32[]{:S(2)}) copy-start(f32[128]{0:T(128)S(1)} %fusion.55) | copy-start | bytes 1540
  12.1 350.2 %copy-start.44 = (f32[128]{0:T(128)}, f32[128]{0:T(128)S(1)}, u32[]{:S(2)}) copy-start(f32[128]{0:T(128)S(1)} %fusion.76) | copy-start | bytes 1540
  13.0 349.3 %copy-start.35 = (f32[1,2048]{1,0:T(1,128)}, f32[1,2048]{1,0:T(1,128)S(1)}, u32[]{:S(2)}) copy-start(f32[1,2048]{1,0:T(1,128)S(1)} %get-tuple-element.68) | copy-start | bytes 24580
  13.9 348.5 %copy-start.33 = (f32[1,2048]{1,0:T(1,128)}, f32[1,2048]{1,0:T(1,128)S(1)}, u32[]{:S(2)}) copy-start(f32[1,2048]{1,0:T(1,128)S(1)} %get-tuple-element.66) | copy-start | bytes 24580
  16.0 346.4 %copy-start.31 = (bf16[3,128,128]{2,1,0:T(8,128)(2,1)}, bf16[3,128,128]{2,1,0:T(8,128)(2,1)S(1)}, u32[]{:S(2)}) copy-start(bf16[3,128,128]{2,1,0:T(8,128)(2,1)S(1)} %fusion.46) | copy-start | bytes 294916
  393.2 46.3 %copy-start.15 = (bf16[1,8,128,2,128]{4,2,1,3,0:T(8,128)(2,1)}, bf16[1,8,128,2,128]{4,2,1,3,0:T(8,128)(2,1)S(1)}, u32[]{:S(2)}) copy-start(bf16[1,8,128,2,128]{4,2,1,3,0:T(8,128)(2,1)S(1)} %get-tuple-element.59) | copy-start | bytes 1572868
  393.3 62.8 %all-gather.9.cloned.1.call-start = ((), (), s32[]{:S(2)}) async-start(), calls=%async_computation.7 | async-start | bytes 2621440 | tf_op jit(solution)/shard_map/all_gather | solution.py:134
  395.5 372.9 %all-gather.13.cloned.1.call-start = ((), (), s32[]{:S(2)}) async-start(), calls=%async_computation.9 | async-start | bytes 8454144 | tf_op jit(solution)/shard_map/all_gather | solution.py:94
  396.1 725.7 %all-gather.15.cloned.1.call-start = ((), (), s32[]{:S(2)}) async-start(), calls=%async_computation.10 | async-start | bytes 33816576 | tf_op jit(solution)/shard_map/all_gather | solution.py:157
  396.7 1076.0 %all-gather.17.cloned.1.call-start = ((), (), s32[]{:S(2)}) async-start(), calls=%async_computation.11 | async-start | bytes 33816576 | tf_op jit(solution)/shard_map/all_gather | solution.py:158
  456.1 24.8 %copy-start.10 = (bf16[1,128,2048]{2,1,0:T(8,128)(2,1)S(1)}, bf16[1,128,2048]{2,1,0:T(8,128)(2,1)}, u32[]{:S(2)}) copy-start(bf16[1,128,2048]{2,1,0:T(8,128)(2,1)} %param.35) | copy-start | bytes 1572868
  474.4 18.0 all-to-all-start.1
  480.8 1130.4 %reduce-scatter.5.cloned.1.call-start = ((), (), s32[]{:S(2)}) async-start(), calls=%async_computation.13 | async-start | bytes 2621440 | tf_op jit(solution)/shard_map/reduce_scatter | solution.py:242
  773.3 348.5 %copy-start.41 = (f32[8192]{0:T(1024)S(1)}, f32[8192]{0:T(1024)}, u32[]{:S(2)}) copy-start(f32[8192]{0:T(1024)} %param.28) | copy-start | bytes 98308
  1561.1 62.7 %reduce-scatter.3.cloned.1.call-start = ((), (), s32[]{:S(2)}) async-start(), calls=%async_computation.12 | async-start | bytes 2621440 | tf_op jit(solution)/shard_map/reduce_scatter | solution.py:239
  1562.5 23.9 %copy-start.16 = (bf16[1,8,128,2,128]{4,2,1,3,0:T(8,128)(2,1)S(1)}, bf16[1,8,128,2,128]{4,2,1,3,0:T(8,128)(2,1)}, u32[]{:S(2)}) copy-start(bf16[1,8,128,2,128]{4,2,1,3,0:T(8,128)(2,1)} %copy-done.15) | copy-start | bytes 1572868
  1631.3 28.5 %all-to-all-start.3 = ((bf16[3,1024,2,128]{3,2,0,1:T(2,128)(2,1)}), bf16[3,1024,2,128]{3,2,0,1:T(2,128)(2,1)}, u32[]{:S(2)}, u32[]{:S(2)}) async-start(bf16[3,1024,2,128]{3,2,0,1:T(2,128)(2,1)} %copy.97), calls=%async_computation.5 | async-start | bytes 3145728 | tf_op jit(solution)/shard_map/all_to_all | solution.py:247
  1637.7 260.4 %all-reduce.3.cloned.1.call-start = ((), (), s32[]{:S(2)}) async-start(), calls=%async_computation.14 | async-start | bytes 37748736 | tf_op jit(solution)/shard_map/psum | solution.py:281
  1649.0 18.2 copy-start.38
  (36 other events, 260.9 us)
Sparse Core Ops, SparseCore 0:
  9.7 342.2 all-gather.6
  393.4 28.7 all-gather.10
  424.4 30.9 all-gather.8
  456.9 311.4 all-gather.12
  769.9 351.8 all-gather.14
  1123.3 349.3 all-gather.16
  1561.2 27.5 reduce-scatter.4
  1596.2 27.5 reduce-scatter.2
  1676.1 221.9 all-reduce.2
where the time goes:
time: 1930 us; the launch traced here: 1920 us
  waiting for transfers between devices  1520 us (79%)
  matrix products  244 us (13%)
  local copies, waits for them, and re-layouts  47.2 us (2%)
  blocking collectives  46 us (2%)
  other arithmetic  40.7 us (2%)
    all_gather x1, waiting for transfers between devices, per_device(): lax.all_gather(up_weight, ('stream', 'blk', 'uly'), axis=0, tiled=True)  345 us
    all_gather x1, waiting for transfers between devices, per_device(): lax.all_gather(projection_weight, ('stream', 'blk', 'uly'), axis=0, tiled...  335 us
    all_gather x1, waiting for transfers between devices, per_device(): lax.all_gather(down_weight, ('stream', 'blk', 'uly'), axis=0, tiled=True)  326 us
    all_gather x1, waiting for transfers between devices, per_device(): lax.all_gather(output_weight, ('stream', 'blk', 'uly'), axis=0, tiled=True)  270 us
    psum x1, waiting for transfers between devices, per_device(): lax.psum((grad_a_attn, grad_b_attn, grad_a_up, grad_b_up, grad_a_down, gr...  184 us
    dot_general x9, matrix products, product_right_transposed(): lax.dot_general(left, right, (((1,), (1,)), ((), ())), preferred_element_...  51.7 us
    dot_general x9, matrix products, simple_product(): return jnp.dot(left, right, preferred_element_type=jnp.float32)  51.5 us
  transfers between devices with their start and end apart: 11, of which 9 were waited for; matrix products, arithmetic and copies ran while one was open for 11% of the time, Pallas kernels for 0%

commit v1 on v0

v1 whole, which is shorter than its diff:
```python
import functools

import jax
import jax.numpy as jnp
import numpy as np
from jax import lax
from jax.experimental import pallas as pl
from jax.experimental.pallas import tpu as pltpu
from jax.sharding import PartitionSpec as P

HEADS = 16
ADAPTER_RANK = 16
MESH = pl.DeviceIdType.MESH
AXES = ("xl", "c", "z", "y", "xh")
SIZES = (2, 2, 4, 4, 2)
STREAM = ("xl", "c")
TOKEN = ("z", "y", "xh")
HEAD = ("z", "y")
bf16 = jnp.bfloat16
f32 = jnp.float32
LOG2E = 1.4426950408889634
MIB = 2**20
Q_TILE = 256
K_TILE = 512


def layer_norm(values, gain, shift):
    center = values - jnp.mean(values, axis=-1, keepdims=True)
    spread = jnp.mean(center * center, axis=-1, keepdims=True)
    return center * lax.rsqrt(spread + 1e-05) * gain + shift


def dot(left, right):
    return jnp.dot(left, right, preferred_element_type=f32)


def dot_nt(left, right):
    return lax.dot_general(left, right, (((1,), (1,)), ((), ())), preferred_element_type=f32)


def dot_tn(left, right):
    return lax.dot_general(left, right, (((0,), (0,)), ((), ())), preferred_element_type=f32)


def exact_gelu(values):
    return jax.nn.gelu(values, approximate=False)


class Place:
    def __init__(self):
        self.xl, self.c, self.z, self.y, self.xh = (lax.axis_index(a) for a in AXES)
        self.x = self.xh * 2 + self.xl

    def at(self, axis):
        return {"x": self.x, "y": self.y, "z": self.z, "xh": self.xh}[axis]

    def toward(self, axis, step):
        if axis == "c":
            return {"c": 1 - self.c}
        if axis == "xh":
            return {"xh": 1 - self.xh}
        to = lax.rem(self.at(axis) + (step + 4), 4)
        if axis == "x":
            return {"xl": lax.rem(to, 2), "xh": to // 2}
        return {axis: to}


class Sends:
    def __init__(self, send, recv):
        self.send, self.recv, self.used, self.open = send, recv, 0, []

    def push(self, src, dst, device):
        k = self.used
        self.used += 1
        copy = pltpu.make_async_remote_copy(
            src_ref=src,
            dst_ref=dst,
            send_sem=self.send.at[k],
            recv_sem=self.recv.at[k],
            device_id=device,
            device_id_type=MESH,
        )
        copy.start()
        self.open.append(copy)
        return copy


def greet(devices):
    barrier = pltpu.get_barrier_semaphore()
    for device in devices:
        pl.semaphore_signal(barrier, inc=1, device_id=device, device_id_type=MESH)
    pl.semaphore_wait(barrier, len(devices))


def run_all(parts):
    parts = list(parts)
    while parts:
        left = []
        for part in parts:
            try:
                next(part)
                left.append(part)
            except StopIteration:
                pass
        parts = left


ALL = slice(None)
LOWER, UPPER = pl.ds(0, 1024), pl.ds(1024, 1024)


def ring_gather(place, sends, view, order, chunk, landed, forward):
    fixed = {a: place.at(a) for a in order}
    across = place.toward("c", 1)
    later, passed = [], []
    if forward:
        passed.append(sends.push(chunk, view(fixed, ALL), across))
    for number, axis in enumerate(order):
        own = view(fixed, ALL)
        src = chunk if number == 0 else own
        here = place.at(axis)
        if axis == "xh":
            sent = sends.push(src, own, place.toward("xh", 1))
            yield
            sent.wait_recv()
            if number == 0:
                landed.wait()
            later.append(sent)
            del fixed[axis]
            continue
        up = sends.push(src, own, place.toward(axis, 1))
        down = sends.push(src, own, place.toward(axis, -1))
        yield
        before = dict(fixed) | {axis: lax.rem(here + 3, 4)}
        after = dict(fixed) | {axis: lax.rem(here + 1, 4)}
        opposite = dict(fixed) | {axis: lax.rem(here + 2, 4)}
        up.wait_recv()
        half = view(before, LOWER)
        up_two = sends.push(half, half, place.toward(axis, 1))
        down.wait_recv()
        half = view(after, UPPER)
        down_two = sends.push(half, half, place.toward(axis, -1))
        if forward:
            for block in (before, after):
                passed.append(sends.push(view(block, ALL), view(block, ALL), across))
        yield
        up_two.wait_recv()
        down_two.wait_recv()
        if number == 0:
            landed.wait()
        if forward:
            passed.append(sends.push(view(opposite, ALL), view(opposite, ALL), across))
        later += [up, down, up_two, down_two]
        del fixed[axis]
    yield
    for copy in later:
        copy.wait_send()
    for copy in passed:
        copy.wait()


def weights_kernel(wp, wo, up, dn, qkv_all, out_all, up_all, dn_all, send, recv, local):
    place = Place()
    sends = Sends(send, recv)
    partner = place.toward("c", 1)
    mates = [{"c": 1 - place.c}, {"xl": 1 - place.xl}, {"xl": 1 - place.xl, "c": 1 - place.c}]
    peers = mates + [place.toward("xh", 1)]
    peers += [place.toward(a, s) for a in ("x", "y", "z") for s in (1, -1)]
    greet(peers)
    home = (place.xl, place.c, place.z, place.y, place.xh)

    def whole(ref, lead):
        def view(fixed, columns):
            xl, xh = (ALL, ALL)
            if "x" in fixed:
                xl, xh = lax.rem(fixed["x"], 2), fixed["x"] // 2
            return ref.at[lead + (xl, place.c, fixed.get("z", ALL), fixed.get("y", ALL), xh, ALL, columns)]

        return view

    def up_view(fixed, columns):
        return up_all.at[ALL, ALL, fixed.get("z", ALL), fixed.get("y", ALL), fixed.get("xh", ALL), ALL, columns]

    def dn_view(fixed, columns):
        return dn_all.at[fixed.get("z", ALL), fixed.get("y", ALL), fixed.get("xh", ALL), ALL, columns]

    stream = place.xl * 2 + place.c

    def cols(device):
        to = device.get("xl", place.xl) * 2 + device.get("c", place.c)
        return pl.ds(pl.multiple_of(to * 2048, 2048), 2048)

    copies = [pltpu.make_async_copy(wp.at[p], qkv_all.at[(p,) + home], local.at[p]) for p in range(3)]
    copies.append(pltpu.make_async_copy(wo, out_all.at[home], local.at[3]))
    copies.append(pltpu.make_async_copy(dn, dn_all.at[home[2:]], local.at[4]))
    copies.append(pltpu.make_async_copy(up.at[:, cols({})], up_all.at[home], local.at[5]))
    for copy in copies:
        copy.start()
    spread = [sends.push(up.at[:, cols(m)], up_all.at[home], m) for m in mates]

    class Many:
        def wait(self):
            copies[5].wait()
            for s in spread:
                s.wait()

    class Nothing:
        def wait(self):
            pass

    def up_part():
        yield
        Many().wait()
        fixed = {"xh": place.xh, "y": place.y, "z": place.z}
        yield from ring_gather(place, sends, up_view, ("xh", "y", "z"), up_view(fixed, ALL), Nothing(), False)

    parts = [
        ring_gather(place, sends, whole(qkv_all, (0,)), ("y", "z", "x"), wp.at[0], copies[0], True),
        ring_gather(place, sends, whole(qkv_all, (1,)), ("z", "y", "x"), wp.at[1], copies[1], True),
        ring_gather(place, sends, whole(qkv_all, (2,)), ("x", "y", "z"), wp.at[2], copies[2], True),
        ring_gather(place, sends, whole(out_all, ()), ("x", "z", "y"), wo, copies[3], True),
        up_part(),
        ring_gather(place, sends, dn_view, ("xh", "z", "y"), dn, copies[4], False),
    ]
    run_all(parts)


def gather_weights(wp, wo, up, dn):
    n = 160
    any_ = pl.BlockSpec(memory_space=pl.ANY)
    return pl.pallas_call(
        weights_kernel,
        name="gather_weights",
        out_shape=[
            jax.ShapeDtypeStruct((3, 2, 2, 4, 4, 2, 16, 2048), bf16),
            jax.ShapeDtypeStruct((2, 2, 4, 4, 2, 16, 2048), bf16),
            jax.ShapeDtypeStruct((2, 2, 4, 4, 2, 16, 2048), bf16),
            jax.ShapeDtypeStruct((4, 4, 2, 64, 2048), bf16),
        ],
        in_specs=[any_] * 4,
        out_specs=[any_] * 4,
        scratch_shapes=[
            pltpu.SemaphoreType.DMA((n,)),
            pltpu.SemaphoreType.DMA((n,)),
            pltpu.SemaphoreType.DMA((6,)),
        ],
        compiler_params=pltpu.CompilerParams(collective_id=0, has_side_effects=True),
    )(wp, wo, up, dn)


def positions_of(local, parity):
    return (2 * (local // 128) + parity) * 128 + lax.rem(local, 128)


def flash_kernel(info, q_ref, lo_ref, ko_ref, vo_ref, kx_ref, vx_ref, o_ref, low_ref, lse_ref, *, scale):
    tile = pl.program_id(0)
    parity = info[0]
    first = info[1 + tile]
    last = (tile * Q_TILE + Q_TILE + K_TILE - 1) // K_TILE
    q = q_ref[...]
    shape = (Q_TILE, K_TILE)
    q_pos = positions_of(tile * Q_TILE + lax.broadcasted_iota(jnp.int32, (Q_TILE, 1), 0), parity)
    lo = lo_ref[...]
    ones = jnp.ones((K_TILE, 128), bf16)

    def step(kt, carry):
        top, acc = carry
        rows = pl.ds(pl.multiple_of(kt * K_TILE, K_TILE), K_TILE)
        local = kt * K_TILE + lax.broadcasted_iota(jnp.int32, (1, K_TILE), 1)
        scores = []
        for k_ref, par in ((ko_ref, parity), (kx_ref, 1 - parity)):
            k_pos = positions_of(local, par)
            s = dot_nt(q, k_ref[rows, :])
            scores.append(jnp.where((k_pos >= lo) & (k_pos <= q_pos), s, -1e30))
        new = jnp.maximum(jnp.max(scores[0], axis=1, keepdims=True), jnp.max(scores[1], axis=1, keepdims=True))
        new = jnp.maximum(top, new)
        acc = acc * jnp.exp2((top - new) * (scale * LOG2E))
        for s, v_ref in zip(scores, (vo_ref, vx_ref)):
            p = jnp.exp2((s - new) * (scale * LOG2E)).astype(bf16)
            acc = acc + dot(p, jnp.concatenate([v_ref[rows, :], ones], axis=1))
        return new, acc

    top, acc = lax.fori_loop(
        first, last, step, (jnp.full((Q_TILE, 1), -1e30, f32), jnp.zeros((Q_TILE, 256), f32))
    )
    total = acc[:, 128:]
    o = acc[:, :128] / total
    o_ref[...] = o
    low_ref[...] = o.astype(bf16)
    lse = top * (scale * LOG2E) + jnp.log2(total)
    lse_ref[...] = jnp.transpose(lse)[0:8, :]


def flash_forward(info, q, lo, ko, vo, kx, vx, scale):
    rows = q.shape[0]
    tiles = rows // Q_TILE
    whole = pl.BlockSpec((rows, 128), lambda t, s: (0, 0))
    block = pl.BlockSpec((Q_TILE, 128), lambda t, s: (t, 0))
    return pl.pallas_call(
        functools.partial(flash_kernel, scale=scale),
        name="attention_forward",
        grid_spec=pltpu.PrefetchScalarGridSpec(
            num_scalar_prefetch=1,
            grid=(tiles,),
            in_specs=[block, pl.BlockSpec((Q_TILE, 1), lambda t, s: (t, 0)), whole, whole, whole, whole],
            out_specs=[block, block, pl.BlockSpec((8, Q_TILE), lambda t, s: (t, 0))],
        ),
        out_shape=[
            jax.ShapeDtypeStruct((rows, 128), f32),
            jax.ShapeDtypeStruct((rows, 128), bf16),
            jax.ShapeDtypeStruct((tiles * 8, Q_TILE), f32),
        ],
        compiler_params=pltpu.CompilerParams(vmem_limit_bytes=40 * MIB),
    )(info, q, lo, ko, vo, kx, vx)


def flash_back_kernel(info, q_ref, do_ref, lse_ref, delta_ref, lo_ref, k_ref, v_ref, dq_ref, dk_ref, dv_ref, dq_acc, *, scale):
    other = pl.program_id(0) == 0
    kt = pl.program_id(1)
    parity = info[0]
    k_parity = jnp.where(other, 1 - parity, parity)

    @pl.when(other & (kt == 0))
    def _():
        dq_acc[...] = jnp.zeros_like(dq_acc)

    k = k_ref[0]
    v = v_ref[0]
    k_pos = positions_of(kt * K_TILE + lax.broadcasted_iota(jnp.int32, (K_TILE, 1), 0), k_parity)
    first = kt * (K_TILE // Q_TILE)
    last = info[1 + kt]

    def step(qt, carry):
        dk, dv = carry
        rows = pl.ds(pl.multiple_of(qt * Q_TILE, Q_TILE), Q_TILE)
        q = q_ref[rows, :]
        do = do_ref[rows, :]
        q_pos = positions_of(qt * Q_TILE + lax.broadcasted_iota(jnp.int32, (1, Q_TILE), 1), parity)
        lo = lo_ref[pl.ds(qt, 1), :]
        lse = lse_ref[pl.ds(qt, 1), :]
        delta = delta_ref[pl.ds(qt, 1), :]
        s = dot_nt(k, q)
        p = jnp.exp2(jnp.where((k_pos >= lo) & (k_pos <= q_pos), s * (scale * LOG2E) - lse, -1e30))
        dv = dv + dot(p.astype(bf16), do)
        dp = dot_nt(v, do)
        ds = (p * (dp - delta) * scale).astype(bf16)
        dk = dk + dot(ds, q)
        dq_acc[rows, :] += dot_tn(ds, k)
        return dk, dv

    zero = jnp.zeros((K_TILE, 128), f32)
    dk, dv = lax.fori_loop(first, last, step, (zero, zero))
    dk_ref[0] = dk.astype(dk_ref.dtype)
    dv_ref[0] = dv.astype(dv_ref.dtype)

    @pl.when(jnp.logical_not(other) & (kt == pl.num_programs(1) - 1))
    def _():
        dq_ref[...] = dq_acc[...].astype(bf16)


def flash_backward(info, q, do, lse, delta, lo, k_two, v_two, scale):
    rows = q.shape[0]
    tiles = rows // K_TILE
    whole = pl.BlockSpec((rows, 128), lambda o, t, s: (0, 0))
    line = pl.BlockSpec((rows // Q_TILE, Q_TILE), lambda o, t, s: (0, 0))
    block = pl.BlockSpec((1, K_TILE, 128), lambda o, t, s: (o, t, 0))
    return pl.pallas_call(
        functools.partial(flash_back_kernel, scale=scale),
        name="attention_backward",
        grid_spec=pltpu.PrefetchScalarGridSpec(
            num_scalar_prefetch=1,
            grid=(2, tiles),
            in_specs=[whole, whole, line, line, line, block, block],
            out_specs=[whole, block, block],
            scratch_shapes=[pltpu.VMEM((rows, 128), f32)],
        ),
        out_shape=[
            jax.ShapeDtypeStruct((rows, 128), bf16),
            jax.ShapeDtypeStruct((2, rows, 128), f32),
            jax.ShapeDtypeStruct((2, rows, 128), f32),
        ],
        compiler_params=pltpu.CompilerParams(vmem_limit_bytes=40 * MIB),
    )(info, q, do, lse, delta, lo, k_two, v_two)


def per_device(
    tokens,
    document_starts,
    document_adapter,
    layernorm_gain,
    layernorm_bias,
    projection_weight,
    output_weight,
    up_weight,
    down_weight,
    projection_bias,
    upper_bias,
    attention_down_maps,
    attention_up_maps,
    upper_down_maps,
    upper_up_maps,
    lower_down_maps,
    lower_up_maps,
    cotangent,
):
    local_rows, width = tokens.shape[1:]
    head_size = width // HEADS
    seq = local_rows * 32
    scale = head_size ** (-0.5)
    starts = document_starts[0]
    chosen = document_adapter[0]
    xl, c, z, y, xh = (lax.axis_index(a) for a in AXES)
    stream = xl * 2 + c
    first_row = ((z * 4 + y) * 2 + xh) * local_rows
    local_pos = first_row + jnp.arange(local_rows, dtype=jnp.int32)
    local_seg = jnp.sum((starts[None, :] <= local_pos[:, None]).astype(jnp.int32), axis=1) - 1
    doc_ids = jnp.arange(starts.shape[0], dtype=jnp.int32)
    token_adapter = jnp.sum(jnp.where(local_seg[:, None] == doc_ids[None, :], chosen[None, :], 0), axis=1)
    columns = jnp.arange(upper_down_maps.shape[1], dtype=jnp.int32) // ADAPTER_RANK
    mask = (token_adapter[:, None] == columns[None, :]).astype(f32)

    rows = seq // 2
    q_pos = positions_of(jnp.arange(rows, dtype=jnp.int32), xh)
    doc_lo = jnp.max(jnp.where(starts[None, :] <= q_pos[:, None], starts[None, :], 0), axis=1)
    first_tile = (doc_lo[::Q_TILE] // 256) * 128 // K_TILE
    info = jnp.concatenate([xh[None], first_tile]).astype(jnp.int32)
    last_key = (2 * ((jnp.arange(rows // K_TILE) + 1) * K_TILE // 128 - 1) + 1) * 128 + 127
    doc_end = jnp.min(jnp.where(starts[None, :] > last_key[:, None], starts[None, :], seq), axis=1)
    last_q_tile = jnp.minimum((doc_end + 255) // 256 * 128 + Q_TILE - 1, rows + Q_TILE - 1) // Q_TILE
    info_back = jnp.concatenate([xh[None], last_q_tile]).astype(jnp.int32)

    inputs = tokens[0].astype(f32)
    qkv_all, out_all, up_all, dn_all = gather_weights(
        jnp.transpose(projection_weight, (1, 0, 2)), output_weight, up_weight, down_weight
    )
    w_qkv = qkv_all.reshape(3, width, width)
    w_out = out_all.reshape(width, width)
    w_up = up_all.reshape(width, -1)
    w_down = dn_all.reshape(-1, width)
    hidden = w_up.shape[1]

    def mine(array, axis):
        return lax.dynamic_slice_in_dim(array, stream * hidden, hidden, axis)

    normed_one, norm_one_back = jax.vjp(
        lambda v: layer_norm(v, layernorm_gain[0], layernorm_bias[0]), inputs
    )
    first_in = normed_one.astype(bf16)
    adapt_qkv = (
        jnp.einsum("td,pdr->ptr", first_in, attention_down_maps[:3], preferred_element_type=f32) * mask
    ).astype(bf16)
    bias_rows = jnp.stack([projection_bias[0], jnp.zeros_like(projection_bias[0]), projection_bias[1]])
    projected = (
        jnp.einsum("td,pde->pte", first_in, w_qkv, preferred_element_type=f32)
        + bias_rows[:, None, :]
        + jnp.einsum("ptr,pre->pte", adapt_qkv, attention_up_maps[:3], preferred_element_type=f32)
    )
    by_token = projected.astype(bf16).reshape(3, local_rows, HEADS, head_size)
    by_head = lax.all_to_all(by_token, HEAD, split_axis=2, concat_axis=1, tiled=True)
    by_head = by_head.reshape(3, rows, head_size)
    across = lax.ppermute(by_head[1:], "xh", [(0, 1), (1, 0)])
    queries = by_head[0]
    attended, attended_low, lse = flash_forward(
        info, queries, doc_lo[:, None], by_head[1], by_head[2], across[0], across[1], scale
    )
    lse = lse.reshape(rows // Q_TILE, 8, Q_TILE)[:, 0]
    back = lax.all_to_all(
        attended_low.reshape(HEADS, local_rows, head_size), HEAD, split_axis=0, concat_axis=0, tiled=True
    )
    merged = jnp.transpose(back, (1, 0, 2)).reshape(local_rows, width)

    adapt_out = (dot(merged, attention_down_maps[3]) * mask).astype(bf16)
    residual = inputs + dot(merged, w_out) + projection_bias[2] + dot(adapt_out, attention_up_maps[3])
    normed_two, norm_two_back = jax.vjp(
        lambda v: layer_norm(v, layernorm_gain[1], layernorm_bias[1]), residual
    )
    second_in = normed_two.astype(bf16)
    adapt_up = (dot(second_in, upper_down_maps) * mask).astype(bf16)
    cot = cotangent[0]
    grad_adapt_down = (dot_nt(cot, lower_up_maps) * mask).astype(bf16)

    def to_all(*arrays):
        return lax.all_gather(jnp.concatenate(arrays, axis=1), STREAM, axis=0, tiled=True)

    def to_owner(*arrays):
        return lax.psum_scatter(
            jnp.concatenate(arrays, axis=1).astype(bf16), STREAM, scatter_dimension=0, tiled=True
        ).astype(f32)

    cot_all = to_all(cot, grad_adapt_down)
    cot_all, gad_all = cot_all[:, :width], cot_all[:, width:]
    second_all = to_all(second_in, adapt_up)
    second_all, up_low_all = second_all[:, :width], second_all[:, width:]
    my_up_maps = mine(upper_up_maps, 1)
    my_down_maps = mine(lower_down_maps, 0)
    grad_act = dot_nt(cot_all, w_down) + dot_nt(gad_all, my_down_maps)
    pre_act = dot(second_all, w_up) + mine(upper_bias, 0) + dot(up_low_all, my_up_maps)
    activated, gelu_back = jax.vjp(exact_gelu, pre_act)
    act_low = activated.astype(bf16)
    grad_pre = gelu_back(grad_act)[0].astype(bf16)
    back_sum = to_owner(dot_nt(grad_pre, w_up), dot_nt(grad_pre, my_up_maps))
    forth_sum = to_owner(dot(act_low, w_down), dot(act_low, my_down_maps))
    grad_b_up = dot_tn(up_low_all, grad_pre)
    grad_a_down = dot_tn(act_low, gad_all)

    adapt_down = (forth_sum[:, width:] * mask).astype(bf16)
    output = residual + forth_sum[:, :width] + projection_bias[3] + dot(adapt_down, lower_up_maps)
    grad_b_down = dot_tn(adapt_down, cot)

    grad_adapt_up = (back_sum[:, width:] * mask).astype(bf16)
    grad_a_up = dot_tn(second_in, grad_adapt_up)
    grad_second = back_sum[:, :width] + dot_nt(grad_adapt_up, upper_down_maps)
    grad_residual = cot.astype(f32) + norm_two_back(grad_second)[0]
    grad_branch = grad_residual.astype(bf16)
    grad_b_out = dot_tn(adapt_out, grad_branch)
    grad_adapt_out = (dot_nt(grad_branch, attention_up_maps[3]) * mask).astype(bf16)
    grad_a_out = dot_tn(merged, grad_adapt_out)
    grad_merged = (dot_nt(grad_branch, w_out) + dot_nt(grad_adapt_out, attention_down_maps[3])).astype(bf16)

    grad_heads = lax.all_to_all(
        jnp.transpose(grad_merged.reshape(local_rows, HEADS, head_size), (1, 0, 2)),
        HEAD, split_axis=0, concat_axis=0, tiled=True,
    ).reshape(rows, head_size)
    row_dot = jnp.sum(grad_heads.astype(f32) * attended, axis=-1).reshape(rows // Q_TILE, Q_TILE)
    dq, dk, dv = flash_backward(
        info_back, queries, grad_heads, lse, row_dot, doc_lo.reshape(rows // Q_TILE, Q_TILE),
        jnp.stack([across[0], by_head[1]]), jnp.stack([across[1], by_head[2]]), scale,
    )
    from_other = lax.ppermute(jnp.stack([dk[0], dv[0]]).astype(bf16), "xh", [(0, 1), (1, 0)])
    dk = (dk[1] + from_other[0].astype(f32)).astype(bf16)
    dv = (dv[1] + from_other[1].astype(f32)).astype(bf16)
    grad_stack = jnp.stack([dq, dk, dv]).reshape(3, HEADS, local_rows, head_size)
    grad_tokens = lax.all_to_all(grad_stack, HEAD, split_axis=1, concat_axis=1, tiled=True)
    grad_qkv = jnp.transpose(grad_tokens, (0, 2, 1, 3)).reshape(3, local_rows, width)

    grad_b_qkv = jnp.einsum("ptr,pte->pre", adapt_qkv, grad_qkv, preferred_element_type=f32)
    grad_adapt_qkv = (
        jnp.einsum("pte,pre->ptr", grad_qkv, attention_up_maps[:3], preferred_element_type=f32) * mask
    ).astype(bf16)
    grad_a_qkv = jnp.einsum("td,ptr->pdr", first_in, grad_adapt_qkv, preferred_element_type=f32)
    grad_first = jnp.einsum("pte,pde->td", grad_qkv, w_qkv, preferred_element_type=f32) + jnp.einsum(
        "ptr,pdr->td", grad_adapt_qkv, attention_down_maps[:3], preferred_element_type=f32
    )
    input_grad = grad_residual + norm_one_back(grad_first)[0]

    grad_a_attn = jnp.concatenate([grad_a_qkv, grad_a_out[None]], axis=0)
    grad_b_attn = jnp.concatenate([grad_b_qkv, grad_b_out[None]], axis=0)
    sums = lax.psum((grad_a_attn, grad_b_attn, grad_a_up, grad_b_down), AXES)
    part_b, part_a = lax.psum((grad_b_up, grad_a_down), TOKEN)
    full_b_up = lax.all_gather(part_b, STREAM, axis=1, tiled=True)
    full_a_down = lax.all_gather(part_a, STREAM, axis=0, tiled=True)
    return (
        output.astype(bf16)[None],
        input_grad.astype(bf16)[None],
        sums[0],
        sums[1],
        sums[2],
        full_b_up,
        full_a_down,
        sums[3],
    )


def solution(mesh):
    fine = jax.sharding.Mesh(mesh.devices.reshape(SIZES), AXES)
    by_token = P(STREAM, TOKEN, None)
    shard = AXES
    in_specs = (
        by_token,
        P(STREAM, None),
        P(STREAM, None),
        P(),
        P(),
        P(shard, None, None),
        P(shard, None),
        P(shard, None),
        P(shard, None),
        P(),
        P(),
        P(),
        P(),
        P(),
        P(),
        P(),
        P(),
        by_token,
    )
    out_specs = (by_token, by_token, P(), P(), P(), P(), P(), P())
    return jax.shard_map(per_device, mesh=fine, in_specs=in_specs, out_specs=out_specs, check_vma=False)
```

time: 1930 us -> 1140 us (0.59)
  waiting for transfers between devices: 1520 us -> 661 us
  Pallas kernels: 0 us -> 223 us
  matrix products: 244 us -> 126 us
  blocking collectives: 46 us -> 13 us
    all_gather x6 -> x4, waiting for transfers between devices: 1300 us -> 21.4 us  [the longest x2 21.4 us: to_all(): lax.all_gather(jnp.concatenate(arrays, axis=1), STREAM, axis=0, tiled=True)]
    psum x1 -> x2, waiting for transfers between devices: 184 us -> 472 us  [the longest x1 317 us: per_device(): part_b, part_a = lax.psum((grad_b_up, grad_a_down), TOKEN)]
    pallas_call x0 -> x3, Pallas kernels: none -> 223 us  [the longest x1 169 us: gather_weights(): pl.pallas_call(weights_kernel, name='gather_weights', out_shape=[jax.Shap...]
    dot_general x38 -> x32, matrix products: 244 us -> 126 us  [the longest x9 38.5 us: dot(): return jnp.dot(left, right, preferred_element_type=f32)]
    ppermute x0 -> x2, waiting for transfers between devices: none -> 68.1 us  [the longest x1 36 us: per_device(): lax.ppermute(jnp.stack([dk[0], dv[0]]).astype(bf16), 'xh', [(0, 1), (1, 0)])]
    reduce_scatter x2, waiting for transfers between devices: 12.6 us -> 51.9 us  [to_owner(): lax.psum_scatter(jnp.concatenate(arrays, axis=1).astype(bf16), STREAM, sc...]
    all_to_all x2 -> x1, blocking collectives: 46 us -> 13 us  [per_device(): lax.all_to_all(attended_low.reshape(HEADS, local_rows, head_size), HEAD,...]
    all_to_all x2 -> x3, waiting for transfers between devices: 20.9 us -> 47.2 us  [the longest x1 24.5 us: per_device(): lax.all_to_all(by_token, HEAD, split_axis=2, concat_axis=1, tiled=True)]
  transfers between devices with their start and end apart: 11 -> 13, of which waited for: 9 -> 9; matrix products, arithmetic and copies ran while one was open for 11% -> 10% of each run, Pallas kernels for 0% -> 5%
where the time goes in v1:
time: 1140 us; the launch traced here: 1130 us
  waiting for transfers between devices  661 us (58%)
  Pallas kernels  223 us (20%)
  matrix products  126 us (11%)
  local copies, waits for them, and re-layouts  44.2 us (4%)
  starting transfers between devices  25.5 us (2%)
  other arithmetic  24.8 us (2%)
  between operations  15.3 us (1%)
  blocking collectives  13 us (1%)
    psum x1, waiting for transfers between devices, per_device(): part_b, part_a = lax.psum((grad_b_up, grad_a_down), TOKEN)  317 us
    pallas_call x1, Pallas kernels, gather_weights(): pl.pallas_call(weights_kernel, name='gather_weights', out_shape=[jax.Shap...  169 us
    psum x1, waiting for transfers between devices, per_device(): sums = lax.psum((grad_a_attn, grad_b_attn, grad_a_up, grad_b_down), AXES)  155 us
    reduce_scatter x2, waiting for transfers between devices, to_owner(): lax.psum_scatter(jnp.concatenate(arrays, axis=1).astype(bf16), STREAM, sc...  51.9 us
    dot_general x9, matrix products, dot(): return jnp.dot(left, right, preferred_element_type=f32)  38.5 us
    ppermute x1, waiting for transfers between devices, per_device(): lax.ppermute(jnp.stack([dk[0], dv[0]]).astype(bf16), 'xh', [(0, 1), (1, 0)])  36 us
    dot_general x9, matrix products, dot_nt(): lax.dot_general(left, right, (((1,), (1,)), ((), ())), preferred_element_...  35.2 us
    pallas_call x1, Pallas kernels, flash_backward(): pl.pallas_call(functools.partial(flash_back_kernel, scale=scale), name='a...  32.7 us
  transfers between devices with their start and end apart: 13, of which 9 were waited for; matrix products, arithmetic and copies ran while one was open for 10% of the time, Pallas kernels for 5%

profile of v1, /device:TPU:1, one launch (start us, length us, event | category | flops | bytes accessed | tf_op | source)
XLA Modules:
  0.0 1132.3 jit_solution(12355590656240726367)
XLA Ops:
  14.0 168.8 %gather_weights.1 = (bf16[3,2,2,4,4,2,16,2048]{7,6,5,4,3,2,1,0:T(8,128)(2,1)}, bf16[2,2,4,4,2,16,2048]{6,5,4,3,2,1,0:T(8,128)(2,1)}, bf16[2,2,4,4,2,16,2048]{6,5...) custom-call(bf16[3,16,2048]{2,1,0:T(8,128)(2,1)} %bitcast.222, bf16[16,2048]{1,0:T(8,128)(2,1)} %wo.1, bf16[16,8192]{1,0:T(8,128)(2,1)} %up.1, ...), custom_call_target="tpu_custom_call" | custom-call | tf_op jit(solution)/shard_map/gather_weights/pallas_call | solution.py:231
  182.8 15.5 %fusion.73 = f32[3,2048,128]{2,1,0:T(8,128)S(1)} fusion(bf16[3,2048,2048]{2,1,0:T(8,128)(2,1)} %bitcast.213, bf16[1,128,2048]{2,1,0:T(8,128)(2,1)} %param.18, f32[2048]{0:T(1024)S(1)} %bitcast.230, f32[2048]{0:T(1024)S(1)} %bitcast.223, f32[128]{0:T(128)S(1)} %fusion.111, f32[128]{0:T(128)S(1)} %broadcast_multiply_fusion.1), kind=kOutput, calls=%fused_computation.116 | convolution fusion | flops 3222798336 | bytes 28853248 | tf_op jit(solution)/shard_map/td,pde->pte/dot_general | solution.py:454
  210.4 24.5 %all-to-all-done = bf16[3,128,16,128]{3,1,0,2:T(8,128)(2,1)} async-done(((bf16[3,128,16,128]{3,1,0,2:T(8,128)(2,1)}), bf16[3,128,16,128]{3,1,0,2:T(8,128)(2,1)}, u32[]{:S(2)}, u32[]{:S(2)}) %all-to-all-start) | async-done | bytes 1572896 | tf_op jit(solution)/shard_map/all_to_all | solution.py:459
  245.1 32.1 %collective-permute-done = bf16[2,2048,128]{2,1,0:T(8,128)(2,1)} collective-permute-done((bf16[2,2048,128]{2,1,0:T(8,128)(2,1)}, bf16[2,2048,128]{2,1,0:T(8,128)(2,1)}, u32[]{:S(2)}, u32[]{:S(2)}) %collective-permute-start) | collective-permute-done | bytes 1048608 | tf_op jit(solution)/shard_map/ppermute | solution.py:461
  279.6 21.2 %attention_forward.1 = (f32[2048,128]{1,0:T(8,128)S(1)}, bf16[2048,128]{1,0:T(8,128)(2,1)S(1)}, f32[64,256]{1,0:T(8,128)S(1)}) custom-call(s32[9]{0:T(128)S(1)} %pad_add_fusion.info, bf16[2048,128]{1,0:T(8,128)(2,1)S(1)} %bitcast.201, s32[2048,1]{1,0:T(8,128)S(1)} %copy-done.5, bf16[2048,128]{1,0:T(8,128)(2,1)S(1)} %bitcast.205, ...), custom_call_target="tpu_custom_call" | custom-call | tf_op jit(solution)/shard_map/attention_forward/pallas_call | solution.py:299
  304.7 13.0 %all_to_all.30 = bf16[16,128,128]{1,2,0:T(8,128)(2,1)S(1)} all-to-all(bf16[16,128,128]{1,2,0:T(8,128)(2,1)} %copy.80), channel_id=1, replica_groups=mesh['xl'=2,'c'=2,'z'=4,'y'=4,'xh'=2] {'z','y'}, dimensions={0} | all-to-all | bytes 1048576 | tf_op jit(solution)/shard_map/all_to_all | solution.py:467
  328.4 10.6 fusion.14
  339.0 21.4 %all-gather.5.cloned.1.call-done = bf16[512,2176]{1,0:T(8,128)(2,1)} async-done(((bf16[128,2176]{1,0:T(8,128)(2,1)}), bf16[512,2176]{1,0:T(8,128)(2,1)}) %all-gather.5.cloned.1.call-update) | async-done | bytes 2228240 | tf_op jit(solution)/shard_map/all_gather | solution.py:483
  360.4 7.7 fusion.16
  368.1 10.5 multiply_convert_fusion
  391.3 8.6 convolution_convert_fusion
  404.0 8.1 convolution_convert_fusion.1
  413.8 316.7 %all-reduce.7.cloned.1.call-done = (f32[128,2048]{1,0:T(8,128)}, f32[2048,128]{1,0:T(8,128)}) async-done(((f32[128,2048]{1,0:T(8,128)}, f32[2048,128]{1,0:T(8,128)}), (f32[128,2048]{1,0:T(8,128)}, f32[2048,128]{1,0:T(8,128)})) %all-reduce.7.cloned.1.call-update) | async-done | bytes 2097168 | tf_op jit(solution)/shard_map/psum | solution.py:549
  731.3 51.9 %reduce-scatter.5.cloned.1.call-done = bf16[128,2176]{1,0:T(8,128)(2,1)} async-done(((bf16[512,2176]{1,0:T(8,128)(2,1)}), bf16[128,2176]{1,0:T(8,128)(2,1)}) %reduce-scatter.5.cloned.1.call-update) | async-done | bytes 557072 | tf_op jit(solution)/shard_map/reduce_scatter | solution.py:486
  786.9 6.4 fusion.132
  797.1 6.9 all-to-all-start.2
  806.5 8.2 all-to-all-done.2
  817.5 32.7 %attention_backward.1 = (bf16[2048,128]{1,0:T(8,128)(2,1)S(1)}, f32[2,2048,128]{2,1,0:T(8,128)S(1)}, f32[2,2048,128]{2,1,0:T(8,128)S(1)}) custom-call(s32[5]{0:T(128)S(1)} %pad_add_fusion.1.info, bf16[2048,128]{1,0:T(8,128)(2,1)S(1)} %bitcast.202, bf16[2048,128]{1,0:T(8,128)(2,1)S(1)} %bitcast.200, f32[8,256]{1,0:T(8,128)S(1)} %bitcast.209, ...), custom_call_target="tpu_custom_call" | custom-call | tf_op jit(solution)/shard_map/attention_backward/pallas_call | solution.py:367
  852.9 36.0 %collective-permute-done.1 = bf16[2,2048,128]{2,1,0:T(8,128)(2,1)S(1)} collective-permute-done((bf16[2,2048,128]{2,1,0:T(8,128)(2,1)S(1)}, bf16[2,2048,128]{2,1,0:T(8,128)(2,1)S(1)}, u32[]{:S(2)}, u32[]{:S(2)}) %collective-permute-start.1) | collective-permute-done | bytes 1048608 | tf_op jit(solution)/shard_map/ppermute | solution.py:529
  890.5 7.1 all-to-all-start.3
  905.0 14.5 %all-to-all-done.3 = bf16[3,16,128,128]{3,2,0,1:T(8,128)(2,1)} async-done(((bf16[3,16,128,128]{3,2,0,1:T(8,128)(2,1)}), bf16[3,16,128,128]{3,2,0,1:T(8,128)(2,1)}, u32[]{:S(2)}, u32[]{:S(2)}) %all-to-all-start.3) | async-done | bytes 1572896 | tf_op jit(solution)/shard_map/all_to_all | solution.py:533
  936.3 14.0 %fusion.64 = (f32[128]{0:T(128)S(1)}, f32[128,2048]{1,0:T(8,128)S(1)}) fusion(bf16[1,128,2048]{2,1,0:T(8,128)(2,1)S(1)} %copy-done.12, f32[128]{0:T(128)S(1)} %broadcast_multiply_fusion.1, f32[2048]{0:T(1024)S(1)} %bitcast.226, f32[128,2048]{1,0:T(8,128)} %convolution_bitcast_fusion.4, bf16[3,2048,2048]{2,1,0:T(8,128)(2,1)} %bitcast.214, ...), kind=kOutput, calls=%fused_computation.91 | convolution fusion | flops 3222798336 | bytes 29369344 | tf_op jit(solution)/shard_map/pte,pde->td/dot_general | solution.py:541
  952.0 155.2 %all-reduce.5.cloned.1.call-done = (f32[4,2048,128]{1,2,0:T(8,128)}, f32[4,128,2048]{2,1,0:T(8,128)}, f32[2048,128]{1,0:T(8,128)}, f32[128,2048]{1,0:T(8,128)}) async-done(((f32[4,2048,128]{1,2,0:T(8,128)}, f32[4,128,2048]{2,1,0:T(8,128)}, f32[2048,128]{1,0:T(8,128)}, f32[128,2048]{1,0:T(8,128)}), (f32[4,2048,128]{1,2,0:T(8,128)}, f32[4,128,2048]{2,1,0:T(8,128)}, f32[2048,128]{1,0:T(8,128)}, ...) | async-done | bytes 10485776 | tf_op jit(solution)/shard_map/psum | solution.py:548
  1107.2 5.3 copy.94
  (203 shorter events, 120.1 us)
Async XLA Ops:
  7.2 360.9 %copy-start = (bf16[128,8192]{1,0:T(8,128)(2,1)S(1)}, bf16[128,8192]{1,0:T(8,128)(2,1)}, u32[]{:S(2)}) copy-start(bf16[128,8192]{1,0:T(8,128)(2,1)} %param.32) | copy-start | bytes 6291460
  182.8 15.6 %copy-start.11 = (bf16[1,128,2048]{2,1,0:T(8,128)(2,1)S(1)}, bf16[1,128,2048]{2,1,0:T(8,128)(2,1)}, u32[]{:S(2)}) copy-start(bf16[1,128,2048]{2,1,0:T(8,128)(2,1)} %param.18) | copy-start | bytes 1572868
  182.8 15.6 %copy-start.36 = (bf16[4,2048,128]{2,1,0:T(8,128)(2,1)S(1)}, bf16[4,2048,128]{2,1,0:T(8,128)(2,1)}, u32[]{:S(2)}) copy-start(bf16[4,2048,128]{2,1,0:T(8,128)(2,1)} %param.29) | copy-start | bytes 6291460
  204.9 30.0 %all-to-all-start = ((bf16[3,128,16,128]{3,1,0,2:T(8,128)(2,1)}), bf16[3,128,16,128]{3,1,0,2:T(8,128)(2,1)}, u32[]{:S(2)}, u32[]{:S(2)}) async-start(bf16[3,128,16,128]{3,1,0,2:T(8,128)(2,1)} %copy.77), calls=%async_computation | async-start | bytes 3145728 | tf_op jit(solution)/shard_map/all_to_all | solution.py:459
  210.0 31.8 %copy-start.41 = (s32[1,8]{1,0:T(1,128)S(1)}, s32[1,8]{1,0:T(1,128)}, u32[]{:S(2)}) copy-start(s32[1,8]{1,0:T(1,128)} %param.19) | copy-start | bytes 100
  210.0 118.4 %all-gather.7.cloned.1.call-start = ((), (), s32[]{:S(2)}) async-start(), calls=%async_computation.8 | async-start | bytes 2785280 | tf_op jit(solution)/shard_map/all_gather | solution.py:483
  237.3 39.9 %collective-permute-start = (bf16[2,2048,128]{2,1,0:T(8,128)(2,1)}, bf16[2,2048,128]{2,1,0:T(8,128)(2,1)}, u32[]{:S(2)}, u32[]{:S(2)}) collective-permute-start(bf16[2,2048,128]{2,1,0:T(8,128)(2,1)} %bitcast.21), channel_id=1, source_target_pairs={{0,1},{1,0},{2,3},{3,2},{4,5},{5,4},{6,7},{7,6},{8,9},{9,8},{10,11... | collective-permute-start | bytes 3145736 | tf_op jit(solution)/shard_map/ppermute | solution.py:461
  241.8 118.6 %all-gather.5.cloned.1.call-start = ((), (), s32[]{:S(2)}) async-start(), calls=%async_computation.6 | async-start | bytes 2785280 | tf_op jit(solution)/shard_map/all_gather | solution.py:483
  243.4 36.2 %copy-start.5 = (s32[2048,1]{1,0:T(8,128)S(1)}, s32[2048,1]{1,0:T(8,128)}, u32[]{:S(2)}) copy-start(s32[2048,1]{1,0:T(8,128)} %copy.79.lo_ref) | copy-start | bytes 24580
  245.1 34.6 %copy-start.2 = (bf16[1,16,128,1,128]{4,2,0,1,3:T(8,128)(2,1)}, bf16[1,16,128,1,128]{4,2,0,1,3:T(8,128)(2,1)S(1)}, u32[]{:S(2)}) copy-start(bf16[1,16,128,1,128]{4,2,0,1,3:T(8,128)(2,1)S(1)} %get-tuple-element.71) | copy-start | bytes 1572868
  328.4 402.1 %all-reduce.7.cloned.1.call-start = ((), (), s32[]{:S(2)}) async-start(), calls=%async_computation.13 | async-start | bytes 4194304 | tf_op jit(solution)/shard_map/psum | solution.py:549
  388.9 394.2 %reduce-scatter.5.cloned.1.call-start = ((), (), s32[]{:S(2)}) async-start(), calls=%async_computation.9 | async-start | bytes 2785280 | tf_op jit(solution)/shard_map/reduce_scatter | solution.py:486
  401.5 496.2 %reduce-scatter.3.cloned.1.call-start = ((), (), s32[]{:S(2)}) async-start(), calls=%async_computation.7 | async-start | bytes 2785280 | tf_op jit(solution)/shard_map/reduce_scatter | solution.py:486
  412.1 372.2 %copy-start.9 = (f32[128,2048]{1,0:T(8,128)S(1)}, f32[128,2048]{1,0:T(8,128)}, u32[]{:S(2)}) copy-start(f32[128,2048]{1,0:T(8,128)} %copy-done.8) | copy-start | bytes 3145732
  412.1 372.2 %copy-start.32 = (bf16[2048,128]{1,0:T(8,128)(2,1)S(1)}, bf16[2048,128]{1,0:T(8,128)(2,1)}, u32[]{:S(2)}) copy-start(bf16[2048,128]{1,0:T(8,128)(2,1)} %param.31) | copy-start | bytes 1572868
  413.7 538.3 %all-gather.9.cloned.1.call-start = ((), (), s32[]{:S(2)}) async-start(), calls=%async_computation.10 | async-start | bytes 5242880 | tf_op jit(solution)/shard_map/all_gather | solution.py:550
  730.5 221.5 %all-gather.11.cloned.1.call-start = ((), (), s32[]{:S(2)}) async-start(), calls=%async_computation.11 | async-start | bytes 5242880 | tf_op jit(solution)/shard_map/all_gather | solution.py:551
  730.8 55.9 %copy-start.14 = (bf16[1,128,2048]{2,1,0:T(8,128)(2,1)S(1)}, bf16[1,128,2048]{2,1,0:T(8,128)(2,1)}, u32[]{:S(2)}) copy-start(bf16[1,128,2048]{2,1,0:T(8,128)(2,1)} %param.35) | copy-start | bytes 1572868
  797.1 17.6 %all-to-all-start.2 = ((bf16[16,128,128]{2,1,0:T(8,128)(2,1)}), bf16[16,128,128]{2,1,0:T(8,128)(2,1)S(1)}, u32[]{:S(2)}, u32[]{:S(2)}) async-start(bf16[16,128,128]{2,1,0:T(8,128)(2,1)} %bitcast.198), calls=%async_computation.4 | async-start | bytes 1048576 | tf_op jit(solution)/shard_map/all_to_all | solution.py:520
  850.5 38.5 %collective-permute-start.1 = (bf16[2,2048,128]{2,1,0:T(8,128)(2,1)S(1)}, bf16[2,2048,128]{2,1,0:T(8,128)(2,1)S(1)}, u32[]{:S(2)}, u32[]{:S(2)}) collective-permute-start(bf16[2,2048,128]{2,1,0:T(8,128)(2,1)S(1)} %pad_maximum_fusion.7), channel_id=1, source_target_pairs={{0,1},{1,0},{2,3},{3,2},{4,5},{5,4},{6,7},{7,6},{8,9},{9,8},{10,11... | collective-permute-start | bytes 3145736 | tf_op jit(solution)/shard_map/ppermute | solution.py:529
  890.5 29.1 %all-to-all-start.3 = ((bf16[3,16,128,128]{3,2,0,1:T(8,128)(2,1)}), bf16[3,16,128,128]{3,2,0,1:T(8,128)(2,1)}, u32[]{:S(2)}, u32[]{:S(2)}) async-start(bf16[3,16,128,128]{3,2,0,1:T(8,128)(2,1)} %pad_maximum_fusion.4), calls=%async_computation.5 | async-start | bytes 3145728 | tf_op jit(solution)/shard_map/all_to_all | solution.py:533
  897.6 209.6 %all-reduce.5.cloned.1.call-start = ((), (), s32[]{:S(2)}) async-start(), calls=%async_computation.12 | async-start | bytes 20971520 | tf_op jit(solution)/shard_map/psum | solution.py:548
  901.4 20.6 %copy-start.12 = (bf16[1,128,2048]{2,1,0:T(8,128)(2,1)S(1)}, bf16[1,128,2048]{2,1,0:T(8,128)(2,1)}, u32[]{:S(2)}) copy-start(bf16[1,128,2048]{2,1,0:T(8,128)(2,1)} %param.18) | copy-start | bytes 1572868
  905.0 17.7 %copy-start.29 = (f32[1,2048,128]{1,2,0:T(8,128)S(1)}, f32[1,2048,128]{1,2,0:T(8,128)}, u32[]{:S(2)}) copy-start(f32[1,2048,128]{1,2,0:T(8,128)} %convolution_bitcast_fusion.3) | copy-start | bytes 3145732
  (33 other events, 171.7 us)
Sparse Core Ops, SparseCore 0:
  241.9 41.3 all-gather.6
  328.5 31.8 all-gather.4
  389.1 341.3 all-reduce.6
  733.5 49.6 reduce-scatter.4
  786.2 30.3 reduce-scatter.2
  818.2 61.5 all-gather.8
  881.5 52.0 all-gather.10
  940.9 166.2 all-reduce.4

commit v2 on v1

v2 whole, which is shorter than its diff:
```python
import functools

import jax
import jax.numpy as jnp
import numpy as np
from jax import lax
from jax.experimental import pallas as pl
from jax.experimental.pallas import tpu as pltpu
from jax.sharding import PartitionSpec as P

HEADS = 16
ADAPTER_RANK = 16
MESH = pl.DeviceIdType.MESH
AXES = ("xl", "c", "z", "y", "xh")
SIZES = (2, 2, 4, 4, 2)
STREAM = ("xl", "c")
TOKEN = ("z", "y", "xh")
HEAD = ("z", "y")
bf16 = jnp.bfloat16
f32 = jnp.float32
LOG2E = 1.4426950408889634
MIB = 2**20
Q_TILE = 256
K_TILE = 512


def layer_norm(values, gain, shift):
    center = values - jnp.mean(values, axis=-1, keepdims=True)
    spread = jnp.mean(center * center, axis=-1, keepdims=True)
    return center * lax.rsqrt(spread + 1e-05) * gain + shift


def dot(left, right):
    return jnp.dot(left, right, preferred_element_type=f32)


def dot_nt(left, right):
    return lax.dot_general(left, right, (((1,), (1,)), ((), ())), preferred_element_type=f32)


def dot_tn(left, right):
    return lax.dot_general(left, right, (((0,), (0,)), ((), ())), preferred_element_type=f32)


def exact_gelu(values):
    return jax.nn.gelu(values, approximate=False)


class Place:
    def __init__(self):
        self.xl, self.c, self.z, self.y, self.xh = (lax.axis_index(a) for a in AXES)
        self.x = self.xh * 2 + self.xl

    def at(self, axis):
        return {"x": self.x, "y": self.y, "z": self.z, "xh": self.xh}[axis]

    def toward(self, axis, step):
        if axis == "c":
            return {"c": 1 - self.c}
        if axis == "xh":
            return {"xh": 1 - self.xh}
        to = lax.rem(self.at(axis) + (step + 4), 4)
        if axis == "x":
            return {"xl": lax.rem(to, 2), "xh": to // 2}
        return {axis: to}


class Sends:
    def __init__(self, send, recv):
        self.send, self.recv, self.used, self.open = send, recv, 0, []

    def push(self, src, dst, device):
        k = self.used
        self.used += 1
        copy = pltpu.make_async_remote_copy(
            src_ref=src,
            dst_ref=dst,
            send_sem=self.send.at[k],
            recv_sem=self.recv.at[k],
            device_id=device,
            device_id_type=MESH,
        )
        copy.start()
        self.open.append(copy)
        return copy


def greet(devices):
    barrier = pltpu.get_barrier_semaphore()
    for device in devices:
        pl.semaphore_signal(barrier, inc=1, device_id=device, device_id_type=MESH)
    pl.semaphore_wait(barrier, len(devices))


def run_all(parts):
    parts = list(parts)
    while parts:
        left = []
        for part in parts:
            try:
                next(part)
                left.append(part)
            except StopIteration:
                pass
        parts = left


ALL = slice(None)


def ring_gather(place, sends, view, order, chunk, landed, forward):
    fixed = {a: place.at(a) for a in order}
    across = place.toward("c", 1)
    later, passed = [], []

    def pass_on(block):
        if forward:
            passed.append(sends.push(view(block, None), view(block, None), across))

    if forward:
        passed.append(sends.push(chunk, view(fixed, None), across))
    for number, axis in enumerate(order):
        own = view(fixed, None)
        src = chunk if number == 0 else own
        here = place.at(axis)
        if axis == "xh" or number == 0:
            steps = (1,) if axis == "xh" else (2, 1, 3)
            sent = [sends.push(src, own, place.toward(axis, s)) for s in steps]
            yield
            for s, copy in zip(steps, sent):
                copy.wait_recv()
                size = 2 if axis == "xh" else 4
                pass_on(dict(fixed) | {axis: lax.rem(here + size - s, size)})
            if number == 0:
                landed.wait()
            later += sent
            del fixed[axis]
            continue
        up = sends.push(src, own, place.toward(axis, 1))
        down = sends.push(src, own, place.toward(axis, -1))
        yield
        before = dict(fixed) | {axis: lax.rem(here + 3, 4)}
        after = dict(fixed) | {axis: lax.rem(here + 1, 4)}
        opposite = dict(fixed) | {axis: lax.rem(here + 2, 4)}
        up.wait_recv()
        half = view(before, 0)
        up_two = sends.push(half, half, place.toward(axis, 1))
        down.wait_recv()
        half = view(after, 1)
        down_two = sends.push(half, half, place.toward(axis, -1))
        pass_on(before)
        pass_on(after)
        yield
        up_two.wait_recv()
        down_two.wait_recv()
        pass_on(opposite)
        later += [up, down, up_two, down_two]
        del fixed[axis]
    yield
    for copy in later:
        copy.wait_send()
    for copy in passed:
        copy.wait()


class Nothing:
    def wait(self):
        pass


def neighbours(place, axes):
    return [place.toward(a, s) for a in axes for s in ((1, 2, 3) if a in "xyz" else (1,))]


def stream_gather(place, sends, pairs, local, first_local):
    across, over = {"c": 1 - place.c}, {"xl": 1 - place.xl}
    mine = place.xl * 2 + place.c
    theirs = (1 - place.xl) * 2 + place.c
    sent, passed, kept = [], [], []
    for n, (src, dst) in enumerate(pairs):
        sent.append(sends.push(src, dst.at[mine], over))
        passed.append(sends.push(src, dst.at[mine], across))
        copy = pltpu.make_async_copy(src, dst.at[mine], local.at[first_local + n])
        copy.start()
        kept.append(copy)
    yield
    for copy, (src, dst) in zip(sent, pairs):
        copy.wait_recv()
        passed.append(sends.push(dst.at[theirs], dst.at[theirs], across))
    yield
    for copy in sent:
        copy.wait_send()
    for copy in passed + kept:
        copy.wait()


def stream_gather_kernel(a, b, a_all, b_all, send, recv, local):
    place = Place()
    greet([{"c": 1 - place.c}, {"xl": 1 - place.xl}])
    pieces = [(a.at[pl.ds(r, 32)], a_all.at[:, pl.ds(r, 32)]) for r in range(0, 128, 32)] + [(b, b_all)]
    run_all([stream_gather(place, Sends(send, recv), pieces, local, 0)])


def gather_stream(a, b):
    any_ = pl.BlockSpec(memory_space=pl.ANY)
    return pl.pallas_call(
        stream_gather_kernel,
        name="gather_stream",
        out_shape=[jax.ShapeDtypeStruct((4,) + v.shape, v.dtype) for v in (a, b)],
        in_specs=[any_] * 2,
        out_specs=[any_] * 2,
        scratch_shapes=[pltpu.SemaphoreType.DMA((n,)) for n in (15, 15, 5)],
        compiler_params=pltpu.CompilerParams(collective_id=1, has_side_effects=True),
    )(a, b)


def stream_sum(place, sends, pairs):
    across, over = {"c": 1 - place.c}, {"xl": 1 - place.xl}
    mine = place.xl * 2 + place.c
    theirs = (1 - place.xl) * 2 + place.c
    far, near = [], []
    for parts, from_core, _, _, _ in pairs:
        far.append(sends.push(parts.at[(1 - place.xl) * 2 + 1 - place.c], from_core.at[1], across))
    for parts, from_core, _, _, _ in pairs:
        near.append(sends.push(parts.at[place.xl * 2 + 1 - place.c], from_core.at[0], across))
    gone = []
    for copy, (parts, from_core, leaving, from_chip, _) in zip(far, pairs):
        copy.wait()
        leaving[...] = (parts[theirs].astype(f32) + from_core[1].astype(f32)).astype(bf16)
        gone.append(sends.push(leaving, from_chip, over))
    yield
    for copy, back, (parts, from_core, _, from_chip, result) in zip(near, gone, pairs):
        copy.wait()
        back.wait()
        result[...] = parts[mine].astype(f32) + from_core[0].astype(f32) + from_chip[...].astype(f32)


def stream_sum_scratch(arrays):
    shapes = []
    for a in arrays:
        one = a.shape[1:]
        shapes += [pltpu.VMEM((2,) + one, bf16), pltpu.VMEM(one, bf16), pltpu.VMEM(one, bf16)]
    return shapes


def stream_sum_kernel(a, b, a_sum, b_sum, a_core, a_leave, a_chip, b_core, b_leave, b_chip, send, recv):
    place = Place()
    greet([{"c": 1 - place.c}, {"xl": 1 - place.xl}])
    pairs = [(a, a_core, a_leave, a_chip, a_sum), (b, b_core, b_leave, b_chip, b_sum)]
    run_all([stream_sum(place, Sends(send, recv), pairs)])


def sum_stream(a, b):
    vmem = pl.BlockSpec(memory_space=pltpu.VMEM)
    return pl.pallas_call(
        stream_sum_kernel,
        name="sum_stream",
        out_shape=[jax.ShapeDtypeStruct(v.shape[1:], f32) for v in (a, b)],
        in_specs=[vmem] * 2,
        out_specs=[vmem] * 2,
        scratch_shapes=stream_sum_scratch((a, b)) + [pltpu.SemaphoreType.DMA((6,)), pltpu.SemaphoreType.DMA((6,))],
        compiler_params=pltpu.CompilerParams(collective_id=2, has_side_effects=True, vmem_limit_bytes=40 * MIB),
    )(a, b)


def plane(place):
    steps = [(i, j) for i in (2, 1, 3, 0) for j in (2, 1, 3, 0) if i or j]
    return [(lax.rem(place.z + i, 4), lax.rem(place.y + j, 4)) for i, j in steps]


def from_plane(place):
    steps = [(i, j) for i in (2, 1, 3, 0) for j in (2, 1, 3, 0) if i or j]
    return [(lax.rem(place.z + 4 - i, 4), lax.rem(place.y + 4 - j, 4)) for i, j in steps]


def head_columns(z, y):
    return pl.ds(pl.multiple_of((z * 4 + y) * 128, 128), 128)


def greet_plane(place, more=()):
    greet([{"z": z, "y": y} for z, y in plane(place)] + list(more))


def to_heads_kernel(qkv, mine, others, send, recv, local):
    place = Place()
    partner = {"xh": 1 - place.xh}
    greet_plane(place, [partner])
    sends = Sends(send, recv)
    here = place.z * 4 + place.y
    own = qkv.at[:, :, head_columns(place.z, place.y)]
    keep = pltpu.make_async_copy(own, mine.at[:, here], local.at[0])
    keep.start()
    kv = pl.ds(1, 2)
    swaps = [sends.push(qkv.at[kv, :, head_columns(place.z, place.y)], others.at[:, here], partner)]
    sent = []
    for z, y in plane(place):
        sent.append(sends.push(qkv.at[:, :, head_columns(z, y)], mine.at[:, here], {"z": z, "y": y}))
    for copy, (z, y) in zip(sent, from_plane(place)):
        copy.wait_recv()
        at = z * 4 + y
        swaps.append(sends.push(mine.at[kv, at], others.at[:, at], partner))
    for copy in sent:
        copy.wait_send()
    for copy in swaps:
        copy.wait()
    keep.wait()


def to_heads(qkv):
    any_ = pl.BlockSpec(memory_space=pl.ANY)
    return pl.pallas_call(
        to_heads_kernel,
        name="to_heads",
        out_shape=[jax.ShapeDtypeStruct((3, 16, 128, 128), bf16), jax.ShapeDtypeStruct((2, 16, 128, 128), bf16)],
        in_specs=[any_],
        out_specs=[any_] * 2,
        scratch_shapes=[pltpu.SemaphoreType.DMA((n,)) for n in (31, 31, 1)],
        compiler_params=pltpu.CompilerParams(collective_id=3, has_side_effects=True),
    )(qkv)


def heads_out(place, sends, blocks, merged, local):
    cols = head_columns(place.z, place.y)
    keep = pltpu.make_async_copy(blocks.at[place.z * 4 + place.y], merged.at[:, cols], local)
    keep.start()
    sent = [sends.push(blocks.at[z * 4 + y], merged.at[:, cols], {"z": z, "y": y}) for z, y in plane(place)]
    yield
    for copy in sent:
        copy.wait()
    keep.wait()


def to_tokens_kernel(blocks, merged, send, recv, local):
    place = Place()
    greet_plane(place)
    run_all([heads_out(place, Sends(send, recv), blocks, merged, local.at[0])])


def to_tokens(blocks):
    any_ = pl.BlockSpec(memory_space=pl.ANY)
    return pl.pallas_call(
        to_tokens_kernel,
        name="to_tokens",
        out_shape=jax.ShapeDtypeStruct((128, 2048), bf16),
        in_specs=[any_],
        out_specs=any_,
        scratch_shapes=[pltpu.SemaphoreType.DMA((n,)) for n in (15, 15, 1)],
        compiler_params=pltpu.CompilerParams(collective_id=4, has_side_effects=True),
    )(blocks)


def grads_in_kernel(
    grad, a, b, heads, a_sum, b_sum, a_core, a_leave, a_chip, b_core, b_leave, b_chip, send, recv, local
):
    place = Place()
    greet_plane(place, [{"c": 1 - place.c}, {"xl": 1 - place.xl}])
    sends = Sends(send, recv)

    def heads_part():
        here = place.z * 4 + place.y
        keep = pltpu.make_async_copy(grad.at[:, head_columns(place.z, place.y)], heads.at[here], local.at[0])
        keep.start()
        sent = [
            sends.push(grad.at[:, head_columns(z, y)], heads.at[here], {"z": z, "y": y}) for z, y in plane(place)
        ]
        yield
        for copy in sent:
            copy.wait()
        keep.wait()

    pairs = [(a, a_core, a_leave, a_chip, a_sum), (b, b_core, b_leave, b_chip, b_sum)]
    run_all([heads_part(), stream_sum(place, sends, pairs)])


def grads_in(grad, a, b):
    any_ = pl.BlockSpec(memory_space=pl.ANY)
    vmem = pl.BlockSpec(memory_space=pltpu.VMEM)
    return pl.pallas_call(
        grads_in_kernel,
        name="grads_in",
        out_shape=[jax.ShapeDtypeStruct((16, 128, 128), bf16)]
        + [jax.ShapeDtypeStruct(v.shape[1:], f32) for v in (a, b)],
        in_specs=[any_] + [vmem] * 2,
        out_specs=[any_] + [vmem] * 2,
        scratch_shapes=stream_sum_scratch((a, b)) + [pltpu.SemaphoreType.DMA((n,)) for n in (21, 21, 1)],
        compiler_params=pltpu.CompilerParams(collective_id=5, has_side_effects=True, vmem_limit_bytes=40 * MIB),
    )(grad, a, b)


def grads_out_kernel(dq, other, own, grads, came, sums, send, recv, local):
    place = Place()
    partner = {"xh": 1 - place.xh}
    greet_plane(place, [partner])
    sends = Sends(send, recv)
    cols = head_columns(place.z, place.y)
    here = place.z * 4 + place.y
    places = plane(place) + [(place.z, place.y)]
    swaps = [sends.push(other.at[z * 4 + y], came.at[z * 4 + y], partner) for z, y in places]
    keep = pltpu.make_async_copy(dq.at[here], grads.at[0, :, cols], local.at[0])
    keep.start()
    sent = [sends.push(dq.at[z * 4 + y], grads.at[0, :, cols], {"z": z, "y": y}) for z, y in places[:-1]]
    for n, (copy, (z, y)) in enumerate(zip(swaps, places)):
        copy.wait_recv()
        at = z * 4 + y
        sums[at] = (came[at].astype(f32) + own[at]).astype(bf16)
        if n < 15:
            sent.append(sends.push(sums.at[at], grads.at[pl.ds(1, 2), :, cols], {"z": z, "y": y}))
    last = pltpu.make_async_copy(sums.at[here], grads.at[pl.ds(1, 2), :, cols], local.at[1])
    last.start()
    for copy in swaps:
        copy.wait_send()
    for copy in sent:
        copy.wait()
    keep.wait()
    last.wait()


def grads_out(dq, other, own):
    any_ = pl.BlockSpec(memory_space=pl.ANY)
    vmem = pl.BlockSpec(memory_space=pltpu.VMEM)
    return pl.pallas_call(
        grads_out_kernel,
        name="grads_out",
        out_shape=jax.ShapeDtypeStruct((3, 128, 2048), bf16),
        in_specs=[vmem] * 3,
        out_specs=any_,
        scratch_shapes=[pltpu.VMEM((16, 2, 128, 128), bf16)] * 2
        + [pltpu.SemaphoreType.DMA((n,)) for n in (46, 46, 2)],
        compiler_params=pltpu.CompilerParams(collective_id=6, has_side_effects=True, vmem_limit_bytes=40 * MIB),
    )(dq, other, own)


ORDERS = (("x", "y", "z"), ("y", "z", "x"), ("z", "x", "y"))


def spread_sum(place, sends, order, steps, first, result_view, final, landed, across):
    if across:
        src, came, own, out = first
        copy = sends.push(src, came, place.toward("c", 1))
        yield
        copy.wait()
        out[...] = (own[...].astype(f32) + came[...].astype(f32)).astype(bf16)
    for axis, (held, slots, out) in zip(order, steps):
        size = 2 if axis == "xh" else 4
        here = place.at(axis)
        hops = (1,) if size == 2 else (2, 1, 3)
        sent = [
            sends.push(held(lax.rem(here + d, size)), slots.at[d - 1], place.toward(axis, d)) for d in hops
        ]
        yield
        for copy in sent:
            copy.wait()
        total = held(here)[...].astype(f32)
        for d in hops:
            total = total + slots[d - 1].astype(f32)
        out[...] = total.astype(bf16)
    landed.start()
    yield from ring_gather(place, sends, result_view[0], result_view[1], final, landed, True)


def rows_of(ref, size):
    return lambda p: ref.at[pl.ds(pl.multiple_of(p * size, size), size)]


def cols_of(ref, size):
    return lambda p: ref.at[:, pl.ds(pl.multiple_of(p * size, size), size)]


def sums_kernel(count, early, *refs):
    refs = list(refs)
    a, b = refs[:2]
    del refs[:2]
    if early:
        a_two, b_two = refs[:2]
        del refs[:2]
    a_res, b_res = refs[:2]
    del refs[:2]
    if early:
        a_two_res, b_two_res = refs[:2]
        del refs[:2]
    scratch, (send, recv, local) = refs[:-3], refs[-3:]
    place = Place()
    sends = Sends(send, recv)
    greet(neighbours(place, ("x", "y", "z", "c")))
    parts = []
    mine, theirs = place.c, 1 - place.c

    def line(fixed, axis):
        return fixed.get(axis, ALL)

    def a_view(i, order):
        def view(fixed, half):
            at = [line(fixed, x) for x in order]
            if half is not None:
                k = max(n for n in range(3) if order[n] not in fixed)
                at[k] = pl.ds(half * 2, 2)
            return a_res.at[(i, place.c) + tuple(at)]

        return view

    def b_view(i, order):
        def view(fixed, half):
            start, size = 0, 2048
            if order[1] in fixed:
                start, size = fixed[order[1]] * 512, 512
            if order[2] in fixed:
                start, size = start + fixed[order[2]] * 128, 128
            if half is not None:
                size = size // 2
                start = start + half * size
            cols = pl.ds(start, size) if isinstance(start, int) else pl.ds(pl.multiple_of(start, 128), size)
            return b_res.at[i, place.c, line(fixed, order[0]), :, cols]

        return view

    for i in range(count):
        order = ORDERS[i % 3]
        ca, ha, sa1, qa, sa2, ra, sa3, fa, cb, hb, sb1, qb, sb2, rb, sb3, fb = scratch[:16]
        del scratch[:16]
        half = lambda c, n: pl.ds(pl.multiple_of(c * n, n), n)
        keep = pltpu.make_async_copy(
            fa, a_view(i, order)({x: place.at(x) for x in order}, None), local.at[2 * i]
        )
        parts.append(
            spread_sum(
                place, sends, order,
                [(rows_of(ha, 256), sa1, qa), (rows_of(qa, 64), sa2, ra), (rows_of(ra, 16), sa3, fa)],
                (a.at[i, half(theirs, 1024)], ca, a.at[i, half(mine, 1024)], ha),
                (a_view(i, order), order[::-1]), fa, keep, True,
            )
        )
        keep = pltpu.make_async_copy(
            fb, b_view(i, order)({x: place.at(x) for x in order}, None), local.at[2 * i + 1]
        )
        parts.append(
            spread_sum(
                place, sends, order,
                [(rows_of(hb, 16), sb1, qb), (cols_of(qb, 512), sb2, rb), (cols_of(rb, 128), sb3, fb)],
                (b.at[i, half(theirs, 64)], cb, b.at[i, half(mine, 64)], hb),
                (b_view(i, order), order[::-1]), fb, keep, True,
            )
        )
    if early:
        sa1, qa, sa2, ra, sa3, fa, sb1, qb, sb2, rb, sb3, fb = scratch

        def two(ref):
            def view(fixed, half):
                xl, xh = (ALL, ALL)
                if "x" in fixed:
                    xl, xh = lax.rem(fixed["x"], 2), fixed["x"] // 2
                if half is not None:
                    xl = pl.ds(half, 1)
                return ref.at[xl, place.c, line(fixed, "z"), line(fixed, "y"), xh]

            return view

        home = {x: place.at(x) for x in "xyz"}
        keep = pltpu.make_async_copy(fa, two(a_two_res)(home, None), local.at[2 * count])
        parts.append(
            spread_sum(
                place, sends, ("z", "y", "xh"),
                [(rows_of(a_two, 512), sa1, qa), (rows_of(qa, 128), sa2, ra), (rows_of(ra, 64), sa3, fa)],
                None, (two(a_two_res), ("x", "z", "y")), fa, keep, False,
            )
        )
        keep = pltpu.make_async_copy(fb, two(b_two_res)(home, None), local.at[2 * count + 1])
        parts.append(
            spread_sum(
                place, sends, ("y", "z", "xh"),
                [(rows_of(b_two, 32), sb1, qb), (cols_of(qb, 512), sb2, rb), (cols_of(rb, 256), sb3, fb)],
                None, (two(b_two_res), ("x", "y", "z")), fb, keep, False,
            )
        )
    run_all(parts)


def sum_all(collective_id, a, b, a_two=None, b_two=None):
    count = a.shape[0]
    early = a_two is not None
    vm = lambda *shape: pltpu.VMEM(shape, bf16)
    scratch = []
    for _ in range(count):
        scratch += [vm(1024, 128), vm(1024, 128), vm(3, 256, 128), vm(256, 128), vm(3, 64, 128), vm(64, 128)]
        scratch += [vm(3, 16, 128), vm(16, 128)]
        scratch += [vm(64, 2048), vm(64, 2048), vm(3, 16, 2048), vm(16, 2048), vm(3, 16, 512), vm(16, 512)]
        scratch += [vm(3, 16, 128), vm(16, 128)]
    shapes = [(count, 2, 4, 4, 4, 16, 128), (count, 2, 4, 16, 2048)]
    ins = [a, b]
    if early:
        scratch += [vm(3, 512, 128), vm(512, 128), vm(3, 128, 128), vm(128, 128), vm(1, 64, 128), vm(64, 128)]
        scratch += [vm(3, 32, 2048), vm(32, 2048), vm(3, 32, 512), vm(32, 512), vm(1, 32, 256), vm(32, 256)]
        shapes += [(2, 2, 4, 4, 2, 64, 128), (2, 2, 4, 4, 2, 32, 256)]
        ins += [a_two, b_two]
    n = 62 * count + (60 if early else 0)
    out = pl.pallas_call(
        functools.partial(sums_kernel, count, early),
        name="sum_all",
        out_shape=[jax.ShapeDtypeStruct(s, bf16) for s in shapes],
        in_specs=[pl.BlockSpec(memory_space=pltpu.VMEM)] * len(ins),
        out_specs=[pl.BlockSpec(memory_space=pl.ANY)] * len(shapes),
        scratch_shapes=scratch
        + [pltpu.SemaphoreType.DMA((k,)) for k in (n, n, 2 * count + 2)],
        compiler_params=pltpu.CompilerParams(
            collective_id=collective_id, has_side_effects=True, vmem_limit_bytes=48 * MIB
        ),
    )(*ins)
    result = [out[0].reshape(count, 2048, 128), out[1].reshape(count, 128, 2048)]
    if early:
        result.append(out[2].reshape(8192, 128))
        result.append(jnp.transpose(out[3], (3, 5, 0, 1, 2, 4, 6)).reshape(128, 8192))
    return result


def weights_kernel(wp, wo, up, dn, cot, gad, qkv_all, out_all, up_all, dn_all, cot_all, gad_all, send, recv, local):
    place = Place()
    sends = Sends(send, recv)
    mates = [{"c": 1 - place.c}, {"xl": 1 - place.xl}, {"xl": 1 - place.xl, "c": 1 - place.c}]
    greet([mates[0], mates[2]] + neighbours(place, ("x", "y", "z")))
    home = (place.xl, place.c, place.z, place.y, place.xh)

    halves = {None: ALL, 0: pl.ds(0, 1024), 1: pl.ds(1024, 1024)}

    def whole(ref, lead):
        def view(fixed, half):
            columns = halves[half]
            xl, xh = (ALL, ALL)
            if "x" in fixed:
                xl, xh = lax.rem(fixed["x"], 2), fixed["x"] // 2
            return ref.at[lead + (xl, place.c, fixed.get("z", ALL), fixed.get("y", ALL), xh, ALL, columns)]

        return view

    def up_view(fixed, half):
        columns = halves[half]
        return up_all.at[ALL, ALL, fixed.get("z", ALL), fixed.get("y", ALL), fixed.get("xh", ALL), ALL, columns]

    def dn_view(fixed, half):
        columns = halves[half]
        return dn_all.at[fixed.get("z", ALL), fixed.get("y", ALL), fixed.get("xh", ALL), ALL, columns]

    stream = place.xl * 2 + place.c

    def cols(device):
        to = device.get("xl", place.xl) * 2 + device.get("c", place.c)
        return pl.ds(pl.multiple_of(to * 2048, 2048), 2048)

    copies = [pltpu.make_async_copy(wp.at[p], qkv_all.at[(p,) + home], local.at[p]) for p in range(3)]
    copies.append(pltpu.make_async_copy(wo, out_all.at[home], local.at[3]))
    copies.append(pltpu.make_async_copy(dn, dn_all.at[home[2:]], local.at[4]))
    copies.append(pltpu.make_async_copy(up.at[:, cols({})], up_all.at[home], local.at[5]))
    for copy in copies:
        copy.start()
    spread = [sends.push(up.at[:, cols(m)], up_all.at[home], m) for m in mates]

    class Many:
        def wait(self):
            copies[5].wait()
            for s in spread:
                s.wait()

    def up_part():
        yield
        Many().wait()
        fixed = {"xh": place.xh, "y": place.y, "z": place.z}
        yield from ring_gather(place, sends, up_view, ("xh", "y", "z"), up_view(fixed, None), Nothing(), False)

    parts = [
        stream_gather(place, sends, ((cot, cot_all), (gad, gad_all)), local, 6),
        ring_gather(place, sends, whole(qkv_all, (0,)), ("y", "z", "x"), wp.at[0], copies[0], True),
        ring_gather(place, sends, whole(qkv_all, (1,)), ("z", "y", "x"), wp.at[1], copies[1], True),
        ring_gather(place, sends, whole(qkv_all, (2,)), ("x", "y", "z"), wp.at[2], copies[2], True),
        ring_gather(place, sends, whole(out_all, ()), ("x", "z", "y"), wo, copies[3], True),
        up_part(),
        ring_gather(place, sends, dn_view, ("xh", "z", "y"), dn, copies[4], False),
    ]
    run_all(parts)


def gather_weights(wp, wo, up, dn, cot, gad):
    n = 180
    any_ = pl.BlockSpec(memory_space=pl.ANY)
    return pl.pallas_call(
        weights_kernel,
        name="gather_weights",
        out_shape=[
            jax.ShapeDtypeStruct((3, 2, 2, 4, 4, 2, 16, 2048), bf16),
            jax.ShapeDtypeStruct((2, 2, 4, 4, 2, 16, 2048), bf16),
            jax.ShapeDtypeStruct((2, 2, 4, 4, 2, 16, 2048), bf16),
            jax.ShapeDtypeStruct((4, 4, 2, 64, 2048), bf16),
            jax.ShapeDtypeStruct((4, 128, 2048), bf16),
            jax.ShapeDtypeStruct((4, 128, 128), bf16),
        ],
        in_specs=[any_] * 6,
        out_specs=[any_] * 6,
        scratch_shapes=[
            pltpu.SemaphoreType.DMA((n,)),
            pltpu.SemaphoreType.DMA((n,)),
            pltpu.SemaphoreType.DMA((8,)),
        ],
        compiler_params=pltpu.CompilerParams(collective_id=0, has_side_effects=True),
    )(wp, wo, up, dn, cot, gad)


def positions_of(local, parity):
    return (2 * (local // 128) + parity) * 128 + lax.rem(local, 128)


def flash_kernel(info, lo_ref, q_ref, ko_ref, vo_ref, kx_ref, vx_ref, o_ref, low_ref, lse_ref, *, scale):
    tile = pl.program_id(0)
    parity = info[0]
    first = info[1 + tile]
    last = (tile * Q_TILE + Q_TILE + K_TILE - 1) // K_TILE
    q = q_ref[0]
    q_pos = positions_of(tile * Q_TILE + lax.broadcasted_iota(jnp.int32, (Q_TILE, 1), 0), parity)
    lo = lo_ref[...]
    ones = jnp.ones((K_TILE, 128), bf16)

    def step(kt, carry):
        top, acc = carry
        rows = pl.ds(pl.multiple_of(kt * K_TILE, K_TILE), K_TILE)
        local = kt * K_TILE + lax.broadcasted_iota(jnp.int32, (1, K_TILE), 1)
        scores = []
        for k_ref, par in ((ko_ref, parity), (kx_ref, 1 - parity)):
            k_pos = positions_of(local, par)
            s = dot_nt(q, k_ref[0, rows, :])
            scores.append(jnp.where((k_pos >= lo) & (k_pos <= q_pos), s, -1e30))
        new = jnp.maximum(jnp.max(scores[0], axis=1, keepdims=True), jnp.max(scores[1], axis=1, keepdims=True))
        new = jnp.maximum(top, new)
        acc = acc * jnp.exp2((top - new) * (scale * LOG2E))
        for s, v_ref in zip(scores, (vo_ref, vx_ref)):
            p = jnp.exp2((s - new) * (scale * LOG2E)).astype(bf16)
            acc = acc + dot(p, jnp.concatenate([v_ref[0, rows, :], ones], axis=1))
        return new, acc

    top, acc = lax.fori_loop(
        first, last, step, (jnp.full((Q_TILE, 1), -1e30, f32), jnp.zeros((Q_TILE, 256), f32))
    )
    total = acc[:, 128:]
    o = acc[:, :128] / total
    o_ref[...] = o
    low_ref[...] = o.astype(bf16)
    lse = top * (scale * LOG2E) + jnp.log2(total)
    lse_ref[...] = jnp.transpose(lse)[0:8, :]


def flash_forward(info, lo, by_head, across, scale):
    rows = by_head.shape[1]
    tiles = rows // Q_TILE
    whole = lambda n: pl.BlockSpec((1, rows, 128), lambda t, s: (n, 0, 0))
    block = pl.BlockSpec((Q_TILE, 128), lambda t, s: (t, 0))
    return pl.pallas_call(
        functools.partial(flash_kernel, scale=scale),
        name="attention_forward",
        grid_spec=pltpu.PrefetchScalarGridSpec(
            num_scalar_prefetch=1,
            grid=(tiles,),
            in_specs=[
                pl.BlockSpec((Q_TILE, 1), lambda t, s: (t, 0)),
                pl.BlockSpec((1, Q_TILE, 128), lambda t, s: (0, t, 0)),
                whole(1), whole(2), whole(0), whole(1),
            ],
            out_specs=[block, block, pl.BlockSpec((8, Q_TILE), lambda t, s: (t, 0))],
        ),
        out_shape=[
            jax.ShapeDtypeStruct((rows, 128), f32),
            jax.ShapeDtypeStruct((rows, 128), bf16),
            jax.ShapeDtypeStruct((tiles * 8, Q_TILE), f32),
        ],
        compiler_params=pltpu.CompilerParams(vmem_limit_bytes=40 * MIB),
    )(info, lo, by_head, by_head, by_head, across, across)


def flash_back_kernel(
    info, q_ref, do_ref, lse_ref, delta_ref, lo_ref, ko_ref, vo_ref, kx_ref, vx_ref, dq_ref, other_ref, own_ref, dq_acc, *, scale
):
    kt = pl.program_id(0)
    parity = info[0]

    @pl.when(kt == 0)
    def _():
        dq_acc[...] = jnp.zeros_like(dq_acc)

    first = kt * (K_TILE // Q_TILE)
    last = info[1 + kt]
    blocks = K_TILE // 128
    for k_ref, v_ref, k_parity, out in ((kx_ref, vx_ref, 1 - parity, other_ref), (ko_ref, vo_ref, parity, own_ref)):
        k = k_ref[0]
        v = v_ref[0]
        k_pos = positions_of(kt * K_TILE + lax.broadcasted_iota(jnp.int32, (K_TILE, 1), 0), k_parity)

        def step(qt, carry):
            dk, dv = carry
            rows = pl.ds(pl.multiple_of(qt * Q_TILE, Q_TILE), Q_TILE)
            q = q_ref[0, rows, :]
            do = do_ref[rows, :]
            q_pos = positions_of(qt * Q_TILE + lax.broadcasted_iota(jnp.int32, (1, Q_TILE), 1), parity)
            lo = lo_ref[pl.ds(qt, 1), :]
            lse = lse_ref[pl.ds(qt, 1), :]
            delta = delta_ref[pl.ds(qt, 1), :]
            s = dot_nt(k, q)
            p = jnp.exp2(jnp.where((k_pos >= lo) & (k_pos <= q_pos), s * (scale * LOG2E) - lse, -1e30))
            dv = dv + dot(p.astype(bf16), do)
            dp = dot_nt(v, do)
            ds = (p * (dp - delta) * scale).astype(bf16)
            dk = dk + dot(ds, q)
            dq_acc[rows, :] += dot_tn(ds, k)
            return dk, dv

        zero = jnp.zeros((K_TILE, 128), f32)
        dk, dv = lax.fori_loop(first, last, step, (zero, zero))
        for b in range(blocks):
            out[b, 0] = dk[b * 128 : (b + 1) * 128].astype(out.dtype)
            out[b, 1] = dv[b * 128 : (b + 1) * 128].astype(out.dtype)

    @pl.when(kt == pl.num_programs(0) - 1)
    def _():
        dq_ref[...] = dq_acc[...].astype(bf16)


def flash_backward(info, do, lse, delta, lo, by_head, across, scale):
    rows = do.shape[0]
    tiles = rows // K_TILE
    whole = pl.BlockSpec((rows, 128), lambda t, s: (0, 0))
    line = pl.BlockSpec((rows // Q_TILE, Q_TILE), lambda t, s: (0, 0))
    block = lambda n: pl.BlockSpec((1, K_TILE, 128), lambda t, s: (n, t, 0))
    grads = pl.BlockSpec((K_TILE // 128, 2, 128, 128), lambda t, s: (t, 0, 0, 0))
    return pl.pallas_call(
        functools.partial(flash_back_kernel, scale=scale),
        name="attention_backward",
        grid_spec=pltpu.PrefetchScalarGridSpec(
            num_scalar_prefetch=1,
            grid=(tiles,),
            in_specs=[
                pl.BlockSpec((1, rows, 128), lambda t, s: (0, 0, 0)),
                whole, line, line, line, block(1), block(2), block(0), block(1),
            ],
            out_specs=[whole, grads, grads],
            scratch_shapes=[pltpu.VMEM((rows, 128), f32)],
        ),
        out_shape=[
            jax.ShapeDtypeStruct((rows, 128), bf16),
            jax.ShapeDtypeStruct((rows // 128, 2, 128, 128), bf16),
            jax.ShapeDtypeStruct((rows // 128, 2, 128, 128), f32),
        ],
        compiler_params=pltpu.CompilerParams(vmem_limit_bytes=40 * MIB),
    )(info, by_head, do, lse, delta, lo, by_head, by_head, across, across)


def per_device(
    tokens,
    document_starts,
    document_adapter,
    layernorm_gain,
    layernorm_bias,
    projection_weight,
    output_weight,
    up_weight,
    down_weight,
    projection_bias,
    upper_bias,
    attention_down_maps,
    attention_up_maps,
    upper_down_maps,
    upper_up_maps,
    lower_down_maps,
    lower_up_maps,
    cotangent,
):
    local_rows, width = tokens.shape[1:]
    head_size = width // HEADS
    seq = local_rows * 32
    scale = head_size ** (-0.5)
    starts = document_starts[0]
    chosen = document_adapter[0]
    xl, c, z, y, xh = (lax.axis_index(a) for a in AXES)
    stream = xl * 2 + c
    first_row = ((z * 4 + y) * 2 + xh) * local_rows
    local_pos = first_row + jnp.arange(local_rows, dtype=jnp.int32)
    local_seg = jnp.sum((starts[None, :] <= local_pos[:, None]).astype(jnp.int32), axis=1) - 1
    doc_ids = jnp.arange(starts.shape[0], dtype=jnp.int32)
    token_adapter = jnp.sum(jnp.where(local_seg[:, None] == doc_ids[None, :], chosen[None, :], 0), axis=1)
    columns = jnp.arange(upper_down_maps.shape[1], dtype=jnp.int32) // ADAPTER_RANK
    mask = (token_adapter[:, None] == columns[None, :]).astype(f32)

    rows = seq // 2
    q_pos = positions_of(jnp.arange(rows, dtype=jnp.int32), xh)
    doc_lo = jnp.max(jnp.where(starts[None, :] <= q_pos[:, None], starts[None, :], 0), axis=1)
    first_tile = (doc_lo[::Q_TILE] // 256) * 128 // K_TILE
    info = jnp.concatenate([xh[None], first_tile]).astype(jnp.int32)
    last_key = (2 * ((jnp.arange(rows // K_TILE) + 1) * K_TILE // 128 - 1) + 1) * 128 + 127
    doc_end = jnp.min(jnp.where(starts[None, :] > last_key[:, None], starts[None, :], seq), axis=1)
    last_q_tile = jnp.minimum((doc_end + 255) // 256 * 128 + Q_TILE - 1, rows + Q_TILE - 1) // Q_TILE
    info_back = jnp.concatenate([xh[None], last_q_tile]).astype(jnp.int32)

    inputs = tokens[0].astype(f32)
    cot = cotangent[0]
    grad_adapt_down = (dot_nt(cot, lower_up_maps) * mask).astype(bf16)
    qkv_all, out_all, up_all, dn_all, cot_all, gad_all = gather_weights(
        jnp.transpose(projection_weight, (1, 0, 2)), output_weight, up_weight, down_weight, cot, grad_adapt_down
    )
    w_qkv = qkv_all.reshape(3, width, width)
    w_out = out_all.reshape(width, width)
    w_up = up_all.reshape(width, -1)
    w_down = dn_all.reshape(-1, width)
    cot_all = cot_all.reshape(-1, width)
    gad_all = gad_all.reshape(-1, 128)
    hidden = w_up.shape[1]

    def mine(array, axis):
        return lax.dynamic_slice_in_dim(array, stream * hidden, hidden, axis)

    normed_one, norm_one_back = jax.vjp(
        lambda v: layer_norm(v, layernorm_gain[0], layernorm_bias[0]), inputs
    )
    first_in = normed_one.astype(bf16)
    adapt_qkv = (
        jnp.einsum("td,pdr->ptr", first_in, attention_down_maps[:3], preferred_element_type=f32) * mask
    ).astype(bf16)
    bias_rows = jnp.stack([projection_bias[0], jnp.zeros_like(projection_bias[0]), projection_bias[1]])
    projected = (
        jnp.einsum("td,pde->pte", first_in, w_qkv, preferred_element_type=f32)
        + bias_rows[:, None, :]
        + jnp.einsum("ptr,pre->pte", adapt_qkv, attention_up_maps[:3], preferred_element_type=f32)
    )
    by_head, across = to_heads(projected.astype(bf16))
    by_head = by_head.reshape(3, rows, head_size)
    across = across.reshape(2, rows, head_size)
    attended, attended_low, lse = flash_forward(info, doc_lo[:, None], by_head, across, scale)
    lse = lse.reshape(rows // Q_TILE, 8, Q_TILE)[:, 0]
    merged = to_tokens(attended_low.reshape(HEADS, local_rows, head_size))

    adapt_out = (dot(merged, attention_down_maps[3]) * mask).astype(bf16)
    residual = inputs + dot(merged, w_out) + projection_bias[2] + dot(adapt_out, attention_up_maps[3])
    normed_two, norm_two_back = jax.vjp(
        lambda v: layer_norm(v, layernorm_gain[1], layernorm_bias[1]), residual
    )
    second_in = normed_two.astype(bf16)
    adapt_up = (dot(second_in, upper_down_maps) * mask).astype(bf16)

    second_all, up_low_all = gather_stream(second_in, adapt_up)
    second_all = second_all.reshape(-1, width)
    up_low_all = up_low_all.reshape(-1, 128)
    my_up_maps = mine(upper_up_maps, 1)
    my_down_maps = mine(lower_down_maps, 0)
    grad_act = dot_nt(cot_all, w_down) + dot_nt(gad_all, my_down_maps)
    pre_act = dot(second_all, w_up) + mine(upper_bias, 0) + dot(up_low_all, my_up_maps)
    activated, gelu_back = jax.vjp(exact_gelu, pre_act)
    act_low = activated.astype(bf16)
    grad_pre = gelu_back(grad_act)[0].astype(bf16)

    def parts_of(value):
        return value.astype(bf16).reshape(4, local_rows, -1)

    back_sum, back_adapt = sum_stream(
        parts_of(dot_nt(grad_pre, w_up)), parts_of(dot_nt(grad_pre, my_up_maps))
    )
    grad_b_up = dot_tn(up_low_all, grad_pre)
    grad_a_down = dot_tn(act_low, gad_all)

    grad_adapt_up = (back_adapt * mask).astype(bf16)
    grad_a_up = dot_tn(second_in, grad_adapt_up)
    grad_second = back_sum + dot_nt(grad_adapt_up, upper_down_maps)
    grad_residual = cot.astype(f32) + norm_two_back(grad_second)[0]
    grad_branch = grad_residual.astype(bf16)
    grad_b_out = dot_tn(adapt_out, grad_branch)
    grad_adapt_out = (dot_nt(grad_branch, attention_up_maps[3]) * mask).astype(bf16)
    grad_a_out = dot_tn(merged, grad_adapt_out)
    grad_merged = (dot_nt(grad_branch, w_out) + dot_nt(grad_adapt_out, attention_down_maps[3])).astype(bf16)

    grad_heads, forth_sum, forth_adapt = grads_in(
        grad_merged, parts_of(dot(act_low, w_down)), parts_of(dot(act_low, my_down_maps))
    )
    adapt_down = (forth_adapt * mask).astype(bf16)
    output = residual + forth_sum + projection_bias[3] + dot(adapt_down, lower_up_maps)
    grad_b_down = dot_tn(adapt_down, cot)

    grad_heads = grad_heads.reshape(rows, head_size)
    row_dot = jnp.sum(grad_heads.astype(f32) * attended, axis=-1).reshape(rows // Q_TILE, Q_TILE)
    dq, other, own = flash_backward(
        info_back, grad_heads, lse, row_dot, doc_lo.reshape(rows // Q_TILE, Q_TILE), by_head, across, scale
    )
    grad_qkv = grads_out(dq.reshape(HEADS, local_rows, head_size), other, own)

    grad_b_qkv = jnp.einsum("ptr,pte->pre", adapt_qkv, grad_qkv, preferred_element_type=f32)
    grad_adapt_qkv = (
        jnp.einsum("pte,pre->ptr", grad_qkv, attention_up_maps[:3], preferred_element_type=f32) * mask
    ).astype(bf16)
    grad_a_qkv = jnp.einsum("td,ptr->pdr", first_in, grad_adapt_qkv, preferred_element_type=f32)
    grad_first = jnp.einsum("pte,pde->td", grad_qkv, w_qkv, preferred_element_type=f32) + jnp.einsum(
        "ptr,pdr->td", grad_adapt_qkv, attention_down_maps[:3], preferred_element_type=f32
    )
    input_grad = grad_residual + norm_one_back(grad_first)[0]

    early = sum_all(
        7,
        jnp.stack([grad_a_out, grad_a_up]).astype(bf16),
        jnp.stack([grad_b_out, grad_b_down]).astype(bf16),
        grad_a_down.astype(bf16),
        grad_b_up.astype(bf16),
    )
    late = sum_all(8, grad_a_qkv.astype(bf16), grad_b_qkv.astype(bf16))
    return (
        output.astype(bf16)[None],
        input_grad.astype(bf16)[None],
        jnp.concatenate([late[0], early[0][:1]]).astype(f32),
        jnp.concatenate([late[1], early[1][:1]]).astype(f32),
        early[0][1].astype(f32),
        early[3].astype(f32),
        early[2].astype(f32),
        early[1][1].astype(f32),
    )


def solution(mesh):
    fine = jax.sharding.Mesh(mesh.devices.reshape(SIZES), AXES)
    by_token = P(STREAM, TOKEN, None)
    shard = AXES
    in_specs = (
        by_token,
        P(STREAM, None),
        P(STREAM, None),
        P(),
        P(),
        P(shard, None, None),
        P(shard, None),
        P(shard, None),
        P(shard, None),
        P(),
        P(),
        P(),
        P(),
        P(),
        P(),
        P(),
        P(),
        by_token,
    )
    out_specs = (by_token, by_token, P(), P(), P(), P(), P(), P())
    return jax.shard_map(per_device, mesh=fine, in_specs=in_specs, out_specs=out_specs, check_vma=False)
```

time: 1140 us -> 623 us (0.55)
  waiting for transfers between devices: 661 us -> 0 us
  Pallas kernels: 223 us -> 455 us
  starting transfers between devices: 25.5 us -> 0 us
  local copies, waits for them, and re-layouts: 44.2 us -> 22.3 us
  matrix products: 126 us -> 110 us
  between operations: 15.3 us -> 1.7 us
  blocking collectives: 13 us -> 0 us
    psum x2 -> x0, waiting for transfers between devices: 472 us -> none  [the longest x1 317 us: per_device(): part_b, part_a = lax.psum((grad_b_up, grad_a_down), TOKEN)]
    pallas_call x0 -> x8, Pallas kernels: none -> 230 us  [the longest x2 96.4 us: sum_all(): pl.pallas_call(functools.partial(sums_kernel, count, early), name='sum_al...]
    ppermute x2 -> x0, waiting for transfers between devices: 68.1 us -> none  [the longest x1 36 us: per_device(): lax.ppermute(jnp.stack([dk[0], dv[0]]).astype(bf16), 'xh', [(0, 1), (1, 0)])]
    reduce_scatter x2 -> x0, waiting for transfers between devices: 51.9 us -> none  [to_owner(): lax.psum_scatter(jnp.concatenate(arrays, axis=1).astype(bf16), STREAM, sc...]
    all_to_all x3 -> x0, waiting for transfers between devices: 47.2 us -> none  [the longest x1 24.5 us: per_device(): lax.all_to_all(by_token, HEAD, split_axis=2, concat_axis=1, tiled=True)]
    all_gather x4 -> x0, waiting for transfers between devices: 21.4 us -> none  [the longest x2 21.4 us: to_all(): lax.all_gather(jnp.concatenate(arrays, axis=1), STREAM, axis=0, tiled=True)]
    unnamed x93 -> x85, local copies, waits for them, and re-layouts: 28 us -> 7.24 us
    all_to_all x3 -> x0, starting transfers between devices: 19.1 us -> none  [the longest x1 7.08 us: per_device(): lax.all_to_all(grad_stack, HEAD, split_axis=1, concat_axis=1, tiled=True)]
  transfers between devices with their start and end apart: 13 -> 0, of which waited for: 9 -> 0; matrix products, arithmetic and copies ran while one was open for 10% -> 0% of each run, Pallas kernels for 5% -> 0%
where the time goes in v2:
time: 623 us; the launch traced here: 615 us
  Pallas kernels  455 us (73%)
  matrix products  110 us (18%)
  other arithmetic  26.2 us (4%)
  local copies, waits for them, and re-layouts  22.3 us (4%)
    pallas_call x1, Pallas kernels, gather_weights(): pl.pallas_call(weights_kernel, name='gather_weights', out_shape=[jax.Shap...  172 us
    pallas_call x2, Pallas kernels, sum_all(): pl.pallas_call(functools.partial(sums_kernel, count, early), name='sum_al...  96.4 us
    dot_general x9, matrix products, dot(): return jnp.dot(left, right, preferred_element_type=f32)  37.1 us
    pallas_call x1, Pallas kernels, to_heads(): pl.pallas_call(to_heads_kernel, name='to_heads', out_shape=[jax.ShapeDtyp...  33.2 us
    pallas_call x1, Pallas kernels, flash_backward(): pl.pallas_call(functools.partial(flash_back_kernel, scale=scale), name='a...  31.7 us
    dot_general x9, matrix products, dot_nt(): lax.dot_general(left, right, (((1,), (1,)), ((), ())), preferred_element_...  29.9 us
    pallas_call x1, Pallas kernels, grads_out(): pl.pallas_call(grads_out_kernel, name='grads_out', out_shape=jax.ShapeDty...  27.4 us
    pallas_call x1, Pallas kernels, flash_forward(): pl.pallas_call(functools.partial(flash_kernel, scale=scale), name='attent...  21.4 us

profile of v2, /device:TPU:1, one launch (start us, length us, event | category | flops | bytes accessed | tf_op | source)
XLA Modules:
  0.0 615.4 jit_solution(1860596051725014154)
XLA Ops:
  14.2 171.7 %gather_weights.1 = (bf16[3,2,2,4,4,2,16,2048]{7,6,5,4,3,2,1,0:T(8,128)(2,1)}, bf16[2,2,4,4,2,16,2048]{6,5,4,3,2,1,0:T(8,128)(2,1)}, bf16[2,2,4,4,2,16,2048]{6,5...) custom-call(bf16[3,16,2048]{2,1,0:T(8,128)(2,1)} %bitcast.218, ...), custom_call_target="tpu_custom_call" | custom-call | tf_op jit(solution)/shard_map/gather_weights/pallas_call | solution.py:682
  185.9 10.7 %fusion.61 = f32[3,2048,128]{1,2,0:T(8,128)S(1)} fusion(bf16[3,2048,2048]{2,1,0:T(8,128)(2,1)} %bitcast.202, bf16[1,128,2048]{2,1,0:T(8,128)(2,1)} %param.18, f32[2048]{0:T(1024)S(1)} %bitcast.216, f32[2048]{0:T(1024)S(1)} %bitcast.212, f32[128]{0:T(128)S(1)} %fusion.93, f32[128]{0:T(128)S(1)} %broadcast_multiply_fusion.1), kind=kOutput, calls=%fused_computation.104 | convolution fusion | flops 3222798336 | bytes 28853248 | tf_op jit(solution)/shard_map/td,pde->pte/dot_general | solution.py:921
  198.4 33.2 %to_heads.1 = (bf16[3,16,128,128]{3,2,1,0:T(8,128)(2,1)}, bf16[2,16,128,128]{3,2,1,0:T(8,128)(2,1)}) custom-call(bf16[3,128,2048]{2,1,0:T(8,128)(2,1)} %fusion.6.qkv), custom_call_target="tpu_custom_call" | custom-call | tf_op jit(solution)/shard_map/to_heads/pallas_call | solution.py:311
  234.3 21.4 %attention_forward.1 = (f32[2048,128]{1,0:T(8,128)S(1)}, bf16[2048,128]{1,0:T(8,128)(2,1)S(1)}, f32[64,256]{1,0:T(8,128)S(1)}) custom-call(s32[9]{0:T(128)S(1)} %pad_add_fusion.info, s32[2048,1]{1,0:T(8,128)S(1)} %copy.41.lo_ref, bf16[3,2048,128]{2,1,0:T(8,128)(2,1)S(1)} %bitcast.181, bf16[3,2048,128]{2,1,0:T(8,128)(2,1)S(1)} %bitcast.182, ...), custom_call_target="tpu_custom_call" | custom-call | tf_op jit(solution)/shard_map/attention_forward/pallas_call | solution.py:751
  257.4 18.4 %to_tokens.1 = bf16[128,2048]{1,0:T(8,128)(2,1)} custom-call(bf16[16,128,128]{2,1,0:T(8,128)(2,1)} %bitcast.197), custom_call_target="tpu_custom_call" | custom-call | tf_op jit(solution)/shard_map/to_tokens/pallas_call | solution.py:341
  277.3 4.8 fusion.11
  285.9 18.6 %gather_stream.1 = (bf16[4,128,2048]{2,1,0:T(8,128)(2,1)}, bf16[4,128,128]{2,1,0:T(8,128)(2,1)}) custom-call(bf16[128,2048]{1,0:T(8,128)(2,1)} %copy-done.23, bf16[128,128]{1,0:T(8,128)(2,1)} %fusion.47.b), custom_call_target="tpu_custom_call" | custom-call | tf_op jit(solution)/shard_map/gather_stream/pallas_call | solution.py:206
  304.5 10.7 %fusion.112 = f32[512,2048]{1,0:T(8,128)} fusion(bf16[512,2048]{1,0:T(8,128)(2,1)} %bitcast.239, bf16[2048,2048]{1,0:T(8,128)(2,1)} %bitcast.232), kind=kOutput, calls=%fused_computation.200 | convolution fusion | flops 4294967296 | bytes 14680064 | tf_op jit(solution)/shard_map/dot_general | solution.py:34
  315.2 10.3 %fusion.113 = f32[512,2048]{1,0:T(8,128)} fusion(bf16[512,2048]{1,0:T(8,128)(2,1)S(1)} %bitcast.238, bf16[2048,2048]{1,0:T(8,128)(2,1)} %bitcast.234), kind=kOutput, calls=%fused_computation.201 | convolution fusion | flops 4294967296 | bytes 14680064 | tf_op jit(solution)/shard_map/dot_general | solution.py:38
  325.5 11.2 %multiply_convert_fusion = (bf16[512,2048]{1,0:T(8,128)(2,1)S(1)}, f32[512,2048]{1,0:T(8,128)S(1)}, f32[512,2048]{1,0:T(8,128)S(1)}) fusion(bf16[512,128]{1,0:T(8,128)(2,1)S(1)} %bitcast.221, bf16[128,8192]{1,0:T(8,128)(2,1)S(1)} %copy-done, s32[]{:T(128)} %select_n.64, f32[512,2048]{1,0:T(8,128)} %fusion.112, f32[2048]{0:T(1024)S(1)} %dynamic-slice-done), kind=kOutput, calls=%fused_computation.3 | convolution fusion | flops 338690048 | bytes 15343620 | tf_op jit(solution)/shard_map/dot_general | solution.py:34
  336.8 4.7 convolution_convert_fusion
  343.7 8.3 %convolution_convert_fusion.1 = bf16[512,2048]{1,0:T(8,128)(2,1)S(1)} fusion(bf16[512,2048]{1,0:T(8,128)(2,1)S(1)} %add_convert_fusion, bf16[2048,2048]{1,0:T(8,128)(2,1)} %bitcast.233), kind=kOutput, calls=%fused_computation.22 | convolution fusion | flops 4296015872 | bytes 12582912 | tf_op jit(solution)/shard_map/dot_general | solution.py:38
  354.0 16.9 %sum_stream.1 = (f32[128,2048]{1,0:T(8,128)S(1)}, f32[128,128]{1,0:T(8,128)S(1)}) custom-call(bf16[4,128,2048]{2,1,0:T(8,128)(2,1)S(1)} %bitcast.193, bf16[4,128,128]{2,1,0:T(8,128)(2,1)S(1)} %bitcast.198), custom_call_target="tpu_custom_call" | custom-call | tf_op jit(solution)/shard_map/sum_stream/pallas_call | solution.py:255
  376.1 2.9 fusion.114
  382.0 19.4 %grads_in.1 = (bf16[16,128,128]{2,1,0:T(8,128)(2,1)S(1)}, f32[128,2048]{1,0:T(8,128)S(1)}, f32[128,128]{1,0:T(8,128)S(1)}) custom-call(bf16[128,2048]{1,0:T(8,128)(2,1)S(1)} %fusion.12.grad, bf16[4,128,2048]{2,1,0:T(8,128)(2,1)S(1)} %bitcast.192, bf16[4,128,128]{2,1,0:T(8,128)(2,1)S(1)} %bitcast.199), custom_call_target="tpu_custom_call" | custom-call | tf_op jit(solution)/shard_map/grads_in/pallas_call | solution.py:378
  411.3 31.7 %attention_backward.1 = (bf16[2048,128]{1,0:T(8,128)(2,1)S(1)}, bf16[16,2,128,128]{3,2,1,0:T(8,128)(2,1)S(1)}, f32[16,2,128,128]{3,2,1,0:T(8,128)S(1)}) custom-call(s32[5]{0:T(128)S(1)} %pad_add_fusion.1.info, bf16[3,2048,128]{2,1,0:T(8,128)(2,1)S(1)} %bitcast.184, bf16[2048,128]{1,0:T(8,128)(2,1)S(1)} %bitcast.191, f32[8,256]{1,0:T(8,128)S(1)} %bitcast.200, ...), custom_call_target="tpu_custom_call" | custom-call | tf_op jit(solution)/shard_map/attention_backward/pallas_call | solution.py:827
  443.1 27.4 %grads_out.1 = bf16[3,128,2048]{2,1,0:T(8,128)(2,1)S(1)} custom-call(bf16[16,128,128]{2,1,0:T(8,128)(2,1)S(1)} %bitcast.196, bf16[16,2,128,128]{3,2,1,0:T(8,128)(2,1)S(1)} %get-tuple-element.54.other, f32[16,2,128,128]{3,2,1,0:T(8,128)S(1)} %get-tuple-element.55.own), custom_call_target="tpu_custom_call" | custom-call | tf_op jit(solution)/shard_map/grads_out/pallas_call | solution.py:421
  473.8 14.6 %fusion.53 = (f32[128]{0:T(128)S(1)}, f32[128,2048]{1,0:T(8,128)}) fusion(bf16[1,128,2048]{2,1,0:T(8,128)(2,1)S(1)} %copy-done.15, f32[128]{0:T(128)S(1)} %broadcast_multiply_fusion.1, f32[2048]{0:T(1024)S(1)} %bitcast.213, f32[128,2048]{1,0:T(8,128)} %convolution_bitcast_fusion.1, bf16[3,128,2048]{2,1,0:T(8,128)(2,1)} %copy-done.5, ...), kind=kOutput, calls=%fused_computation.88 | convolution fusion | flops 3222798336 | bytes 29369344 | tf_op jit(solution)/shard_map/pte,pde->td/dot_general | solution.py:989
  488.4 3.3 convolution_convert_fusion.2.refs_1_
  495.4 43.7 %sum_all.2 = (bf16[3,2,4,4,4,16,128]{6,5,4,3,2,1,0:T(8,128)(2,1)S(1)}, bf16[3,2,4,16,2048]{4,3,2,1,0:T(8,128)(2,1)S(1)}) custom-call(bf16[3,2048,128]{2,1,0:T(8,128)(2,1)S(1)} %fusion.7.refs_0_, bf16[3,128,2048]{2,1,0:T(8,128)(2,1)} %convolution_convert_fusion.2.refs_1_), custom_call_target="tpu_custom_call" | custom-call | tf_op jit(solution)/shard_map/sum_all/pallas_call | solution.py:595
  539.2 52.6 %sum_all.3 = (bf16[2,2,4,4,4,16,128]{6,5,4,3,2,1,0:T(8,128)(2,1)S(1)}, bf16[2,2,4,16,2048]{4,3,2,1,0:T(8,128)(2,1)S(1)}, bf16[2,2,4,4,2,64,128]{6,5,4,3,2,1,0:T(8,128)(2,1)}, bf16[2,2,4,4,2,32,256]{6,5,4,3,2,1,0:T(8,128)(2,1)}) custom-call(bf16[2,2048,128]{2,1,0:T(8,128)(2,1)S(1)} %copy-done.7, bf16[2,128,2048]{2,1,0:T(8,128)(2,1)S(1)} %copy-done.8, ...), custom_call_target="tpu_custom_call" | custom-call | tf_op jit(solution)/shard_map/sum_all/pallas_call | solution.py:595
  599.6 5.3 copy.46
  604.9 6.4 %reshape.289 = f32[128,8192]{1,0:T(8,128)} reshape(f32[4,32,2,2,4,2,256]{6,5,4,3,2,1,0:T(2,128)} %copy.46) | data formatting | bytes 8388608 | tf_op jit(solution)/shard_map/convert_element_type | solution.py:1008
  611.3 3.9 bitcast_convert_fusion
  (161 shorter events, 61.6 us)
Async XLA Ops:
  0.6 324.8 %copy-start = (bf16[128,8192]{1,0:T(8,128)(2,1)S(1)}, bf16[128,8192]{1,0:T(8,128)(2,1)}, u32[]{:S(2)}) copy-start(bf16[128,8192]{1,0:T(8,128)(2,1)} %param.32) | copy-start | bytes 6291460
  185.9 10.8 %copy-start.30 = (bf16[4,128,2048]{2,1,0:T(8,128)(2,1)S(1)}, bf16[4,128,2048]{2,1,0:T(8,128)(2,1)}, u32[]{:S(2)}) copy-start(bf16[4,128,2048]{2,1,0:T(8,128)(2,1)} %param.30) | copy-start | bytes 6291460
  283.7 88.9 %copy-start.16 = (f32[128,2048]{1,0:T(8,128)}, f32[128,2048]{1,0:T(8,128)S(1)}, u32[]{:S(2)}) copy-start(f32[128,2048]{1,0:T(8,128)S(1)} %get-tuple-element.79) | copy-start | bytes 3145732
  304.5 10.7 %copy-start.36 = (bf16[4,128,2048]{2,1,0:T(8,128)(2,1)S(1)}, bf16[4,128,2048]{2,1,0:T(8,128)(2,1)}, u32[]{:S(2)}) copy-start(bf16[4,128,2048]{2,1,0:T(8,128)(2,1)} %get-tuple-element.43) | copy-start | bytes 6291460
  315.2 10.3 %copy-start.34 = (bf16[4,128,128]{2,1,0:T(8,128)(2,1)S(1)}, bf16[4,128,128]{2,1,0:T(8,128)(2,1)}, u32[]{:S(2)}) copy-start(bf16[4,128,128]{2,1,0:T(8,128)(2,1)} %get-tuple-element.42) | copy-start | bytes 393220
  315.2 10.3 %dynamic-slice-start = ((f32[8192]{0:T(1024)}, s32[]{:T(128)}), f32[2048]{0:T(1024)S(1)}, s32[]{:S(2)}) async-start(f32[8192]{0:T(1024)} %param.28, s32[]{:T(128)} %select_n.64), calls=%async_computation.2 | async-start | bytes 16896 | tf_op jit(solution)/shard_map/dynamic_slice | solution.py:910
  315.2 21.5 %slice-start.2 = ((s8[8388608]{0:T(1024)(128)(4,1)}), s8[4194304]{0:T(1024)(128)(4,1)S(1)}, s32[]{:S(2)}) async-start(s8[8388608]{0:T(1024)(128)(4,1)} %bitcast.235), calls=%async_computation.3 | async-start | bytes 8388608
  325.5 11.2 %slice-start.3 = ((s8[8388608]{0:T(1024)(128)(4,1)}), s8[4194304]{0:T(1024)(128)(4,1)S(1)}, s32[]{:S(2)}) async-start(s8[8388608]{0:T(1024)(128)(4,1)} %bitcast.235), calls=%async_computation.4 | async-start | bytes 8388608
  352.0 18.9 %copy-start.28 = (bf16[2048,128]{1,0:T(8,128)(2,1)S(1)}, bf16[2048,128]{1,0:T(8,128)(2,1)}, u32[]{:S(2)}) copy-start(bf16[2048,128]{1,0:T(8,128)(2,1)} %param.31) | copy-start | bytes 1572868
  352.7 18.7 %copy-start.24 = (bf16[128,2048]{1,0:T(8,128)(2,1)S(1)}, bf16[128,2048]{1,0:T(8,128)(2,1)}, u32[]{:S(2)}) copy-start(bf16[128,2048]{1,0:T(8,128)(2,1)} %copy-done.23) | copy-start | bytes 1572868
  379.0 22.4 %copy-start.25 = (bf16[128,2048]{1,0:T(8,128)(2,1)S(1)}, bf16[128,2048]{1,0:T(8,128)(2,1)}, u32[]{:S(2)}) copy-start(bf16[128,2048]{1,0:T(8,128)(2,1)} %to_tokens.1) | copy-start | bytes 1572868
  379.0 24.7 %copy-start.13 = (f32[2048,128]{1,0:T(8,128)S(1)}, f32[2048,128]{1,0:T(8,128)}, u32[]{:S(2)}) copy-start(f32[2048,128]{1,0:T(8,128)} %copy-done.12) | copy-start | bytes 3145732
  380.5 23.6 %copy-start.17 = (f32[128,2048]{1,0:T(8,128)S(1)}, f32[128,2048]{1,0:T(8,128)}, u32[]{:S(2)}) copy-start(f32[128,2048]{1,0:T(8,128)} %copy-done.16) | copy-start | bytes 3145732
  380.5 23.6 %copy-start.29 = (bf16[128,2048]{1,0:T(8,128)(2,1)S(1)}, bf16[128,2048]{1,0:T(8,128)(2,1)}, u32[]{:S(2)}) copy-start(bf16[128,2048]{1,0:T(8,128)(2,1)} %param.34) | copy-start | bytes 1572868
  404.1 7.1 %copy-start.4 = (bf16[2,16,128,128]{3,2,1,0:T(8,128)(2,1)S(1)}, bf16[2,16,128,128]{3,2,1,0:T(8,128)(2,1)}, u32[]{:S(2)}) copy-start(bf16[2,16,128,128]{3,2,1,0:T(8,128)(2,1)} %get-tuple-element.37) | copy-start | bytes 3145732
  405.3 6.0 copy-start.2
  405.3 6.0 copy-start.10
  443.0 28.5 %copy-start.31 = (bf16[4,128,2048]{2,1,0:T(8,128)(2,1)S(1)}, bf16[4,128,2048]{2,1,0:T(8,128)(2,1)}, u32[]{:S(2)}) copy-start(bf16[4,128,2048]{2,1,0:T(8,128)(2,1)} %param.30) | copy-start | bytes 6291460
  443.1 29.1 %copy-start.32 = (bf16[4,2048,128]{2,1,0:T(8,128)(2,1)S(1)}, bf16[4,2048,128]{2,1,0:T(8,128)(2,1)}, u32[]{:S(2)}) copy-start(bf16[4,2048,128]{2,1,0:T(8,128)(2,1)} %param.29) | copy-start | bytes 6291460
  488.4 5.0 copy-start.22
  493.4 45.8 %copy-start.6 = (bf16[2048,128]{1,0:T(8,128)(2,1)S(1)}, bf16[2048,128]{1,0:T(8,128)(2,1)}, u32[]{:S(2)}) copy-start(bf16[2048,128]{1,0:T(8,128)(2,1)} %convolution_convert_fusion.5.refs_2_) | copy-start | bytes 1572868
  493.4 45.8 %copy-start.7 = (bf16[2,2048,128]{2,1,0:T(8,128)(2,1)S(1)}, bf16[2,2048,128]{2,1,0:T(8,128)(2,1)}, u32[]{:S(2)}) copy-start(bf16[2,2048,128]{2,1,0:T(8,128)(2,1)} %pad_maximum_fusion.refs_0_) | copy-start | bytes 3145732
  493.4 45.8 %copy-start.8 = (bf16[2,128,2048]{2,1,0:T(8,128)(2,1)S(1)}, bf16[2,128,2048]{2,1,0:T(8,128)(2,1)}, u32[]{:S(2)}) copy-start(bf16[2,128,2048]{2,1,0:T(8,128)(2,1)} %pad_maximum_fusion.1.refs_1_) | copy-start | bytes 3145732
  493.4 45.8 %copy-start.11 = (bf16[128,2048]{1,0:T(8,128)(2,1)S(1)}, bf16[128,2048]{1,0:T(8,128)(2,1)}, u32[]{:S(2)}) copy-start(bf16[128,2048]{1,0:T(8,128)(2,1)} %convolution_convert_fusion.4.refs_3_) | copy-start | bytes 1572868
  (19 other events, 52.6 us)

commit v3 on v1

v3 whole, which is shorter than its diff:
```python
import functools

import jax
import jax.numpy as jnp
from jax import lax
from jax.experimental import pallas as pl
from jax.experimental.pallas import tpu as pltpu
from jax.sharding import PartitionSpec as P

HEADS = 16
ADAPTER_RANK = 16
MESH = pl.DeviceIdType.MESH
AXES = ("xl", "c", "z", "y", "xh")
SIZES = (2, 2, 4, 4, 2)
STREAM = ("xl", "c")
TOKEN = ("z", "y", "xh")
bf16 = jnp.bfloat16
f32 = jnp.float32
LOG2E = 1.4426950408889634
MIB = 2**20
Q_TILE = 256
K_TILE = 512
ALL = slice(None)


def layer_norm(values, gain, shift):
    center = values - jnp.mean(values, axis=-1, keepdims=True)
    spread = jnp.mean(center * center, axis=-1, keepdims=True)
    return center * lax.rsqrt(spread + 1e-05) * gain + shift


def layer_norm_back(values, gain, grad):
    center = values - jnp.mean(values, axis=-1, keepdims=True)
    scale = lax.rsqrt(jnp.mean(center * center, axis=-1, keepdims=True) + 1e-05)
    unit = center * scale
    grad = grad * gain
    along = jnp.mean(grad * unit, axis=-1, keepdims=True)
    return scale * (grad - jnp.mean(grad, axis=-1, keepdims=True) - unit * along)


def dot(left, right):
    return jnp.dot(left, right, preferred_element_type=f32)


def dot_nt(left, right):
    return lax.dot_general(left, right, (((1,), (1,)), ((), ())), preferred_element_type=f32)


def dot_tn(left, right):
    return lax.dot_general(left, right, (((0,), (0,)), ((), ())), preferred_element_type=f32)


def piece(n, size):
    return pl.ds(pl.multiple_of(n * size, size), size)


class Place:
    def __init__(self):
        self.xl, self.c, self.z, self.y, self.xh = (lax.axis_index(a) for a in AXES)
        self.x = self.xh * 2 + self.xl
        self.g = self.x * 2 + self.c

    def at(self, axis):
        return {"x": self.x, "y": self.y, "z": self.z}[axis]

    def step(self, axis, step):
        return lax.rem(self.at(axis) + (step + 4), 4)

    def toward(self, axis, step=1):
        if axis == "c":
            return {"c": 1 - self.c}
        to = self.step(axis, step)
        if axis == "x":
            return {"xl": lax.rem(to, 2), "xh": to // 2}
        return {axis: to}

    def member(self, dx, dc):
        to = {}
        if dx:
            to |= self.toward("x", dx)
        if dc:
            to |= {"c": 1 - self.c}
        return to


MEMBERS = [(dx, dc) for dx in (2, 1, 3, 0) for dc in (0, 1) if dx or dc]


class Sends:
    def __init__(self, send, recv):
        self.send, self.recv, self.used, self.open = send, recv, 0, []

    def push(self, src, dst, device):
        k = self.used
        self.used += 1
        copy = pltpu.make_async_remote_copy(
            src_ref=src,
            dst_ref=dst,
            send_sem=self.send.at[k],
            recv_sem=self.recv.at[k],
            device_id=device,
            device_id_type=MESH,
        )
        copy.start()
        self.open.append(copy)
        return copy


def greet(devices, perhaps=()):
    barrier = pltpu.get_barrier_semaphore()
    for device in devices:
        pl.semaphore_signal(barrier, inc=1, device_id=device, device_id_type=MESH)
    amount = len(devices) + len(perhaps)
    for device, myself in perhaps:
        amount = amount - myself.astype(jnp.int32)

        @pl.when(jnp.logical_not(myself))
        def _():
            pl.semaphore_signal(barrier, inc=1, device_id=device, device_id_type=MESH)

    pl.semaphore_wait(barrier, amount)


def run_all(parts):
    parts = list(parts)
    while parts:
        left = []
        for part in parts:
            try:
                next(part)
                left.append(part)
            except StopIteration:
                pass
        parts = left


def ring_gather(place, sends, view, order, chunk, landed, forward):
    fixed = {a: place.at(a) for a in order}
    across = place.toward("c")
    later, passed = [], []

    def pass_on(block):
        if forward:
            passed.append(sends.push(view(block, None), view(block, None), across))

    if forward:
        passed.append(sends.push(chunk, view(fixed, None), across))
    for number, axis in enumerate(order):
        own = view(fixed, None)
        src = chunk if number == 0 else own
        if number == 0:
            sent = [sends.push(src, own, place.toward(axis, s)) for s in (2, 1, 3)]
            yield
            for s, copy in zip((2, 1, 3), sent):
                copy.wait_recv()
                pass_on(fixed | {axis: place.step(axis, -s)})
            landed.wait()
            later += sent
            del fixed[axis]
            continue
        up = sends.push(src, own, place.toward(axis, 1))
        down = sends.push(src, own, place.toward(axis, -1))
        yield
        before = fixed | {axis: place.step(axis, -1)}
        after = fixed | {axis: place.step(axis, 1)}
        opposite = fixed | {axis: place.step(axis, 2)}
        up.wait_recv()
        half = view(before, 0)
        up_two = sends.push(half, half, place.toward(axis, 1))
        down.wait_recv()
        half = view(after, 1)
        down_two = sends.push(half, half, place.toward(axis, -1))
        pass_on(before)
        pass_on(after)
        yield
        up_two.wait_recv()
        down_two.wait_recv()
        pass_on(opposite)
        later += [up, down, up_two, down_two]
        del fixed[axis]
    yield
    for copy in later:
        copy.wait_send()
    for copy in passed:
        copy.wait()


class Nothing:
    def wait(self):
        pass


def neighbours(place, axes):
    return [place.toward(a, s) for a in axes for s in ((1, 2, 3) if a in "xyz" else (1,))]


def members(place):
    return [place.member(*m) for m in MEMBERS]


class GroupGather:
    def __init__(self, place, sends, buf):
        self.place, self.sends, self.buf = place, sends, buf
        self.mine = buf.at[place.x, place.c]
        self.right, self.left = place.toward("x", 1), place.toward("x", -1)
        self.up = sends.push(self.mine, self.mine, self.right)
        self.down = sends.push(self.mine, self.mine, self.left)
        self.passed = [self.pass_on(self.mine)]

    def pass_on(self, ref):
        return self.sends.push(ref, ref, self.place.toward("c"))

    def own(self):
        self.passed[0].wait_recv()

    def near(self, wait=True):
        x, c = self.place.step("x", -1), self.place.c
        self.up.wait_recv()
        half = self.buf.at[x, c, pl.ds(0, 64)]
        self.up_two = self.sends.push(half, half, self.right)
        self.passed.append(self.pass_on(self.buf.at[x, c]))
        x = self.place.step("x", 1)
        self.down.wait_recv()
        half = self.buf.at[x, c, pl.ds(64, 64)]
        self.down_two = self.sends.push(half, half, self.left)
        self.passed.append(self.pass_on(self.buf.at[x, c]))
        if wait:
            self.near_done()

    def near_done(self):
        self.passed[1].wait_recv()
        self.passed[2].wait_recv()

    def far(self):
        self.up_two.wait_recv()
        self.down_two.wait_recv()
        self.passed.append(self.pass_on(self.buf.at[self.place.step("x", 2), self.place.c]))

    def far_done(self):
        self.passed[3].wait_recv()

    def finish(self):
        for copy in [self.up, self.down, self.up_two, self.down_two] + self.passed:
            copy.wait_send()


def group_gather(place, sends, buf):
    gather = GroupGather(place, sends, buf)
    yield
    gather.own()
    gather.near()
    yield
    gather.far()
    yield
    gather.far_done()
    gather.finish()


class GroupSum:
    def __init__(self, place, sends, parts, scratch):
        self.place, self.sends, self.parts = place, sends, parts
        self.came, self.own, self.left_one, self.right_one, self.left_two, self.right_two = scratch
        self.xs = [place.step("x", s) for s in (2, 1, -1, 0)]
        self.right, self.left = place.toward("x", 1), place.toward("x", -1)
        self.crossed = {}

    @staticmethod
    def scratch(n):
        vm = lambda *s: pltpu.VMEM(s, bf16)
        return [vm(4, 128, n), vm(3, 128, n), vm(64, n), vm(64, n), vm(128, n), vm(128, n)]

    def cross(self, k):
        place = self.place
        self.crossed[k] = self.sends.push(
            self.parts.at[self.xs[k], 1 - place.c], self.came.at[k], place.toward("c")
        )

    def merge(self, k):
        self.crossed[k].wait()
        both = self.parts[self.xs[k], self.place.c].astype(f32) + self.came[k].astype(f32)
        self.own[k] = both.astype(bf16)

    def first(self):
        self.up = self.sends.push(self.own.at[0, pl.ds(0, 64)], self.left_one, self.right)
        self.down = self.sends.push(self.own.at[0, pl.ds(64, 64)], self.right_one, self.left)

    def second(self):
        self.up.wait()
        both = self.own[1, 0:64].astype(f32) + self.left_one[...].astype(f32)
        self.own[1, 0:64] = both.astype(bf16)
        self.up_two = self.sends.push(self.own.at[1], self.left_two, self.right)
        self.down.wait()
        both = self.own[2, 64:128].astype(f32) + self.right_one[...].astype(f32)
        self.own[2, 64:128] = both.astype(bf16)
        self.down_two = self.sends.push(self.own.at[2], self.right_two, self.left)

    def result(self):
        self.crossed[3].wait()
        total = self.parts[self.xs[3], self.place.c].astype(f32) + self.came[3].astype(f32)
        self.up_two.wait()
        self.down_two.wait()
        return total + self.left_two[...].astype(f32) + self.right_two[...].astype(f32)


def group_sum(place, sends, parts, scratch, out):
    total = GroupSum(place, sends, parts, scratch)
    for k in range(4):
        total.cross(k)
    yield
    total.merge(0)
    total.first()
    total.merge(1)
    total.merge(2)
    yield
    total.second()
    yield
    out[...] = total.result()


def plane(place):
    steps = [(i, j) for i in (2, 1, 3, 0) for j in (2, 1, 3, 0) if i or j]
    return [(lax.rem(place.z + i, 4), lax.rem(place.y + j, 4)) for i, j in steps]


def from_plane(place):
    steps = [(i, j) for i in (2, 1, 3, 0) for j in (2, 1, 3, 0) if i or j]
    return [(lax.rem(place.z + 4 - i, 4), lax.rem(place.y + 4 - j, 4)) for i, j in steps]


def projectors(place):
    x, c = place.z, place.y // 2
    member = {"xl": lax.rem(x, 2), "xh": x // 2, "c": c}
    mine = (place.x == x) & (place.c == c)
    return [(member | {"z": z, "y": y}, None) for z, y in plane(place)] + [
        (member | {"z": place.z, "y": place.y}, mine)
    ]


def attenders(place):
    found = []
    for dx, dc in MEMBERS + [(0, 0)]:
        for j in range(2):
            z, y = place.x, 2 * place.c + j
            device = place.member(dx, dc) | {"z": z, "y": y}
            mine = None if dx or dc else (place.z == z) & (place.y == y)
            found.append((dx, dc, j, device, mine))
    return found


def head_columns(z, y):
    return pl.ds(pl.multiple_of((z * 4 + y) * 128, 128), 128)


def split_greeting(pairs):
    return [d for d, m in pairs if m is None], [(d, m) for d, m in pairs if m is not None]


def plane_devices(place):
    return [{"z": z, "y": y} for z, y in plane(place)]


class Post:
    def __init__(self, src, dst, device, myself, send_sem, recv_sem):
        self.remote = pltpu.make_async_remote_copy(
            src_ref=src, dst_ref=dst, send_sem=send_sem, recv_sem=recv_sem, device_id=device, device_id_type=MESH
        )
        self.myself = myself
        if myself is None:
            self.remote.start()
        else:
            pl.when(myself)(pltpu.make_async_copy(src, dst, recv_sem).start)
            pl.when(jnp.logical_not(myself))(self.remote.start)

    def wait_send(self):
        if self.myself is None:
            self.remote.wait_send()
        else:
            pl.when(jnp.logical_not(self.myself))(self.remote.wait_send)


def heads_out(place, sends, blocks, merged, local):
    cols = head_columns(place.z, place.y)
    keep = pltpu.make_async_copy(blocks.at[place.z * 4 + place.y], merged.at[:, cols], local)
    keep.start()
    sent = [sends.push(blocks.at[z * 4 + y], merged.at[:, cols], {"z": z, "y": y}) for z, y in plane(place)]
    yield
    for copy in sent:
        copy.wait()
    keep.wait()


def grads_in_kernel(grad, parts, heads, total, *refs):
    scratch, (send, recv, local) = refs[:-3], refs[-3:]
    place = Place()
    greet(plane_devices(place) + members(place))
    sends = Sends(send, recv)

    def heads_part():
        here = place.z * 4 + place.y
        keep = pltpu.make_async_copy(grad.at[:, head_columns(place.z, place.y)], heads.at[here], local.at[0])
        keep.start()
        sent = [
            sends.push(grad.at[:, head_columns(z, y)], heads.at[here], {"z": z, "y": y}) for z, y in plane(place)
        ]
        yield
        for copy in sent:
            copy.wait()
        keep.wait()

    run_all([heads_part(), group_sum(place, sends, parts, scratch, total)])


def grads_in(grad, parts):
    any_ = pl.BlockSpec(memory_space=pl.ANY)
    vmem = pl.BlockSpec(memory_space=pltpu.VMEM)
    n = parts.shape[-1]
    return pl.pallas_call(
        grads_in_kernel,
        name="grads_in",
        out_shape=[jax.ShapeDtypeStruct((16, 128, 128), bf16), jax.ShapeDtypeStruct((128, n), f32)],
        in_specs=[any_, vmem],
        out_specs=[any_, vmem],
        scratch_shapes=GroupSum.scratch(n) + [pltpu.SemaphoreType.DMA((k,)) for k in (23, 23, 1)],
        compiler_params=pltpu.CompilerParams(collective_id=2, has_side_effects=True, vmem_limit_bytes=40 * MIB),
    )(grad, parts)


def grads_out_kernel(dq, other, own, grads, came, sums, by_head, send, recv, a_recv, local):
    place = Place()
    partner = {"xh": 1 - place.xh}
    greet(plane_devices(place) + members(place))
    sends = Sends(send, recv)
    here = place.z * 4 + place.y
    places = plane(place) + [(place.z, place.y)]
    kv = pl.ds(1, 2)
    swaps = [sends.push(other.at[z * 4 + y], came.at[z * 4 + y], partner) for z, y in places]
    gone = []

    def send_block(k, src, part, z, y, last):
        dst = by_head.at[part, here]
        if last:
            pltpu.make_async_copy(src, dst, a_recv.at[k, here]).start()
            return
        copy = pltpu.make_async_remote_copy(
            src_ref=src, dst_ref=dst, send_sem=local.at[len(gone)], recv_sem=a_recv.at[k, here],
            device_id={"z": z, "y": y}, device_id_type=MESH,
        )
        copy.start()
        gone.append(copy)

    for n, (z, y) in enumerate(places):
        send_block(0, dq.at[z * 4 + y], 0, z, y, n == 15)
    for n, (copy, (z, y)) in enumerate(zip(swaps, places)):
        copy.wait_recv()
        at = z * 4 + y
        sums[at] = (came[at].astype(f32) + own[at]).astype(bf16)
        send_block(1, sums.at[at], kv, z, y, n == 15)

    mine = None
    shared = []
    for dx, dc in MEMBERS + [(0, 0)]:
        g = place.step("x", dx) * 2 + (1 - place.c if dc else place.c)
        for k, part in ((0, 0), (1, kv)):
            for j in range(2):
                dst = by_head.at[part, g * 2 + j]
                pltpu.make_async_copy(dst, dst, a_recv.at[k, g * 2 + j]).wait()
        src, dst = by_head.at[:, piece(g, 2)], grads.at[:, place.x, place.c]
        if dx or dc:
            shared.append(sends.push(src, dst, place.member(dx, dc)))
        else:
            mine = pltpu.make_async_copy(src, dst, local.at[30])
            mine.start()
    for copy in swaps + gone:
        copy.wait_send()
    for copy in shared:
        copy.wait()
    mine.wait()


def grads_out(dq, other, own):
    any_ = pl.BlockSpec(memory_space=pl.ANY)
    vmem = pl.BlockSpec(memory_space=pltpu.VMEM)
    return pl.pallas_call(
        grads_out_kernel,
        name="grads_out",
        out_shape=jax.ShapeDtypeStruct((3, 4, 2, 2, 128, 128), bf16),
        in_specs=[vmem] * 3,
        out_specs=any_,
        scratch_shapes=[pltpu.VMEM((16, 2, 128, 128), bf16)] * 2
        + [pltpu.VMEM((3, 16, 128, 128), bf16)]
        + [pltpu.SemaphoreType.DMA(k) for k in ((23,), (23,), (2, 16), (31,))],
        compiler_params=pltpu.CompilerParams(collective_id=3, has_side_effects=True, vmem_limit_bytes=40 * MIB),
    )(dq, other, own)


ORDERS = (("x", "y", "z"), ("y", "z", "x"), ("z", "x", "y"))


def spread_sum(place, sends, order, steps, result_view, final, landed, across=None):
    if across:
        src, came, own, out = across
        copy = sends.push(src, came, place.toward("c"))
        yield
        copy.wait()
        out[...] = (own[...].astype(f32) + came[...].astype(f32)).astype(bf16)
    for axis, (held, slots, out) in zip(order, steps):
        sent = [
            sends.push(held(place.step(axis, d)), slots.at[d - 1], place.toward(axis, d)) for d in (2, 1, 3)
        ]
        yield
        for copy in sent:
            copy.wait()
        total = held(place.at(axis))[...].astype(f32)
        for d in range(3):
            total = total + slots[d].astype(f32)
        out[...] = total.astype(bf16)
    landed.start()
    yield from ring_gather(place, sends, result_view[0], result_view[1], final, landed, True)


def rows_of(ref, size):
    return lambda p: ref.at[piece(p, size)]


def cols_of(ref, size):
    return lambda p: ref.at[:, piece(p, size)]


def mid_rows_of(ref, size):
    return lambda p: ref.at[:, piece(p, size)]


def sums_kernel(count, a, b, two, a_res, b_res, two_res, *refs):
    scratch, (send, recv, local) = list(refs[:-3]), refs[-3:]
    place = Place()
    sends = Sends(send, recv)
    greet(neighbours(place, ("x", "y", "z", "c")))
    parts = []
    mine, theirs = place.c, 1 - place.c
    here = {x: place.at(x) for x in "xyz"}

    def a_view(i, order):
        def view(fixed, half):
            at = [fixed.get(x, ALL) for x in order]
            if half is not None:
                at[max(n for n in range(3) if order[n] not in fixed)] = pl.ds(half * 2, 2)
            return a_res.at[(i, place.c) + tuple(at)]

        return view

    def b_view(i, order):
        def view(fixed, half):
            start, size = 0, 2048
            if order[1] in fixed:
                start, size = fixed[order[1]] * 512, 512
            if order[2] in fixed:
                start, size = start + fixed[order[2]] * 128, 128
            if half is not None:
                size = size // 2
                start = start + half * size
            cols = pl.ds(start, size) if isinstance(start, int) else pl.ds(pl.multiple_of(start, 128), size)
            return b_res.at[i, place.c, fixed.get(order[0], ALL), :, cols]

        return view

    for i in range(count):
        order = ORDERS[i % 3]
        ca, ha, sa1, qa, sa2, ra, sa3, fa, cb, hb, sb1, qb, sb2, rb, sb3, fb = scratch[:16]
        del scratch[:16]
        keep = pltpu.make_async_copy(fa, a_view(i, order)(here, None), local.at[2 * i])
        parts.append(
            spread_sum(
                place, sends, order,
                [(rows_of(ha, 256), sa1, qa), (rows_of(qa, 64), sa2, ra), (rows_of(ra, 16), sa3, fa)],
                (a_view(i, order), order[::-1]), fa, keep,
                (a.at[i, piece(theirs, 1024)], ca, a.at[i, piece(mine, 1024)], ha),
            )
        )
        keep = pltpu.make_async_copy(fb, b_view(i, order)(here, None), local.at[2 * i + 1])
        parts.append(
            spread_sum(
                place, sends, order,
                [(rows_of(hb, 16), sb1, qb), (cols_of(qb, 512), sb2, rb), (cols_of(rb, 128), sb3, fb)],
                (b_view(i, order), order[::-1]), fb, keep,
                (b.at[i, piece(theirs, 64)], cb, b.at[i, piece(mine, 64)], hb),
            )
        )
    s1, q1, s2, f2 = scratch

    def two_view(n):
        def view(fixed, half):
            xl, xh = (ALL, ALL)
            if "x" in fixed:
                xl, xh = lax.rem(fixed["x"], 2), fixed["x"] // 2
            if half is not None:
                xl = pl.ds(half, 1)
            return two_res.at[n, xl, place.c, fixed.get("z", ALL), fixed.get("y", ALL), xh]

        return view

    for n, axes in enumerate((("z", "y"), ("y", "z"))):
        if n == 0:
            steps = [
                (lambda p: two.at[0, p], s1.at[0], q1.at[0]),
                (lambda p: q1.at[0, p], s2.at[0], f2.at[0]),
            ]
        else:
            steps = [
                (lambda p: two.at[1, :, p], s1.at[1], q1.at[1]),
                (lambda p: q1.at[1, p], s2.at[1], f2.at[1]),
            ]
        keep = pltpu.make_async_copy(f2.at[n], two_view(n)(here, None), local.at[2 * count + n])
        order = (("x", "z", "y"), ("x", "y", "z"))[n]
        parts.append(spread_sum(place, sends, axes, steps, (two_view(n), order), f2.at[n], keep))
    run_all(parts)
    assert sends.used <= send.shape[0], sends.used


def sum_all(a, b, two):
    count = a.shape[0]
    vm = lambda *shape: pltpu.VMEM(shape, bf16)
    scratch = []
    for _ in range(count):
        scratch += [vm(1024, 128), vm(1024, 128), vm(3, 256, 128), vm(256, 128), vm(3, 64, 128), vm(64, 128)]
        scratch += [vm(3, 16, 128), vm(16, 128)]
        scratch += [vm(64, 2048), vm(64, 2048), vm(3, 16, 2048), vm(16, 2048), vm(3, 16, 512), vm(16, 512)]
        scratch += [vm(3, 16, 128), vm(16, 128)]
    scratch += [vm(2, 3, 4, 64, 128), vm(2, 4, 64, 128), vm(2, 3, 64, 128), vm(2, 64, 128)]
    shapes = [(count, 2, 4, 4, 4, 16, 128), (count, 2, 4, 16, 2048), (2, 2, 2, 4, 4, 2, 64, 128)]
    n = 62 * count + 60
    a_all, b_all, two_all = pl.pallas_call(
        functools.partial(sums_kernel, count),
        name="sum_all",
        out_shape=[jax.ShapeDtypeStruct(s, bf16) for s in shapes],
        in_specs=[pl.BlockSpec(memory_space=pltpu.VMEM)] * 3,
        out_specs=[pl.BlockSpec(memory_space=pl.ANY)] * 3,
        scratch_shapes=scratch + [pltpu.SemaphoreType.DMA((k,)) for k in (n, n, 2 * count + 2)],
        compiler_params=pltpu.CompilerParams(collective_id=4, has_side_effects=True, vmem_limit_bytes=48 * MIB),
    )(a, b, two.reshape(2, 4, 4, 64, 128))
    return a_all.reshape(count, 2048, 128), b_all.reshape(count, 128, 2048), two_all.reshape(2, 8192, 128)


def positions_of(local, parity):
    return (2 * (local // 128) + parity) * 128 + lax.rem(local, 128)


def flash_back_kernel(
    info, q_ref, do_ref, lse_ref, delta_ref, lo_ref, ko_ref, vo_ref, kx_ref, vx_ref, dq_ref, other_ref, own_ref, dq_acc, *, scale
):
    kt = pl.program_id(0)
    parity = info[0]

    @pl.when(kt == 0)
    def _():
        dq_acc[...] = jnp.zeros_like(dq_acc)

    first = kt * (K_TILE // Q_TILE)
    last = info[1 + kt]
    blocks = K_TILE // 128
    for k_ref, v_ref, k_parity, out in ((kx_ref, vx_ref, 1 - parity, other_ref), (ko_ref, vo_ref, parity, own_ref)):
        k = k_ref[0]
        v = v_ref[0]
        k_pos = positions_of(kt * K_TILE + lax.broadcasted_iota(jnp.int32, (K_TILE, 1), 0), k_parity)

        def step(qt, carry):
            dk, dv = carry
            rows = pl.ds(pl.multiple_of(qt * Q_TILE, Q_TILE), Q_TILE)
            q = q_ref[0, rows, :]
            do = do_ref[rows, :]
            q_pos = positions_of(qt * Q_TILE + lax.broadcasted_iota(jnp.int32, (1, Q_TILE), 1), parity)
            lo = lo_ref[pl.ds(qt, 1), :]
            lse = lse_ref[pl.ds(qt, 1), :]
            delta = delta_ref[pl.ds(qt, 1), :]
            s = dot_nt(k, q)
            p = jnp.exp2(jnp.where((k_pos >= lo) & (k_pos <= q_pos), s * (scale * LOG2E) - lse, -1e30))
            dv = dv + dot(p.astype(bf16), do)
            dp = dot_nt(v, do)
            ds = (p * (dp - delta) * scale).astype(bf16)
            dk = dk + dot(ds, q)
            dq_acc[rows, :] += dot_tn(ds, k)
            return dk, dv

        zero = jnp.zeros((K_TILE, 128), f32)
        dk, dv = lax.fori_loop(first, last, step, (zero, zero))
        for b in range(blocks):
            out[b, 0] = dk[b * 128 : (b + 1) * 128].astype(out.dtype)
            out[b, 1] = dv[b * 128 : (b + 1) * 128].astype(out.dtype)

    @pl.when(kt == pl.num_programs(0) - 1)
    def _():
        dq_ref[...] = dq_acc[...].astype(bf16)


def flash_backward(info, do, lse, delta, lo, by_head, across, scale):
    rows = do.shape[0]
    tiles = rows // K_TILE
    whole = pl.BlockSpec((rows, 128), lambda t, s: (0, 0))
    line = pl.BlockSpec((rows // Q_TILE, Q_TILE), lambda t, s: (0, 0))
    block = lambda n: pl.BlockSpec((1, K_TILE, 128), lambda t, s: (n, t, 0))
    grads = pl.BlockSpec((K_TILE // 128, 2, 128, 128), lambda t, s: (t, 0, 0, 0))
    return pl.pallas_call(
        functools.partial(flash_back_kernel, scale=scale),
        name="attention_backward",
        grid_spec=pltpu.PrefetchScalarGridSpec(
            num_scalar_prefetch=1,
            grid=(tiles,),
            in_specs=[
                pl.BlockSpec((1, rows, 128), lambda t, s: (0, 0, 0)),
                whole, line, line, line, block(1), block(2), block(0), block(1),
            ],
            out_specs=[whole, grads, grads],
            scratch_shapes=[pltpu.VMEM((rows, 128), f32)],
        ),
        out_shape=[
            jax.ShapeDtypeStruct((rows, 128), bf16),
            jax.ShapeDtypeStruct((rows // 128, 2, 128, 128), bf16),
            jax.ShapeDtypeStruct((rows // 128, 2, 128, 128), f32),
        ],
        compiler_params=pltpu.CompilerParams(vmem_limit_bytes=40 * MIB),
    )(info, by_head, do, lse, delta, lo, by_head, by_head, across, across)


def attend(t, mine, others, lo_ref, att, low, lse_ref, parity, scale):
    at = pl.ds(pl.multiple_of(t * Q_TILE, Q_TILE), Q_TILE)
    q = mine[0, at, :]
    q_pos = positions_of(t * Q_TILE + lax.broadcasted_iota(jnp.int32, (Q_TILE, 1), 0), parity)
    lo = lo_ref[at, :]
    ones = jnp.ones((K_TILE, 128), bf16)

    def step(kt, carry):
        top, acc = carry
        rows = pl.ds(pl.multiple_of(kt * K_TILE, K_TILE), K_TILE)
        local = kt * K_TILE + lax.broadcasted_iota(jnp.int32, (1, K_TILE), 1)
        scores = []
        for k, par in ((mine[1, rows, :], parity), (others[0, rows, :], 1 - parity)):
            k_pos = positions_of(local, par)
            scores.append(jnp.where((k_pos >= lo) & (k_pos <= q_pos), dot_nt(q, k), -1e30))
        new = jnp.maximum(jnp.max(scores[0], axis=1, keepdims=True), jnp.max(scores[1], axis=1, keepdims=True))
        new = jnp.maximum(top, new)
        acc = acc * jnp.exp2((top - new) * (scale * LOG2E))
        for s, v in zip(scores, (mine[2, rows, :], others[1, rows, :])):
            p = jnp.exp2((s - new) * (scale * LOG2E)).astype(bf16)
            acc = acc + dot(p, jnp.concatenate([v, ones], axis=1))
        return new, acc

    start = (jnp.full((Q_TILE, 1), -1e30, f32), jnp.zeros((Q_TILE, 256), f32))
    top, acc = lax.fori_loop(0, (t * Q_TILE + Q_TILE + K_TILE - 1) // K_TILE, step, start)
    total = acc[:, 128:]
    o = acc[:, :128] / total
    att[at, :] = o
    for b in range(Q_TILE // 128):
        low[t * (Q_TILE // 128) + b] = o[b * 128 : (b + 1) * 128].astype(bf16)
    lse = top * (scale * LOG2E) + jnp.log2(total)
    lse_ref[pl.ds(pl.multiple_of(t * 8, 8), 8), :] = jnp.transpose(lse)[0:8, :]


def front_kernel(
    tok, gain, shift, bias, dmaps, umaps, mask, cot, lum, lo, wp, wo, up, dn,
    act_all, qkv_w, out_all, up_all, dn_all, cot_all, heads, across, merged, att, lse,
    act, cotbuf, wq, rows, mine, others, low, send, recv, a_send, a_recv, local, *, scale,
):
    place = Place()
    sends = Sends(send, recv)
    partner = {"xh": 1 - place.xh}
    always, perhaps = split_greeting(projectors(place))
    greet(plane_devices(place) + members(place) + always, perhaps)
    home = (place.xl, place.c, place.z, place.y, place.xh)

    def out_view(halfs):
        def view(fixed, half):
            xl, xh = (ALL, ALL)
            if "x" in fixed:
                xl, xh = lax.rem(fixed["x"], 2), fixed["x"] // 2
            cols = pl.ds(halfs * 1024, 1024) if half is None else pl.ds(halfs * 1024 + half * 512, 512)
            return out_all.at[xl, place.c, fixed.get("z", ALL), fixed.get("y", ALL), xh, ALL, cols]

        return view

    def up_view(fixed, half):
        xl = ALL if half is None else pl.ds(half, 1)
        return up_all.at[xl, ALL, fixed.get("z", ALL), fixed.get("y", ALL)]

    def dn_view(fixed, half):
        cols = ALL if half is None else pl.ds(half * 1024, 1024)
        return dn_all.at[fixed.get("z", ALL), fixed.get("y", ALL), :, cols]

    def wq_view(p, cols):
        def view(fixed, half):
            xl = ALL if half is None else pl.ds(half, 1)
            return wq.at[p, xl, ALL, fixed.get("z", ALL), fixed.get("y", ALL), ALL, ALL, cols]

        return view

    def index(dx, dc):
        return place.step("x", dx) * 2 + (1 - place.c if dc else place.c)

    copies = [
        pltpu.make_async_copy(
            wp.at[:, :, piece(place.g, 256)], wq.at[:, place.xl, place.c, place.z, place.y, place.xh], local.at[0]
        ),
        pltpu.make_async_copy(up.at[:, piece(place.g, 1024)], up_all.at[home], local.at[1]),
        pltpu.make_async_copy(dn, dn_all.at[place.z, place.y], local.at[2]),
    ]
    copies += [
        pltpu.make_async_copy(
            wo.at[:, pl.ds(h * 1024, 1024)],
            out_view(h)({a: place.at(a) for a in "xyz"}, None),
            local.at[3 + h],
        )
        for h in range(2)
    ]
    for copy in copies:
        copy.start()
    wq_spread = [
        sends.push(
            wp.at[:, :, piece(index(*m), 256)],
            wq.at[:, place.xl, place.c, place.z, place.y, place.xh],
            place.member(*m),
        )
        for m in MEMBERS
    ]
    up_spread = [
        sends.push(up.at[:, piece(index(*m), 1024)], up_all.at[home], place.member(*m)) for m in MEMBERS
    ]

    values = tok[...].astype(f32)
    normed = layer_norm(values, gain[...], shift[...]).astype(bf16)
    own = act.at[place.x, place.c]
    own[:, 0:2048] = normed
    for p in range(3):
        own[:, 2048 + p * 128 : 2176 + p * 128] = (dot(normed, dmaps[p]) * mask[...]).astype(bf16)
    act_gather = GroupGather(place, sends, act)
    own = cotbuf.at[place.x, place.c]
    own[:, 0:2048] = cot[...]
    own[:, 2048:2176] = (dot_nt(cot[...], lum[...]) * mask[...]).astype(bf16)

    copies[0].wait()
    for copy in wq_spread:
        copy.wait()
    fixed = {"z": place.z, "y": place.y}
    qkv_parts = []
    for p, cols, order in (
        (0, ALL, ("y", "z")), (1, ALL, ("z", "y")), (2, pl.ds(0, 128), ("y", "z")), (2, pl.ds(128, 128), ("z", "y"))
    ):
        view = wq_view(p, cols)
        qkv_parts.append(ring_gather(place, sends, view, order, view(fixed, None), Nothing(), False))
    up_gather = ring_gather(place, sends, up_view, ("y", "z"), up_view(fixed, None), Nothing(), False)
    dn_gather = ring_gather(place, sends, dn_view, ("z", "y"), dn, copies[2], False)
    out_gathers = [
        ring_gather(place, sends, out_view(h), order, wo.at[:, pl.ds(h * 1024, 1024)], copies[3 + h], True)
        for h, order in enumerate((("y", "z", "x"), ("x", "z", "y")))
    ]

    def tick(*parts):
        for part in parts:
            next(part)

    tick(*qkv_parts)
    act_gather.own()
    tick(*qkv_parts)
    act_gather.near()
    tick(*qkv_parts)
    copies[1].wait()
    for copy in up_spread:
        copy.wait()
    act_gather.far()
    act_gather.far_done()
    cot_gather = group_gather(place, sends, cotbuf)
    run_all(qkv_parts)
    tick(up_gather, dn_gather, cot_gather)
    kept = [
        pltpu.make_async_copy(wq, qkv_w, local.at[5]),
        pltpu.make_async_copy(act, act_all, local.at[6]),
    ]
    for copy in kept:
        copy.start()

    def project(x, _):
        left = act[x, :, :, 0:2048].reshape(256, 2048)
        for p in range(3):
            low_rank = act[x, :, :, 2048 + p * 128 : 2176 + p * 128].reshape(256, 128)
            value = dot(left, wq[p].reshape(2048, 256)) + bias[p] + dot(low_rank, umaps[p])
            rows[p, x] = value.astype(bf16).reshape(2, 128, 256)
        return 0

    lax.fori_loop(0, 4, project, 0)

    here = place.z * 4 + place.y
    kv = pl.ds(1, 2)
    posts = []
    for n, (dx, dc, j, device, myself) in enumerate(attenders(place)):
        src = rows.at[:, place.step("x", dx), 1 - place.c if dc else place.c, :, pl.ds(j * 128, 128)]
        posts.append(
            Post(src, mine.at[:, piece(here, 128)], device, myself, a_send.at[n], a_recv.at[here])
        )
    swaps = []
    for z, y in plane(place) + [(place.z, place.y)]:
        n = z * 4 + y
        dst = mine.at[:, piece(n, 128)]
        pltpu.make_async_copy(dst, dst, a_recv.at[n]).wait()
        swaps.append(sends.push(mine.at[kv, piece(n, 128)], others.at[:, piece(n, 128)], partner))
    tick(up_gather, dn_gather, cot_gather, *out_gathers)
    for copy in swaps:
        copy.wait()
    kept += [
        pltpu.make_async_copy(mine, heads, local.at[7]),
        pltpu.make_async_copy(others, across, local.at[8]),
    ]
    for copy in kept[2:]:
        copy.start()
    tick(*out_gathers, cot_gather)

    def tile(t, _):
        attend(t, mine, others, lo, att, low, lse, place.xh, scale)
        return 0

    tiles = mine.shape[1] // Q_TILE
    lax.fori_loop(0, tiles - 2, tile, 0)
    tick(up_gather, dn_gather, *out_gathers)
    lax.fori_loop(tiles - 2, tiles, tile, 0)
    back = heads_out(place, sends, low, merged, local.at[9])
    tick(back, *out_gathers)
    for copy in posts:
        copy.wait_send()
    for copy in kept:
        copy.wait()
    act_gather.finish()
    run_all([back, up_gather, dn_gather, cot_gather, *out_gathers])
    last = pltpu.make_async_copy(cotbuf, cot_all, local.at[10])
    last.start()
    last.wait()
    assert sends.used <= send.shape[0], sends.used


def front(tok, gain, shift, bias, dmaps, umaps, mask, cot, lum, lo, wp, wo, up, dn, scale):
    any_ = pl.BlockSpec(memory_space=pl.ANY)
    vmem = pl.BlockSpec(memory_space=pltpu.VMEM)
    shape = lambda *s: jax.ShapeDtypeStruct(s, bf16)
    vm = lambda *s: pltpu.VMEM(s, bf16)
    return pl.pallas_call(
        functools.partial(front_kernel, scale=scale),
        name="front",
        out_shape=[
            shape(4, 2, 128, 2432),
            shape(3, 2, 2, 4, 4, 2, 16, 256),
            shape(2, 2, 4, 4, 2, 16, 2048),
            shape(2, 2, 4, 4, 2, 16, 1024),
            shape(4, 4, 64, 2048),
            shape(4, 2, 128, 2176),
            shape(3, 2048, 128),
            shape(2, 2048, 128),
            shape(128, 2048),
            jax.ShapeDtypeStruct((2048, 128), f32),
            jax.ShapeDtypeStruct((64, 256), f32),
        ],
        in_specs=[vmem] * 14,
        out_specs=[any_] * 9 + [vmem] * 2,
        scratch_shapes=[
            vm(4, 2, 128, 2432),
            vm(4, 2, 128, 2176),
            vm(3, 2, 2, 4, 4, 2, 16, 256),
            vm(3, 4, 2, 128, 256),
            vm(3, 2048, 128),
            vm(2, 2048, 128),
            vm(16, 128, 128),
        ]
        + [pltpu.SemaphoreType.DMA((n,)) for n in (160, 160, 16, 16, 11)],
        compiler_params=pltpu.CompilerParams(
            collective_id=0, has_side_effects=True, vmem_limit_bytes=56 * MIB
        ),
    )(tok, gain, shift, bias, dmaps, umaps, mask, cot, lum, lo, wp, wo, up, dn)


def feed_forward_kernel(
    second, cot_all, up, dn, umap, dmap, bias, back, forth, two,
    sa, cot, up_v, dn_v, grad_act, act, pre, parts, total, *refs,
):
    scratch, (send, recv, local) = refs[:-3], refs[-3:]
    place = Place()
    greet(members(place))
    sends = Sends(send, recv)
    sa[place.x, place.c] = second[...]
    gather = GroupGather(place, sends, sa)
    loads = [
        pltpu.make_async_copy(src, dst, local.at[n])
        for n, (src, dst) in enumerate(((dn, dn_v), (cot_all, cot), (up, up_v)))
    ]
    for copy in loads:
        copy.start()

    def rows(ref, x, start, size):
        return ref[x, :, :, pl.ds(start, size)].reshape(256, size)

    loads[0].wait()
    loads[1].wait()

    def grad_tile(n, _):
        x, cols = n // 4, piece(lax.rem(n, 4), 256)
        value = dot_nt(rows(cot, x, 0, 2048), dn_v[cols, :])
        grad_act[x, :, cols] = value + dot_nt(rows(cot, x, 2048, 128), dmap[cols, :])
        return 0

    lax.fori_loop(0, 16, grad_tile, 0)
    loads[2].wait()

    def hidden(x):
        def tile(n, _):
            cols = piece(n, 256)
            value = dot(rows(sa, x, 0, 2048), up_v[:, cols]) + bias[:, cols]
            value = value + dot(rows(sa, x, 2048, 128), umap[:, cols])
            phi = 0.5 * (1.0 + lax.erf(value * 0.7071067811865476))
            slope = phi + value * (0.3989422804014327 * jnp.exp2(value * value * (-0.5 * LOG2E)))
            act[x, :, cols] = (value * phi).astype(bf16)
            pre[x, :, cols] = (grad_act[x, :, cols] * slope).astype(bf16)
            return 0

        lax.fori_loop(0, 4, tile, 0)

    def backward(x):
        def tile(n, _):
            cols = piece(n, 256)
            parts[x, :, :, cols] = dot_nt(pre[x], up_v[cols, :]).astype(bf16).reshape(2, 128, 256)
            return 0

        lax.fori_loop(0, 8, tile, 0)
        parts[x, :, :, pl.ds(2048, 128)] = dot_nt(pre[x], umap[...]).astype(bf16).reshape(2, 128, 128)

    gather.own()
    hidden(place.x)
    gather.near()
    hidden(place.step("x", -1))
    hidden(place.step("x", 1))
    gather.far()
    gather.far_done()
    hidden(place.step("x", 2))

    sums = GroupSum(place, sends, parts, scratch)
    backward(sums.xs[0])
    sums.cross(0)
    backward(sums.xs[1])
    sums.cross(1)
    sums.merge(0)
    sums.first()
    backward(sums.xs[2])
    sums.cross(2)
    backward(sums.xs[3])
    sums.cross(3)
    sums.merge(1)
    sums.merge(2)
    sums.second()

    def forward(n, _):
        x, cols = n // 4, piece(lax.rem(n, 4), 512)
        value = dot(act[x], dn_v[:, cols])
        forth[x, :, :, cols] = value.astype(bf16).reshape(2, 128, 512)
        return 0

    lax.fori_loop(0, 16, forward, 0)

    def small(x, _):
        forth[x, :, :, pl.ds(2048, 128)] = dot(act[x], dmap[...]).astype(bf16).reshape(2, 128, 128)
        one = dot_tn(act[x], rows(cot, x, 2048, 128))
        other = dot_tn(pre[x], rows(sa, x, 2048, 128))

        @pl.when(x == 0)
        def _():
            total[0] = one
            total[1] = other

        @pl.when(x > 0)
        def _():
            total[0] += one
            total[1] += other

        return 0

    lax.fori_loop(0, 4, small, 0)
    two[...] = total[...].astype(bf16)
    back[...] = sums.result()
    gather.finish()


def feed_forward(second, cot_all, up, dn, umap, dmap, bias):
    any_ = pl.BlockSpec(memory_space=pl.ANY)
    vmem = pl.BlockSpec(memory_space=pltpu.VMEM)
    vm = lambda *s: pltpu.VMEM(s, bf16)
    return pl.pallas_call(
        feed_forward_kernel,
        name="feed_forward",
        out_shape=[
            jax.ShapeDtypeStruct((128, 2176), f32),
            jax.ShapeDtypeStruct((4, 2, 128, 2176), bf16),
            jax.ShapeDtypeStruct((2, 1024, 128), bf16),
        ],
        in_specs=[vmem] + [any_] * 3 + [vmem] * 3,
        out_specs=[vmem] * 3,
        scratch_shapes=[
            vm(4, 2, 128, 2176),
            vm(4, 2, 128, 2176),
            vm(2048, 1024),
            vm(1024, 2048),
            pltpu.VMEM((4, 256, 1024), f32),
            vm(4, 256, 1024),
            vm(4, 256, 1024),
            vm(4, 2, 128, 2176),
            pltpu.VMEM((2, 1024, 128), f32),
        ]
        + GroupSum.scratch(2176)
        + [pltpu.SemaphoreType.DMA((k,)) for k in (16, 16, 3)],
        compiler_params=pltpu.CompilerParams(collective_id=1, has_side_effects=True, vmem_limit_bytes=60 * MIB),
    )(second, cot_all, up, dn, umap, dmap, bias)


def both_heads(gq, p, x):
    heads = [gq[p, x, :, j].reshape(256, 128) for j in range(2)]
    return jnp.concatenate(heads, axis=1)


def tail_kernel(
    grads, qkv_w, act_all, umaps, dmaps, mask, tok, gain, grad_res,
    input_grad, a_final, b_final,
    a_res, b_res, gq, wq, act, parts, gaq, a_sum, b_sum, a_s1, a_q1, a_s2, a_f, b_s1, b_q1, b_s2, b_f, *refs,
):
    scratch, (send, recv, local) = refs[:-3], refs[-3:]
    place = Place()
    greet(members(place) + neighbours(place, ("y", "z")))
    sends = Sends(send, recv)
    loads = [
        pltpu.make_async_copy(src, dst, local.at[n])
        for n, (src, dst) in enumerate(((grads, gq), (qkv_w, wq), (act_all, act)))
    ]
    for copy in loads:
        copy.start()
    loads[0].wait()
    loads[1].wait()

    def partial(x):
        left = [both_heads(gq, p, x) for p in range(3)]

        def tile(n, _):
            xl, c, z = n // 4, lax.rem(n // 2, 2), piece(lax.rem(n, 2), 2)
            value = dot_nt(left[0], wq[0, xl, c, z].reshape(256, 256))
            for p in (1, 2):
                value = value + dot_nt(left[p], wq[p, xl, c, z].reshape(256, 256))
            parts[x, :, :, piece(n, 256)] = value.astype(bf16).reshape(2, 128, 256)
            return 0

        lax.fori_loop(0, 8, tile, 0)
        for p in range(3):
            value = dot_nt(left[p], umaps[p]).astype(bf16)
            parts[x, :, :, 2048 + p * 128 : 2176 + p * 128] = value.reshape(2, 128, 128)

    sums = GroupSum(place, sends, parts, scratch)
    partial(sums.xs[0])
    sums.cross(0)
    partial(sums.xs[1])
    sums.cross(1)
    sums.merge(0)
    sums.first()
    partial(sums.xs[2])
    sums.cross(2)
    partial(sums.xs[3])
    sums.cross(3)
    sums.merge(1)
    sums.merge(2)
    sums.second()

    loads[2].wait()
    for p in range(3):
        total = jnp.zeros((128, 256), f32)
        for x in range(4):
            low_rank = act[x, :, :, 2048 + p * 128 : 2176 + p * 128].reshape(256, 128)
            total = total + dot_tn(low_rank, both_heads(gq, p, x))
        b_sum[p] = total.astype(bf16)

    here = {a: place.at(a) for a in "xyz"}

    def b_view(fixed, half):
        y = fixed.get("y")
        yr, yc = (ALL, ALL) if y is None else (y // 2, lax.rem(y, 2))
        if half is not None:
            yr = pl.ds(half, 1)
        return b_res.at[:, fixed.get("x", ALL), place.c, fixed.get("z", ALL), yr, yc]

    keep = pltpu.make_async_copy(b_f, b_view(here, None), local.at[3])
    b_part = spread_sum(
        place, sends, ("z", "y"),
        [
            (lambda p: b_sum.at[:, piece(p, 32)], b_s1, b_q1),
            (lambda p: b_q1.at[:, piece(p // 2, 16), piece(lax.rem(p, 2), 128)], b_s2, b_f),
        ],
        (b_view, ("y", "z", "x")), b_f, keep,
    )
    next(b_part)
    total = sums.result()
    own = gaq.at[place.x, place.c]
    grad_first = total[:, 0:2048]
    for p in range(3):
        low_rank = (total[:, 2048 + p * 128 : 2176 + p * 128] * mask[...]).astype(bf16)
        own[:, p * 128 : p * 128 + 128] = low_rank
        grad_first = grad_first + dot_nt(low_rank, dmaps[p])
    gather = GroupGather(place, sends, gaq)
    next(b_part)
    result = grad_res[...] + layer_norm_back(tok[...].astype(f32), gain[...], grad_first)
    input_grad[...] = result.astype(bf16)
    gather.own()
    gather.near()
    next(b_part)
    gather.far()
    gather.far_done()

    cols = piece(place.g, 256)
    left = act[:, :, :, cols].reshape(1024, 256)
    for p in range(3):
        right = gaq[:, :, :, p * 128 : p * 128 + 128].reshape(1024, 128)
        a_sum[p] = dot_tn(left, right).astype(bf16)

    def a_view(fixed, half):
        y = fixed.get("y", ALL)
        if half is not None:
            y = pl.ds(half * 2, 2)
        return a_res.at[:, fixed.get("x", ALL), place.c, fixed.get("z", ALL), y]

    keep = pltpu.make_async_copy(a_f, a_view(here, None), local.at[4])
    a_part = spread_sum(
        place, sends, ("z", "y"),
        [
            (lambda p: a_sum.at[:, piece(p, 64)], a_s1, a_q1),
            (lambda p: a_q1.at[:, piece(p, 16)], a_s2, a_f),
        ],
        (a_view, ("y", "x", "z")), a_f, keep,
    )
    run_all([a_part, b_part])
    gather.finish()
    moves = [pltpu.make_async_copy(a_res, a_final, local.at[5])]
    for g in range(8):
        for yc in range(2):
            src = b_res.at[:, g // 2, g % 2, :, :, yc]
            dst = b_final.at[:, :, :, :, pl.ds(g * 256 + yc * 128, 128)]
            moves.append(pltpu.make_async_copy(src, dst, local.at[6 + g * 2 + yc]))
    for copy in moves:
        copy.start()
    for copy in moves:
        copy.wait()
    assert sends.used <= send.shape[0], sends.used


def tail(grads, qkv_w, act_all, umaps, dmaps, mask, tok, gain, grad_res):
    any_ = pl.BlockSpec(memory_space=pl.ANY)
    vmem = pl.BlockSpec(memory_space=pltpu.VMEM)
    vm = lambda *s: pltpu.VMEM(s, bf16)
    shape = lambda *s: jax.ShapeDtypeStruct(s, bf16)
    a_shape, b_shape = (3, 4, 2, 4, 4, 16, 128), (3, 4, 2, 4, 2, 2, 16, 128)
    return pl.pallas_call(
        tail_kernel,
        name="tail",
        out_shape=[shape(128, 2048), shape(*a_shape), shape(3, 4, 2, 16, 2048)],
        in_specs=[any_] * 3 + [vmem] * 6,
        out_specs=[vmem] + [any_] * 2,
        scratch_shapes=[
            vm(*a_shape),
            vm(*b_shape),
            vm(3, 4, 2, 2, 128, 128),
            vm(3, 2, 2, 4, 4, 2, 16, 256),
            vm(4, 2, 128, 2432),
            vm(4, 2, 128, 2432),
            vm(4, 2, 128, 384),
            vm(3, 256, 128),
            vm(3, 128, 256),
            vm(3, 3, 64, 128),
            vm(3, 64, 128),
            vm(3, 3, 16, 128),
            vm(3, 16, 128),
            vm(3, 3, 32, 256),
            vm(3, 32, 256),
            vm(3, 3, 16, 128),
            vm(3, 16, 128),
        ]
        + GroupSum.scratch(2432)
        + [pltpu.SemaphoreType.DMA((k,)) for k in (100, 100, 22)],
        compiler_params=pltpu.CompilerParams(collective_id=5, has_side_effects=True, vmem_limit_bytes=56 * MIB),
    )(grads, qkv_w, act_all, umaps, dmaps, mask, tok, gain, grad_res)


def per_device(
    tokens,
    document_starts,
    document_adapter,
    layernorm_gain,
    layernorm_bias,
    projection_weight,
    output_weight,
    up_weight,
    down_weight,
    projection_bias,
    upper_bias,
    attention_down_maps,
    attention_up_maps,
    upper_down_maps,
    upper_up_maps,
    lower_down_maps,
    lower_up_maps,
    cotangent,
):
    local_rows, width = tokens.shape[1:]
    head_size = width // HEADS
    seq = local_rows * 32
    scale = head_size ** (-0.5)
    starts = document_starts[0]
    chosen = document_adapter[0]
    xl, c, z, y, xh = (lax.axis_index(a) for a in AXES)
    group = (xh * 2 + xl) * 2 + c
    first_row = ((z * 4 + y) * 2 + xh) * local_rows
    local_pos = first_row + jnp.arange(local_rows, dtype=jnp.int32)
    local_seg = jnp.sum((starts[None, :] <= local_pos[:, None]).astype(jnp.int32), axis=1) - 1
    doc_ids = jnp.arange(starts.shape[0], dtype=jnp.int32)
    token_adapter = jnp.sum(jnp.where(local_seg[:, None] == doc_ids[None, :], chosen[None, :], 0), axis=1)
    columns = jnp.arange(upper_down_maps.shape[1], dtype=jnp.int32) // ADAPTER_RANK
    mask = (token_adapter[:, None] == columns[None, :]).astype(f32)

    rows = seq // 2
    q_pos = positions_of(jnp.arange(rows, dtype=jnp.int32), xh)
    doc_lo = jnp.max(jnp.where(starts[None, :] <= q_pos[:, None], starts[None, :], 0), axis=1)
    last_key = (2 * ((jnp.arange(rows // K_TILE) + 1) * K_TILE // 128 - 1) + 1) * 128 + 127
    doc_end = jnp.min(jnp.where(starts[None, :] > last_key[:, None], starts[None, :], seq), axis=1)
    last_q_tile = jnp.minimum((doc_end + 255) // 256 * 128 + Q_TILE - 1, rows + Q_TILE - 1) // Q_TILE
    info_back = jnp.concatenate([xh[None], last_q_tile]).astype(jnp.int32)

    inputs = tokens[0].astype(f32)
    cot = cotangent[0]
    bias_rows = jnp.stack([projection_bias[0], jnp.zeros_like(projection_bias[0]), projection_bias[1]])

    def my_columns(array):
        return lax.dynamic_slice_in_dim(array, group * 256, 256, array.ndim - 1)

    def my_hidden(array):
        lead = array.shape[:-1]
        part = lax.dynamic_slice_in_dim(array, (xl * 2 + c) * 2048, 2048, array.ndim - 1)
        part = part.reshape(lead + (16, 2, 64))
        return lax.dynamic_index_in_dim(part, xh, len(lead) + 1, False).reshape(lead + (1024,))

    up_members = jnp.transpose(up_weight.reshape(16, 2, 2, 16, 2, 64), (0, 4, 1, 2, 3, 5)).reshape(16, 8192)
    my_up_maps = my_columns(attention_up_maps[:3])
    (
        act_all, qkv_w, out_all, up_all, dn_all, cot_all, by_head, across, merged, attended, lse
    ) = front(
        tokens[0], layernorm_gain[:1], layernorm_bias[:1], my_columns(bias_rows)[:, None, :],
        attention_down_maps[:3], my_up_maps, mask, cot, lower_up_maps, doc_lo[:, None],
        jnp.transpose(projection_weight, (1, 0, 2)), output_weight, up_members, down_weight, scale,
    )
    w_out = out_all.reshape(width, width)
    lse = lse.reshape(rows // Q_TILE, 8, Q_TILE)[:, 0]

    adapt_out = (dot(merged, attention_down_maps[3]) * mask).astype(bf16)
    residual = inputs + dot(merged, w_out) + projection_bias[2] + dot(adapt_out, attention_up_maps[3])
    second_in = layer_norm(residual, layernorm_gain[1], layernorm_bias[1]).astype(bf16)
    adapt_up = (dot(second_in, upper_down_maps) * mask).astype(bf16)

    down_maps = lax.dynamic_slice_in_dim(lower_down_maps, (xl * 2 + c) * 2048, 2048, 0)
    down_maps = lax.dynamic_index_in_dim(down_maps.reshape(16, 2, 64, 128), xh, 1, False).reshape(1024, 128)
    back, forth, two = feed_forward(
        jnp.concatenate([second_in, adapt_up], axis=1), cot_all, up_all.reshape(width, 1024),
        dn_all.reshape(1024, width), my_hidden(upper_up_maps), down_maps, my_hidden(upper_bias)[None],
    )

    grad_adapt_up = (back[:, width:] * mask).astype(bf16)
    grad_a_up = dot_tn(second_in, grad_adapt_up)
    grad_second = back[:, :width] + dot_nt(grad_adapt_up, upper_down_maps)
    grad_residual = cot.astype(f32) + layer_norm_back(residual, layernorm_gain[1], grad_second)
    grad_branch = grad_residual.astype(bf16)
    grad_b_out = dot_tn(adapt_out, grad_branch)
    grad_adapt_out = (dot_nt(grad_branch, attention_up_maps[3]) * mask).astype(bf16)
    grad_a_out = dot_tn(merged, grad_adapt_out)
    grad_merged = (dot_nt(grad_branch, w_out) + dot_nt(grad_adapt_out, attention_down_maps[3])).astype(bf16)

    grad_heads, forth_sum = grads_in(grad_merged, forth)
    adapt_down = (forth_sum[:, width:] * mask).astype(bf16)
    output = residual + forth_sum[:, :width] + projection_bias[3] + dot(adapt_down, lower_up_maps)
    grad_b_down = dot_tn(adapt_down, cot)

    grad_heads = grad_heads.reshape(rows, head_size)
    row_dot = jnp.sum(grad_heads.astype(f32) * attended, axis=-1).reshape(rows // Q_TILE, Q_TILE)
    dq, other, own = flash_backward(
        info_back, grad_heads, lse, row_dot, doc_lo.reshape(rows // Q_TILE, Q_TILE), by_head, across, scale
    )
    grad_qkv = grads_out(dq.reshape(HEADS, local_rows, head_size), other, own)
    early = sum_all(
        jnp.stack([grad_a_out, grad_a_up]).astype(bf16), jnp.stack([grad_b_out, grad_b_down]).astype(bf16), two
    )
    input_grad, late_a, late_b = tail(
        grad_qkv, qkv_w, act_all, my_up_maps, attention_down_maps[:3], mask, tokens[0], layernorm_gain[:1],
        grad_residual,
    )
    late_a = late_a.reshape(3, width, 128)
    late_b = late_b.reshape(3, 128, width)
    return (
        output.astype(bf16)[None],
        input_grad[None],
        jnp.concatenate([late_a, early[0][:1]]).astype(f32),
        jnp.concatenate([late_b, early[1][:1]]).astype(f32),
        early[0][1].astype(f32),
        jnp.transpose(early[2][1]).astype(f32),
        early[2][0].astype(f32),
        early[1][1].astype(f32),
    )


def solution(mesh):
    fine = jax.sharding.Mesh(mesh.devices.reshape(SIZES), AXES)
    by_token = P(STREAM, TOKEN, None)
    shard = AXES
    in_specs = (
        by_token,
        P(STREAM, None),
        P(STREAM, None),
        P(),
        P(),
        P(shard, None, None),
        P(shard, None),
        P(shard, None),
        P(shard, None),
        P(),
        P(),
        P(),
        P(),
        P(),
        P(),
        P(),
        P(),
        by_token,
    )
    out_specs = (by_token, by_token, P(), P(), P(), P(), P(), P())
    return jax.shard_map(per_device, mesh=fine, in_specs=in_specs, out_specs=out_specs, check_vma=False)
```

time: 1140 us -> 560 us (0.49)
  waiting for transfers between devices: 661 us -> 0 us
  Pallas kernels: 223 us -> 482 us
  matrix products: 126 us -> 23.6 us
  starting transfers between devices: 25.5 us -> 0 us
  local copies, waits for them, and re-layouts: 44.2 us -> 28.5 us
  between operations: 15.3 us -> 1.59 us
  blocking collectives: 13 us -> 0 us
    psum x2 -> x0, waiting for transfers between devices: 472 us -> none  [the longest x1 317 us: per_device(): part_b, part_a = lax.psum((grad_b_up, grad_a_down), TOKEN)]
    pallas_call x2 -> x6, Pallas kernels: 190 us -> 450 us  [the longest x1 177 us: front(): pl.pallas_call(functools.partial(front_kernel, scale=scale), name='front'...]
    ppermute x2 -> x0, waiting for transfers between devices: 68.1 us -> none  [the longest x1 36 us: per_device(): lax.ppermute(jnp.stack([dk[0], dv[0]]).astype(bf16), 'xh', [(0, 1), (1, 0)])]
    reduce_scatter x2 -> x0, waiting for transfers between devices: 51.9 us -> none  [to_owner(): lax.psum_scatter(jnp.concatenate(arrays, axis=1).astype(bf16), STREAM, sc...]
    all_to_all x3 -> x0, waiting for transfers between devices: 47.2 us -> none  [the longest x1 24.5 us: per_device(): lax.all_to_all(by_token, HEAD, split_axis=2, concat_axis=1, tiled=True)]
    dot_general x8 -> x0, matrix products: 40.6 us -> none  [the longest x1 15.5 us: per_device(): jnp.einsum('td,pde->pte', first_in, w_qkv, preferred_element_type=f32)]
    dot_general x9 -> x5, matrix products: 38.5 us -> 8.32 us  [dot(): return jnp.dot(left, right, preferred_element_type=f32)]
    dot_general x9 -> x4, matrix products: 35.2 us -> 10.6 us  [dot_nt(): lax.dot_general(left, right, (((1,), (1,)), ((), ())), preferred_element_...]
  transfers between devices with their start and end apart: 13 -> 0, of which waited for: 9 -> 0; matrix products, arithmetic and copies ran while one was open for 10% -> 0% of each run, Pallas kernels for 5% -> 0%
where the time goes in v3:
time: 560 us; the launch traced here: 555 us
  Pallas kernels  482 us (86%)
  local copies, waits for them, and re-layouts  28.5 us (5%)
  matrix products  23.6 us (4%)
  other arithmetic  19.6 us (4%)
    pallas_call x1, Pallas kernels, front(): pl.pallas_call(functools.partial(front_kernel, scale=scale), name='front'...  177 us
    pallas_call x1, Pallas kernels, tail(): pl.pallas_call(tail_kernel, name='tail', out_shape=[shape(128, 2048), sha...  80.3 us
    pallas_call x1, Pallas kernels, feed_forward(): pl.pallas_call(feed_forward_kernel, name='feed_forward', out_shape=[jax.S...  59.5 us
    pallas_call x1, Pallas kernels, sum_all(): pl.pallas_call(functools.partial(sums_kernel, count), name='sum_all', out...  50.7 us
    pallas_call x1, Pallas kernels, grads_out(): pl.pallas_call(grads_out_kernel, name='grads_out', out_shape=jax.ShapeDty...  50.4 us
    pallas_call x1, Pallas kernels, grads_in(): pl.pallas_call(grads_in_kernel, name='grads_in', out_shape=[jax.ShapeDtyp...  31.8 us
    pallas_call x1, Pallas kernels, flash_backward(): pl.pallas_call(functools.partial(flash_back_kernel, scale=scale), name='a...  31.4 us

profile of v3, /device:TPU:1, one launch (start us, length us, event | category | flops | bytes accessed | tf_op | source)
XLA Modules:
  0.0 554.9 jit_solution(2188927747784369076)
XLA Ops:
  5.6 1.4 fusion.44
  9.4 1.5 reshape.177
  15.2 1.3 copy.37.lo
  17.8 1.4 slice-done.2
  19.9 177.4 %front.1 = (bf16[4,2,128,2432]{3,2,1,0:T(8,128)(2,1)}, bf16[3,2,2,4,4,2,16,256]{7,6,5,4,3,2,1,0:T(8,128)(2,1)}, bf16[2,2,4,4,2,16,2048]{6,5,4,3,2,1,0:T(8,128)(2...) custom-call(bf16[128,2048]{1,0:T(8,128)(2,1)} %bitcast.99, ...), custom_call_target="tpu_custom_call" | custom-call | tf_op jit(solution)/shard_map/front/pallas_call | solution.py:940
  198.2 1.5 fusion.9
  199.7 5.0 fusion.1
  206.9 59.5 %feed_forward.1 = (f32[128,2176]{1,0:T(8,128)}, bf16[4,2,128,2176]{3,2,1,0:T(8,128)(2,1)}, bf16[2,1024,128]{2,1,0:T(8,128)(2,1)}) custom-call(bf16[128,2176]{1,0:T(8,128)(2,1)} %pad_maximum_fusion.2.second, bf16[4,2,128,2176]{3,2,1,0:T(8,128)(2,1)} %get-tuple-element.35.cot_all, bf16[2048,1024]{1,0:T(8,128)(2,1)} %bitcast.101, bf16[1024,2048]{1,0:T(8,128)(2,1)} %bitcast.102, ...), custom_call_target="tpu_custom_call" | custom-call | tf_op jit(solution)/shard_map/feed_forward/pallas_call | solution.py:1087
  266.4 2.1 fusion.5
  268.5 1.8 fusion.39
  270.9 7.1 %fusion.33 = f32[128,2048]{1,0:T(8,128)S(1)} fusion(bf16[2048,2048]{1,0:T(8,128)(2,1)} %bitcast.97, f32[128,2048]{1,0:T(8,128)S(1)} %multiply_add_fusion.grad_res), kind=kOutput, calls=%fused_computation.106 | convolution fusion | flops 1074003968 | bytes 10485760 | tf_op jit(solution)/shard_map/dot_general | solution.py:46
  278.4 1.3 fusion.2.grad
  279.8 31.8 %grads_in.1 = (bf16[16,128,128]{2,1,0:T(8,128)(2,1)S(1)}, f32[128,2176]{1,0:T(8,128)S(1)}) custom-call(bf16[128,2048]{1,0:T(8,128)(2,1)S(1)} %fusion.2.grad, bf16[4,2,128,2176]{3,2,1,0:T(8,128)(2,1)S(1)} %bitcast.91), custom_call_target="tpu_custom_call" | custom-call | tf_op jit(solution)/shard_map/grads_in/pallas_call | solution.py:417
  315.5 1.4 pad_maximum_fusion.a
  318.6 31.4 %attention_backward.1 = (bf16[2048,128]{1,0:T(8,128)(2,1)S(1)}, bf16[16,2,128,128]{3,2,1,0:T(8,128)(2,1)S(1)}, f32[16,2,128,128]{3,2,1,0:T(8,128)S(1)}) custom-call(s32[5]{0:T(128)S(1)} %pad_add_fusion.info, bf16[3,2048,128]{2,1,0:T(8,128)(2,1)S(1)} %copy-done.2, bf16[2048,128]{1,0:T(8,128)(2,1)S(1)} %bitcast.92, f32[8,256]{1,0:T(8,128)S(1)} %bitcast.95, ...), custom_call_target="tpu_custom_call" | custom-call | tf_op jit(solution)/shard_map/attention_backward/pallas_call | solution.py:701
  350.0 50.4 %grads_out.1.grads = bf16[3,4,2,2,128,128]{5,4,3,2,1,0:T(8,128)(2,1)S(1)} custom-call(bf16[16,128,128]{2,1,0:T(8,128)(2,1)S(1)} %bitcast.94, bf16[16,2,128,128]{3,2,1,0:T(8,128)(2,1)S(1)} %get-tuple-element.47.other, f32[16,2,128,128]{3,2,1,0:T(8,128)S(1)} %get-tuple-element.48.own), custom_call_target="tpu_custom_call" | custom-call | tf_op jit(solution)/shard_map/grads_out/pallas_call | solution.py:483
  401.6 80.3 %tail.1 = (bf16[128,2048]{1,0:T(8,128)(2,1)}, bf16[3,4,2,4,4,16,128]{6,5,4,3,2,1,0:T(8,128)(2,1)}, bf16[3,4,2,16,2048]{4,3,2,1,0:T(8,128)(2,1)}) custom-call(bf16[3,4,2,2,128,128]{5,4,3,2,1,0:T(8,128)(2,1)} %copy-done.3, bf16[3,2,2,4,4,2,16,256]{7,6,5,4,3,2,1,0:T(8,128)(2,1)} %get-tuple-element.49.qkv_w, ...), custom_call_target="tpu_custom_call" | custom-call | tf_op jit(solution)/shard_map/tail/pallas_call | solution.py:1254
  481.9 50.7 %sum_all.1 = (bf16[2,2,4,4,4,16,128]{6,5,4,3,2,1,0:T(8,128)(2,1)S(1)}, bf16[2,2,4,16,2048]{4,3,2,1,0:T(8,128)(2,1)S(1)}, bf16[2,2,2,4,4,2,64,128]{7,6,5,4,3,2,1,0:T(8,128)(2,1)}) custom-call(bf16[2,2048,128]{2,1,0:T(8,128)(2,1)S(1)} %pad_maximum_fusion.a, bf16[2,128,2048]{2,1,0:T(8,128)(2,1)S(1)} %pad_maximum_fusion.1.b, bf16[2,4,4,64,128]{4,3,2,1,0:T(8,128)(2,1)S(1)} %bitcast.93), custom_call_target="tpu_custom_call" | custom-call | tf_op jit(solution)/shard_map/sum_all/pallas_call | solution.py:631
  535.7 2.3 maximum_convert_fusion.1
  538.0 2.4 maximum_convert_fusion
  541.7 1.4 fusion.40
  543.1 2.4 bitcast_convert_fusion
  545.5 2.4 bitcast_convert_fusion.1
  547.9 5.7 %copy.42 = f32[8192,128]{0,1:T(8,128)} copy(f32[8192,128]{1,0:T(8,128)} %bitcast_convert_fusion.1) | data formatting | bytes 8388608 | tf_op jit(solution)/shard_map/convert_element_type | solution.py:1402
  (106 shorter events, 29.3 us)
Async XLA Ops:
  0.6 11.5 %copy-start = (bf16[128,8192]{1,0:T(8,128)(2,1)S(1)}, bf16[128,8192]{1,0:T(8,128)(2,1)}, u32[]{:S(2)}) copy-start(bf16[128,8192]{1,0:T(8,128)(2,1)} %param.32) | copy-start | bytes 6291460
  12.5 4.1 copy-start.14
  17.8 1.4 slice-start.2
  19.9 179.8 %copy-start.9 = (bf16[1,128,2048]{2,1,0:T(8,128)(2,1)S(1)}, bf16[1,128,2048]{2,1,0:T(8,128)(2,1)}, u32[]{:S(2)}) copy-start(bf16[1,128,2048]{2,1,0:T(8,128)(2,1)} %param.18) | copy-start | bytes 1572868
  199.7 5.0 copy-start.12
  266.4 3.9 copy-start.8
  270.3 9.5 %slice-start = ((s8[4456448]{0:T(1024)(128)(4,1)}), s8[4194304]{0:T(1024)(128)(4,1)S(1)}, s32[]{:S(2)}) async-start(s8[4456448]{0:T(1024)(128)(4,1)} %bitcast.90), calls=%async_computation | async-start | bytes 8388608
  270.9 7.2 %copy-start.6 = (f32[128,2048]{1,0:T(8,128)}, f32[128,2048]{1,0:T(8,128)S(1)}, u32[]{:S(2)}) copy-start(f32[128,2048]{1,0:T(8,128)S(1)} %multiply_add_fusion.grad_res) | copy-start | bytes 3145732
  270.9 7.2 %copy-start.13 = (bf16[4,128,2048]{2,1,0:T(8,128)(2,1)S(1)}, bf16[4,128,2048]{2,1,0:T(8,128)(2,1)}, u32[]{:S(2)}) copy-start(bf16[4,128,2048]{2,1,0:T(8,128)(2,1)} %param.30) | copy-start | bytes 6291460
  270.9 8.9 %slice-start.1 = ((s8[4456448]{0:T(1024)(128)(4,1)}), s8[262144]{0:T(1024)(128)(4,1)S(1)}, s32[]{:S(2)}) async-start(s8[4456448]{0:T(1024)(128)(4,1)} %bitcast.90), calls=%async_computation.1 | async-start | bytes 524288
  279.8 31.8 %copy-start.11 = (bf16[128,2048]{1,0:T(8,128)(2,1)S(1)}, bf16[128,2048]{1,0:T(8,128)(2,1)}, u32[]{:S(2)}) copy-start(bf16[128,2048]{1,0:T(8,128)(2,1)} %get-tuple-element.33) | copy-start | bytes 1572868
  279.8 32.9 %copy-start.20 = (f32[2048,128]{1,0:T(8,128)S(1)}, f32[2048,128]{1,0:T(8,128)}, u32[]{:S(2)}) copy-start(f32[2048,128]{1,0:T(8,128)} %get-tuple-element.44) | copy-start | bytes 3145732
  311.6 1.5 copy-start.17
  314.3 2.6 copy-start.7
  315.5 1.7 copy-start.16
  316.9 1.4 copy-start.2
  316.9 1.7 copy-start.4
  400.4 1.1 copy-start.3
  401.6 80.3 %copy-start.5 = (bf16[2,1024,128]{2,1,0:T(8,128)(2,1)S(1)}, bf16[2,1024,128]{2,1,0:T(8,128)(2,1)}, u32[]{:S(2)}) copy-start(bf16[2,1024,128]{2,1,0:T(8,128)(2,1)} %get-tuple-element.53) | copy-start | bytes 1572868
  533.9 1.8 copy-start.19
  535.7 2.3 copy-start.18
  538.0 3.7 copy-start.10
  547.9 5.7 %copy-start.21 = (bf16[128,2048]{1,0:T(8,128)(2,1)S(1)}, bf16[128,2048]{1,0:T(8,128)(2,1)}, u32[]{:S(2)}) copy-start(bf16[128,2048]{1,0:T(8,128)(2,1)} %get-tuple-element.51) | copy-start | bytes 1572868
  547.9 6.5 %copy-start.1 = (bf16[128,8192]{1,0:T(8,128)(2,1)S(1)}, bf16[128,8192]{1,0:T(8,128)(2,1)}, u32[]{:S(2)}) copy-start(bf16[128,8192]{1,0:T(8,128)(2,1)} %param.32) | copy-start | bytes 6291460
  (1 other events, 1.0 us)

commit v4 on v3

v4 whole, which is shorter than its diff:
```python
import functools

import jax
import jax.numpy as jnp
from jax import lax
from jax.experimental import pallas as pl
from jax.experimental.pallas import tpu as pltpu
from jax.sharding import PartitionSpec as P

HEADS = 16
ADAPTER_RANK = 16
MESH = pl.DeviceIdType.MESH
AXES = ("xl", "c", "z", "y", "xh")
SIZES = (2, 2, 4, 4, 2)
STREAM = ("xl", "c")
TOKEN = ("z", "y", "xh")
bf16 = jnp.bfloat16
f32 = jnp.float32
LOG2E = 1.4426950408889634
MIB = 2**20
Q_TILE = 256
K_TILE = 512
F_TILE = 256
ALL = slice(None)


def layer_norm(values, gain, shift):
    center = values - jnp.mean(values, axis=-1, keepdims=True)
    spread = jnp.mean(center * center, axis=-1, keepdims=True)
    return center * lax.rsqrt(spread + 1e-05) * gain + shift


def layer_norm_back(values, gain, grad):
    center = values - jnp.mean(values, axis=-1, keepdims=True)
    scale = lax.rsqrt(jnp.mean(center * center, axis=-1, keepdims=True) + 1e-05)
    unit = center * scale
    grad = grad * gain
    along = jnp.mean(grad * unit, axis=-1, keepdims=True)
    return scale * (grad - jnp.mean(grad, axis=-1, keepdims=True) - unit * along)


def dot(left, right):
    return jnp.dot(left, right, preferred_element_type=f32)


def dot_nt(left, right):
    return lax.dot_general(left, right, (((1,), (1,)), ((), ())), preferred_element_type=f32)


def dot_tn(left, right):
    return lax.dot_general(left, right, (((0,), (0,)), ((), ())), preferred_element_type=f32)


def piece(n, size):
    return pl.ds(pl.multiple_of(n * size, size), size)


class Place:
    def __init__(self):
        self.xl, self.c, self.z, self.y, self.xh = (lax.axis_index(a) for a in AXES)
        self.x = self.xh * 2 + self.xl
        self.g = self.x * 2 + self.c

    def at(self, axis):
        return {"x": self.x, "y": self.y, "z": self.z}[axis]

    def step(self, axis, step):
        return lax.rem(self.at(axis) + (step + 4), 4)

    def toward(self, axis, step=1):
        if axis == "c":
            return {"c": 1 - self.c}
        to = self.step(axis, step)
        if axis == "x":
            return {"xl": lax.rem(to, 2), "xh": to // 2}
        return {axis: to}

    def member(self, dx, dc):
        to = {}
        if dx:
            to |= self.toward("x", dx)
        if dc:
            to |= {"c": 1 - self.c}
        return to


MEMBERS = [(dx, dc) for dx in (2, 1, 3, 0) for dc in (0, 1) if dx or dc]


class Sends:
    def __init__(self, send, recv):
        self.send, self.recv, self.used, self.open = send, recv, 0, []

    def push(self, src, dst, device):
        k = self.used
        self.used += 1
        copy = pltpu.make_async_remote_copy(
            src_ref=src,
            dst_ref=dst,
            send_sem=self.send.at[k],
            recv_sem=self.recv.at[k],
            device_id=device,
            device_id_type=MESH,
        )
        copy.start()
        self.open.append(copy)
        return copy


def greet(devices, perhaps=()):
    barrier = pltpu.get_barrier_semaphore()
    for device in devices:
        pl.semaphore_signal(barrier, inc=1, device_id=device, device_id_type=MESH)
    amount = len(devices) + len(perhaps)
    for device, myself in perhaps:
        amount = amount - myself.astype(jnp.int32)

        @pl.when(jnp.logical_not(myself))
        def _():
            pl.semaphore_signal(barrier, inc=1, device_id=device, device_id_type=MESH)

    pl.semaphore_wait(barrier, amount)


def run_all(parts):
    parts = list(parts)
    while parts:
        left = []
        for part in parts:
            try:
                next(part)
                left.append(part)
            except StopIteration:
                pass
        parts = left


def ring_gather(place, sends, view, order, chunk, landed, forward):
    fixed = {a: place.at(a) for a in order}
    across = place.toward("c")
    later, passed = [], []

    def pass_on(block):
        if forward:
            passed.append(sends.push(view(block, None), view(block, None), across))

    if forward:
        passed.append(sends.push(chunk, view(fixed, None), across))
    for number, axis in enumerate(order):
        own = view(fixed, None)
        src = chunk if number == 0 else own
        if number == 0:
            sent = [sends.push(src, own, place.toward(axis, s)) for s in (2, 1, 3)]
            yield
            for s, copy in zip((2, 1, 3), sent):
                copy.wait_recv()
                pass_on(fixed | {axis: place.step(axis, -s)})
            landed.wait()
            later += sent
            del fixed[axis]
            continue
        up = sends.push(src, own, place.toward(axis, 1))
        down = sends.push(src, own, place.toward(axis, -1))
        yield
        before = fixed | {axis: place.step(axis, -1)}
        after = fixed | {axis: place.step(axis, 1)}
        opposite = fixed | {axis: place.step(axis, 2)}
        up.wait_recv()
        half = view(before, 0)
        up_two = sends.push(half, half, place.toward(axis, 1))
        down.wait_recv()
        half = view(after, 1)
        down_two = sends.push(half, half, place.toward(axis, -1))
        pass_on(before)
        pass_on(after)
        yield
        up_two.wait_recv()
        down_two.wait_recv()
        pass_on(opposite)
        later += [up, down, up_two, down_two]
        del fixed[axis]
    yield
    for copy in later:
        copy.wait_send()
    for copy in passed:
        copy.wait()


class Nothing:
    def wait(self):
        pass


def neighbours(place, axes):
    return [place.toward(a, s) for a in axes for s in ((1, 2, 3) if a in "xyz" else (1,))]


def members(place):
    return [place.member(*m) for m in MEMBERS]


class GroupGather:
    def __init__(self, place, sends, buf):
        self.place, self.sends, self.buf = place, sends, buf
        self.mine = buf.at[place.x, place.c]
        self.right, self.left = place.toward("x", 1), place.toward("x", -1)
        self.up = sends.push(self.mine, self.mine, self.right)
        self.down = sends.push(self.mine, self.mine, self.left)
        self.passed = [self.pass_on(self.mine)]

    def pass_on(self, ref):
        return self.sends.push(ref, ref, self.place.toward("c"))

    def own(self):
        self.passed[0].wait_recv()

    def near(self, wait=True):
        x, c = self.place.step("x", -1), self.place.c
        self.up.wait_recv()
        half = self.buf.at[x, c, pl.ds(0, 64)]
        self.up_two = self.sends.push(half, half, self.right)
        self.passed.append(self.pass_on(self.buf.at[x, c]))
        x = self.place.step("x", 1)
        self.down.wait_recv()
        half = self.buf.at[x, c, pl.ds(64, 64)]
        self.down_two = self.sends.push(half, half, self.left)
        self.passed.append(self.pass_on(self.buf.at[x, c]))
        if wait:
            self.near_done()

    def near_done(self):
        self.passed[1].wait_recv()
        self.passed[2].wait_recv()

    def far(self):
        self.up_two.wait_recv()
        self.down_two.wait_recv()
        self.passed.append(self.pass_on(self.buf.at[self.place.step("x", 2), self.place.c]))

    def far_done(self):
        self.passed[3].wait_recv()

    def finish(self):
        for copy in [self.up, self.down, self.up_two, self.down_two] + self.passed:
            copy.wait_send()


def group_gather(place, sends, buf):
    gather = GroupGather(place, sends, buf)
    yield
    gather.own()
    gather.near()
    yield
    gather.far()
    yield
    gather.far_done()
    gather.finish()


def places_in_turn(place):
    return [place.step("x", s) for s in (2, 1, -1, 0)]


class GroupSum:
    def __init__(self, place, sends, parts, scratch):
        self.place, self.sends, self.parts = place, sends, parts
        self.came, self.own, self.left_one, self.right_one, self.left_two, self.right_two = scratch
        self.right, self.left = place.toward("x", 1), place.toward("x", -1)
        self.crossed = {}

    @staticmethod
    def scratch(n):
        vm = lambda *s: pltpu.VMEM(s, bf16)
        return [vm(4, 128, n), vm(3, 128, n), vm(64, n), vm(64, n), vm(128, n), vm(128, n)]

    def cross(self, k):
        place = self.place
        self.crossed[k] = self.sends.push(
            self.parts.at[k, 1 - place.c], self.came.at[k], place.toward("c")
        )

    def merge(self, k):
        self.crossed[k].wait()
        both = self.parts[k, self.place.c].astype(f32) + self.came[k].astype(f32)
        self.own[k] = both.astype(bf16)

    def first(self):
        self.up = self.sends.push(self.own.at[0, pl.ds(0, 64)], self.left_one, self.right)
        self.down = self.sends.push(self.own.at[0, pl.ds(64, 64)], self.right_one, self.left)

    def second(self):
        self.up.wait()
        both = self.own[1, 0:64].astype(f32) + self.left_one[...].astype(f32)
        self.own[1, 0:64] = both.astype(bf16)
        self.up_two = self.sends.push(self.own.at[1], self.left_two, self.right)
        self.down.wait()
        both = self.own[2, 64:128].astype(f32) + self.right_one[...].astype(f32)
        self.own[2, 64:128] = both.astype(bf16)
        self.down_two = self.sends.push(self.own.at[2], self.right_two, self.left)

    def result(self):
        self.crossed[3].wait()
        total = self.parts[3, self.place.c].astype(f32) + self.came[3].astype(f32)
        self.up_two.wait()
        self.down_two.wait()
        return total + self.left_two[...].astype(f32) + self.right_two[...].astype(f32)


def group_sum(place, sends, parts, scratch, out):
    total = GroupSum(place, sends, parts, scratch)
    for k in range(4):
        total.cross(k)
    yield
    total.merge(0)
    total.first()
    total.merge(1)
    total.merge(2)
    yield
    total.second()
    yield
    out[...] = total.result()


def plane(place):
    steps = [(i, j) for i in (2, 1, 3, 0) for j in (2, 1, 3, 0) if i or j]
    return [(lax.rem(place.z + i, 4), lax.rem(place.y + j, 4)) for i, j in steps]


def from_plane(place):
    steps = [(i, j) for i in (2, 1, 3, 0) for j in (2, 1, 3, 0) if i or j]
    return [(lax.rem(place.z + 4 - i, 4), lax.rem(place.y + 4 - j, 4)) for i, j in steps]


def projectors(place):
    x, c = place.z, place.y // 2
    member = {"xl": lax.rem(x, 2), "xh": x // 2, "c": c}
    mine = (place.x == x) & (place.c == c)
    return [(member | {"z": z, "y": y}, None) for z, y in plane(place)] + [
        (member | {"z": place.z, "y": place.y}, mine)
    ]


def attenders(place):
    found = []
    for dx, dc in MEMBERS + [(0, 0)]:
        for j in range(2):
            z, y = place.x, 2 * place.c + j
            device = place.member(dx, dc) | {"z": z, "y": y}
            mine = None if dx or dc else (place.z == z) & (place.y == y)
            found.append((dx, dc, j, device, mine))
    return found


def head_columns(z, y):
    return pl.ds(pl.multiple_of((z * 4 + y) * 128, 128), 128)


def split_greeting(pairs):
    return [d for d, m in pairs if m is None], [(d, m) for d, m in pairs if m is not None]


def plane_devices(place):
    return [{"z": z, "y": y} for z, y in plane(place)]


class Post:
    def __init__(self, src, dst, device, myself, send_sem, recv_sem):
        self.remote = pltpu.make_async_remote_copy(
            src_ref=src, dst_ref=dst, send_sem=send_sem, recv_sem=recv_sem, device_id=device, device_id_type=MESH
        )
        self.myself = myself
        if myself is None:
            self.remote.start()
        else:
            pl.when(myself)(pltpu.make_async_copy(src, dst, recv_sem).start)
            pl.when(jnp.logical_not(myself))(self.remote.start)

    def wait_send(self):
        if self.myself is None:
            self.remote.wait_send()
        else:
            pl.when(jnp.logical_not(self.myself))(self.remote.wait_send)


def heads_out(place, sends, blocks, merged, local):
    cols = head_columns(place.z, place.y)
    keep = pltpu.make_async_copy(blocks.at[place.z * 4 + place.y], merged.at[:, cols], local)
    keep.start()
    sent = [sends.push(blocks.at[z * 4 + y], merged.at[:, cols], {"z": z, "y": y}) for z, y in plane(place)]
    yield
    for copy in sent:
        copy.wait()
    keep.wait()


def reduce_piece(place, sends, final, across, plane_step, along):
    if across:
        src, came, own, out = across
        copy = sends.push(src, came, place.toward("c"))
        yield
        copy.wait()
        out[...] = (own[...].astype(f32) + came[...].astype(f32)).astype(bf16)
    held, slots, out = plane_step
    sent = [sends.push(held(z, y), slots.at[n], {"z": z, "y": y}) for n, (z, y) in enumerate(plane(place))]
    yield
    for copy in sent:
        copy.wait()
    total = held(place.z, place.y)[...].astype(f32)
    for n in range(15):
        total = total + slots[n].astype(f32)
    out[...] = total.astype(bf16)
    if along:
        held, slots, out = along
        sent = [sends.push(held(place.step("x", d)), slots.at[d - 1], place.toward("x", d)) for d in (2, 1, 3)]
        yield
        for copy in sent:
            copy.wait()
        total = held(place.x)[...].astype(f32)
        for d in range(3):
            total = total + slots[d].astype(f32)
        out[...] = total.astype(bf16)


def give_all(place, sends, order, final, view, local):
    here = {a: place.at(a) for a in "xyz"}
    keep = pltpu.make_async_copy(final, view(here), local)
    keep.start()

    def fixed_view(fixed, half):
        at = {a: fixed.get(a, ALL) for a in "xyz"}
        if half is not None:
            at[order[0]] = pl.ds(half * 2, 2)
        return view(at)

    return ring_gather(place, sends, fixed_view, order, final, keep, True)


def a_sum_scratch():
    vm = lambda *shape: pltpu.VMEM(shape, bf16)
    return [vm(1024, 128), vm(1024, 128), vm(15, 64, 128), vm(64, 128), vm(3, 16, 128)]


def b_sum_scratch():
    vm = lambda *shape: pltpu.VMEM(shape, bf16)
    return [vm(64, 2048), vm(64, 2048), vm(15, 64, 128), vm(64, 128), vm(3, 16, 128)]


def a_sum(place, sends, a, final, scratch):
    came, half, s1, quarter, s2 = scratch
    return reduce_piece(
        place, sends, final,
        (a.at[piece(1 - place.c, 1024)], came, a.at[piece(place.c, 1024)], half),
        (lambda z, y: half.at[piece(z * 4 + y, 64)], s1, quarter),
        (lambda x: quarter.at[piece(x, 16)], s2, final),
    )


def b_sum(place, sends, b, final, scratch):
    came, half, s1, quarter, s2 = scratch
    return reduce_piece(
        place, sends, final,
        (b.at[piece(1 - place.c, 64)], came, b.at[piece(place.c, 64)], half),
        (lambda z, y: half.at[:, piece(z * 4 + y, 128)], s1, quarter),
        (lambda x: quarter.at[piece(x, 16)], s2, final),
    )


def two_parts(at):
    x = at["x"]
    if x is ALL:
        return ALL, ALL
    if isinstance(x, pl.Slice):
        return pl.ds(x.start // 2, 1), ALL
    return lax.rem(x, 2), x // 2


def positions_of(local, parity):
    return (2 * (local // 128) + parity) * 128 + lax.rem(local, 128)


def document_start(starts, positions):
    found = jnp.zeros_like(positions)
    for d in range(8):
        found = jnp.where(positions >= starts[0, d], starts[0, d], found)
    return found


def attend(t, mine, others, starts, parity, scale):
    q = mine[0, piece(t, F_TILE), :]
    q_pos = positions_of(t * F_TILE + lax.broadcasted_iota(jnp.int32, (F_TILE, 1), 0), parity)
    lo = document_start(starts, q_pos)
    ones = jnp.ones((K_TILE, 128), bf16)

    def step(kt, carry):
        top, acc = carry
        rows = piece(kt, K_TILE)
        local = kt * K_TILE + lax.broadcasted_iota(jnp.int32, (1, K_TILE), 1)
        scores = []
        for k, k_parity in ((mine[1, rows, :], parity), (others[0, rows, :], 1 - parity)):
            k_pos = positions_of(local, k_parity)
            scores.append(jnp.where((k_pos >= lo) & (k_pos <= q_pos), dot_nt(q, k), -1e30))
        new = jnp.maximum(jnp.max(scores[0], axis=1, keepdims=True), jnp.max(scores[1], axis=1, keepdims=True))
        new = jnp.maximum(top, new)
        acc = acc * jnp.exp2((top - new) * (scale * LOG2E))
        for s, v in zip(scores, (mine[2, rows, :], others[1, rows, :])):
            p = jnp.exp2((s - new) * (scale * LOG2E)).astype(bf16)
            acc = acc + dot(p, jnp.concatenate([v, ones], axis=1))
        return new, acc

    start = (jnp.full((F_TILE, 1), -1e30, f32), jnp.zeros((F_TILE, 256), f32))
    return lax.fori_loop(0, (t * F_TILE + F_TILE + K_TILE - 1) // K_TILE, step, start)


def front_kernel(
    starts, chosen, tok, gain, shift, bias, dmaps, umaps, cot, lum, wp, wo, up, dn,
    act_all, qkv_w, out_all, up_all, dn_all, cot_all, heads, across, merged, att, lse, mask,
    act, cotbuf, wq, up_own, rows, mine, others, low, wq_t, send, recv, a_send, a_recv, local, *, scale,
):
    place = Place()
    sends = Sends(send, recv)
    always, perhaps = split_greeting(projectors(place))
    greet(plane_devices(place) + members(place) + always, perhaps)
    home = (place.xl, place.c, place.z, place.y, place.xh)

    def out_view(h):
        def view(fixed, half):
            xl, xh = (ALL, ALL)
            if "x" in fixed:
                xl, xh = lax.rem(fixed["x"], 2), fixed["x"] // 2
            cols = pl.ds(h * 1024, 1024) if half is None else pl.ds(h * 1024 + half * 512, 512)
            return out_all.at[xl, place.c, fixed.get("z", ALL), fixed.get("y", ALL), xh, ALL, cols]

        return view

    def up_view(fixed, half):
        xl = ALL if half is None else pl.ds(half, 1)
        return up_all.at[xl, ALL, fixed.get("z", ALL), fixed.get("y", ALL)]

    def dn_view(fixed, half):
        cols = ALL if half is None else pl.ds(half * 1024, 1024)
        return dn_all.at[fixed.get("z", ALL), fixed.get("y", ALL), :, cols]

    def wq_view(p, cols):
        def view(fixed, half):
            xl = ALL if half is None else pl.ds(half, 1)
            return wq.at[p, xl, ALL, fixed.get("z", ALL), fixed.get("y", ALL), ALL, ALL, cols]

        return view

    def index(dx, dc):
        return place.step("x", dx) * 2 + (1 - place.c if dc else place.c)

    copies = [
        pltpu.make_async_copy(
            wp.at[:, :, piece(place.g, 256)], wq.at[:, place.xl, place.c, place.z, place.y, place.xh], local.at[0]
        ),
        pltpu.make_async_copy(dn, dn_all.at[place.z, place.y], local.at[2]),
    ]
    copies += [
        pltpu.make_async_copy(
            wo.at[:, pl.ds(h * 1024, 1024)],
            out_view(h)({a: place.at(a) for a in "xyz"}, None),
            local.at[3 + h],
        )
        for h in range(2)
    ]
    for copy in copies:
        copy.start()
    wq_spread = [
        sends.push(
            wp.at[:, :, piece(index(*m), 256)],
            wq.at[:, place.xl, place.c, place.z, place.y, place.xh],
            place.member(*m),
        )
        for m in MEMBERS
    ]

    values = tok[...].astype(f32)
    normed = layer_norm(values, gain[...], shift[...]).astype(bf16)
    position = ((place.z * 4 + place.y) * 2 + place.xh) * 128 + lax.broadcasted_iota(jnp.int32, (128, 1), 0)
    adapter = jnp.zeros_like(position)
    for d in range(8):
        adapter = jnp.where(position >= starts[0, d], chosen[0, d], adapter)
    column = lax.broadcasted_iota(jnp.int32, (128, 128), 1) // ADAPTER_RANK
    keep = (column == adapter).astype(f32)
    mask[...] = keep
    own = act.at[place.x, place.c]
    own[:, 0:2048] = normed
    for p in range(3):
        own[:, 2048 + p * 128 : 2176 + p * 128] = (dot(normed, dmaps[p]) * keep).astype(bf16)
    act_gather = GroupGather(place, sends, act)

    for lead in range(4):
        for pair in range(8):
            at = lead * 2048 + pair * 256
            one, two = up[:, at : at + 128], up[:, at + 128 : at + 256]
            for h in range(2):
                to = (h * 4 + lead) * 1024 + pair * 128
                sides = [v[:, h * 64 : h * 64 + 64] for v in (one, two)]
                up_own[:, to : to + 128] = jnp.concatenate(sides, axis=1)
    up_keep = pltpu.make_async_copy(up_own.at[:, piece(place.g, 1024)], up_all.at[home], local.at[1])
    up_keep.start()
    up_spread = [
        sends.push(up_own.at[:, piece(index(*m), 1024)], up_all.at[home], place.member(*m)) for m in MEMBERS
    ]

    copies[0].wait()
    for copy in wq_spread:
        copy.wait()
    fixed = {"z": place.z, "y": place.y}
    qkv_parts = []
    for p, cols, order in (
        (0, ALL, ("y", "z")), (1, ALL, ("z", "y")), (2, pl.ds(0, 128), ("y", "z")), (2, pl.ds(128, 128), ("z", "y"))
    ):
        view = wq_view(p, cols)
        qkv_parts.append(ring_gather(place, sends, view, order, view(fixed, None), Nothing(), False))
    up_gather = ring_gather(place, sends, up_view, ("y", "z"), up_view(fixed, None), Nothing(), False)
    dn_gather = ring_gather(place, sends, dn_view, ("z", "y"), dn, copies[1], False)
    out_gathers = [
        ring_gather(place, sends, out_view(h), order, wo.at[:, pl.ds(h * 1024, 1024)], copies[2 + h], True)
        for h, order in enumerate((("y", "z", "x"), ("z", "y", "x")))
    ]

    def tick(*parts):
        for part in parts:
            next(part)

    tick(*qkv_parts, dn_gather, *out_gathers)
    own = cotbuf.at[place.x, place.c]
    own[:, 0:2048] = cot[...]
    own[:, 2048:2176] = (dot_nt(cot[...], lum[...]) * keep).astype(bf16)
    act_gather.own()
    tick(*qkv_parts)
    act_gather.near(False)
    tick(*qkv_parts, *out_gathers)
    run_all(qkv_parts)
    tick(*out_gathers)
    up_keep.wait()
    for copy in up_spread:
        copy.wait()
    tick(up_gather)
    kept = []

    def project(x):
        left = act[x, :, :, 0:2048].reshape(256, 2048)
        for p in range(3):
            low_rank = act[x, :, :, 2048 + p * 128 : 2176 + p * 128].reshape(256, 128)
            value = dot(left, wq[p].reshape(2048, 256)) + bias[p] + dot(low_rank, umaps[p])
            rows[p, x] = value.astype(bf16).reshape(2, 128, 256)

    here = place.z * 4 + place.y
    kv = pl.ds(1, 2)
    posts = []

    def post(dx):
        x = place.step("x", dx)
        for n, (to, dc, j, device, myself) in enumerate(attenders(place)):
            if to == dx:
                src = rows.at[:, x, 1 - place.c if dc else place.c, :, pl.ds(j * 128, 128)]
                posts.append(
                    Post(src, mine.at[:, piece(here, 128)], device, myself, a_send.at[0, n], a_recv.at[0, here])
                )
        for n, (to, dc, j, device, _) in enumerate(attenders(place)):
            if to == dx:
                src = rows.at[kv, x, 1 - place.c if dc else place.c, :, pl.ds(j * 128, 128)]
                device = place.member((dx + 2) % 4, dc) | {"z": device["z"], "y": device["y"]}
                myself = None if dc or dx != 2 else (place.z == device["z"]) & (place.y == device["y"])
                posts.append(
                    Post(src, others.at[:, piece(here, 128)], device, myself, a_send.at[1, n], a_recv.at[1, here])
                )

    project(place.x)
    post(0)
    act_gather.near_done()
    project(place.step("x", -1))
    project(place.step("x", 1))
    post(1)
    post(3)
    act_gather.far()
    act_gather.far_done()
    project(place.step("x", 2))
    post(2)
    tick(dn_gather, up_gather, *out_gathers)
    kept.append(pltpu.make_async_copy(act, act_all, local.at[6]))
    kept[-1].start()
    for p in range(3):
        for n in range(4):
            wq_t[p, :, n * 512 : n * 512 + 512] = jnp.transpose(wq[p, n // 2, n % 2].reshape(512, 256))
    kept.append(pltpu.make_async_copy(wq_t, qkv_w, local.at[5]))
    kept[-1].start()
    for n in range(16):
        dst = mine.at[:, piece(n, 128)]
        pltpu.make_async_copy(dst, dst, a_recv.at[0, n]).wait()
    kept.append(pltpu.make_async_copy(mine, heads, local.at[7]))
    kept[-1].start()
    for n in range(16):
        dst = others.at[:, piece(n, 128)]
        pltpu.make_async_copy(dst, dst, a_recv.at[1, n]).wait()
    kept.append(pltpu.make_async_copy(others, across, local.at[8]))
    kept[-1].start()
    cot_gather = group_gather(place, sends, cotbuf)
    tick(cot_gather)

    def tile(t, _):
        peak, total = attend(t, mine, others, starts, place.xh, scale)
        weight = total[:, 128:]
        o = total[:, :128] / weight
        att[piece(t, F_TILE), :] = o
        for b in range(F_TILE // 128):
            low[t * (F_TILE // 128) + b] = o[b * 128 : (b + 1) * 128].astype(bf16)
        line = jnp.transpose(peak * (scale * LOG2E) + jnp.log2(weight))
        for n in range(F_TILE // Q_TILE):
            lse[pl.ds(t * (F_TILE // Q_TILE) + n, 1), :] = line[0:1, n * Q_TILE : n * Q_TILE + Q_TILE]
        return 0

    tiles = mine.shape[1] // F_TILE
    lax.fori_loop(0, tiles // 2, tile, 0)
    tick(dn_gather, up_gather)
    lax.fori_loop(tiles // 2, tiles * 3 // 4, tile, 0)
    tick(cot_gather, *out_gathers)
    lax.fori_loop(tiles * 3 // 4, tiles, tile, 0)
    back = heads_out(place, sends, low, merged, local.at[9])
    tick(back)
    for copy in posts:
        copy.wait_send()
    for copy in kept:
        copy.wait()
    act_gather.finish()
    run_all([back, up_gather, dn_gather, cot_gather, *out_gathers])
    last = pltpu.make_async_copy(cotbuf, cot_all, local.at[10])
    last.start()
    last.wait()
    assert sends.used <= send.shape[0], sends.used


def front(starts, chosen, tok, gain, shift, bias, dmaps, umaps, cot, lum, wp, wo, up, dn, scale):
    any_ = pl.BlockSpec(memory_space=pl.ANY)
    vmem = pl.BlockSpec(memory_space=pltpu.VMEM)
    smem = pl.BlockSpec(memory_space=pltpu.SMEM)
    shape = lambda *s: jax.ShapeDtypeStruct(s, bf16)
    vm = lambda *s: pltpu.VMEM(s, bf16)
    return pl.pallas_call(
        functools.partial(front_kernel, scale=scale),
        name="front",
        out_shape=[
            shape(4, 2, 128, 2432),
            shape(3, 256, 2048),
            shape(2, 2, 4, 4, 2, 16, 2048),
            shape(2, 2, 4, 4, 2, 16, 1024),
            shape(4, 4, 64, 2048),
            shape(4, 2, 128, 2176),
            shape(3, 2048, 128),
            shape(2, 2048, 128),
            shape(128, 2048),
            jax.ShapeDtypeStruct((2048, 128), f32),
            jax.ShapeDtypeStruct((8, 256), f32),
            jax.ShapeDtypeStruct((128, 128), f32),
        ],
        in_specs=[smem] * 2 + [vmem] * 12,
        out_specs=[any_] * 9 + [vmem] * 3,
        scratch_shapes=[
            vm(4, 2, 128, 2432),
            vm(4, 2, 128, 2176),
            vm(3, 2, 2, 4, 4, 2, 16, 256),
            vm(16, 8192),
            vm(3, 4, 2, 128, 256),
            vm(3, 2048, 128),
            vm(2, 2048, 128),
            vm(16, 128, 128),
            vm(3, 256, 2048),
        ]
        + [pltpu.SemaphoreType.DMA(n) for n in ((150,), (150,), (2, 16), (2, 16), (11,))],
        compiler_params=pltpu.CompilerParams(
            collective_id=0, has_side_effects=True, vmem_limit_bytes=56 * MIB
        ),
    )(starts, chosen, tok, gain, shift, bias, dmaps, umaps, cot, lum, wp, wo, up, dn)


def middle_kernel(
    starts, grad, queries, others, att, lse, umaps, mask, parts, a_own, b_own, two,
    by_member, low_rank, total, a_final, b_final, two_final,
    do, delta, dq_acc, dq, own_low, other_low, by_head, from_other, *refs, scale,
):
    scratch, (send, recv, a_send, a_recv, local) = list(refs[:-5]), refs[-5:]
    place = Place()
    across = [{"xh": 1 - place.xh, "z": z, "y": y} for z, y in plane(place)]
    greet(plane_devices(place) + members(place) + across)
    sends = Sends(send, recv)
    here = place.z * 4 + place.y
    parity = place.xh
    kv = pl.ds(1, 2)

    keep = pltpu.make_async_copy(grad.at[:, head_columns(place.z, place.y)], do.at[piece(here, 128)], local.at[0])
    keep.start()
    grads_sent = [
        sends.push(grad.at[:, head_columns(z, y)], do.at[piece(here, 128)], {"z": z, "y": y})
        for z, y in plane(place)
    ]

    def take(n):
        got = scratch[:n]
        del scratch[:n]
        return got

    forth = group_sum(place, sends, parts, take(6), total)
    early = [
        a_sum(place, sends, a_own, a_final, take(5)),
        b_sum(place, sends, b_own, b_final, take(5)),
    ]
    early += [
        reduce_piece(
            place, sends, two_final.at[n], None,
            (lambda z, y, n=n: two.at[n, z, y], scratch[n], two_final.at[n]), None,
        )
        for n in range(2)
    ]

    def tick(*parts):
        for part in parts:
            try:
                next(part)
            except StopIteration:
                pass

    tick(forth, *early)
    dq_acc[...] = jnp.zeros_like(dq_acc)
    keep.wait()
    for copy in grads_sent:
        copy.wait_recv()
    ones = jnp.ones((8, 128), bf16)
    tiles, key_tiles = do.shape[0] // Q_TILE, do.shape[0] // K_TILE

    def row_dots(t, _):
        rows = piece(t, Q_TILE)
        value = do[rows, :].astype(f32) * att[rows, :]
        high = value.astype(bf16)
        low = (value - high.astype(f32)).astype(bf16)
        delta[t] = dot_nt(ones, high) + dot_nt(ones, low)
        return 0

    lax.fori_loop(0, tiles, row_dots, 0)
    tick(forth, *early[:2])

    def keys(kt):
        rows = piece(kt, K_TILE)
        sides = ((others[0, rows, :], others[1, rows, :], 1 - parity), (queries[1, rows, :], queries[2, rows, :], parity))
        local = kt * K_TILE + lax.broadcasted_iota(jnp.int32, (K_TILE, 1), 0)

        def step(qt, carry):
            rows = piece(qt, Q_TILE)
            q = queries[0, rows, :]
            d = do[rows, :]
            q_pos = positions_of(qt * Q_TILE + lax.broadcasted_iota(jnp.int32, (1, Q_TILE), 1), parity)
            lo = document_start(starts, q_pos)
            found, dq_part = [], None
            for (k, v, k_parity), (dk, dv) in zip(sides, carry):
                k_pos = positions_of(local, k_parity)
                s = dot_nt(k, q)
                allowed = (k_pos >= lo) & (k_pos <= q_pos)
                p = jnp.exp2(jnp.where(allowed, s * (scale * LOG2E) - lse[pl.ds(qt, 1), :], -1e30))
                dv = dv + dot(p.astype(bf16), d)
                ds = (p * (dot_nt(v, d) - delta[qt, 0:1, :]) * scale).astype(bf16)
                dk = dk + dot(ds, q)
                part = dot_tn(ds, k)
                dq_part = part if dq_part is None else dq_part + part
                found.append((dk, dv))
            dq_acc[rows, :] += dq_part
            return tuple(found)

        zero = jnp.zeros((K_TILE, 128), f32)
        return lax.fori_loop(kt * (K_TILE // Q_TILE), tiles, step, ((zero, zero),) * 2)

    blocks = K_TILE // 128
    gone = []

    def to_token(k, n, src, dst, other, away):
        z, y = n // 4, lax.rem(n, 4)
        myself = None if other or away else (place.z == z) & (place.y == y)
        device = {"z": z, "y": y} | ({"xh": 1 - place.xh} if other else {})
        gone.append(Post(src, dst, device, myself, a_send.at[k, n], a_recv.at[k, here]))

    for turn in (2, 1, 3, 0):
        kt = lax.rem(place.z + turn, key_tiles)
        for k, low, (dk, dv) in zip((2, 1), (other_low, own_low), keys(kt)):
            for b in range(blocks):
                n = kt * blocks + b
                low[n, 0] = dk[b * 128 : (b + 1) * 128].astype(bf16)
                low[n, 1] = dv[b * 128 : (b + 1) * 128].astype(bf16)
                dst = from_other.at[:, here] if k == 2 else by_head.at[kv, here]
                to_token(k, n, low.at[n], dst, k == 2, turn != 0)
        if turn == 1:
            tick(forth, *early)
    for n in range(16):
        dq[n] = dq_acc[n * 128 : (n + 1) * 128].astype(bf16)
    for turn in (2, 1, 3, 0):
        for b in range(blocks):
            n = lax.rem(place.z + turn, 4) * 4 + b
            to_token(0, n, dq.at[n], by_head.at[0, here], False, turn != 0)
    tick(*early)

    mine = None
    shared = []
    for dx, dc in MEMBERS + [(0, 0)]:
        g = place.step("x", dx) * 2 + (1 - place.c if dc else place.c)
        for j in range(2):
            for k, dst in ((2, from_other.at[:, 0]), (1, by_head.at[kv, 0]), (0, by_head.at[0, 0])):
                pltpu.make_async_copy(dst, dst, a_recv.at[k, g * 2 + j]).wait()
        pair = piece(g, 2)
        by_head[1:3, pair] = (by_head[1:3, pair].astype(f32) + from_other[:, pair].astype(f32)).astype(bf16)
        src, dst = by_head.at[:, pair], by_member.at[:, place.x, place.c]
        if dx or dc:
            shared.append(sends.push(src, dst, place.member(dx, dc)))
        else:
            mine = pltpu.make_async_copy(src, dst, local.at[7])
            mine.start()
    for p in range(3):
        whole = jnp.concatenate([by_head[p, n] for n in range(16)], axis=1)
        low_rank[:, p * 128 : p * 128 + 128] = (dot_nt(whole, umaps[p]) * mask[...]).astype(bf16)
    run_all([forth] + early)
    for copy in gone + grads_sent:
        copy.wait_send()
    for copy in shared:
        copy.wait()
    mine.wait()
    assert sends.used <= send.shape[0], sends.used


def middle(starts, grad, queries, others, att, lse, umaps, mask, parts, a_own, b_own, two, scale):
    any_ = pl.BlockSpec(memory_space=pl.ANY)
    vmem = pl.BlockSpec(memory_space=pltpu.VMEM)
    smem = pl.BlockSpec(memory_space=pltpu.SMEM)
    vm = lambda *s: pltpu.VMEM(s, bf16)
    shape = lambda *s: jax.ShapeDtypeStruct(s, bf16)
    return pl.pallas_call(
        functools.partial(middle_kernel, scale=scale),
        name="attention_backward",
        out_shape=[
            shape(3, 4, 2, 2, 128, 128),
            shape(128, 384),
            jax.ShapeDtypeStruct((128, 2048), f32),
            shape(16, 128),
            shape(16, 128),
            shape(2, 64, 128),
        ],
        in_specs=[smem] + [vmem] * 11,
        out_specs=[any_] + [vmem] * 5,
        scratch_shapes=[
            vm(2048, 128),
            pltpu.VMEM((8, 8, 256), f32),
            pltpu.VMEM((2048, 128), f32),
            vm(16, 128, 128),
            vm(16, 2, 128, 128),
            vm(16, 2, 128, 128),
            vm(3, 16, 128, 128),
            vm(2, 16, 128, 128),
        ]
        + GroupSum.scratch(2048)
        + a_sum_scratch()
        + b_sum_scratch()
        + [vm(15, 64, 128)] * 2
        + [pltpu.SemaphoreType.DMA(k) for k in ((100,), (100,), (3, 16), (3, 16), (8,))],
        compiler_params=pltpu.CompilerParams(collective_id=2, has_side_effects=True, vmem_limit_bytes=58 * MIB),
    )(starts, grad, queries, others, att, lse, umaps, mask, parts, a_own, b_own, two.reshape(2, 4, 4, 64, 128))


def feed_forward_kernel(
    second, cot_all, up, dn, umap, dmap, bias, back, forth, two, mine_in, mine_cot,
    sa, cot, up_v, dn_v, grad_act, act, pre, parts, total, *refs,
):
    scratch, (send, recv, local) = refs[:-3], refs[-3:]
    place = Place()
    greet(members(place))
    sends = Sends(send, recv)
    sa[place.x, place.c] = second[...]
    gather = GroupGather(place, sends, sa)
    loads = [
        pltpu.make_async_copy(src, dst, local.at[n])
        for n, (src, dst) in enumerate(((dn, dn_v), (cot_all, cot), (up, up_v)))
    ]
    for copy in loads:
        copy.start()

    def rows(ref, x, start, size):
        return ref[x, :, :, pl.ds(start, size)].reshape(256, size)

    loads[0].wait()
    loads[1].wait()

    def grad_tile(n, _):
        xs, cols = piece(n // 4, 2), piece(lax.rem(n, 4), 256)
        value = dot_nt(cot[xs, :, :, 0:2048].reshape(512, 2048), dn_v[cols, :])
        value = value + dot_nt(cot[xs, :, :, 2048:2176].reshape(512, 128), dmap[cols, :])
        grad_act[xs, :, cols] = value.reshape(2, 256, 256)
        return 0

    lax.fori_loop(0, 8, grad_tile, 0)
    loads[2].wait()
    xs = places_in_turn(place)

    def hidden(k):
        x = xs[k]

        def tile(n, _):
            cols = piece(n, 256)
            value = dot(rows(sa, x, 0, 2048), up_v[:, cols]) + bias[:, cols]
            value = value + dot(rows(sa, x, 2048, 128), umap[:, cols])
            phi = 0.5 * (1.0 + lax.erf(value * 0.7071067811865476))
            slope = phi + value * (0.3989422804014327 * jnp.exp2(value * value * (-0.5 * LOG2E)))
            act[k, :, cols] = (value * phi).astype(bf16)
            pre[k, :, cols] = (grad_act[x, :, cols] * slope).astype(bf16)
            return 0

        lax.fori_loop(0, 4, tile, 0)

    def backward(k, n):
        ks = pl.ds(k, n)

        def tile(t, _):
            cols = piece(t, 256)
            value = dot_nt(pre[ks].reshape(n * 256, 1024), up_v[cols, :]).astype(bf16)
            parts[ks, :, :, cols] = value.reshape(n, 2, 128, 256)
            return 0

        lax.fori_loop(0, 8, tile, 0)
        value = dot_nt(pre[ks].reshape(n * 256, 1024), umap[...]).astype(bf16)
        parts[ks, :, :, 2048:2176] = value.reshape(n, 2, 128, 128)
        value = dot(act[ks].reshape(n * 256, 1024), dmap[...]).astype(bf16)
        parts[ks, :, :, 2176:2304] = value.reshape(n, 2, 128, 128)

    gather.own()
    hidden(3)
    gather.near()
    hidden(2)
    hidden(1)
    gather.far()
    gather.far_done()
    hidden(0)

    sums = GroupSum(place, sends, parts, scratch)
    backward(0, 1)
    sums.cross(0)
    backward(1, 1)
    sums.cross(1)
    sums.merge(0)
    sums.first()
    backward(2, 2)
    sums.cross(2)
    sums.cross(3)
    sums.merge(1)
    sums.merge(2)
    sums.second()

    def forward(n, _):
        ks, cols = piece(n // 4, 2), piece(lax.rem(n, 4), 512)
        value = dot(act[ks].reshape(512, 1024), dn_v[:, cols]).astype(bf16)
        forth[ks, :, :, cols] = value.reshape(2, 2, 128, 512)
        return 0

    lax.fori_loop(0, 8, forward, 0)

    def small(k, _):
        x = lax.rem(place.x + jnp.where(k == 3, 0, jnp.where(k == 2, 3, 2 - k)), 4)
        one = dot_tn(act[k], rows(cot, x, 2048, 128))
        other = dot_tn(pre[k], rows(sa, x, 2048, 128))

        @pl.when(k == 0)
        def _():
            total[0] = one
            total[1] = other

        @pl.when(k > 0)
        def _():
            total[0] += one
            total[1] += other

        return 0

    lax.fori_loop(0, 4, small, 0)
    cols = piece(place.g, 256)
    mine_in[...] = sa[:, :, :, cols].reshape(1024, 256)
    mine_cot[...] = cot[:, :, :, cols].reshape(1024, 256)
    two[...] = total[...].astype(bf16)
    back[...] = sums.result()
    gather.finish()


def feed_forward(second, cot_all, up, dn, umap, dmap, bias):
    any_ = pl.BlockSpec(memory_space=pl.ANY)
    vmem = pl.BlockSpec(memory_space=pltpu.VMEM)
    vm = lambda *s: pltpu.VMEM(s, bf16)
    return pl.pallas_call(
        feed_forward_kernel,
        name="feed_forward",
        out_shape=[
            jax.ShapeDtypeStruct((128, 2304), f32),
            jax.ShapeDtypeStruct((4, 2, 128, 2048), bf16),
            jax.ShapeDtypeStruct((2, 1024, 128), bf16),
            jax.ShapeDtypeStruct((1024, 256), bf16),
            jax.ShapeDtypeStruct((1024, 256), bf16),
        ],
        in_specs=[vmem] + [any_] * 3 + [vmem] * 3,
        out_specs=[vmem] * 5,
        scratch_shapes=[
            vm(4, 2, 128, 2176),
            vm(4, 2, 128, 2176),
            vm(2048, 1024),
            vm(1024, 2048),
            pltpu.VMEM((4, 256, 1024), f32),
            vm(4, 256, 1024),
            vm(4, 256, 1024),
            vm(4, 2, 128, 2304),
            pltpu.VMEM((2, 1024, 128), f32),
        ]
        + GroupSum.scratch(2304)
        + [pltpu.SemaphoreType.DMA((k,)) for k in (16, 16, 3)],
        compiler_params=pltpu.CompilerParams(collective_id=1, has_side_effects=True, vmem_limit_bytes=60 * MIB),
    )(second, cot_all, up, dn, umap, dmap, bias)


def both_heads(gq, p, x):
    heads = [gq[p, x, :, j].reshape(256, 128) for j in range(2)]
    return jnp.concatenate(heads, axis=1)


def tail_kernel(
    grads, qkv_w, act_all, dmaps, low_rank, small, tok, gain, grad_res, mine_in, mine_cot, a_piece, b_piece, two_piece,
    input_grad, a_final, b_final, a_early, b_early, two_res,
    a_res, b_res, gq, wq, act, left, parts, lows, a_sums, b_sums, a_s, a_f, b_s, b_f, *refs,
):
    scratch, (send, recv, local) = refs[:-3], refs[-3:]
    place = Place()
    greet(members(place) + plane_devices(place))
    sends = Sends(send, recv)
    loads = [
        pltpu.make_async_copy(src, dst, local.at[n])
        for n, (src, dst) in enumerate(((grads, gq), (qkv_w, wq), (act_all, act)))
    ]
    for copy in loads:
        copy.start()
    own = lows.at[place.x, place.c]
    own[:, 0:384] = low_rank[...]
    own[:, 384:640] = small[...]
    spread = [sends.push(own, own, place.member(*m)) for m in MEMBERS]

    def two_view(n):
        def view(at):
            xl, xh = two_parts(at)
            return two_res.at[n, xl, place.c, at["z"], at["y"], xh]

        return view

    def b_early_view(at):
        z, y = at["z"], at["y"]
        if isinstance(y, pl.Slice):
            cols = pl.ds(y.start * 128 if z is ALL else pl.multiple_of(z * 512 + y.start * 128, 128), 256)
        elif z is ALL:
            cols = ALL
        else:
            cols = piece(z, 512) if y is ALL else piece(z * 4 + y, 128)
        return b_early.at[place.c, at["x"], :, cols]

    early = [
        give_all(place, sends, ("z", "y", "x"), two_piece.at[0], two_view(0), local.at[3]),
        give_all(place, sends, ("z", "x", "y"), two_piece.at[1], two_view(1), local.at[4]),
        give_all(
            place, sends, ("y", "z", "x"), a_piece,
            lambda at: a_early.at[place.c, at["z"], at["y"], at["x"]], local.at[5],
        ),
        give_all(place, sends, ("x", "y", "z"), b_piece, b_early_view, local.at[6]),
    ]

    def tick(*parts):
        for part in parts:
            next(part)

    tick(*early)
    loads[0].wait()
    loads[1].wait()
    xs = places_in_turn(place)
    for k in range(4):
        left[k] = jnp.concatenate([both_heads(gq, p, xs[k]) for p in range(3)], axis=1)

    def partial(k, n):
        ks = pl.ds(k, n)

        def tile(t, _):
            cols = piece(t, 512)
            value = dot(left[ks].reshape(n * 256, 768), wq[:, :, cols].reshape(768, 512)).astype(bf16)
            parts[ks, :, :, cols] = value.reshape(n, 2, 128, 512)
            return 0

        lax.fori_loop(0, 4, tile, 0)

    sums = GroupSum(place, sends, parts, scratch)
    partial(0, 1)
    sums.cross(0)
    partial(1, 1)
    sums.cross(1)
    sums.merge(0)
    sums.first()
    partial(2, 2)
    sums.cross(2)
    sums.cross(3)

    loads[2].wait()
    for p in range(3):
        total = jnp.zeros((128, 256), f32)
        for x in range(4):
            left_rows = act[x, :, :, 2048 + p * 128 : 2176 + p * 128].reshape(256, 128)
            total = total + dot_tn(left_rows, both_heads(gq, p, x))
        b_sums[p] = total.astype(bf16)
    for copy in spread:
        copy.wait()
    b_sums[3] = dot_tn(lows[:, :, :, 512:640].reshape(1024, 128), mine_cot[...]).astype(bf16)
    rows = act[:, :, :, piece(place.g, 256)].reshape(1024, 256)
    for p in range(4):
        right = lows[:, :, :, p * 128 : p * 128 + 128].reshape(1024, 128)
        a_sums[p] = dot_tn(rows if p < 3 else mine_in[...], right).astype(bf16)

    def a_view(at):
        return a_res.at[:, at["x"], place.c, at["z"], at["y"]]

    def a_held(z, y):
        return a_sums.at[:, piece(z * 4 + y, 16)]

    def b_view(at):
        y = at["y"]
        if y is ALL:
            yr, yc = ALL, ALL
        elif isinstance(y, pl.Slice):
            yr, yc = pl.ds(y.start // 2, 1), ALL
        else:
            yr, yc = y // 2, lax.rem(y, 2)
        return b_res.at[:, at["x"], place.c, at["z"], yr, yc]

    def b_held(z, y):
        return b_sums.at[:, pl.ds(pl.multiple_of(z * 32 + y // 2 * 16, 16), 16), piece(lax.rem(y, 2), 128)]

    def late_part(final, held, slots, order, view, sem):
        yield from reduce_piece(place, sends, final, None, (held, slots, final), None)
        yield from give_all(place, sends, order, final, view, sem)

    late = [
        late_part(a_f, a_held, a_s, ("z", "x", "y"), a_view, local.at[7]),
        late_part(b_f, b_held, b_s, ("y", "x", "z"), b_view, local.at[8]),
    ]
    tick(*late)
    tick(*early)
    sums.merge(1)
    sums.merge(2)
    sums.second()
    tick(*late, *early)
    tick(*late, *early)
    grad_first = sums.result()
    for p in range(3):
        grad_first = grad_first + dot_nt(low_rank[:, p * 128 : p * 128 + 128], dmaps[p])
    result = grad_res[...] + layer_norm_back(tok[...].astype(f32), gain[...], grad_first)
    input_grad[...] = result.astype(bf16)
    run_all(late + early)
    moves = [pltpu.make_async_copy(a_res, a_final, local.at[9])]
    for g in range(8):
        for yc in range(2):
            src = b_res.at[:, g // 2, g % 2, :, :, yc]
            dst = b_final.at[:, :, :, :, pl.ds(g * 256 + yc * 128, 128)]
            moves.append(pltpu.make_async_copy(src, dst, local.at[10 + g * 2 + yc]))
    for copy in moves:
        copy.start()
    for copy in moves:
        copy.wait()
    assert sends.used <= send.shape[0], sends.used


def tail(grads, qkv_w, act_all, dmaps, low_rank, small, tok, gain, grad_res, mine_in, mine_cot, a_piece, b_piece, two_piece):
    any_ = pl.BlockSpec(memory_space=pl.ANY)
    vmem = pl.BlockSpec(memory_space=pltpu.VMEM)
    vm = lambda *s: pltpu.VMEM(s, bf16)
    shape = lambda *s: jax.ShapeDtypeStruct(s, bf16)
    a_shape, b_shape = (4, 4, 2, 4, 4, 16, 128), (4, 4, 2, 4, 2, 2, 16, 128)
    input_grad, late_a, late_b, early_a, early_b, early_two = pl.pallas_call(
        tail_kernel,
        name="tail",
        out_shape=[
            shape(128, 2048),
            shape(*a_shape),
            shape(4, 4, 2, 16, 2048),
            shape(2, 4, 4, 4, 16, 128),
            shape(2, 4, 16, 2048),
            shape(2, 2, 2, 4, 4, 2, 64, 128),
        ],
        in_specs=[any_] * 3 + [vmem] * 11,
        out_specs=[vmem] + [any_] * 5,
        scratch_shapes=[
            vm(*a_shape),
            vm(*b_shape),
            vm(3, 4, 2, 2, 128, 128),
            vm(3, 256, 2048),
            vm(4, 2, 128, 2432),
            vm(4, 256, 768),
            vm(4, 2, 128, 2048),
            vm(4, 2, 128, 640),
            vm(4, 256, 128),
            vm(4, 128, 256),
            vm(15, 4, 16, 128),
            vm(4, 16, 128),
            vm(15, 4, 16, 128),
            vm(4, 16, 128),
        ]
        + GroupSum.scratch(2048)
        + [pltpu.SemaphoreType.DMA((k,)) for k in (200, 200, 26)],
        compiler_params=pltpu.CompilerParams(collective_id=3, has_side_effects=True, vmem_limit_bytes=60 * MIB),
    )(
        grads, qkv_w, act_all, dmaps, low_rank, small, tok, gain, grad_res, mine_in, mine_cot, a_piece, b_piece, two_piece
    )
    return (
        input_grad,
        late_a.reshape(4, 2048, 128),
        late_b.reshape(4, 128, 2048),
        early_a.reshape(2048, 128),
        early_b.reshape(128, 2048),
        early_two.reshape(2, 8192, 128),
    )


def per_device(
    tokens,
    document_starts,
    document_adapter,
    layernorm_gain,
    layernorm_bias,
    projection_weight,
    output_weight,
    up_weight,
    down_weight,
    projection_bias,
    upper_bias,
    attention_down_maps,
    attention_up_maps,
    upper_down_maps,
    upper_up_maps,
    lower_down_maps,
    lower_up_maps,
    cotangent,
):
    local_rows, width = tokens.shape[1:]
    head_size = width // HEADS
    seq = local_rows * 32
    scale = head_size ** (-0.5)
    xl, c, z, y, xh = (lax.axis_index(a) for a in AXES)
    group = (xh * 2 + xl) * 2 + c
    inputs = tokens[0].astype(f32)
    cot = cotangent[0]
    bias_rows = jnp.stack([projection_bias[0], jnp.zeros_like(projection_bias[0]), projection_bias[1]])

    def my_columns(array):
        return lax.dynamic_slice_in_dim(array, group * 256, 256, array.ndim - 1)

    def my_hidden(array):
        lead = array.shape[:-1]
        part = lax.dynamic_slice_in_dim(array, (xl * 2 + c) * 2048, 2048, array.ndim - 1)
        part = part.reshape(lead + (16, 2, 64))
        return lax.dynamic_index_in_dim(part, xh, len(lead) + 1, False).reshape(lead + (1024,))

    my_up_maps = my_columns(attention_up_maps[:3])
    (
        act_all, qkv_w, out_all, up_all, dn_all, cot_all, by_head, across, merged, attended, lse, mask
    ) = front(
        document_starts, document_adapter, tokens[0], layernorm_gain[:1], layernorm_bias[:1],
        my_columns(bias_rows)[:, None, :], attention_down_maps, my_up_maps, cot, lower_up_maps,
        jnp.transpose(projection_weight, (1, 0, 2)), output_weight, up_weight, down_weight, scale,
    )
    w_out = out_all.reshape(width, width)

    adapt_out = (dot(merged, attention_down_maps[3]) * mask).astype(bf16)
    residual = inputs + dot(merged, w_out) + projection_bias[2] + dot(adapt_out, attention_up_maps[3])
    second_in = layer_norm(residual, layernorm_gain[1], layernorm_bias[1]).astype(bf16)
    adapt_up = (dot(second_in, upper_down_maps) * mask).astype(bf16)

    down_maps = lax.dynamic_slice_in_dim(lower_down_maps, (xl * 2 + c) * 2048, 2048, 0)
    down_maps = lax.dynamic_index_in_dim(down_maps.reshape(16, 2, 64, 128), xh, 1, False).reshape(1024, 128)
    back, forth, two, mine_in, mine_cot = feed_forward(
        jnp.concatenate([second_in, adapt_up], axis=1), cot_all, up_all.reshape(width, 1024),
        dn_all.reshape(1024, width), my_hidden(upper_up_maps), down_maps, my_hidden(upper_bias)[None],
    )

    grad_adapt_up = (back[:, width : width + 128] * mask).astype(bf16)
    grad_second = back[:, :width] + dot_nt(grad_adapt_up, upper_down_maps)
    grad_residual = cot.astype(f32) + layer_norm_back(residual, layernorm_gain[1], grad_second)
    grad_branch = grad_residual.astype(bf16)
    grad_b_out = dot_tn(adapt_out, grad_branch)
    grad_adapt_out = (dot_nt(grad_branch, attention_up_maps[3]) * mask).astype(bf16)
    grad_a_out = dot_tn(merged, grad_adapt_out)
    grad_merged = (dot_nt(grad_branch, w_out) + dot_nt(grad_adapt_out, attention_down_maps[3])).astype(bf16)

    adapt_down = (back[:, width + 128 :] * mask).astype(bf16)
    grad_qkv, grad_adapt_qkv, forth_sum, a_piece, b_piece, two_piece = middle(
        document_starts, grad_merged, by_head, across, attended, lse, attention_up_maps, mask, forth,
        grad_a_out.astype(bf16), grad_b_out.astype(bf16), two, scale,
    )
    input_grad, late_a, late_b, early_a, early_b, early_two = tail(
        grad_qkv, qkv_w, act_all, attention_down_maps, grad_adapt_qkv,
        jnp.concatenate([grad_adapt_up, adapt_down], axis=1), tokens[0], layernorm_gain[:1], grad_residual,
        mine_in, mine_cot, a_piece, b_piece, two_piece,
    )
    output = residual + forth_sum + projection_bias[3] + dot(adapt_down, lower_up_maps)
    return (
        output.astype(bf16)[None],
        input_grad[None],
        jnp.concatenate([late_a[:3], early_a[None]]).astype(f32),
        jnp.concatenate([late_b[:3], early_b[None]]).astype(f32),
        late_a[3].astype(f32),
        jnp.transpose(early_two[1]).astype(f32),
        early_two[0].astype(f32),
        late_b[3].astype(f32),
    )


def solution(mesh):
    fine = jax.sharding.Mesh(mesh.devices.reshape(SIZES), AXES)
    by_token = P(STREAM, TOKEN, None)
    shard = AXES
    in_specs = (
        by_token,
        P(STREAM, None),
        P(STREAM, None),
        P(),
        P(),
        P(shard, None, None),
        P(shard, None),
        P(shard, None),
        P(shard, None),
        P(),
        P(),
        P(),
        P(),
        P(),
        P(),
        P(),
        P(),
        by_token,
    )
    out_specs = (by_token, by_token, P(), P(), P(), P(), P(), P())
    return jax.shard_map(per_device, mesh=fine, in_specs=in_specs, out_specs=out_specs, check_vma=False)
```

time: 560 us -> 456 us (0.81)
  Pallas kernels: 482 us -> 393 us
  local copies, waits for them, and re-layouts: 28.5 us -> 20.3 us
    pallas_call x4 -> x1, Pallas kernels: 164 us -> 89.5 us  [middle(): pl.pallas_call(functools.partial(middle_kernel, scale=scale), name='atten...]
    pallas_call x1, Pallas kernels: 177 us -> 164 us  [front(): pl.pallas_call(functools.partial(front_kernel, scale=scale), name='front'...]
where the time goes in v4:
time: 456 us; the launch traced here: 451 us
  Pallas kernels  393 us (86%)
  matrix products  21.3 us (5%)
  local copies, waits for them, and re-layouts  20.3 us (4%)
  other arithmetic  15.3 us (3%)
    pallas_call x1, Pallas kernels, front(): pl.pallas_call(functools.partial(front_kernel, scale=scale), name='front'...  164 us
    pallas_call x1, Pallas kernels, middle(): pl.pallas_call(functools.partial(middle_kernel, scale=scale), name='atten...  89.5 us
    pallas_call x1, Pallas kernels, tail(): pl.pallas_call(tail_kernel, name='tail', out_shape=[shape(128, 2048), sha...  78 us
    pallas_call x1, Pallas kernels, feed_forward(): pl.pallas_call(feed_forward_kernel, name='feed_forward', out_shape=[jax.S...  61.4 us
    dot_general x4, matrix products, dot_nt(): lax.dot_general(left, right, (((1,), (1,)), ((), ())), preferred_element_...  10.8 us

profile of v4, /device:TPU:1, one launch (start us, length us, event | category | flops | bytes accessed | tf_op | source)
XLA Modules:
  0.0 450.6 jit_solution(2566891057754913934)
XLA Ops:
  2.4 1.4 fusion.24
  6.6 1.1 constant_dynamic-slice_fusion.1
  9.9 163.7 %front.1 = (bf16[4,2,128,2432]{3,2,1,0:T(8,128)(2,1)}, bf16[3,256,2048]{2,1,0:T(8,128)(2,1)}, bf16[2,2,4,4,2,16,2048]{6,5,4,3,2,1,0:T(8,128)(2,1)}, bf16[2,2,4,4...) custom-call(s32[1,8]{1,0:T(1,128)} %starts.3, ...), custom_call_target="tpu_custom_call" | custom-call | tf_op jit(solution)/shard_map/front/pallas_call | solution.py:742
  173.6 1.5 fusion.5
  175.1 5.0 %fusion.1 = f32[128,2048]{1,0:T(8,128)S(1)} fusion(bf16[128,2048]{1,0:T(8,128)(2,1)} %get-tuple-element.37, bf16[2048,2048]{1,0:T(8,128)(2,1)} %bitcast.65, f32[2048]{0:T(1024)S(1)} %bitcast.86, bf16[1,128,2048]{2,1,0:T(8,128)(2,1)S(1)} %copy-done.6), kind=kOutput, calls=%fused_computation.6 | convolution fusion | flops 1074528256 | bytes 10493952 | tf_op jit(solution)/shard_map/dot_general | solution.py:43
  182.2 61.4 %feed_forward.1 = (f32[128,2304]{1,0:T(8,128)}, bf16[4,2,128,2048]{3,2,1,0:T(8,128)(2,1)}, bf16[2,1024,128]{2,1,0:T(8,128)(2,1)}, bf16[1024,256]{1,0:T(8,128)(2,1)}, bf16[1024,256]{1,0:T(8,128)(2,1)}) custom-call(bf16[128,2176]{1,0:T(8,128)(2,1)} %pad_maximum_fusion.second, bf16[4,2,128,2176]{3,2,1,0:T(8,128)(2,1)} %get-tuple-element.40.cot_all, ...), custom_call_target="tpu_custom_call" | custom-call | tf_op jit(solution)/shard_map/feed_forward/pallas_call | solution.py:1091
  243.7 0.9 multiply_convert_fusion.1
  244.6 1.7 fusion.21
  247.0 6.7 %fusion.19 = f32[128,2048]{1,0:T(8,128)S(1)} fusion(bf16[2048,2048]{1,0:T(8,128)(2,1)} %bitcast.66, f32[128,2048]{1,0:T(8,128)S(1)} %multiply_add_fusion.grad_res), kind=kOutput, calls=%fused_computation.56 | convolution fusion | flops 1074003968 | bytes 10485760 | tf_op jit(solution)/shard_map/dot_general | solution.py:47
  254.0 2.1 fusion.2.grad
  256.1 1.1 convolution_convert_fusion.1.a_own
  257.9 1.1 convolution_convert_fusion.b_own
  259.0 89.5 %attention_backward.1 = (bf16[3,4,2,2,128,128]{5,4,3,2,1,0:T(8,128)(2,1)}, bf16[128,384]{1,0:T(8,128)(2,1)}, f32[128,2048]{1,0:T(8,128)}, bf16[16,128]{1,0:T(8,1...) custom-call(s32[1,8]{1,0:T(1,128)} %starts.3, bf16[128,2048]{1,0:T(8,128)(2,1)} %fusion.2.grad, ...), custom_call_target="tpu_custom_call" | custom-call | tf_op jit(solution)/shard_map/attention_backward/pallas_call | solution.py:934
  348.6 78.0 %tail.1 = (bf16[128,2048]{1,0:T(8,128)(2,1)}, bf16[4,4,2,4,4,16,128]{6,5,4,3,2,1,0:T(8,128)(2,1)}, bf16[4,4,2,16,2048]{4,3,2,1,0:T(8,128)(2,1)}, bf16[2,4,4,4,16...) custom-call(bf16[3,4,2,2,128,128]{5,4,3,2,1,0:T(8,128)(2,1)} %get-tuple-e, ...), custom_call_target="tpu_custom_call" | custom-call | tf_op jit(solution)/shard_map/tail/pallas_call | solution.py:1279
  426.6 1.1 fusion.4
  428.7 1.1 bitcast_convert_fusion.3
  430.6 1.1 bitcast_convert_fusion.2
  431.7 2.3 maximum_convert_fusion.1
  434.0 2.4 maximum_convert_fusion
  436.4 1.3 copy-done.7
  437.7 1.4 fusion.22
  439.0 2.4 bitcast_convert_fusion
  441.5 2.4 bitcast_convert_fusion.1
  443.8 5.7 %copy.31 = f32[8192,128]{0,1:T(8,128)} copy(f32[8192,128]{1,0:T(8,128)} %bitcast_convert_fusion.1) | data formatting | bytes 8388608 | tf_op jit(solution)/shard_map/convert_element_type | solution.py:1411
  (68 shorter events, 13.0 us)
Async XLA Ops:
  0.6 4.8 %copy-start = (bf16[128,8192]{1,0:T(8,128)(2,1)S(1)}, bf16[128,8192]{1,0:T(8,128)(2,1)}, u32[]{:S(2)}) copy-start(bf16[128,8192]{1,0:T(8,128)(2,1)} %param.32) | copy-start | bytes 6291460
  7.7 1.5 slice-start
  9.9 165.2 %copy-start.6 = (bf16[1,128,2048]{2,1,0:T(8,128)(2,1)S(1)}, bf16[1,128,2048]{2,1,0:T(8,128)(2,1)}, u32[]{:S(2)}) copy-start(bf16[1,128,2048]{2,1,0:T(8,128)(2,1)} %param.18) | copy-start | bytes 1572868
  175.1 5.0 %copy-start.3 = (bf16[4,128,2048]{2,1,0:T(8,128)(2,1)S(1)}, bf16[4,128,2048]{2,1,0:T(8,128)(2,1)}, u32[]{:S(2)}) copy-start(bf16[4,128,2048]{2,1,0:T(8,128)(2,1)} %umaps.1) | copy-start | bytes 6291460
  180.0 1.0 copy-start.8
  180.1 1.0 copy-start.13
  243.7 2.7 copy-start.11
  246.9 11.0 %copy-start.2 = (f32[128,2048]{1,0:T(8,128)}, f32[128,2048]{1,0:T(8,128)S(1)}, u32[]{:S(2)}) copy-start(f32[128,2048]{1,0:T(8,128)S(1)} %multiply_add_fusion.grad_res) | copy-start | bytes 3145732
  247.0 6.7 %copy-start.4 = (bf16[4,128,2048]{2,1,0:T(8,128)(2,1)S(1)}, bf16[4,128,2048]{2,1,0:T(8,128)(2,1)}, u32[]{:S(2)}) copy-start(bf16[4,128,2048]{2,1,0:T(8,128)(2,1)} %umaps.1) | copy-start | bytes 6291460
  253.7 2.5 copy-start.5
  348.5 78.0 %copy-start.12 = (bf16[128,2048]{1,0:T(8,128)(2,1)S(1)}, bf16[128,2048]{1,0:T(8,128)(2,1)}, u32[]{:S(2)}) copy-start(bf16[128,2048]{1,0:T(8,128)(2,1)} %lum.1) | copy-start | bytes 1572868
  348.5 78.0 %copy-start.14 = (f32[128,2048]{1,0:T(8,128)S(1)}, f32[128,2048]{1,0:T(8,128)}, u32[]{:S(2)}) copy-start(f32[128,2048]{1,0:T(8,128)} %get-tuple-element.50) | copy-start | bytes 3145732
  426.5 1.8 copy-start.10
  428.4 2.0 copy-start.9
  430.4 1.3 copy-start.16
  431.7 2.3 copy-start.15
  434.0 3.7 copy-start.7
  443.8 5.7 %copy-start.17 = (bf16[128,2048]{1,0:T(8,128)(2,1)S(1)}, bf16[128,2048]{1,0:T(8,128)(2,1)}, u32[]{:S(2)}) copy-start(bf16[128,2048]{1,0:T(8,128)(2,1)} %get-tuple-element.60) | copy-start | bytes 1572868
  443.8 6.5 %copy-start.1 = (bf16[128,8192]{1,0:T(8,128)(2,1)S(1)}, bf16[128,8192]{1,0:T(8,128)(2,1)}, u32[]{:S(2)}) copy-start(bf16[128,8192]{1,0:T(8,128)(2,1)} %param.32) | copy-start | bytes 6291460

commit v5 on v4

--- a/solution.py
+++ b/solution.py
@@ -135,7 +135,7 @@
         parts = left
 
 
-def ring_gather(place, sends, view, order, chunk, landed, forward):
+def ring_gather(place, sends, view, order, chunk, landed, forward, direct=False):
     fixed = {a: place.at(a) for a in order}
     across = place.toward("c")
     later, passed = [], []
@@ -149,13 +149,14 @@
     for number, axis in enumerate(order):
         own = view(fixed, None)
         src = chunk if number == 0 else own
-        if number == 0:
+        if number == 0 or direct:
             sent = [sends.push(src, own, place.toward(axis, s)) for s in (2, 1, 3)]
             yield
             for s, copy in zip((2, 1, 3), sent):
                 copy.wait_recv()
                 pass_on(fixed | {axis: place.step(axis, -s)})
-            landed.wait()
+            if number == 0:
+                landed.wait()
             later += sent
             del fixed[axis]
             continue
@@ -421,7 +422,7 @@
         out[...] = total.astype(bf16)
 
 
-def give_all(place, sends, order, final, view, local):
+def give_all(place, sends, order, final, view, local, direct=False):
     here = {a: place.at(a) for a in "xyz"}
     keep = pltpu.make_async_copy(final, view(here), local)
     keep.start()
@@ -432,7 +433,7 @@
             at[order[0]] = pl.ds(half * 2, 2)
         return view(at)
 
-    return ring_gather(place, sends, fixed_view, order, final, keep, True)
+    return ring_gather(place, sends, fixed_view, order, final, keep, True, direct)
 
 
 def a_sum_scratch():
@@ -512,8 +513,8 @@
 
 
 def front_kernel(
-    starts, chosen, tok, gain, shift, bias, dmaps, umaps, cot, lum, wp, wo, up, dn,
-    act_all, qkv_w, out_all, up_all, dn_all, cot_all, heads, across, merged, att, lse, mask,
+    starts, chosen, tok, gain, shift, bias, dmaps, umaps, cot, lum, wp, wo, up,
+    act_all, qkv_w, out_all, up_all, cot_all, heads, across, merged, att, lse, mask,
     act, cotbuf, wq, up_own, rows, mine, others, low, wq_t, send, recv, a_send, a_recv, local, *, scale,
 ):
     place = Place()
@@ -532,18 +533,17 @@
 
         return view
 
-    def up_view(fixed, half):
-        xl = ALL if half is None else pl.ds(half, 1)
-        return up_all.at[xl, ALL, fixed.get("z", ALL), fixed.get("y", ALL)]
-
-    def dn_view(fixed, half):
-        cols = ALL if half is None else pl.ds(half * 1024, 1024)
-        return dn_all.at[fixed.get("z", ALL), fixed.get("y", ALL), :, cols]
-
-    def wq_view(p, cols):
+    def up_view(xl):
         def view(fixed, half):
-            xl = ALL if half is None else pl.ds(half, 1)
-            return wq.at[p, xl, ALL, fixed.get("z", ALL), fixed.get("y", ALL), ALL, ALL, cols]
+            c = ALL if half is None else pl.ds(half, 1)
+            return up_all.at[pl.ds(xl, 1), c, fixed.get("z", ALL), fixed.get("y", ALL)]
+
+        return view
+
+    def wq_view(p, xl):
+        def view(fixed, half):
+            c = ALL if half is None else pl.ds(half, 1)
+            return wq.at[p, xl, c, fixed.get("z", ALL), fixed.get("y", ALL)]
 
         return view
 
@@ -554,7 +554,6 @@
         pltpu.make_async_copy(
             wp.at[:, :, piece(place.g, 256)], wq.at[:, place.xl, place.c, place.z, place.y, place.xh], local.at[0]
         ),
-        pltpu.make_async_copy(dn, dn_all.at[place.z, place.y], local.at[2]),
     ]
     copies += [
         pltpu.make_async_copy(
@@ -609,23 +608,25 @@
         copy.wait()
     fixed = {"z": place.z, "y": place.y}
     qkv_parts = []
-    for p, cols, order in (
-        (0, ALL, ("y", "z")), (1, ALL, ("z", "y")), (2, pl.ds(0, 128), ("y", "z")), (2, pl.ds(128, 128), ("z", "y"))
+    for p, xl, order in (
+        (0, ALL, ("y", "z")), (1, ALL, ("z", "y")), (2, pl.ds(0, 1), ("y", "z")), (2, pl.ds(1, 1), ("z", "y"))
     ):
-        view = wq_view(p, cols)
+        view = wq_view(p, xl)
         qkv_parts.append(ring_gather(place, sends, view, order, view(fixed, None), Nothing(), False))
-    up_gather = ring_gather(place, sends, up_view, ("y", "z"), up_view(fixed, None), Nothing(), False)
-    dn_gather = ring_gather(place, sends, dn_view, ("z", "y"), dn, copies[1], False)
+    up_gathers = [
+        ring_gather(place, sends, up_view(n), order, up_view(n)(fixed, None), Nothing(), False)
+        for n, order in enumerate((("y", "z"), ("z", "y")))
+    ]
     out_gathers = [
-        ring_gather(place, sends, out_view(h), order, wo.at[:, pl.ds(h * 1024, 1024)], copies[2 + h], True)
-        for h, order in enumerate((("y", "z", "x"), ("z", "y", "x")))
+        ring_gather(place, sends, out_view(h), order, wo.at[:, pl.ds(h * 1024, 1024)], copies[1 + h], True)
+        for h, order in enumerate((("x", "y", "z"), ("z", "y", "x")))
     ]
 
     def tick(*parts):
         for part in parts:
             next(part)
 
-    tick(*qkv_parts, dn_gather, *out_gathers)
+    tick(*qkv_parts, *out_gathers)
     own = cotbuf.at[place.x, place.c]
     own[:, 0:2048] = cot[...]
     own[:, 2048:2176] = (dot_nt(cot[...], lum[...]) * keep).astype(bf16)
@@ -638,7 +639,7 @@
     up_keep.wait()
     for copy in up_spread:
         copy.wait()
-    tick(up_gather)
+    tick(*up_gathers)
     kept = []
 
     def project(x):
@@ -646,7 +647,8 @@
         for p in range(3):
             low_rank = act[x, :, :, 2048 + p * 128 : 2176 + p * 128].reshape(256, 128)
             value = dot(left, wq[p].reshape(2048, 256)) + bias[p] + dot(low_rank, umaps[p])
-            rows[p, x] = value.astype(bf16).reshape(2, 128, 256)
+            for j in range(2):
+                rows[p, x, :, j] = value[:, j * 128 : j * 128 + 128].astype(bf16).reshape(2, 128, 128)
 
     here = place.z * 4 + place.y
     kv = pl.ds(1, 2)
@@ -656,13 +658,13 @@
         x = place.step("x", dx)
         for n, (to, dc, j, device, myself) in enumerate(attenders(place)):
             if to == dx:
-                src = rows.at[:, x, 1 - place.c if dc else place.c, :, pl.ds(j * 128, 128)]
+                src = rows.at[:, x, 1 - place.c if dc else place.c, j]
                 posts.append(
                     Post(src, mine.at[:, piece(here, 128)], device, myself, a_send.at[0, n], a_recv.at[0, here])
                 )
         for n, (to, dc, j, device, _) in enumerate(attenders(place)):
             if to == dx:
-                src = rows.at[kv, x, 1 - place.c if dc else place.c, :, pl.ds(j * 128, 128)]
+                src = rows.at[kv, x, 1 - place.c if dc else place.c, j]
                 device = place.member((dx + 2) % 4, dc) | {"z": device["z"], "y": device["y"]}
                 myself = None if dc or dx != 2 else (place.z == device["z"]) & (place.y == device["y"])
                 posts.append(
@@ -680,7 +682,7 @@
     act_gather.far_done()
     project(place.step("x", 2))
     post(2)
-    tick(dn_gather, up_gather, *out_gathers)
+    tick(*up_gathers, *out_gathers)
     kept.append(pltpu.make_async_copy(act, act_all, local.at[6]))
     kept[-1].start()
     for p in range(3):
@@ -715,7 +717,7 @@
 
     tiles = mine.shape[1] // F_TILE
     lax.fori_loop(0, tiles // 2, tile, 0)
-    tick(dn_gather, up_gather)
+    tick(*up_gathers)
     lax.fori_loop(tiles // 2, tiles * 3 // 4, tile, 0)
     tick(cot_gather, *out_gathers)
     lax.fori_loop(tiles * 3 // 4, tiles, tile, 0)
@@ -726,14 +728,14 @@
     for copy in kept:
         copy.wait()
     act_gather.finish()
-    run_all([back, up_gather, dn_gather, cot_gather, *out_gathers])
+    run_all([back, *up_gathers, cot_gather, *out_gathers])
     last = pltpu.make_async_copy(cotbuf, cot_all, local.at[10])
     last.start()
     last.wait()
     assert sends.used <= send.shape[0], sends.used
 
 
-def front(starts, chosen, tok, gain, shift, bias, dmaps, umaps, cot, lum, wp, wo, up, dn, scale):
+def front(starts, chosen, tok, gain, shift, bias, dmaps, umaps, cot, lum, wp, wo, up, scale):
     any_ = pl.BlockSpec(memory_space=pl.ANY)
     vmem = pl.BlockSpec(memory_space=pltpu.VMEM)
     smem = pl.BlockSpec(memory_space=pltpu.SMEM)
@@ -747,7 +749,6 @@
             shape(3, 256, 2048),
             shape(2, 2, 4, 4, 2, 16, 2048),
             shape(2, 2, 4, 4, 2, 16, 1024),
-            shape(4, 4, 64, 2048),
             shape(4, 2, 128, 2176),
             shape(3, 2048, 128),
             shape(2, 2048, 128),
@@ -756,14 +757,14 @@
             jax.ShapeDtypeStruct((8, 256), f32),
             jax.ShapeDtypeStruct((128, 128), f32),
         ],
-        in_specs=[smem] * 2 + [vmem] * 12,
-        out_specs=[any_] * 9 + [vmem] * 3,
+        in_specs=[smem] * 2 + [vmem] * 11,
+        out_specs=[any_] * 8 + [vmem] * 3,
         scratch_shapes=[
             vm(4, 2, 128, 2432),
             vm(4, 2, 128, 2176),
             vm(3, 2, 2, 4, 4, 2, 16, 256),
             vm(16, 8192),
-            vm(3, 4, 2, 128, 256),
+            vm(3, 4, 2, 2, 128, 128),
             vm(3, 2048, 128),
             vm(2, 2048, 128),
             vm(16, 128, 128),
@@ -773,15 +774,15 @@
         compiler_params=pltpu.CompilerParams(
             collective_id=0, has_side_effects=True, vmem_limit_bytes=56 * MIB
         ),
-    )(starts, chosen, tok, gain, shift, bias, dmaps, umaps, cot, lum, wp, wo, up, dn)
+    )(starts, chosen, tok, gain, shift, bias, dmaps, umaps, cot, lum, wp, wo, up)
 
 
 def middle_kernel(
-    starts, grad, queries, others, att, lse, umaps, mask, parts, a_own, b_own, two,
-    by_member, low_rank, total, a_final, b_final, two_final,
-    do, delta, dq_acc, dq, own_low, other_low, by_head, from_other, *refs, scale,
+    starts, grad, queries_in, others_in, att_in, lse, umaps_in, mask, a_own, b_own, two,
+    by_member, low_rank, a_final, b_final, two_final,
+    queries, others, att, umaps, do, delta, dq_acc, dq, own_low, other_low, by_head, from_other, *refs, scale,
 ):
-    scratch, (send, recv, a_send, a_recv, local) = list(refs[:-5]), refs[-5:]
+    scratch, (send, recv, a_send, a_recv, s_send, s_recv, local) = list(refs[:-7]), refs[-7:]
     place = Place()
     across = [{"xh": 1 - place.xh, "z": z, "y": y} for z, y in plane(place)]
     greet(plane_devices(place) + members(place) + across)
@@ -792,6 +793,14 @@
 
     keep = pltpu.make_async_copy(grad.at[:, head_columns(place.z, place.y)], do.at[piece(here, 128)], local.at[0])
     keep.start()
+    loads = [
+        pltpu.make_async_copy(src, dst, local.at[1 + n])
+        for n, (src, dst) in enumerate(
+            ((att_in, att), (queries_in, queries), (others_in, others), (umaps_in, umaps))
+        )
+    ]
+    for copy in loads:
+        copy.start()
     grads_sent = [
         sends.push(grad.at[:, head_columns(z, y)], do.at[piece(here, 128)], {"z": z, "y": y})
         for z, y in plane(place)
@@ -802,7 +811,6 @@
         del scratch[:n]
         return got
 
-    forth = group_sum(place, sends, parts, take(6), total)
     early = [
         a_sum(place, sends, a_own, a_final, take(5)),
         b_sum(place, sends, b_own, b_final, take(5)),
@@ -822,11 +830,13 @@
             except StopIteration:
                 pass
 
-    tick(forth, *early)
+    tick(*early)
     dq_acc[...] = jnp.zeros_like(dq_acc)
     keep.wait()
     for copy in grads_sent:
         copy.wait_recv()
+    for copy in loads:
+        copy.wait()
     ones = jnp.ones((8, 128), bf16)
     tiles, key_tiles = do.shape[0] // Q_TILE, do.shape[0] // K_TILE
 
@@ -839,7 +849,7 @@
         return 0
 
     lax.fori_loop(0, tiles, row_dots, 0)
-    tick(forth, *early[:2])
+    tick(*early[:2])
 
     def keys(kt):
         rows = piece(kt, K_TILE)
@@ -879,6 +889,38 @@
         device = {"z": z, "y": y} | ({"xh": 1 - place.xh} if other else {})
         gone.append(Post(src, dst, device, myself, a_send.at[k, n], a_recv.at[k, here]))
 
+    shared = []
+
+    def share(turn, k, part):
+        x = lax.rem(place.z + (4 - turn), 4)
+        for c in range(2):
+            g = x * 2 + c
+            pair = piece(g, 2)
+            if k:
+                both = by_head[1:3, pair].astype(f32) + from_other[:, pair].astype(f32)
+                by_head[1:3, pair] = both.astype(bf16)
+            device = {"xl": lax.rem(x, 2), "xh": x // 2, "c": c}
+            myself = (place.x == x) & (place.c == c)
+            src, dst = by_head.at[part, pair], by_member.at[part, place.x, place.c]
+            n = turn * 2 + c
+            shared.append(Post(src, dst, device, myself, s_send.at[k, n], s_recv.at[k, place.g]))
+
+    def heads_of(turn):
+        x = lax.rem(place.z + (4 - turn), 4)
+        return [x * 4 + y for y in range(4)]
+
+    def share_keys(turn):
+        for head in heads_of(turn):
+            for k, dst in ((2, from_other.at[:, 0]), (1, by_head.at[kv, 0])):
+                pltpu.make_async_copy(dst, dst, a_recv.at[k, head]).wait()
+        share(turn, 1, kv)
+
+    def share_queries(turn):
+        for head in heads_of(turn):
+            dst = by_head.at[0, 0]
+            pltpu.make_async_copy(dst, dst, a_recv.at[0, head]).wait()
+        share(turn, 0, 0)
+
     for turn in (2, 1, 3, 0):
         kt = lax.rem(place.z + turn, key_tiles)
         for k, low, (dk, dv) in zip((2, 1), (other_low, own_low), keys(kt)):
@@ -888,8 +930,6 @@
                 low[n, 1] = dv[b * 128 : (b + 1) * 128].astype(bf16)
                 dst = from_other.at[:, here] if k == 2 else by_head.at[kv, here]
                 to_token(k, n, low.at[n], dst, k == 2, turn != 0)
-        if turn == 1:
-            tick(forth, *early)
     for n in range(16):
         dq[n] = dq_acc[n * 128 : (n + 1) * 128].astype(bf16)
     for turn in (2, 1, 3, 0):
@@ -897,35 +937,24 @@
             n = lax.rem(place.z + turn, 4) * 4 + b
             to_token(0, n, dq.at[n], by_head.at[0, here], False, turn != 0)
     tick(*early)
-
-    mine = None
-    shared = []
-    for dx, dc in MEMBERS + [(0, 0)]:
-        g = place.step("x", dx) * 2 + (1 - place.c if dc else place.c)
-        for j in range(2):
-            for k, dst in ((2, from_other.at[:, 0]), (1, by_head.at[kv, 0]), (0, by_head.at[0, 0])):
-                pltpu.make_async_copy(dst, dst, a_recv.at[k, g * 2 + j]).wait()
-        pair = piece(g, 2)
-        by_head[1:3, pair] = (by_head[1:3, pair].astype(f32) + from_other[:, pair].astype(f32)).astype(bf16)
-        src, dst = by_head.at[:, pair], by_member.at[:, place.x, place.c]
-        if dx or dc:
-            shared.append(sends.push(src, dst, place.member(dx, dc)))
-        else:
-            mine = pltpu.make_async_copy(src, dst, local.at[7])
-            mine.start()
+    for turn in (2, 1, 3, 0):
+        share_keys(turn)
+    tick(*early)
+    for turn in (2, 1, 3, 0):
+        share_queries(turn)
     for p in range(3):
         whole = jnp.concatenate([by_head[p, n] for n in range(16)], axis=1)
         low_rank[:, p * 128 : p * 128 + 128] = (dot_nt(whole, umaps[p]) * mask[...]).astype(bf16)
-    run_all([forth] + early)
-    for copy in gone + grads_sent:
+    for n in range(8):
+        for k, dst in ((0, by_member.at[0, 0, 0]), (1, by_member.at[kv, 0, 0])):
+            pltpu.make_async_copy(dst, dst, s_recv.at[k, n]).wait()
+    run_all(early)
+    for copy in gone + grads_sent + shared:
         copy.wait_send()
-    for copy in shared:
-        copy.wait()
-    mine.wait()
     assert sends.used <= send.shape[0], sends.used
 
 
-def middle(starts, grad, queries, others, att, lse, umaps, mask, parts, a_own, b_own, two, scale):
+def middle(starts, grad, queries, others, att, lse, umaps, mask, a_own, b_own, two, scale):
     any_ = pl.BlockSpec(memory_space=pl.ANY)
     vmem = pl.BlockSpec(memory_space=pltpu.VMEM)
     smem = pl.BlockSpec(memory_space=pltpu.SMEM)
@@ -937,14 +966,17 @@
         out_shape=[
             shape(3, 4, 2, 2, 128, 128),
             shape(128, 384),
-            jax.ShapeDtypeStruct((128, 2048), f32),
             shape(16, 128),
             shape(16, 128),
             shape(2, 64, 128),
         ],
-        in_specs=[smem] + [vmem] * 11,
-        out_specs=[any_] + [vmem] * 5,
+        in_specs=[smem, vmem, any_, any_, any_, vmem, any_, vmem] + [vmem] * 3,
+        out_specs=[any_] + [vmem] * 4,
         scratch_shapes=[
+            vm(3, 2048, 128),
+            vm(2, 2048, 128),
+            pltpu.VMEM((2048, 128), f32),
+            vm(4, 128, 2048),
             vm(2048, 128),
             pltpu.VMEM((8, 8, 256), f32),
             pltpu.VMEM((2048, 128), f32),
@@ -954,47 +986,71 @@
             vm(3, 16, 128, 128),
             vm(2, 16, 128, 128),
         ]
-        + GroupSum.scratch(2048)
         + a_sum_scratch()
         + b_sum_scratch()
         + [vm(15, 64, 128)] * 2
-        + [pltpu.SemaphoreType.DMA(k) for k in ((100,), (100,), (3, 16), (3, 16), (8,))],
+        + [pltpu.SemaphoreType.DMA(k) for k in ((100,), (100,), (3, 16), (3, 16), (2, 8), (2, 8), (8,))],
         compiler_params=pltpu.CompilerParams(collective_id=2, has_side_effects=True, vmem_limit_bytes=58 * MIB),
-    )(starts, grad, queries, others, att, lse, umaps, mask, parts, a_own, b_own, two.reshape(2, 4, 4, 64, 128))
+    )(starts, grad, queries, others, att, lse, umaps, mask, a_own, b_own, two.reshape(2, 4, 4, 64, 128))
 
 
 def feed_forward_kernel(
-    second, cot_all, up, dn, umap, dmap, bias, back, forth, two, mine_in, mine_cot,
-    sa, cot, up_v, dn_v, grad_act, act, pre, parts, total, *refs,
+    merged, tok, gain, shift, bias_out, bias_end, out_down, out_up, up_down, low_up, mask, umap, dmap, bias, dn, cot_own,
+    w_out_in, cot_all, up,
+    grad_merged, grad_res, mixed, small_out, a_out, b_out, two, mine_in, mine_cot,
+    w_out, residual, low_out, sa, cot, up_v, dn_v, slope, act, pre, parts, total, *refs,
 ):
     scratch, (send, recv, local) = refs[:-3], refs[-3:]
+    scratch, forth_scratch = scratch[:6], scratch[6:]
     place = Place()
-    greet(members(place))
+    greet(members(place) + plane_devices(place))
     sends = Sends(send, recv)
-    sa[place.x, place.c] = second[...]
-    gather = GroupGather(place, sends, sa)
     loads = [
-        pltpu.make_async_copy(src, dst, local.at[n])
-        for n, (src, dst) in enumerate(((dn, dn_v), (cot_all, cot), (up, up_v)))
+        pltpu.make_async_copy(src, dst, local.at[n]) for n, (src, dst) in enumerate(((w_out_in, w_out), (up, up_v), (cot_all, cot)))
     ]
     for copy in loads:
         copy.start()
 
+    def dn_view(h):
+        def view(fixed, half):
+            cols = pl.ds(h * 1024, 1024) if half is None else pl.ds(h * 1024 + half * 512, 512)
+            return dn_v.at[fixed.get("z", ALL), fixed.get("y", ALL), :, cols]
+
+        return view
+
+    here = {"z": place.z, "y": place.y}
+    dn_v[place.z, place.y] = dn[...]
+    dn_gathers = [
+        ring_gather(place, sends, dn_view(h), order, dn_view(h)(here, None), Nothing(), False)
+        for h, order in enumerate((("y", "z"), ("z", "y")))
+    ]
+
+    def tick(*parts):
+        for part in parts:
+            next(part)
+
+    tick(*dn_gathers)
+    low_out[...] = (dot(merged[...], out_down[...]) * mask[...]).astype(bf16)
+    loads[0].wait()
+
+    def out_tile(n, _):
+        cols = piece(n, 256)
+        value = tok[:, cols].astype(f32) + dot(merged[...], w_out[:, cols]) + bias_out[:, cols]
+        residual[:, cols] = value + dot(low_out[...], out_up[:, cols])
+        return 0
+
+    lax.fori_loop(0, 6, out_tile, 0)
+    tick(*dn_gathers)
+    lax.fori_loop(6, 8, out_tile, 0)
+    second = layer_norm(residual[...], gain[...], shift[...]).astype(bf16)
+    own = sa.at[place.x, place.c]
+    own[:, 0:2048] = second
+    own[:, 2048:2176] = (dot(second, up_down[...]) * mask[...]).astype(bf16)
+    gather = GroupGather(place, sends, sa)
+
     def rows(ref, x, start, size):
         return ref[x, :, :, pl.ds(start, size)].reshape(256, size)
 
-    loads[0].wait()
-    loads[1].wait()
-
-    def grad_tile(n, _):
-        xs, cols = piece(n // 4, 2), piece(lax.rem(n, 4), 256)
-        value = dot_nt(cot[xs, :, :, 0:2048].reshape(512, 2048), dn_v[cols, :])
-        value = value + dot_nt(cot[xs, :, :, 2048:2176].reshape(512, 128), dmap[cols, :])
-        grad_act[xs, :, cols] = value.reshape(2, 256, 256)
-        return 0
-
-    lax.fori_loop(0, 8, grad_tile, 0)
-    loads[2].wait()
     xs = places_in_turn(place)
 
     def hidden(k):
@@ -1005,9 +1061,20 @@
             value = dot(rows(sa, x, 0, 2048), up_v[:, cols]) + bias[:, cols]
             value = value + dot(rows(sa, x, 2048, 128), umap[:, cols])
             phi = 0.5 * (1.0 + lax.erf(value * 0.7071067811865476))
-            slope = phi + value * (0.3989422804014327 * jnp.exp2(value * value * (-0.5 * LOG2E)))
             act[k, :, cols] = (value * phi).astype(bf16)
-            pre[k, :, cols] = (grad_act[x, :, cols] * slope).astype(bf16)
+            slope[k, :, cols] = phi + value * (0.3989422804014327 * jnp.exp2(value * value * (-0.5 * LOG2E)))
+            return 0
+
+        lax.fori_loop(0, 4, tile, 0)
+
+    def grad_hidden(k):
+        x = xs[k]
+
+        def tile(n, _):
+            cols = piece(n, 256)
+            value = dot_nt(rows(cot, x, 0, 2048), dn_v[n].reshape(256, 2048))
+            value = value + dot_nt(rows(cot, x, 2048, 128), dmap[cols, :])
+            pre[k, :, cols] = (value * slope[k, :, cols]).astype(bf16)
             return 0
 
         lax.fori_loop(0, 4, tile, 0)
@@ -1027,22 +1094,30 @@
         value = dot(act[ks].reshape(n * 256, 1024), dmap[...]).astype(bf16)
         parts[ks, :, :, 2176:2304] = value.reshape(n, 2, 128, 128)
 
+    loads[1].wait()
     gather.own()
     hidden(3)
+    tick(*dn_gathers)
     gather.near()
     hidden(2)
     hidden(1)
+    run_all(dn_gathers)
+    loads[2].wait()
+    grad_hidden(3)
     gather.far()
+    grad_hidden(2)
     gather.far_done()
     hidden(0)
+    grad_hidden(0)
 
     sums = GroupSum(place, sends, parts, scratch)
     backward(0, 1)
     sums.cross(0)
+    grad_hidden(1)
+    sums.merge(0)
+    sums.first()
     backward(1, 1)
     sums.cross(1)
-    sums.merge(0)
-    sums.first()
     backward(2, 2)
     sums.cross(2)
     sums.cross(3)
@@ -1050,14 +1125,6 @@
     sums.merge(2)
     sums.second()
 
-    def forward(n, _):
-        ks, cols = piece(n // 4, 2), piece(lax.rem(n, 4), 512)
-        value = dot(act[ks].reshape(512, 1024), dn_v[:, cols]).astype(bf16)
-        forth[ks, :, :, cols] = value.reshape(2, 2, 128, 512)
-        return 0
-
-    lax.fori_loop(0, 8, forward, 0)
-
     def small(k, _):
         x = lax.rem(place.x + jnp.where(k == 3, 0, jnp.where(k == 2, 3, 2 - k)), 4)
         one = dot_tn(act[k], rows(cot, x, 2048, 128))
@@ -1079,32 +1146,79 @@
     cols = piece(place.g, 256)
     mine_in[...] = sa[:, :, :, cols].reshape(1024, 256)
     mine_cot[...] = cot[:, :, :, cols].reshape(1024, 256)
+    def forward(n, _):
+        ks, cols = piece(n // 4, 2), piece(lax.rem(n, 4), 512)
+        value = dot(act[ks].reshape(512, 1024), dn_v[:, :, :, cols].reshape(1024, 512)).astype(bf16)
+        cot[ks, :, :, cols] = value.reshape(2, 2, 128, 512)
+        return 0
+
+    lax.fori_loop(0, 8, forward, 0)
+
     two[...] = total[...].astype(bf16)
-    back[...] = sums.result()
+    forth = GroupSum(place, sends, cot.at[:, :, :, pl.ds(0, 2048)], forth_scratch)
+    for k in range(4):
+        forth.cross(k)
+    summed = sums.result()
+    forth.merge(0)
+    forth.first()
+    low_up_grad = (summed[:, 2048:2176] * mask[...]).astype(bf16)
+    low_down = (summed[:, 2176:2304] * mask[...]).astype(bf16)
+    small_out[:, 0:128] = low_up_grad
+    small_out[:, 128:256] = low_down
+    grad_second = summed[:, 0:2048] + dot_nt(low_up_grad, up_down[...])
+    value = cot_own[...].astype(f32) + layer_norm_back(residual[...], gain[...], grad_second)
+    grad_res[...] = value
+    branch = value.astype(bf16)
+    low_grad = (dot_nt(branch, out_up[...]) * mask[...]).astype(bf16)
+
+    def merged_tile(n, _):
+        cols = piece(n, 256)
+        value = dot_nt(branch, w_out[cols, :]) + dot_nt(low_grad, out_down[cols, :])
+        grad_merged[:, cols] = value.astype(bf16)
+        return 0
+
+    lax.fori_loop(0, 4, merged_tile, 0)
+    forth.merge(1)
+    forth.merge(2)
+    forth.second()
+    lax.fori_loop(4, 8, merged_tile, 0)
+    b_out[...] = dot_tn(low_out[...], branch).astype(bf16)
+    a_out[...] = dot_tn(merged[...], low_grad).astype(bf16)
+    value = residual[...] + bias_end[...] + dot(low_down, low_up[...])
+    mixed[...] = (value + forth.result()).astype(bf16)
     gather.finish()
-
-
-def feed_forward(second, cot_all, up, dn, umap, dmap, bias):
+    assert sends.used <= send.shape[0], sends.used
+
+
+def feed_forward(*args):
     any_ = pl.BlockSpec(memory_space=pl.ANY)
     vmem = pl.BlockSpec(memory_space=pltpu.VMEM)
     vm = lambda *s: pltpu.VMEM(s, bf16)
+    shape = lambda *s: jax.ShapeDtypeStruct(s, bf16)
     return pl.pallas_call(
         feed_forward_kernel,
         name="feed_forward",
         out_shape=[
-            jax.ShapeDtypeStruct((128, 2304), f32),
-            jax.ShapeDtypeStruct((4, 2, 128, 2048), bf16),
-            jax.ShapeDtypeStruct((2, 1024, 128), bf16),
-            jax.ShapeDtypeStruct((1024, 256), bf16),
-            jax.ShapeDtypeStruct((1024, 256), bf16),
+            shape(128, 2048),
+            jax.ShapeDtypeStruct((128, 2048), f32),
+            shape(128, 2048),
+            shape(128, 256),
+            shape(2048, 128),
+            shape(128, 2048),
+            shape(2, 1024, 128),
+            shape(1024, 256),
+            shape(1024, 256),
         ],
-        in_specs=[vmem] + [any_] * 3 + [vmem] * 3,
-        out_specs=[vmem] * 5,
+        in_specs=[vmem] * 16 + [any_] * 3,
+        out_specs=[vmem] * 9,
         scratch_shapes=[
+            vm(2048, 2048),
+            pltpu.VMEM((128, 2048), f32),
+            vm(128, 128),
             vm(4, 2, 128, 2176),
             vm(4, 2, 128, 2176),
             vm(2048, 1024),
-            vm(1024, 2048),
+            vm(4, 4, 64, 2048),
             pltpu.VMEM((4, 256, 1024), f32),
             vm(4, 256, 1024),
             vm(4, 256, 1024),
@@ -1112,9 +1226,10 @@
             pltpu.VMEM((2, 1024, 128), f32),
         ]
         + GroupSum.scratch(2304)
-        + [pltpu.SemaphoreType.DMA((k,)) for k in (16, 16, 3)],
-        compiler_params=pltpu.CompilerParams(collective_id=1, has_side_effects=True, vmem_limit_bytes=60 * MIB),
-    )(second, cot_all, up, dn, umap, dmap, bias)
+        + GroupSum.scratch(2048)
+        + [pltpu.SemaphoreType.DMA((k,)) for k in (40, 40, 3)],
+        compiler_params=pltpu.CompilerParams(collective_id=1, has_side_effects=True, vmem_limit_bytes=63 * MIB),
+    )(*args)
 
 
 def both_heads(gq, p, x):
@@ -1124,7 +1239,7 @@
 
 def tail_kernel(
     grads, qkv_w, act_all, dmaps, low_rank, small, tok, gain, grad_res, mine_in, mine_cot, a_piece, b_piece, two_piece,
-    input_grad, a_final, b_final, a_early, b_early, two_res,
+    input_grad, a_final, b_final, a_up, b_down, two_a, two_b, a_early, b_early,
     a_res, b_res, gq, wq, act, left, parts, lows, a_sums, b_sums, a_s, a_f, b_s, b_f, *refs,
 ):
     scratch, (send, recv, local) = refs[:-3], refs[-3:]
@@ -1140,12 +1255,13 @@
     own = lows.at[place.x, place.c]
     own[:, 0:384] = low_rank[...]
     own[:, 384:640] = small[...]
-    spread = [sends.push(own, own, place.member(*m)) for m in MEMBERS]
-
-    def two_view(n):
+    spread = [sends.push(own, own, place.member(dx, 0)) for dx in (2, 1, 3)]
+    passed = [sends.push(own, own, place.member(0, 1))]
+
+    def two_view(res):
         def view(at):
             xl, xh = two_parts(at)
-            return two_res.at[n, xl, place.c, at["z"], at["y"], xh]
+            return res.at[xl, place.c, at["z"], at["y"], xh]
 
         return view
 
@@ -1160,10 +1276,10 @@
         return b_early.at[place.c, at["x"], :, cols]
 
     early = [
-        give_all(place, sends, ("z", "y", "x"), two_piece.at[0], two_view(0), local.at[3]),
-        give_all(place, sends, ("z", "x", "y"), two_piece.at[1], two_view(1), local.at[4]),
+        give_all(place, sends, ("x", "z", "y"), two_piece.at[0], two_view(two_a), local.at[3]),
+        give_all(place, sends, ("x", "y", "z"), two_piece.at[1], two_view(two_b), local.at[4]),
         give_all(
-            place, sends, ("y", "z", "x"), a_piece,
+            place, sends, ("x", "y", "z"), a_piece,
             lambda at: a_early.at[place.c, at["z"], at["y"], at["x"]], local.at[5],
         ),
         give_all(place, sends, ("x", "y", "z"), b_piece, b_early_view, local.at[6]),
@@ -1175,6 +1291,40 @@
 
     tick(*early)
     loads[0].wait()
+    loads[2].wait()
+    for p in range(3):
+        total = jnp.zeros((128, 256), f32)
+        for x in range(4):
+            left_rows = act[x, :, :, 2048 + p * 128 : 2176 + p * 128].reshape(256, 128)
+            total = total + dot_tn(left_rows, both_heads(gq, p, x))
+        b_sums[p] = total.astype(bf16)
+    def a_view(at):
+        return a_res.at[:, at["x"], place.c, at["z"], at["y"]]
+
+    def a_held(z, y):
+        return a_sums.at[:, piece(z * 4 + y, 16)]
+
+    def b_view(at):
+        y = at["y"]
+        if y is ALL:
+            yr, yc = ALL, ALL
+        elif isinstance(y, pl.Slice):
+            yr, yc = pl.ds(y.start // 2, 1), ALL
+        else:
+            yr, yc = y // 2, lax.rem(y, 2)
+        return b_res.at[:, at["x"], place.c, at["z"], yr, yc]
+
+    def b_held(z, y):
+        return b_sums.at[:, pl.ds(pl.multiple_of(z * 32 + y // 2 * 16, 16), 16), piece(lax.rem(y, 2), 128)]
+
+    def late_part(final, held, slots, order, view, sem):
+        yield from reduce_piece(place, sends, final, None, (held, slots, final), None)
+        yield from give_all(place, sends, order, final, view, sem, True)
+
+    late = [
+        late_part(a_f, a_held, a_s, ("z", "y", "x"), a_view, local.at[7]),
+        late_part(b_f, b_held, b_s, ("x", "z", "y"), b_view, local.at[8]),
+    ]
     loads[1].wait()
     xs = places_in_turn(place)
     for k in range(4):
@@ -1201,15 +1351,11 @@
     partial(2, 2)
     sums.cross(2)
     sums.cross(3)
-
-    loads[2].wait()
-    for p in range(3):
-        total = jnp.zeros((128, 256), f32)
-        for x in range(4):
-            left_rows = act[x, :, :, 2048 + p * 128 : 2176 + p * 128].reshape(256, 128)
-            total = total + dot_tn(left_rows, both_heads(gq, p, x))
-        b_sums[p] = total.astype(bf16)
-    for copy in spread:
+    for dx, copy in zip((2, 1, 3), spread):
+        copy.wait()
+        came = lows.at[place.step("x", -dx), place.c]
+        passed.append(sends.push(came, came, place.member(0, 1)))
+    for copy in passed:
         copy.wait()
     b_sums[3] = dot_tn(lows[:, :, :, 512:640].reshape(1024, 128), mine_cot[...]).astype(bf16)
     rows = act[:, :, :, piece(place.g, 256)].reshape(1024, 256)
@@ -1217,52 +1363,31 @@
         right = lows[:, :, :, p * 128 : p * 128 + 128].reshape(1024, 128)
         a_sums[p] = dot_tn(rows if p < 3 else mine_in[...], right).astype(bf16)
 
-    def a_view(at):
-        return a_res.at[:, at["x"], place.c, at["z"], at["y"]]
-
-    def a_held(z, y):
-        return a_sums.at[:, piece(z * 4 + y, 16)]
-
-    def b_view(at):
-        y = at["y"]
-        if y is ALL:
-            yr, yc = ALL, ALL
-        elif isinstance(y, pl.Slice):
-            yr, yc = pl.ds(y.start // 2, 1), ALL
-        else:
-            yr, yc = y // 2, lax.rem(y, 2)
-        return b_res.at[:, at["x"], place.c, at["z"], yr, yc]
-
-    def b_held(z, y):
-        return b_sums.at[:, pl.ds(pl.multiple_of(z * 32 + y // 2 * 16, 16), 16), piece(lax.rem(y, 2), 128)]
-
-    def late_part(final, held, slots, order, view, sem):
-        yield from reduce_piece(place, sends, final, None, (held, slots, final), None)
-        yield from give_all(place, sends, order, final, view, sem)
-
-    late = [
-        late_part(a_f, a_held, a_s, ("z", "x", "y"), a_view, local.at[7]),
-        late_part(b_f, b_held, b_s, ("y", "x", "z"), b_view, local.at[8]),
-    ]
     tick(*late)
-    tick(*early)
     sums.merge(1)
     sums.merge(2)
     sums.second()
-    tick(*late, *early)
-    tick(*late, *early)
+    tick(*early)
+    tick(*late)
+    tick(*early)
+    tick(*late)
     grad_first = sums.result()
     for p in range(3):
         grad_first = grad_first + dot_nt(low_rank[:, p * 128 : p * 128 + 128], dmaps[p])
     result = grad_res[...] + layer_norm_back(tok[...].astype(f32), gain[...], grad_first)
     input_grad[...] = result.astype(bf16)
     run_all(late + early)
-    moves = [pltpu.make_async_copy(a_res, a_final, local.at[9])]
-    for g in range(8):
-        for yc in range(2):
-            src = b_res.at[:, g // 2, g % 2, :, :, yc]
-            dst = b_final.at[:, :, :, :, pl.ds(g * 256 + yc * 128, 128)]
-            moves.append(pltpu.make_async_copy(src, dst, local.at[10 + g * 2 + yc]))
+    moves = [
+        pltpu.make_async_copy(a_res.at[pl.ds(0, 3)], a_final, local.at[9]),
+        pltpu.make_async_copy(a_res.at[3], a_up, local.at[10]),
+    ]
+    for part, whole, n in ((pl.ds(0, 3), b_final, 12), (3, b_down, 28)):
+        for g in range(8):
+            for yc in range(2):
+                src = b_res.at[part, g // 2, g % 2, :, :, yc]
+                cols = pl.ds(g * 256 + yc * 128, 128)
+                dst = whole.at[:, :, :, :, cols] if n == 12 else whole.at[:, :, :, cols]
+                moves.append(pltpu.make_async_copy(src, dst, local.at[n + g * 2 + yc]))
     for copy in moves:
         copy.start()
     for copy in moves:
@@ -1276,19 +1401,22 @@
     vm = lambda *s: pltpu.VMEM(s, bf16)
     shape = lambda *s: jax.ShapeDtypeStruct(s, bf16)
     a_shape, b_shape = (4, 4, 2, 4, 4, 16, 128), (4, 4, 2, 4, 2, 2, 16, 128)
-    input_grad, late_a, late_b, early_a, early_b, early_two = pl.pallas_call(
+    input_grad, a_all, b_all, a_up, b_down, two_a, two_b, a_out, b_out = pl.pallas_call(
         tail_kernel,
         name="tail",
         out_shape=[
             shape(128, 2048),
-            shape(*a_shape),
-            shape(4, 4, 2, 16, 2048),
+            shape(3, *a_shape[1:]),
+            shape(3, 4, 2, 16, 2048),
+            shape(*a_shape[1:]),
+            shape(4, 2, 16, 2048),
+            shape(2, 2, 4, 4, 2, 64, 128),
+            shape(2, 2, 4, 4, 2, 64, 128),
             shape(2, 4, 4, 4, 16, 128),
             shape(2, 4, 16, 2048),
-            shape(2, 2, 2, 4, 4, 2, 64, 128),
         ],
         in_specs=[any_] * 3 + [vmem] * 11,
-        out_specs=[vmem] + [any_] * 5,
+        out_specs=[vmem] + [any_] * 8,
         scratch_shapes=[
             vm(*a_shape),
             vm(*b_shape),
@@ -1306,18 +1434,19 @@
             vm(4, 16, 128),
         ]
         + GroupSum.scratch(2048)
-        + [pltpu.SemaphoreType.DMA((k,)) for k in (200, 200, 26)],
+        + [pltpu.SemaphoreType.DMA((k,)) for k in (200, 200, 45)],
         compiler_params=pltpu.CompilerParams(collective_id=3, has_side_effects=True, vmem_limit_bytes=60 * MIB),
     )(
         grads, qkv_w, act_all, dmaps, low_rank, small, tok, gain, grad_res, mine_in, mine_cot, a_piece, b_piece, two_piece
     )
     return (
         input_grad,
-        late_a.reshape(4, 2048, 128),
-        late_b.reshape(4, 128, 2048),
-        early_a.reshape(2048, 128),
-        early_b.reshape(128, 2048),
-        early_two.reshape(2, 8192, 128),
+        jnp.concatenate([a_all.reshape(3, 2048, 128), a_out.reshape(1, 2048, 128)]),
+        jnp.concatenate([b_all.reshape(3, 128, 2048), b_out.reshape(1, 128, 2048)]),
+        a_up.reshape(2048, 128),
+        b_down.reshape(128, 2048),
+        two_a.reshape(8192, 128),
+        two_b.reshape(8192, 128),
     )
 
 
@@ -1347,7 +1476,6 @@
     scale = head_size ** (-0.5)
     xl, c, z, y, xh = (lax.axis_index(a) for a in AXES)
     group = (xh * 2 + xl) * 2 + c
-    inputs = tokens[0].astype(f32)
     cot = cotangent[0]
     bias_rows = jnp.stack([projection_bias[0], jnp.zeros_like(projection_bias[0]), projection_bias[1]])
 
@@ -1362,55 +1490,37 @@
 
     my_up_maps = my_columns(attention_up_maps[:3])
     (
-        act_all, qkv_w, out_all, up_all, dn_all, cot_all, by_head, across, merged, attended, lse, mask
+        act_all, qkv_w, out_all, up_all, cot_all, by_head, across, merged, attended, lse, mask
     ) = front(
         document_starts, document_adapter, tokens[0], layernorm_gain[:1], layernorm_bias[:1],
         my_columns(bias_rows)[:, None, :], attention_down_maps, my_up_maps, cot, lower_up_maps,
-        jnp.transpose(projection_weight, (1, 0, 2)), output_weight, up_weight, down_weight, scale,
+        jnp.transpose(projection_weight, (1, 0, 2)), output_weight, up_weight, scale,
     )
-    w_out = out_all.reshape(width, width)
-
-    adapt_out = (dot(merged, attention_down_maps[3]) * mask).astype(bf16)
-    residual = inputs + dot(merged, w_out) + projection_bias[2] + dot(adapt_out, attention_up_maps[3])
-    second_in = layer_norm(residual, layernorm_gain[1], layernorm_bias[1]).astype(bf16)
-    adapt_up = (dot(second_in, upper_down_maps) * mask).astype(bf16)
-
     down_maps = lax.dynamic_slice_in_dim(lower_down_maps, (xl * 2 + c) * 2048, 2048, 0)
     down_maps = lax.dynamic_index_in_dim(down_maps.reshape(16, 2, 64, 128), xh, 1, False).reshape(1024, 128)
-    back, forth, two, mine_in, mine_cot = feed_forward(
-        jnp.concatenate([second_in, adapt_up], axis=1), cot_all, up_all.reshape(width, 1024),
-        dn_all.reshape(1024, width), my_hidden(upper_up_maps), down_maps, my_hidden(upper_bias)[None],
+    grad_merged, grad_residual, mixed, small, a_out, b_out, two, mine_in, mine_cot = feed_forward(
+        merged, tokens[0], layernorm_gain[1:], layernorm_bias[1:], projection_bias[2:3], projection_bias[3:4],
+        attention_down_maps[3], attention_up_maps[3], upper_down_maps, lower_up_maps, mask, my_hidden(upper_up_maps),
+        down_maps, my_hidden(upper_bias)[None], down_weight, cot,
+        out_all.reshape(width, width), cot_all, up_all.reshape(width, 1024),
     )
-
-    grad_adapt_up = (back[:, width : width + 128] * mask).astype(bf16)
-    grad_second = back[:, :width] + dot_nt(grad_adapt_up, upper_down_maps)
-    grad_residual = cot.astype(f32) + layer_norm_back(residual, layernorm_gain[1], grad_second)
-    grad_branch = grad_residual.astype(bf16)
-    grad_b_out = dot_tn(adapt_out, grad_branch)
-    grad_adapt_out = (dot_nt(grad_branch, attention_up_maps[3]) * mask).astype(bf16)
-    grad_a_out = dot_tn(merged, grad_adapt_out)
-    grad_merged = (dot_nt(grad_branch, w_out) + dot_nt(grad_adapt_out, attention_down_maps[3])).astype(bf16)
-
-    adapt_down = (back[:, width + 128 :] * mask).astype(bf16)
-    grad_qkv, grad_adapt_qkv, forth_sum, a_piece, b_piece, two_piece = middle(
-        document_starts, grad_merged, by_head, across, attended, lse, attention_up_maps, mask, forth,
-        grad_a_out.astype(bf16), grad_b_out.astype(bf16), two, scale,
+    grad_qkv, grad_adapt_qkv, a_piece, b_piece, two_piece = middle(
+        document_starts, grad_merged, by_head, across, attended, lse, attention_up_maps, mask, a_out, b_out, two, scale
     )
-    input_grad, late_a, late_b, early_a, early_b, early_two = tail(
+    input_grad, a_all, b_all, a_up, b_down, hidden_a, hidden_b = tail(
         grad_qkv, qkv_w, act_all, attention_down_maps, grad_adapt_qkv,
-        jnp.concatenate([grad_adapt_up, adapt_down], axis=1), tokens[0], layernorm_gain[:1], grad_residual,
+        small, tokens[0], layernorm_gain[:1], grad_residual,
         mine_in, mine_cot, a_piece, b_piece, two_piece,
     )
-    output = residual + forth_sum + projection_bias[3] + dot(adapt_down, lower_up_maps)
     return (
-        output.astype(bf16)[None],
+        mixed[None],
         input_grad[None],
-        jnp.concatenate([late_a[:3], early_a[None]]).astype(f32),
-        jnp.concatenate([late_b[:3], early_b[None]]).astype(f32),
-        late_a[3].astype(f32),
-        jnp.transpose(early_two[1]).astype(f32),
-        early_two[0].astype(f32),
-        late_b[3].astype(f32),
+        a_all.astype(f32),
+        b_all.astype(f32),
+        a_up.astype(f32),
+        jnp.transpose(hidden_b).astype(f32),
+        hidden_a.astype(f32),
+        b_down.astype(f32),
     )
 
 

time: 456 us -> 434 us (0.952)
  matrix products: 21.3 us -> 0 us
    pallas_call x1, Pallas kernels: 61.4 us -> 94.8 us  [feed_forward(): pl.pallas_call(feed_forward_kernel, name='feed_forward', out_shape=[shape...]
    dot_general x11 -> x0, matrix products: 21.3 us -> none  [the longest x4 10.8 us: dot_nt(): lax.dot_general(left, right, (((1,), (1,)), ((), ())), preferred_element_...]
    pallas_call x1, Pallas kernels: 164 us -> 143 us  [front(): pl.pallas_call(functools.partial(front_kernel, scale=scale), name='front'...]
    pallas_call x1, Pallas kernels: 89.5 us -> 79.1 us  [middle(): pl.pallas_call(functools.partial(middle_kernel, scale=scale), name='atten...]
    convert_element_type x8 -> x6, other arithmetic: 12.9 us -> 13.8 us  [the longest x1 2.42 us: per_device(): hidden_a.astype(f32)]
where the time goes in v5:
time: 434 us; the launch traced here: 428 us
  Pallas kernels  392 us (90%)
  local copies, waits for them, and re-layouts  20.9 us (5%)
  other arithmetic  13.8 us (3%)
    pallas_call x1, Pallas kernels, front(): pl.pallas_call(functools.partial(front_kernel, scale=scale), name='front'...  143 us
    pallas_call x1, Pallas kernels, feed_forward(): pl.pallas_call(feed_forward_kernel, name='feed_forward', out_shape=[shape...  94.8 us
    pallas_call x1, Pallas kernels, middle(): pl.pallas_call(functools.partial(middle_kernel, scale=scale), name='atten...  79.1 us
    pallas_call x1, Pallas kernels, tail(): pl.pallas_call(tail_kernel, name='tail', out_shape=[shape(128, 2048), sha...  75.2 us

profile of v5, /device:TPU:1, one launch (start us, length us, event | category | flops | bytes accessed | tf_op | source)
XLA Modules:
  0.0 427.5 jit_solution(7105634751702245589)
XLA Ops:
  0.7 0.7 dynamic_slice.33
  2.2 1.4 fusion.2
  3.6 1.5 fusion.1
  5.8 1.1 constant_dynamic-slice_fusion.3
  7.2 0.9 copy.28.umap
  8.1 1.1 constant_dynamic-slice_fusion.1
  9.2 0.7 constant_dynamic-slice_fusion
  9.9 1.9 slice_bitcast_fusion.1.out_down
  11.8 0.8 slice_bitcast_fusion.out_up
  12.6 0.8 slice-done
  13.4 0.7 constant_dynamic-slice_fusion.4.umaps
  14.1 142.6 %front.1 = (bf16[4,2,128,2432]{3,2,1,0:T(8,128)(2,1)}, bf16[3,256,2048]{2,1,0:T(8,128)(2,1)}, bf16[2,2,4,4,2,16,2048]{6,5,4,3,2,1,0:T(8,128)(2,1)}, bf16[2,2,4,4...) custom-call(s32[1,8]{1,0:T(1,128)} %starts.3, ...), custom_call_target="tpu_custom_call" | custom-call | tf_op jit(solution)/shard_map/front/pallas_call | solution.py:744
  156.7 94.8 %feed_forward.1 = (bf16[128,2048]{1,0:T(8,128)(2,1)}, f32[128,2048]{1,0:T(8,128)}, bf16[128,2048]{1,0:T(8,128)(2,1)}, bf16[128,256]{1,0:T(8,128)(2,1)}, bf16[204...) custom-call(bf16[128,2048]{1,0:T(8,128)(2,1)} %get-tuple-element.42., ...), custom_call_target="tpu_custom_call" | custom-call | tf_op jit(solution)/shard_map/feed_forward/pallas_call | solution.py:1198
  251.5 79.1 %attention_backward.1 = (bf16[3,4,2,2,128,128]{5,4,3,2,1,0:T(8,128)(2,1)}, bf16[128,384]{1,0:T(8,128)(2,1)}, bf16[16,128]{1,0:T(8,128)(2,1)}, bf16[16,128]{1,0:T(8,128)(2,1)}, bf16[2,64,128]{2,1,0:T(8,128)(2,1)}) custom-call(s32[1,8]{1,0:T(1,128)} %starts.3, bf16[128,2048]{1,0:T(8,128)(2,1)} %get-tuple-element.48.grad, ...), custom_call_target="tpu_custom_call" | custom-call | tf_op jit(solution)/shard_map/attention_backward/pallas_call | solution.py:963
  330.6 75.2 %tail.1 = (bf16[128,2048]{1,0:T(8,128)(2,1)}, bf16[3,4,2,4,4,16,128]{6,5,4,3,2,1,0:T(8,128)(2,1)}, bf16[3,4,2,16,2048]{4,3,2,1,0:T(8,128)(2,1)}, bf16[4,2,4,4,16...) custom-call(bf16[3,4,2,2,128,128]{5,4,3,2,1,0:T(8,128)(2,1)} %get-tu, ...), custom_call_target="tpu_custom_call" | custom-call | tf_op jit(solution)/shard_map/tail/pallas_call | solution.py:1404
  405.8 2.2 bitcast_convert_fusion.3
  408.0 2.1 bitcast_convert_fusion.2
  410.1 2.3 maximum_convert_fusion
  412.5 2.3 maximum_convert_fusion.1
  414.9 2.4 bitcast_convert_fusion.1
  417.3 5.7 %copy.29 = f32[8192,128]{0,1:T(8,128)} copy(f32[8192,128]{1,0:T(8,128)} %bitcast_convert_fusion.1) | data formatting | bytes 8388608 | tf_op jit(solution)/shard_map/convert_element_type | solution.py:1521
  423.1 2.4 bitcast_convert_fusion
  425.5 0.8 copy.33
  426.3 0.8 copy.34
  (27 shorter events, 2.1 us)
Async XLA Ops:
  7.2 4.6 %copy-start = (bf16[4,128,2048]{2,1,0:T(8,128)(2,1)S(1)}, bf16[4,128,2048]{2,1,0:T(8,128)(2,1)}, u32[]{:S(2)}) copy-start(bf16[4,128,2048]{2,1,0:T(8,128)(2,1)} %umaps_in.1) | copy-start | bytes 6291460
  11.8 1.6 slice-start
  405.8 4.4 %copy-start.4 = (bf16[3,4,2,4,4,16,128]{6,5,4,3,2,1,0:T(8,128)(2,1)S(1)}, bf16[3,4,2,4,4,16,128]{6,5,4,3,2,1,0:T(8,128)(2,1)}, u32[]{:S(2)}) copy-start(bf16[3,4,2,4,4,16,128]{6,5,4,3,2,1,0:T(8,128)(2,1)} %get-tuple-element.68) | copy-start | bytes 4718596
  405.8 4.4 %copy-start.6 = (bf16[2,4,4,4,16,128]{5,4,3,2,1,0:T(8,128)(2,1)S(1)}, bf16[2,4,4,4,16,128]{5,4,3,2,1,0:T(8,128)(2,1)}, u32[]{:S(2)}) copy-start(bf16[2,4,4,4,16,128]{5,4,3,2,1,0:T(8,128)(2,1)} %get-tuple-element.69) | copy-start | bytes 1572868
  410.1 2.3 copy-start.3
  410.1 2.3 copy-start.5
  412.5 2.4 copy-start.2
  417.3 5.7 %copy-start.1 = (bf16[2,2,4,4,2,64,128]{6,5,4,3,2,1,0:T(8,128)(2,1)S(1)}, bf16[2,2,4,4,2,64,128]{6,5,4,3,2,1,0:T(8,128)(2,1)}, u32[]{:S(2)}) copy-start(bf16[2,2,4,4,2,64,128]{6,5,4,3,2,1,0:T(8,128)(2,1)} %get-tuple-element.74) | copy-start | bytes 6291460
  423.1 2.4 copy-start.7
  423.1 3.2 copy-start.8

commit v6 on v5

--- a/solution.py
+++ b/solution.py
@@ -513,12 +513,18 @@
 
 
 def front_kernel(
-    starts, chosen, tok, gain, shift, bias, dmaps, umaps, cot, lum, wp, wo, up,
+    starts, chosen, tok, gain, shift, bias, cot, wp, wo, up, umaps_in, dmaps_in, lum_in,
     act_all, qkv_w, out_all, up_all, cot_all, heads, across, merged, att, lse, mask,
-    act, cotbuf, wq, up_own, rows, mine, others, low, wq_t, send, recv, a_send, a_recv, local, *, scale,
+    umaps, dmaps, lum, act, cotbuf, wq, up_own, rows, mine, others, low, wq_t, send, recv, a_send, a_recv, local, *, scale,
 ):
     place = Place()
     sends = Sends(send, recv)
+    loads = [
+        pltpu.make_async_copy(dmaps_in.at[pl.ds(0, 3)], dmaps, local.at[14]),
+        pltpu.make_async_copy(lum_in, lum, local.at[15]),
+    ]
+    for copy in loads:
+        copy.start()
     always, perhaps = split_greeting(projectors(place))
     greet(plane_devices(place) + members(place) + always, perhaps)
     home = (place.xl, place.c, place.z, place.y, place.xh)
@@ -563,6 +569,7 @@
         )
         for h in range(2)
     ]
+    copies.append(pltpu.make_async_copy(umaps_in.at[pl.ds(0, 3), :, piece(place.g, 256)], umaps, local.at[2]))
     for copy in copies:
         copy.start()
     wq_spread = [
@@ -575,7 +582,7 @@
     ]
 
     values = tok[...].astype(f32)
-    normed = layer_norm(values, gain[...], shift[...]).astype(bf16)
+    normed = layer_norm(values, gain[0:1, :], shift[0:1, :]).astype(bf16)
     position = ((place.z * 4 + place.y) * 2 + place.xh) * 128 + lax.broadcasted_iota(jnp.int32, (128, 1), 0)
     adapter = jnp.zeros_like(position)
     for d in range(8):
@@ -585,6 +592,7 @@
     mask[...] = keep
     own = act.at[place.x, place.c]
     own[:, 0:2048] = normed
+    loads[0].wait()
     for p in range(3):
         own[:, 2048 + p * 128 : 2176 + p * 128] = (dot(normed, dmaps[p]) * keep).astype(bf16)
     act_gather = GroupGather(place, sends, act)
@@ -629,24 +637,23 @@
     tick(*qkv_parts, *out_gathers)
     own = cotbuf.at[place.x, place.c]
     own[:, 0:2048] = cot[...]
+    loads[1].wait()
     own[:, 2048:2176] = (dot_nt(cot[...], lum[...]) * keep).astype(bf16)
     act_gather.own()
     tick(*qkv_parts)
     act_gather.near(False)
     tick(*qkv_parts, *out_gathers)
     run_all(qkv_parts)
-    tick(*out_gathers)
-    up_keep.wait()
-    for copy in up_spread:
-        copy.wait()
-    tick(*up_gathers)
     kept = []
+    copies[3].wait()
 
     def project(x):
         left = act[x, :, :, 0:2048].reshape(256, 2048)
         for p in range(3):
             low_rank = act[x, :, :, 2048 + p * 128 : 2176 + p * 128].reshape(256, 128)
-            value = dot(left, wq[p].reshape(2048, 256)) + bias[p] + dot(low_rank, umaps[p])
+            value = dot(left, wq[p].reshape(2048, 256)) + dot(low_rank, umaps[p])
+            if p != 1:
+                value = value + bias[p // 2 : p // 2 + 1, piece(place.g, 256)]
             for j in range(2):
                 rows[p, x, :, j] = value[:, j * 128 : j * 128 + 128].astype(bf16).reshape(2, 128, 128)
 
@@ -678,6 +685,10 @@
     project(place.step("x", 1))
     post(1)
     post(3)
+    up_keep.wait()
+    for copy in up_spread:
+        copy.wait()
+    tick(*up_gathers, *out_gathers)
     act_gather.far()
     act_gather.far_done()
     project(place.step("x", 2))
@@ -701,6 +712,15 @@
     kept.append(pltpu.make_async_copy(others, across, local.at[8]))
     kept[-1].start()
     cot_gather = group_gather(place, sends, cotbuf)
+
+    def keep_cot(n, steps):
+        copies = []
+        for step in steps:
+            x = place.step("x", step)
+            copies.append(pltpu.make_async_copy(cotbuf.at[x], cot_all.at[x], local.at[n + len(copies)]))
+            copies[-1].start()
+        return copies
+
     tick(cot_gather)
 
     def tile(t, _):
@@ -717,9 +737,10 @@
 
     tiles = mine.shape[1] // F_TILE
     lax.fori_loop(0, tiles // 2, tile, 0)
-    tick(*up_gathers)
+    tick(*up_gathers, *out_gathers)
     lax.fori_loop(tiles // 2, tiles * 3 // 4, tile, 0)
     tick(cot_gather, *out_gathers)
+    kept += keep_cot(11, (0, 1, 3))
     lax.fori_loop(tiles * 3 // 4, tiles, tile, 0)
     back = heads_out(place, sends, low, merged, local.at[9])
     tick(back)
@@ -729,13 +750,12 @@
         copy.wait()
     act_gather.finish()
     run_all([back, *up_gathers, cot_gather, *out_gathers])
-    last = pltpu.make_async_copy(cotbuf, cot_all, local.at[10])
-    last.start()
-    last.wait()
+    for copy in keep_cot(10, (2,)):
+        copy.wait()
     assert sends.used <= send.shape[0], sends.used
 
 
-def front(starts, chosen, tok, gain, shift, bias, dmaps, umaps, cot, lum, wp, wo, up, scale):
+def front(starts, chosen, tok, gain, shift, bias, cot, wp, wo, up, umaps, dmaps, lum, scale):
     any_ = pl.BlockSpec(memory_space=pl.ANY)
     vmem = pl.BlockSpec(memory_space=pltpu.VMEM)
     smem = pl.BlockSpec(memory_space=pltpu.SMEM)
@@ -757,9 +777,12 @@
             jax.ShapeDtypeStruct((8, 256), f32),
             jax.ShapeDtypeStruct((128, 128), f32),
         ],
-        in_specs=[smem] * 2 + [vmem] * 11,
+        in_specs=[smem] * 2 + [vmem] * 8 + [any_] * 3,
         out_specs=[any_] * 8 + [vmem] * 3,
         scratch_shapes=[
+            vm(3, 128, 256),
+            vm(3, 2048, 128),
+            vm(128, 2048),
             vm(4, 2, 128, 2432),
             vm(4, 2, 128, 2176),
             vm(3, 2, 2, 4, 4, 2, 16, 256),
@@ -770,11 +793,11 @@
             vm(16, 128, 128),
             vm(3, 256, 2048),
         ]
-        + [pltpu.SemaphoreType.DMA(n) for n in ((150,), (150,), (2, 16), (2, 16), (11,))],
+        + [pltpu.SemaphoreType.DMA(n) for n in ((150,), (150,), (2, 16), (2, 16), (16,))],
         compiler_params=pltpu.CompilerParams(
             collective_id=0, has_side_effects=True, vmem_limit_bytes=56 * MIB
         ),
-    )(starts, chosen, tok, gain, shift, bias, dmaps, umaps, cot, lum, wp, wo, up)
+    )(starts, chosen, tok, gain, shift, bias, cot, wp, wo, up, umaps, dmaps, lum)
 
 
 def middle_kernel(
@@ -995,10 +1018,10 @@
 
 
 def feed_forward_kernel(
-    merged, tok, gain, shift, bias_out, bias_end, out_down, out_up, up_down, low_up, mask, umap, dmap, bias, dn, cot_own,
-    w_out_in, cot_all, up,
+    merged, tok, gains, shifts, biases, up_down, low_up, mask, bias_all, dn, cot_own,
+    w_out_in, cot_all, up, out_down_in, out_up_in, umap_in, dmap_in,
     grad_merged, grad_res, mixed, small_out, a_out, b_out, two, mine_in, mine_cot,
-    w_out, residual, low_out, sa, cot, up_v, dn_v, slope, act, pre, parts, total, *refs,
+    out_down, out_up, umap_all, umap, dmap, bias, w_out, residual, low_out, sa, cot, up_v, dn_v, slope, act, pre, parts, total, *refs,
 ):
     scratch, (send, recv, local) = refs[:-3], refs[-3:]
     scratch, forth_scratch = scratch[:6], scratch[6:]
@@ -1006,7 +1029,13 @@
     greet(members(place) + plane_devices(place))
     sends = Sends(send, recv)
     loads = [
-        pltpu.make_async_copy(src, dst, local.at[n]) for n, (src, dst) in enumerate(((w_out_in, w_out), (up, up_v), (cot_all, cot)))
+        pltpu.make_async_copy(src, dst, local.at[n]) for n, (src, dst) in enumerate(
+            (
+                (out_down_in.at[3], out_down), (w_out_in, w_out), (out_up_in.at[3], out_up),
+                (umap_in.at[:, piece(place.xl * 2 + place.c, 2048)], umap_all),
+                (dmap_in.at[place.xl * 2 + place.c, :, place.xh], dmap), (up, up_v), (cot_all, cot),
+            )
+        )
     ]
     for copy in loads:
         copy.start()
@@ -1030,23 +1059,35 @@
             next(part)
 
     tick(*dn_gathers)
+    gain, shift = gains[1:2, :], shifts[1:2, :]
+    bias_out, bias_end = biases[2:3, :], biases[3:4, :]
+    loads[0].wait()
     low_out[...] = (dot(merged[...], out_down[...]) * mask[...]).astype(bf16)
-    loads[0].wait()
+    loads[1].wait()
+    loads[2].wait()
 
     def out_tile(n, _):
         cols = piece(n, 256)
-        value = tok[:, cols].astype(f32) + dot(merged[...], w_out[:, cols]) + bias_out[:, cols]
+        value = tok[:, cols].astype(f32) + dot(merged[...], w_out[:, cols]) + biases[2:3, cols]
         residual[:, cols] = value + dot(low_out[...], out_up[:, cols])
         return 0
 
     lax.fori_loop(0, 6, out_tile, 0)
     tick(*dn_gathers)
     lax.fori_loop(6, 8, out_tile, 0)
-    second = layer_norm(residual[...], gain[...], shift[...]).astype(bf16)
+    second = layer_norm(residual[...], gain, shift).astype(bf16)
     own = sa.at[place.x, place.c]
     own[:, 0:2048] = second
     own[:, 2048:2176] = (dot(second, up_down[...]) * mask[...]).astype(bf16)
     gather = GroupGather(place, sends, sa)
+
+    loads[3].wait()
+    loads[4].wait()
+    whole_bias = bias_all[:, piece(place.xl * 2 + place.c, 2048)]
+    for n in range(8):
+        for whole, out in ((umap_all[:, n * 256 : n * 256 + 256], umap), (whole_bias[:, n * 256 : n * 256 + 256], bias)):
+            sides = [jnp.concatenate([whole[:, h : h + 64], whole[:, 128 + h : 192 + h]], axis=1) for h in (0, 64)]
+            out[:, n * 128 : n * 128 + 128] = jnp.where(place.xh == 0, sides[0], sides[1])
 
     def rows(ref, x, start, size):
         return ref[x, :, :, pl.ds(start, size)].reshape(256, size)
@@ -1073,7 +1114,7 @@
         def tile(n, _):
             cols = piece(n, 256)
             value = dot_nt(rows(cot, x, 0, 2048), dn_v[n].reshape(256, 2048))
-            value = value + dot_nt(rows(cot, x, 2048, 128), dmap[cols, :])
+            value = value + dot_nt(rows(cot, x, 2048, 128), dmap[piece(n, 4)].reshape(256, 128))
             pre[k, :, cols] = (value * slope[k, :, cols]).astype(bf16)
             return 0
 
@@ -1091,10 +1132,10 @@
         lax.fori_loop(0, 8, tile, 0)
         value = dot_nt(pre[ks].reshape(n * 256, 1024), umap[...]).astype(bf16)
         parts[ks, :, :, 2048:2176] = value.reshape(n, 2, 128, 128)
-        value = dot(act[ks].reshape(n * 256, 1024), dmap[...]).astype(bf16)
+        value = dot(act[ks].reshape(n * 256, 1024), dmap[...].reshape(1024, 128)).astype(bf16)
         parts[ks, :, :, 2176:2304] = value.reshape(n, 2, 128, 128)
 
-    loads[1].wait()
+    loads[5].wait()
     gather.own()
     hidden(3)
     tick(*dn_gathers)
@@ -1102,7 +1143,7 @@
     hidden(2)
     hidden(1)
     run_all(dn_gathers)
-    loads[2].wait()
+    loads[6].wait()
     grad_hidden(3)
     gather.far()
     grad_hidden(2)
@@ -1158,15 +1199,15 @@
     forth = GroupSum(place, sends, cot.at[:, :, :, pl.ds(0, 2048)], forth_scratch)
     for k in range(4):
         forth.cross(k)
-    summed = sums.result()
     forth.merge(0)
     forth.first()
+    summed = sums.result()
     low_up_grad = (summed[:, 2048:2176] * mask[...]).astype(bf16)
     low_down = (summed[:, 2176:2304] * mask[...]).astype(bf16)
     small_out[:, 0:128] = low_up_grad
     small_out[:, 128:256] = low_down
     grad_second = summed[:, 0:2048] + dot_nt(low_up_grad, up_down[...])
-    value = cot_own[...].astype(f32) + layer_norm_back(residual[...], gain[...], grad_second)
+    value = cot_own[...].astype(f32) + layer_norm_back(residual[...], gain, grad_second)
     grad_res[...] = value
     branch = value.astype(bf16)
     low_grad = (dot_nt(branch, out_up[...]) * mask[...]).astype(bf16)
@@ -1184,7 +1225,7 @@
     lax.fori_loop(4, 8, merged_tile, 0)
     b_out[...] = dot_tn(low_out[...], branch).astype(bf16)
     a_out[...] = dot_tn(merged[...], low_grad).astype(bf16)
-    value = residual[...] + bias_end[...] + dot(low_down, low_up[...])
+    value = residual[...] + bias_end + dot(low_down, low_up[...])
     mixed[...] = (value + forth.result()).astype(bf16)
     gather.finish()
     assert sends.used <= send.shape[0], sends.used
@@ -1209,9 +1250,15 @@
             shape(1024, 256),
             shape(1024, 256),
         ],
-        in_specs=[vmem] * 16 + [any_] * 3,
+        in_specs=[vmem] * 11 + [any_] * 7,
         out_specs=[vmem] * 9,
         scratch_shapes=[
+            vm(2048, 128),
+            vm(128, 2048),
+            vm(128, 2048),
+            vm(128, 1024),
+            vm(16, 64, 128),
+            pltpu.VMEM((1, 1024), f32),
             vm(2048, 2048),
             pltpu.VMEM((128, 2048), f32),
             vm(128, 128),
@@ -1227,7 +1274,7 @@
         ]
         + GroupSum.scratch(2304)
         + GroupSum.scratch(2048)
-        + [pltpu.SemaphoreType.DMA((k,)) for k in (40, 40, 3)],
+        + [pltpu.SemaphoreType.DMA((k,)) for k in (40, 40, 7)],
         compiler_params=pltpu.CompilerParams(collective_id=1, has_side_effects=True, vmem_limit_bytes=63 * MIB),
     )(*args)
 
@@ -1238,9 +1285,9 @@
 
 
 def tail_kernel(
-    grads, qkv_w, act_all, dmaps, low_rank, small, tok, gain, grad_res, mine_in, mine_cot, a_piece, b_piece, two_piece,
-    input_grad, a_final, b_final, a_up, b_down, two_a, two_b, a_early, b_early,
-    a_res, b_res, gq, wq, act, left, parts, lows, a_sums, b_sums, a_s, a_f, b_s, b_f, *refs,
+    grads, qkv_w, act_all, dmaps_in, grad_res_in, low_rank, small, tok, gain, mine_in, mine_cot, a_piece, b_piece, two_piece,
+    input_grad, a_res, b_res, two_a, two_b, a_early, b_early,
+    dmaps, grad_res, gq, wq, act, left, parts, lows, a_sums, b_sums, a_s, a_f, b_s, b_f, *refs,
 ):
     scratch, (send, recv, local) = refs[:-3], refs[-3:]
     place = Place()
@@ -1250,6 +1297,8 @@
         pltpu.make_async_copy(src, dst, local.at[n])
         for n, (src, dst) in enumerate(((grads, gq), (qkv_w, wq), (act_all, act)))
     ]
+    loads.append(pltpu.make_async_copy(dmaps_in.at[pl.ds(0, 3)], dmaps, local.at[44]))
+    loads.append(pltpu.make_async_copy(grad_res_in, grad_res, local.at[45]))
     for copy in loads:
         copy.start()
     own = lows.at[place.x, place.c]
@@ -1290,14 +1339,6 @@
             next(part)
 
     tick(*early)
-    loads[0].wait()
-    loads[2].wait()
-    for p in range(3):
-        total = jnp.zeros((128, 256), f32)
-        for x in range(4):
-            left_rows = act[x, :, :, 2048 + p * 128 : 2176 + p * 128].reshape(256, 128)
-            total = total + dot_tn(left_rows, both_heads(gq, p, x))
-        b_sums[p] = total.astype(bf16)
     def a_view(at):
         return a_res.at[:, at["x"], place.c, at["z"], at["y"]]
 
@@ -1323,8 +1364,9 @@
 
     late = [
         late_part(a_f, a_held, a_s, ("z", "y", "x"), a_view, local.at[7]),
-        late_part(b_f, b_held, b_s, ("x", "z", "y"), b_view, local.at[8]),
+        late_part(b_f, b_held, b_s, ("y", "x", "z"), b_view, local.at[8]),
     ]
+    loads[0].wait()
     loads[1].wait()
     xs = places_in_turn(place)
     for k in range(4):
@@ -1348,9 +1390,18 @@
     sums.cross(1)
     sums.merge(0)
     sums.first()
+    tick(*early)
     partial(2, 2)
     sums.cross(2)
     sums.cross(3)
+    tick(*early)
+    loads[2].wait()
+    for p in range(3):
+        total = jnp.zeros((128, 256), f32)
+        for x in range(4):
+            left_rows = act[x, :, :, 2048 + p * 128 : 2176 + p * 128].reshape(256, 128)
+            total = total + dot_tn(left_rows, both_heads(gq, p, x))
+        b_sums[p] = total.astype(bf16)
     for dx, copy in zip((2, 1, 3), spread):
         copy.wait()
         came = lows.at[place.step("x", -dx), place.c]
@@ -1367,59 +1418,44 @@
     sums.merge(1)
     sums.merge(2)
     sums.second()
-    tick(*early)
     tick(*late)
     tick(*early)
     tick(*late)
+    loads[3].wait()
+    loads[4].wait()
     grad_first = sums.result()
     for p in range(3):
         grad_first = grad_first + dot_nt(low_rank[:, p * 128 : p * 128 + 128], dmaps[p])
-    result = grad_res[...] + layer_norm_back(tok[...].astype(f32), gain[...], grad_first)
+    result = grad_res[...] + layer_norm_back(tok[...].astype(f32), gain[0:1, :], grad_first)
     input_grad[...] = result.astype(bf16)
-    run_all(late + early)
-    moves = [
-        pltpu.make_async_copy(a_res.at[pl.ds(0, 3)], a_final, local.at[9]),
-        pltpu.make_async_copy(a_res.at[3], a_up, local.at[10]),
-    ]
-    for part, whole, n in ((pl.ds(0, 3), b_final, 12), (3, b_down, 28)):
-        for g in range(8):
-            for yc in range(2):
-                src = b_res.at[part, g // 2, g % 2, :, :, yc]
-                cols = pl.ds(g * 256 + yc * 128, 128)
-                dst = whole.at[:, :, :, :, cols] if n == 12 else whole.at[:, :, :, cols]
-                moves.append(pltpu.make_async_copy(src, dst, local.at[n + g * 2 + yc]))
-    for copy in moves:
-        copy.start()
-    for copy in moves:
-        copy.wait()
+    tick(*late)
+    run_all(early + late)
     assert sends.used <= send.shape[0], sends.used
 
 
-def tail(grads, qkv_w, act_all, dmaps, low_rank, small, tok, gain, grad_res, mine_in, mine_cot, a_piece, b_piece, two_piece):
+def tail(grads, qkv_w, act_all, dmaps, grad_res, low_rank, small, tok, gain, mine_in, mine_cot, a_piece, b_piece, two_piece):
     any_ = pl.BlockSpec(memory_space=pl.ANY)
     vmem = pl.BlockSpec(memory_space=pltpu.VMEM)
     vm = lambda *s: pltpu.VMEM(s, bf16)
     shape = lambda *s: jax.ShapeDtypeStruct(s, bf16)
     a_shape, b_shape = (4, 4, 2, 4, 4, 16, 128), (4, 4, 2, 4, 2, 2, 16, 128)
-    input_grad, a_all, b_all, a_up, b_down, two_a, two_b, a_out, b_out = pl.pallas_call(
+    return pl.pallas_call(
         tail_kernel,
         name="tail",
         out_shape=[
             shape(128, 2048),
-            shape(3, *a_shape[1:]),
-            shape(3, 4, 2, 16, 2048),
-            shape(*a_shape[1:]),
-            shape(4, 2, 16, 2048),
+            shape(*a_shape),
+            shape(*b_shape),
             shape(2, 2, 4, 4, 2, 64, 128),
             shape(2, 2, 4, 4, 2, 64, 128),
             shape(2, 4, 4, 4, 16, 128),
             shape(2, 4, 16, 2048),
         ],
-        in_specs=[any_] * 3 + [vmem] * 11,
-        out_specs=[vmem] + [any_] * 8,
+        in_specs=[any_] * 5 + [vmem] * 9,
+        out_specs=[vmem] + [any_] * 6,
         scratch_shapes=[
-            vm(*a_shape),
-            vm(*b_shape),
+            vm(3, 2048, 128),
+            pltpu.VMEM((128, 2048), f32),
             vm(3, 4, 2, 2, 128, 128),
             vm(3, 256, 2048),
             vm(4, 2, 128, 2432),
@@ -1434,19 +1470,57 @@
             vm(4, 16, 128),
         ]
         + GroupSum.scratch(2048)
-        + [pltpu.SemaphoreType.DMA((k,)) for k in (200, 200, 45)],
+        + [pltpu.SemaphoreType.DMA((k,)) for k in (200, 200, 46)],
         compiler_params=pltpu.CompilerParams(collective_id=3, has_side_effects=True, vmem_limit_bytes=60 * MIB),
     )(
-        grads, qkv_w, act_all, dmaps, low_rank, small, tok, gain, grad_res, mine_in, mine_cot, a_piece, b_piece, two_piece
+        grads, qkv_w, act_all, dmaps, grad_res, low_rank, small, tok, gain, mine_in, mine_cot, a_piece, b_piece, two_piece
     )
-    return (
-        input_grad,
-        jnp.concatenate([a_all.reshape(3, 2048, 128), a_out.reshape(1, 2048, 128)]),
-        jnp.concatenate([b_all.reshape(3, 128, 2048), b_out.reshape(1, 128, 2048)]),
-        a_up.reshape(2048, 128),
-        b_down.reshape(128, 2048),
-        two_a.reshape(8192, 128),
-        two_b.reshape(8192, 128),
+def widen_kernel(a, a_one, b, b_one, hid_a, hid_b, a_out, b_out, up_out, hid_b_out, hid_a_out, down_out):
+    for n in range(3):
+        a_out[n] = a[n].reshape(256, 128).astype(f32)
+        for yc in range(2):
+            cols = pl.ds(yc * 128, 128)
+            b_out[n, :, cols] = b[n, 0, 0, :, :, yc].reshape(128, 128).astype(f32)
+    for yc in range(2):
+        cols = pl.ds(yc * 128, 128)
+        down_out[:, cols] = b[3, 0, 0, :, :, yc].reshape(128, 128).astype(f32)
+    a_out[3] = a_one[...].astype(f32)
+    up_out[...] = a[3].reshape(256, 128).astype(f32)
+    b_out[3] = b_one[...].astype(f32)
+    hid_a_out[...] = hid_a[...].astype(f32)
+    hid_b_out[...] = jnp.transpose(hid_b[...].astype(f32))
+
+
+def widen(a, b, hid_a, hid_b, a_one, b_one):
+    out = lambda *s: jax.ShapeDtypeStruct(s, f32)
+    spec = pl.BlockSpec
+    return pl.pallas_call(
+        widen_kernel,
+        name="widen",
+        grid=(8,),
+        out_shape=[
+            out(4, 2048, 128), out(4, 128, 2048), out(2048, 128), out(128, 8192), out(8192, 128), out(128, 2048)
+        ],
+        in_specs=[
+            spec((4, 256, 128), lambda g: (0, g, 0)),
+            spec((256, 128), lambda g: (g, 0)),
+            spec((4, 1, 1, 4, 2, 2, 16, 128), lambda g: (0, g // 2, g % 2, 0, 0, 0, 0, 0)),
+            spec((128, 256), lambda g: (0, g)),
+            spec((1024, 128), lambda g: (g, 0)),
+            spec((1024, 128), lambda g: (g, 0)),
+        ],
+        out_specs=[
+            spec((4, 256, 128), lambda g: (0, g, 0)),
+            spec((4, 128, 256), lambda g: (0, 0, g)),
+            spec((256, 128), lambda g: (g, 0)),
+            spec((128, 1024), lambda g: (0, g)),
+            spec((1024, 128), lambda g: (g, 0)),
+            spec((128, 256), lambda g: (0, g)),
+        ],
+        compiler_params=pltpu.CompilerParams(vmem_limit_bytes=62 * MIB),
+    )(
+        a.reshape(4, 2048, 128), a_one.reshape(2048, 128), b, b_one.reshape(128, 2048), hid_a.reshape(8192, 128),
+        hid_b.reshape(8192, 128),
     )
 
 
@@ -1477,51 +1551,26 @@
     xl, c, z, y, xh = (lax.axis_index(a) for a in AXES)
     group = (xh * 2 + xl) * 2 + c
     cot = cotangent[0]
-    bias_rows = jnp.stack([projection_bias[0], jnp.zeros_like(projection_bias[0]), projection_bias[1]])
-
-    def my_columns(array):
-        return lax.dynamic_slice_in_dim(array, group * 256, 256, array.ndim - 1)
-
-    def my_hidden(array):
-        lead = array.shape[:-1]
-        part = lax.dynamic_slice_in_dim(array, (xl * 2 + c) * 2048, 2048, array.ndim - 1)
-        part = part.reshape(lead + (16, 2, 64))
-        return lax.dynamic_index_in_dim(part, xh, len(lead) + 1, False).reshape(lead + (1024,))
-
-    my_up_maps = my_columns(attention_up_maps[:3])
     (
         act_all, qkv_w, out_all, up_all, cot_all, by_head, across, merged, attended, lse, mask
     ) = front(
-        document_starts, document_adapter, tokens[0], layernorm_gain[:1], layernorm_bias[:1],
-        my_columns(bias_rows)[:, None, :], attention_down_maps, my_up_maps, cot, lower_up_maps,
-        jnp.transpose(projection_weight, (1, 0, 2)), output_weight, up_weight, scale,
+        document_starts, document_adapter, tokens[0], layernorm_gain, layernorm_bias, projection_bias, cot,
+        jnp.transpose(projection_weight, (1, 0, 2)), output_weight, up_weight, attention_up_maps, attention_down_maps,
+        lower_up_maps, scale,
     )
-    down_maps = lax.dynamic_slice_in_dim(lower_down_maps, (xl * 2 + c) * 2048, 2048, 0)
-    down_maps = lax.dynamic_index_in_dim(down_maps.reshape(16, 2, 64, 128), xh, 1, False).reshape(1024, 128)
     grad_merged, grad_residual, mixed, small, a_out, b_out, two, mine_in, mine_cot = feed_forward(
-        merged, tokens[0], layernorm_gain[1:], layernorm_bias[1:], projection_bias[2:3], projection_bias[3:4],
-        attention_down_maps[3], attention_up_maps[3], upper_down_maps, lower_up_maps, mask, my_hidden(upper_up_maps),
-        down_maps, my_hidden(upper_bias)[None], down_weight, cot,
-        out_all.reshape(width, width), cot_all, up_all.reshape(width, 1024),
+        merged, tokens[0], layernorm_gain, layernorm_bias, projection_bias, upper_down_maps, lower_up_maps, mask,
+        upper_bias[None], down_weight, cot, out_all.reshape(width, width), cot_all, up_all.reshape(width, 1024),
+        attention_down_maps, attention_up_maps, upper_up_maps, lower_down_maps.reshape(4, 16, 2, 64, 128),
     )
     grad_qkv, grad_adapt_qkv, a_piece, b_piece, two_piece = middle(
         document_starts, grad_merged, by_head, across, attended, lse, attention_up_maps, mask, a_out, b_out, two, scale
     )
-    input_grad, a_all, b_all, a_up, b_down, hidden_a, hidden_b = tail(
-        grad_qkv, qkv_w, act_all, attention_down_maps, grad_adapt_qkv,
-        small, tokens[0], layernorm_gain[:1], grad_residual,
+    input_grad, *sums = tail(
+        grad_qkv, qkv_w, act_all, attention_down_maps, grad_residual, grad_adapt_qkv, small, tokens[0], layernorm_gain,
         mine_in, mine_cot, a_piece, b_piece, two_piece,
     )
-    return (
-        mixed[None],
-        input_grad[None],
-        a_all.astype(f32),
-        b_all.astype(f32),
-        a_up.astype(f32),
-        jnp.transpose(hidden_b).astype(f32),
-        hidden_a.astype(f32),
-        b_down.astype(f32),
-    )
+    return (mixed[None], input_grad[None], *widen(*sums))
 
 
 def solution(mesh):

time: 434 us -> 404 us (0.931)
  local copies, waits for them, and re-layouts: 20.9 us -> 1.6 us
  other arithmetic: 13.8 us -> 0 us
  Pallas kernels: 392 us -> 397 us
    convert_element_type x6 -> x0, other arithmetic: 13.8 us -> none  [the longest x1 2.42 us: per_device(): hidden_a.astype(f32)]
    pallas_call x0 -> x1, Pallas kernels: none -> 11.4 us  [widen(): pl.pallas_call(widen_kernel, name='widen', grid=(8,), out_shape=[out(4, 2...]
    pallas_call x1, Pallas kernels: 75.2 us -> 66 us  [tail(): pl.pallas_call(tail_kernel, name='tail', out_shape=[shape(128, 2048), sha...]
    convert_element_type x1 -> x0, local copies, waits for them, and re-layouts: 5.74 us -> none  [per_device(): jnp.transpose(hidden_b).astype(f32)]
where the time goes in v6:
time: 404 us; the launch traced here: 399 us
  Pallas kernels  397 us (98%)
    pallas_call x1, Pallas kernels, front(): pl.pallas_call(functools.partial(front_kernel, scale=scale), name='front'...  146 us
    pallas_call x1, Pallas kernels, feed_forward(): pl.pallas_call(feed_forward_kernel, name='feed_forward', out_shape=[shape...  93 us
    pallas_call x1, Pallas kernels, middle(): pl.pallas_call(functools.partial(middle_kernel, scale=scale), name='atten...  80.5 us
    pallas_call x1, Pallas kernels, tail(): pl.pallas_call(tail_kernel, name='tail', out_shape=[shape(128, 2048), sha...  66 us
    pallas_call x1, Pallas kernels, widen(): pl.pallas_call(widen_kernel, name='widen', grid=(8,), out_shape=[out(4, 2...  11.4 us

profile of v6, /device:TPU:1, one launch (start us, length us, event | category | flops | bytes accessed | tf_op | source)
XLA Modules:
  0.0 399.4 jit_solution(15582811560493231244)
XLA Ops:
  0.6 145.8 %front.1 = (bf16[4,2,128,2432]{3,2,1,0:T(8,128)(2,1)}, bf16[3,256,2048]{2,1,0:T(8,128)(2,1)}, bf16[2,2,4,4,2,16,2048]{6,5,4,3,2,1,0:T(8,128)(2,1)}, bf16[2,2,4,4...) custom-call(s32[1,8]{1,0:T(1,128)} %starts.3, ...), custom_call_target="tpu_custom_call" | custom-call | tf_op jit(solution)/shard_map/front/pallas_call | solution.py:764
  146.4 93.0 %feed_forward.1 = (bf16[128,2048]{1,0:T(8,128)(2,1)}, f32[128,2048]{1,0:T(8,128)}, bf16[128,2048]{1,0:T(8,128)(2,1)}, bf16[128,256]{1,0:T(8,128)(2,1)}, bf16[204...) custom-call(bf16[128,2048]{1,0:T(8,128)(2,1)} %get-tuple-element.46., ...), custom_call_target="tpu_custom_call" | custom-call | tf_op jit(solution)/shard_map/feed_forward/pallas_call | solution.py:1239
  239.4 80.5 %attention_backward.1 = (bf16[3,4,2,2,128,128]{5,4,3,2,1,0:T(8,128)(2,1)}, bf16[128,384]{1,0:T(8,128)(2,1)}, bf16[16,128]{1,0:T(8,128)(2,1)}, bf16[16,128]{1,0:T(8,128)(2,1)}, bf16[2,64,128]{2,1,0:T(8,128)(2,1)}) custom-call(s32[1,8]{1,0:T(1,128)} %starts.3, bf16[128,2048]{1,0:T(8,128)(2,1)} %get-tuple-element.52.grad, ...), custom_call_target="tpu_custom_call" | custom-call | tf_op jit(solution)/shard_map/attention_backward/pallas_call | solution.py:986
  320.0 66.0 %tail.1 = (bf16[128,2048]{1,0:T(8,128)(2,1)}, bf16[4,4,2,4,4,16,128]{6,5,4,3,2,1,0:T(8,128)(2,1)}, bf16[4,4,2,4,2,2,16,128]{7,6,5,4,3,2,1,0:T(8,128)(2,1)}, bf16...) custom-call(bf16[3,4,2,2,128,128]{5,4,3,2,1,0:T(8,128)(2,1)} %get-tu, ...), custom_call_target="tpu_custom_call" | custom-call | tf_op jit(solution)/shard_map/tail/pallas_call | solution.py:1442
  386.0 0.0 copy-start
  386.0 0.0 copy-start.1
  386.0 11.4 %widen.1 = (f32[4,2048,128]{2,1,0:T(8,128)}, f32[4,128,2048]{2,1,0:T(8,128)}, f32[2048,128]{1,0:T(8,128)}, f32[128,8192]{1,0:T(8,128)}, f32[8192,128]{1,0:T(8,128)}, /*index=5*/f32[128,2048]{1,0:T(8,128)}) custom-call(bf16[4,2048,128]{2,1,0:T(8,128)(2,1)} %bitcast.20, bf16[2048,128]{1,0:T(8,128)(2,1)} %bitcast.26, ...), custom_call_target="tpu_custom_call" | custom-call | tf_op jit(solution)/shard_map/widen/pallas_call | solution.py:1497
  397.4 0.0 copy-done
  397.4 0.8 copy.28
  398.2 0.0 copy-done.1
  398.2 0.8 copy.29
Async XLA Ops:
  386.0 11.4 %copy-start = (bf16[128,2048]{1,0:T(8,128)(2,1)S(1)}, bf16[128,2048]{1,0:T(8,128)(2,1)}, u32[]{:S(2)}) copy-start(bf16[128,2048]{1,0:T(8,128)(2,1)} %get-tuple-element.51) | copy-start | bytes 1572868
  386.0 12.2 %copy-start.1 = (bf16[128,2048]{1,0:T(8,128)(2,1)S(1)}, bf16[128,2048]{1,0:T(8,128)(2,1)}, u32[]{:S(2)}) copy-start(bf16[128,2048]{1,0:T(8,128)(2,1)} %get-tuple-element.71) | copy-start | bytes 1572868

commit v7 on v6

--- a/solution.py
+++ b/solution.py
@@ -1020,11 +1020,10 @@
 def feed_forward_kernel(
     merged, tok, gains, shifts, biases, up_down, low_up, mask, bias_all, dn, cot_own,
     w_out_in, cot_all, up, out_down_in, out_up_in, umap_in, dmap_in,
-    grad_merged, grad_res, mixed, small_out, a_out, b_out, two, mine_in, mine_cot,
+    grad_merged, grad_res, base, forth, small_out, a_out, b_out, two, mine_in, mine_cot,
     out_down, out_up, umap_all, umap, dmap, bias, w_out, residual, low_out, sa, cot, up_v, dn_v, slope, act, pre, parts, total, *refs,
 ):
     scratch, (send, recv, local) = refs[:-3], refs[-3:]
-    scratch, forth_scratch = scratch[:6], scratch[6:]
     place = Place()
     greet(members(place) + plane_devices(place))
     sends = Sends(send, recv)
@@ -1196,11 +1195,8 @@
     lax.fori_loop(0, 8, forward, 0)
 
     two[...] = total[...].astype(bf16)
-    forth = GroupSum(place, sends, cot.at[:, :, :, pl.ds(0, 2048)], forth_scratch)
-    for k in range(4):
-        forth.cross(k)
-    forth.merge(0)
-    forth.first()
+    handed = pltpu.make_async_copy(cot.at[:, :, :, pl.ds(0, 2048)], forth, local.at[7])
+    handed.start()
     summed = sums.result()
     low_up_grad = (summed[:, 2048:2176] * mask[...]).astype(bf16)
     low_down = (summed[:, 2176:2304] * mask[...]).astype(bf16)
@@ -1218,15 +1214,11 @@
         grad_merged[:, cols] = value.astype(bf16)
         return 0
 
-    lax.fori_loop(0, 4, merged_tile, 0)
-    forth.merge(1)
-    forth.merge(2)
-    forth.second()
-    lax.fori_loop(4, 8, merged_tile, 0)
+    lax.fori_loop(0, 8, merged_tile, 0)
     b_out[...] = dot_tn(low_out[...], branch).astype(bf16)
     a_out[...] = dot_tn(merged[...], low_grad).astype(bf16)
-    value = residual[...] + bias_end + dot(low_down, low_up[...])
-    mixed[...] = (value + forth.result()).astype(bf16)
+    base[...] = residual[...] + bias_end + dot(low_down, low_up[...])
+    handed.wait()
     gather.finish()
     assert sends.used <= send.shape[0], sends.used
 
@@ -1242,7 +1234,8 @@
         out_shape=[
             shape(128, 2048),
             jax.ShapeDtypeStruct((128, 2048), f32),
-            shape(128, 2048),
+            jax.ShapeDtypeStruct((128, 2048), f32),
+            shape(4, 2, 128, 2048),
             shape(128, 256),
             shape(2048, 128),
             shape(128, 2048),
@@ -1251,7 +1244,7 @@
             shape(1024, 256),
         ],
         in_specs=[vmem] * 11 + [any_] * 7,
-        out_specs=[vmem] * 9,
+        out_specs=[vmem] * 3 + [any_] + [vmem] * 6,
         scratch_shapes=[
             vm(2048, 128),
             vm(128, 2048),
@@ -1273,8 +1266,7 @@
             pltpu.VMEM((2, 1024, 128), f32),
         ]
         + GroupSum.scratch(2304)
-        + GroupSum.scratch(2048)
-        + [pltpu.SemaphoreType.DMA((k,)) for k in (40, 40, 7)],
+        + [pltpu.SemaphoreType.DMA((k,)) for k in (40, 40, 8)],
         compiler_params=pltpu.CompilerParams(collective_id=1, has_side_effects=True, vmem_limit_bytes=63 * MIB),
     )(*args)
 
@@ -1285,11 +1277,12 @@
 
 
 def tail_kernel(
-    grads, qkv_w, act_all, dmaps_in, grad_res_in, low_rank, small, tok, gain, mine_in, mine_cot, a_piece, b_piece, two_piece,
-    input_grad, a_res, b_res, two_a, two_b, a_early, b_early,
-    dmaps, grad_res, gq, wq, act, left, parts, lows, a_sums, b_sums, a_s, a_f, b_s, b_f, *refs,
+    grads, qkv_w, act_all, dmaps_in, grad_res_in, forth_in, base_in, low_rank, small, tok, gain, mine_in, mine_cot, a_piece, b_piece, two_piece,
+    input_grad, mixed, a_res, b_res, two_a, two_b, a_early, b_early,
+    dmaps, grad_res, forth_parts, base, gq, wq, act, left, parts, lows, a_sums, b_sums, a_s, a_f, b_s, b_f, *refs,
 ):
     scratch, (send, recv, local) = refs[:-3], refs[-3:]
+    scratch, forth_scratch = scratch[:6], scratch[6:]
     place = Place()
     greet(members(place) + plane_devices(place))
     sends = Sends(send, recv)
@@ -1299,6 +1292,8 @@
     ]
     loads.append(pltpu.make_async_copy(dmaps_in.at[pl.ds(0, 3)], dmaps, local.at[44]))
     loads.append(pltpu.make_async_copy(grad_res_in, grad_res, local.at[45]))
+    loads.append(pltpu.make_async_copy(forth_in, forth_parts, local.at[43]))
+    loads.append(pltpu.make_async_copy(base_in, base, local.at[42]))
     for copy in loads:
         copy.start()
     own = lows.at[place.x, place.c]
@@ -1363,8 +1358,8 @@
         yield from give_all(place, sends, order, final, view, sem, True)
 
     late = [
-        late_part(a_f, a_held, a_s, ("z", "y", "x"), a_view, local.at[7]),
-        late_part(b_f, b_held, b_s, ("y", "x", "z"), b_view, local.at[8]),
+        late_part(a_f, a_held, a_s, ("y", "x", "z"), a_view, local.at[7]),
+        late_part(b_f, b_held, b_s, ("z", "x", "y"), b_view, local.at[8]),
     ]
     loads[0].wait()
     loads[1].wait()
@@ -1390,11 +1385,10 @@
     sums.cross(1)
     sums.merge(0)
     sums.first()
-    tick(*early)
-    partial(2, 2)
-    sums.cross(2)
-    sums.cross(3)
-    tick(*early)
+    loads[5].wait()
+    forth = GroupSum(place, sends, forth_parts, forth_scratch)
+    for k in range(4):
+        forth.cross(k)
     loads[2].wait()
     for p in range(3):
         total = jnp.zeros((128, 256), f32)
@@ -1415,12 +1409,22 @@
         a_sums[p] = dot_tn(rows if p < 3 else mine_in[...], right).astype(bf16)
 
     tick(*late)
+    partial(2, 2)
+    sums.cross(2)
+    sums.cross(3)
+    forth.merge(0)
+    forth.first()
+    tick(*early)
     sums.merge(1)
     sums.merge(2)
     sums.second()
     tick(*late)
     tick(*early)
     tick(*late)
+    forth.merge(1)
+    forth.merge(2)
+    forth.second()
+    tick(*early)
     loads[3].wait()
     loads[4].wait()
     grad_first = sums.result()
@@ -1429,11 +1433,14 @@
     result = grad_res[...] + layer_norm_back(tok[...].astype(f32), gain[0:1, :], grad_first)
     input_grad[...] = result.astype(bf16)
     tick(*late)
-    run_all(early + late)
+    tick(*early)
+    run_all(late + early)
+    loads[6].wait()
+    mixed[...] = (base[...] + forth.result()).astype(bf16)
     assert sends.used <= send.shape[0], sends.used
 
 
-def tail(grads, qkv_w, act_all, dmaps, grad_res, low_rank, small, tok, gain, mine_in, mine_cot, a_piece, b_piece, two_piece):
+def tail(grads, qkv_w, act_all, dmaps, grad_res, forth, base, low_rank, small, tok, gain, mine_in, mine_cot, a_piece, b_piece, two_piece):
     any_ = pl.BlockSpec(memory_space=pl.ANY)
     vmem = pl.BlockSpec(memory_space=pltpu.VMEM)
     vm = lambda *s: pltpu.VMEM(s, bf16)
@@ -1444,6 +1451,7 @@
         name="tail",
         out_shape=[
             shape(128, 2048),
+            shape(128, 2048),
             shape(*a_shape),
             shape(*b_shape),
             shape(2, 2, 4, 4, 2, 64, 128),
@@ -1451,10 +1459,12 @@
             shape(2, 4, 4, 4, 16, 128),
             shape(2, 4, 16, 2048),
         ],
-        in_specs=[any_] * 5 + [vmem] * 9,
-        out_specs=[vmem] + [any_] * 6,
+        in_specs=[any_] * 7 + [vmem] * 9,
+        out_specs=[vmem] * 2 + [any_] * 6,
         scratch_shapes=[
             vm(3, 2048, 128),
+            pltpu.VMEM((128, 2048), f32),
+            vm(4, 2, 128, 2048),
             pltpu.VMEM((128, 2048), f32),
             vm(3, 4, 2, 2, 128, 128),
             vm(3, 256, 2048),
@@ -1469,11 +1479,11 @@
             vm(15, 4, 16, 128),
             vm(4, 16, 128),
         ]
-        + GroupSum.scratch(2048)
+        + GroupSum.scratch(2048) * 2
         + [pltpu.SemaphoreType.DMA((k,)) for k in (200, 200, 46)],
         compiler_params=pltpu.CompilerParams(collective_id=3, has_side_effects=True, vmem_limit_bytes=60 * MIB),
     )(
-        grads, qkv_w, act_all, dmaps, grad_res, low_rank, small, tok, gain, mine_in, mine_cot, a_piece, b_piece, two_piece
+        grads, qkv_w, act_all, dmaps, grad_res, forth, base, low_rank, small, tok, gain, mine_in, mine_cot, a_piece, b_piece, two_piece
     )
 def widen_kernel(a, a_one, b, b_one, hid_a, hid_b, a_out, b_out, up_out, hid_b_out, hid_a_out, down_out):
     for n in range(3):
@@ -1558,7 +1568,7 @@
         jnp.transpose(projection_weight, (1, 0, 2)), output_weight, up_weight, attention_up_maps, attention_down_maps,
         lower_up_maps, scale,
     )
-    grad_merged, grad_residual, mixed, small, a_out, b_out, two, mine_in, mine_cot = feed_forward(
+    grad_merged, grad_residual, base, forth, small, a_out, b_out, two, mine_in, mine_cot = feed_forward(
         merged, tokens[0], layernorm_gain, layernorm_bias, projection_bias, upper_down_maps, lower_up_maps, mask,
         upper_bias[None], down_weight, cot, out_all.reshape(width, width), cot_all, up_all.reshape(width, 1024),
         attention_down_maps, attention_up_maps, upper_up_maps, lower_down_maps.reshape(4, 16, 2, 64, 128),
@@ -1566,8 +1576,8 @@
     grad_qkv, grad_adapt_qkv, a_piece, b_piece, two_piece = middle(
         document_starts, grad_merged, by_head, across, attended, lse, attention_up_maps, mask, a_out, b_out, two, scale
     )
-    input_grad, *sums = tail(
-        grad_qkv, qkv_w, act_all, attention_down_maps, grad_residual, grad_adapt_qkv, small, tokens[0], layernorm_gain,
+    input_grad, mixed, *sums = tail(
+        grad_qkv, qkv_w, act_all, attention_down_maps, grad_residual, forth, base, grad_adapt_qkv, small, tokens[0], layernorm_gain,
         mine_in, mine_cot, a_piece, b_piece, two_piece,
     )
     return (mixed[None], input_grad[None], *widen(*sums))

time: 404 us -> 393 us (0.973)
  Pallas kernels: 397 us -> 385 us
    pallas_call x1, Pallas kernels: 93 us -> 80.9 us  [feed_forward(): pl.pallas_call(feed_forward_kernel, name='feed_forward', out_shape=[shape...]
where the time goes in v7:
time: 393 us; the launch traced here: 388 us
  Pallas kernels  385 us (98%)
    pallas_call x1, Pallas kernels, front(): pl.pallas_call(functools.partial(front_kernel, scale=scale), name='front'...  146 us
    pallas_call x1, Pallas kernels, feed_forward(): pl.pallas_call(feed_forward_kernel, name='feed_forward', out_shape=[shape...  80.9 us
    pallas_call x1, Pallas kernels, middle(): pl.pallas_call(functools.partial(middle_kernel, scale=scale), name='atten...  78.6 us
    pallas_call x1, Pallas kernels, tail(): pl.pallas_call(tail_kernel, name='tail', out_shape=[shape(128, 2048), sha...  68.5 us
    pallas_call x1, Pallas kernels, widen(): pl.pallas_call(widen_kernel, name='widen', grid=(8,), out_shape=[out(4, 2...  11.4 us

profile of v7, /device:TPU:1, one launch (start us, length us, event | category | flops | bytes accessed | tf_op | source)
XLA Modules:
  0.0 387.8 jit_solution(14027788464776977571)
XLA Ops:
  0.6 145.7 %front.1 = (bf16[4,2,128,2432]{3,2,1,0:T(8,128)(2,1)}, bf16[3,256,2048]{2,1,0:T(8,128)(2,1)}, bf16[2,2,4,4,2,16,2048]{6,5,4,3,2,1,0:T(8,128)(2,1)}, bf16[2,2,4,4...) custom-call(s32[1,8]{1,0:T(1,128)} %starts.3, ...), custom_call_target="tpu_custom_call" | custom-call | tf_op jit(solution)/shard_map/front/pallas_call | solution.py:764
  146.4 80.9 %feed_forward.1 = (bf16[128,2048]{1,0:T(8,128)(2,1)}, f32[128,2048]{1,0:T(8,128)}, f32[128,2048]{1,0:T(8,128)}, bf16[4,2,128,2048]{3,2,1,0:T(8,128)(2,1)}, bf16[...) custom-call(bf16[128,2048]{1,0:T(8,128)(2,1)} %get-tuple-element.48., ...), custom_call_target="tpu_custom_call" | custom-call | tf_op jit(solution)/shard_map/feed_forward/pallas_call | solution.py:1231
  227.3 78.6 %attention_backward.1 = (bf16[3,4,2,2,128,128]{5,4,3,2,1,0:T(8,128)(2,1)}, bf16[128,384]{1,0:T(8,128)(2,1)}, bf16[16,128]{1,0:T(8,128)(2,1)}, bf16[16,128]{1,0:T(8,128)(2,1)}, bf16[2,64,128]{2,1,0:T(8,128)(2,1)}) custom-call(s32[1,8]{1,0:T(1,128)} %starts.3, bf16[128,2048]{1,0:T(8,128)(2,1)} %get-tuple-element.53.grad, ...), custom_call_target="tpu_custom_call" | custom-call | tf_op jit(solution)/shard_map/attention_backward/pallas_call | solution.py:986
  305.8 68.5 %tail.1 = (bf16[128,2048]{1,0:T(8,128)(2,1)}, bf16[128,2048]{1,0:T(8,128)(2,1)}, bf16[4,4,2,4,4,16,128]{6,5,4,3,2,1,0:T(8,128)(2,1)}, bf16[4,4,2,4,2,2,16,128]{7...) custom-call(bf16[3,4,2,2,128,128]{5,4,3,2,1,0:T(8,128)(2,1)} %get-tu, ...), custom_call_target="tpu_custom_call" | custom-call | tf_op jit(solution)/shard_map/tail/pallas_call | solution.py:1449
  374.4 0.0 copy-start.1
  374.4 0.0 copy-start
  374.4 11.4 %widen.1 = (f32[4,2048,128]{2,1,0:T(8,128)}, f32[4,128,2048]{2,1,0:T(8,128)}, f32[2048,128]{1,0:T(8,128)}, f32[128,8192]{1,0:T(8,128)}, f32[8192,128]{1,0:T(8,128)}, /*index=5*/f32[128,2048]{1,0:T(8,128)}) custom-call(bf16[4,2048,128]{2,1,0:T(8,128)(2,1)} %bitcast.20, bf16[2048,128]{1,0:T(8,128)(2,1)} %bitcast.26, ...), custom_call_target="tpu_custom_call" | custom-call | tf_op jit(solution)/shard_map/widen/pallas_call | solution.py:1507
  385.8 0.0 copy-done.1
  385.8 0.8 copy.28
  386.6 0.0 copy-done
  386.6 0.8 copy.29
Async XLA Ops:
  374.4 11.4 %copy-start.1 = (bf16[128,2048]{1,0:T(8,128)(2,1)S(1)}, bf16[128,2048]{1,0:T(8,128)(2,1)}, u32[]{:S(2)}) copy-start(bf16[128,2048]{1,0:T(8,128)(2,1)} %get-tuple-element.74) | copy-start | bytes 1572868
  374.4 12.2 %copy-start = (bf16[128,2048]{1,0:T(8,128)(2,1)S(1)}, bf16[128,2048]{1,0:T(8,128)(2,1)}, u32[]{:S(2)}) copy-start(bf16[128,2048]{1,0:T(8,128)(2,1)} %get-tuple-element.75) | copy-start | bytes 1572868

commit v8 on v7

--- a/solution.py
+++ b/solution.py
@@ -879,20 +879,25 @@
         sides = ((others[0, rows, :], others[1, rows, :], 1 - parity), (queries[1, rows, :], queries[2, rows, :], parity))
         local = kt * K_TILE + lax.broadcasted_iota(jnp.int32, (K_TILE, 1), 0)
 
-        def step(qt, carry):
-            rows = piece(qt, Q_TILE)
+        def step(qt, carry, diagonal):
+            rows = piece(qt, K_TILE)
             q = queries[0, rows, :]
             d = do[rows, :]
-            q_pos = positions_of(qt * Q_TILE + lax.broadcasted_iota(jnp.int32, (1, Q_TILE), 1), parity)
+            q_pos = positions_of(qt * K_TILE + lax.broadcasted_iota(jnp.int32, (1, K_TILE), 1), parity)
+            both = [qt * 2, qt * 2 + 1]
+            lse_row = jnp.concatenate([lse[pl.ds(n, 1), :] for n in both], axis=1)
+            delta_row = jnp.concatenate([delta[n, 0:1, :] for n in both], axis=1)
             lo = document_start(starts, q_pos)
             found, dq_part = [], None
             for (k, v, k_parity), (dk, dv) in zip(sides, carry):
                 k_pos = positions_of(local, k_parity)
                 s = dot_nt(k, q)
-                allowed = (k_pos >= lo) & (k_pos <= q_pos)
-                p = jnp.exp2(jnp.where(allowed, s * (scale * LOG2E) - lse[pl.ds(qt, 1), :], -1e30))
+                allowed = k_pos >= lo
+                if diagonal:
+                    allowed = allowed & (k_pos <= q_pos)
+                p = jnp.exp2(jnp.where(allowed, s * (scale * LOG2E) - lse_row, -1e30))
                 dv = dv + dot(p.astype(bf16), d)
-                ds = (p * (dot_nt(v, d) - delta[qt, 0:1, :]) * scale).astype(bf16)
+                ds = (p * (dot_nt(v, d) - delta_row)).astype(bf16)
                 dk = dk + dot(ds, q)
                 part = dot_tn(ds, k)
                 dq_part = part if dq_part is None else dq_part + part
@@ -901,7 +906,9 @@
             return tuple(found)
 
         zero = jnp.zeros((K_TILE, 128), f32)
-        return lax.fori_loop(kt * (K_TILE // Q_TILE), tiles, step, ((zero, zero),) * 2)
+        carry = step(kt, ((zero, zero),) * 2, True)
+        carry = lax.fori_loop(kt + 1, key_tiles, lambda qt, c: step(qt, c, False), carry)
+        return [(dk * scale, dv) for dk, dv in carry]
 
     blocks = K_TILE // 128
     gone = []
@@ -954,7 +961,7 @@
                 dst = from_other.at[:, here] if k == 2 else by_head.at[kv, here]
                 to_token(k, n, low.at[n], dst, k == 2, turn != 0)
     for n in range(16):
-        dq[n] = dq_acc[n * 128 : (n + 1) * 128].astype(bf16)
+        dq[n] = (dq_acc[n * 128 : (n + 1) * 128] * scale).astype(bf16)
     for turn in (2, 1, 3, 0):
         for b in range(blocks):
             n = lax.rem(place.z + turn, 4) * 4 + b
@@ -1071,15 +1078,12 @@
         residual[:, cols] = value + dot(low_out[...], out_up[:, cols])
         return 0
 
-    lax.fori_loop(0, 6, out_tile, 0)
-    tick(*dn_gathers)
-    lax.fori_loop(6, 8, out_tile, 0)
+    lax.fori_loop(0, 8, out_tile, 0)
     second = layer_norm(residual[...], gain, shift).astype(bf16)
     own = sa.at[place.x, place.c]
     own[:, 0:2048] = second
     own[:, 2048:2176] = (dot(second, up_down[...]) * mask[...]).astype(bf16)
     gather = GroupGather(place, sends, sa)
-
     loads[3].wait()
     loads[4].wait()
     whole_bias = bias_all[:, piece(place.xl * 2 + place.c, 2048)]
@@ -1087,6 +1091,7 @@
         for whole, out in ((umap_all[:, n * 256 : n * 256 + 256], umap), (whole_bias[:, n * 256 : n * 256 + 256], bias)):
             sides = [jnp.concatenate([whole[:, h : h + 64], whole[:, 128 + h : 192 + h]], axis=1) for h in (0, 64)]
             out[:, n * 128 : n * 128 + 128] = jnp.where(place.xh == 0, sides[0], sides[1])
+    tick(*dn_gathers)
 
     def rows(ref, x, start, size):
         return ref[x, :, :, pl.ds(start, size)].reshape(256, size)
@@ -1487,18 +1492,20 @@
     )
 def widen_kernel(a, a_one, b, b_one, hid_a, hid_b, a_out, b_out, up_out, hid_b_out, hid_a_out, down_out):
     for n in range(3):
-        a_out[n] = a[n].reshape(256, 128).astype(f32)
+        a_out[n] = a[n].astype(f32)
+    a_out[3] = a_one[...].astype(f32)
+    up_out[...] = a[3].astype(f32)
+    for c in range(2):
         for yc in range(2):
-            cols = pl.ds(yc * 128, 128)
-            b_out[n, :, cols] = b[n, 0, 0, :, :, yc].reshape(128, 128).astype(f32)
-    for yc in range(2):
-        cols = pl.ds(yc * 128, 128)
-        down_out[:, cols] = b[3, 0, 0, :, :, yc].reshape(128, 128).astype(f32)
-    a_out[3] = a_one[...].astype(f32)
-    up_out[...] = a[3].reshape(256, 128).astype(f32)
+            cols = pl.ds(c * 256 + yc * 128, 128)
+            for n in range(3):
+                b_out[n, :, cols] = b[n, 0, c, :, :, yc].reshape(128, 128).astype(f32)
+            down_out[:, cols] = b[3, 0, c, :, :, yc].reshape(128, 128).astype(f32)
     b_out[3] = b_one[...].astype(f32)
     hid_a_out[...] = hid_a[...].astype(f32)
-    hid_b_out[...] = jnp.transpose(hid_b[...].astype(f32))
+    for n in range(4):
+        rows = pl.ds(n * 512, 512)
+        hid_b_out[:, rows] = jnp.transpose(hid_b[rows, :].astype(f32))
 
 
 def widen(a, b, hid_a, hid_b, a_one, b_one):
@@ -1507,25 +1514,25 @@
     return pl.pallas_call(
         widen_kernel,
         name="widen",
-        grid=(8,),
+        grid=(4,),
         out_shape=[
             out(4, 2048, 128), out(4, 128, 2048), out(2048, 128), out(128, 8192), out(8192, 128), out(128, 2048)
         ],
         in_specs=[
-            spec((4, 256, 128), lambda g: (0, g, 0)),
-            spec((256, 128), lambda g: (g, 0)),
-            spec((4, 1, 1, 4, 2, 2, 16, 128), lambda g: (0, g // 2, g % 2, 0, 0, 0, 0, 0)),
-            spec((128, 256), lambda g: (0, g)),
-            spec((1024, 128), lambda g: (g, 0)),
-            spec((1024, 128), lambda g: (g, 0)),
+            spec((4, 512, 128), lambda g: (0, g, 0)),
+            spec((512, 128), lambda g: (g, 0)),
+            spec((4, 1, 2, 4, 2, 2, 16, 128), lambda g: (0, g, 0, 0, 0, 0, 0, 0)),
+            spec((128, 512), lambda g: (0, g)),
+            spec((2048, 128), lambda g: (g, 0)),
+            spec((2048, 128), lambda g: (g, 0)),
         ],
         out_specs=[
-            spec((4, 256, 128), lambda g: (0, g, 0)),
-            spec((4, 128, 256), lambda g: (0, 0, g)),
-            spec((256, 128), lambda g: (g, 0)),
-            spec((128, 1024), lambda g: (0, g)),
-            spec((1024, 128), lambda g: (g, 0)),
-            spec((128, 256), lambda g: (0, g)),
+            spec((4, 512, 128), lambda g: (0, g, 0)),
+            spec((4, 128, 512), lambda g: (0, 0, g)),
+            spec((512, 128), lambda g: (g, 0)),
+            spec((128, 2048), lambda g: (0, g)),
+            spec((2048, 128), lambda g: (g, 0)),
+            spec((128, 512), lambda g: (0, g)),
         ],
         compiler_params=pltpu.CompilerParams(vmem_limit_bytes=62 * MIB),
     )(

time: 393 us -> 390 us (level)
  no operation moved by 1% of the time
where the time goes in v8:
time: 390 us; the launch traced here: 385 us
  Pallas kernels  382 us (98%)
    pallas_call x1, Pallas kernels, front(): pl.pallas_call(functools.partial(front_kernel, scale=scale), name='front'...  146 us
    pallas_call x1, Pallas kernels, feed_forward(): pl.pallas_call(feed_forward_kernel, name='feed_forward', out_shape=[shape...  79.4 us
    pallas_call x1, Pallas kernels, middle(): pl.pallas_call(functools.partial(middle_kernel, scale=scale), name='atten...  77.8 us
    pallas_call x1, Pallas kernels, tail(): pl.pallas_call(tail_kernel, name='tail', out_shape=[shape(128, 2048), sha...  68.5 us
    pallas_call x1, Pallas kernels, widen(): pl.pallas_call(widen_kernel, name='widen', grid=(4,), out_shape=[out(4, 2...  10.6 us

profile of v8, /device:TPU:1, one launch (start us, length us, event | category | flops | bytes accessed | tf_op | source)
XLA Modules:
  0.0 385.0 jit_solution(1905810759918533011)
XLA Ops:
  0.6 146.0 %front.1 = (bf16[4,2,128,2432]{3,2,1,0:T(8,128)(2,1)}, bf16[3,256,2048]{2,1,0:T(8,128)(2,1)}, bf16[2,2,4,4,2,16,2048]{6,5,4,3,2,1,0:T(8,128)(2,1)}, bf16[2,2,4,4...) custom-call(s32[1,8]{1,0:T(1,128)} %starts.3, ...), custom_call_target="tpu_custom_call" | custom-call | tf_op jit(solution)/shard_map/front/pallas_call | solution.py:764
  146.6 79.4 %feed_forward.1 = (bf16[128,2048]{1,0:T(8,128)(2,1)}, f32[128,2048]{1,0:T(8,128)}, f32[128,2048]{1,0:T(8,128)}, bf16[4,2,128,2048]{3,2,1,0:T(8,128)(2,1)}, bf16[...) custom-call(bf16[128,2048]{1,0:T(8,128)(2,1)} %get-tuple-element.48., ...), custom_call_target="tpu_custom_call" | custom-call | tf_op jit(solution)/shard_map/feed_forward/pallas_call | solution.py:1236
  226.0 77.8 %attention_backward.1 = (bf16[3,4,2,2,128,128]{5,4,3,2,1,0:T(8,128)(2,1)}, bf16[128,384]{1,0:T(8,128)(2,1)}, bf16[16,128]{1,0:T(8,128)(2,1)}, bf16[16,128]{1,0:T(8,128)(2,1)}, bf16[2,64,128]{2,1,0:T(8,128)(2,1)}) custom-call(s32[1,8]{1,0:T(1,128)} %starts.3, bf16[128,2048]{1,0:T(8,128)(2,1)} %get-tuple-element.53.grad, ...), custom_call_target="tpu_custom_call" | custom-call | tf_op jit(solution)/shard_map/attention_backward/pallas_call | solution.py:993
  303.8 68.5 %tail.1 = (bf16[128,2048]{1,0:T(8,128)(2,1)}, bf16[128,2048]{1,0:T(8,128)(2,1)}, bf16[4,4,2,4,4,16,128]{6,5,4,3,2,1,0:T(8,128)(2,1)}, bf16[4,4,2,4,2,2,16,128]{7...) custom-call(bf16[3,4,2,2,128,128]{5,4,3,2,1,0:T(8,128)(2,1)} %get-tu, ...), custom_call_target="tpu_custom_call" | custom-call | tf_op jit(solution)/shard_map/tail/pallas_call | solution.py:1454
  372.3 0.0 copy-start.1
  372.3 0.0 copy-start
  372.3 10.6 %widen.1 = (f32[4,2048,128]{2,1,0:T(8,128)}, f32[4,128,2048]{2,1,0:T(8,128)}, f32[2048,128]{1,0:T(8,128)}, f32[128,8192]{1,0:T(8,128)}, f32[8192,128]{1,0:T(8,128)}, /*index=5*/f32[128,2048]{1,0:T(8,128)}) custom-call(bf16[4,2048,128]{2,1,0:T(8,128)(2,1)} %bitcast.20, bf16[2048,128]{1,0:T(8,128)(2,1)} %bitcast.26, ...), custom_call_target="tpu_custom_call" | custom-call | tf_op jit(solution)/shard_map/widen/pallas_call | solution.py:1514
  382.9 0.0 copy-done.1
  382.9 0.8 copy.28
  383.7 0.0 copy-done
  383.7 0.8 copy.29
Async XLA Ops:
  372.3 10.6 %copy-start.1 = (bf16[128,2048]{1,0:T(8,128)(2,1)S(1)}, bf16[128,2048]{1,0:T(8,128)(2,1)}, u32[]{:S(2)}) copy-start(bf16[128,2048]{1,0:T(8,128)(2,1)} %get-tuple-element.74) | copy-start | bytes 1572868
  372.3 11.4 %copy-start = (bf16[128,2048]{1,0:T(8,128)(2,1)S(1)}, bf16[128,2048]{1,0:T(8,128)(2,1)}, u32[]{:S(2)}) copy-start(bf16[128,2048]{1,0:T(8,128)(2,1)} %get-tuple-element.75) | copy-start | bytes 1572868

commit v9 on v8

--- a/solution.py
+++ b/solution.py
@@ -736,14 +736,12 @@
         return 0
 
     tiles = mine.shape[1] // F_TILE
-    lax.fori_loop(0, tiles // 2, tile, 0)
-    tick(*up_gathers, *out_gathers)
-    lax.fori_loop(tiles // 2, tiles * 3 // 4, tile, 0)
-    tick(cot_gather, *out_gathers)
-    kept += keep_cot(11, (0, 1, 3))
-    lax.fori_loop(tiles * 3 // 4, tiles, tile, 0)
+    lax.fori_loop(0, tiles, tile, 0)
     back = heads_out(place, sends, low, merged, local.at[9])
     tick(back)
+    tick(cot_gather, *up_gathers, *out_gathers)
+    kept += keep_cot(11, (0, 1, 3))
+    tick(*out_gathers)
     for copy in posts:
         copy.wait_send()
     for copy in kept:

time: 390 us -> 384 us (0.985)
  Pallas kernels: 382 us -> 376 us
    pallas_call x1, Pallas kernels: 146 us -> 137 us  [front(): pl.pallas_call(functools.partial(front_kernel, scale=scale), name='front'...]
where the time goes in v9:
time: 384 us; the launch traced here: 379 us
  Pallas kernels  376 us (98%)
    pallas_call x1, Pallas kernels, front(): pl.pallas_call(functools.partial(front_kernel, scale=scale), name='front'...  137 us
    pallas_call x1, Pallas kernels, feed_forward(): pl.pallas_call(feed_forward_kernel, name='feed_forward', out_shape=[shape...  81.5 us
    pallas_call x1, Pallas kernels, middle(): pl.pallas_call(functools.partial(middle_kernel, scale=scale), name='atten...  78.5 us
    pallas_call x1, Pallas kernels, tail(): pl.pallas_call(tail_kernel, name='tail', out_shape=[shape(128, 2048), sha...  68.6 us
    pallas_call x1, Pallas kernels, widen(): pl.pallas_call(widen_kernel, name='widen', grid=(4,), out_shape=[out(4, 2...  10.6 us

profile of v9, /device:TPU:1, one launch (start us, length us, event | category | flops | bytes accessed | tf_op | source)
XLA Modules:
  0.0 378.6 jit_solution(16867131928351857304)
XLA Ops:
  0.6 136.9 %front.1 = (bf16[4,2,128,2432]{3,2,1,0:T(8,128)(2,1)}, bf16[3,256,2048]{2,1,0:T(8,128)(2,1)}, bf16[2,2,4,4,2,16,2048]{6,5,4,3,2,1,0:T(8,128)(2,1)}, bf16[2,2,4,4...) custom-call(s32[1,8]{1,0:T(1,128)} %starts.3, ...), custom_call_target="tpu_custom_call" | custom-call | tf_op jit(solution)/shard_map/front/pallas_call | solution.py:762
  137.5 81.5 %feed_forward.1 = (bf16[128,2048]{1,0:T(8,128)(2,1)}, f32[128,2048]{1,0:T(8,128)}, f32[128,2048]{1,0:T(8,128)}, bf16[4,2,128,2048]{3,2,1,0:T(8,128)(2,1)}, bf16[...) custom-call(bf16[128,2048]{1,0:T(8,128)(2,1)} %get-tuple-element.48., ...), custom_call_target="tpu_custom_call" | custom-call | tf_op jit(solution)/shard_map/feed_forward/pallas_call | solution.py:1234
  219.1 78.5 %attention_backward.1 = (bf16[3,4,2,2,128,128]{5,4,3,2,1,0:T(8,128)(2,1)}, bf16[128,384]{1,0:T(8,128)(2,1)}, bf16[16,128]{1,0:T(8,128)(2,1)}, bf16[16,128]{1,0:T(8,128)(2,1)}, bf16[2,64,128]{2,1,0:T(8,128)(2,1)}) custom-call(s32[1,8]{1,0:T(1,128)} %starts.3, bf16[128,2048]{1,0:T(8,128)(2,1)} %get-tuple-element.53.grad, ...), custom_call_target="tpu_custom_call" | custom-call | tf_op jit(solution)/shard_map/attention_backward/pallas_call | solution.py:991
  297.5 68.6 %tail.1 = (bf16[128,2048]{1,0:T(8,128)(2,1)}, bf16[128,2048]{1,0:T(8,128)(2,1)}, bf16[4,4,2,4,4,16,128]{6,5,4,3,2,1,0:T(8,128)(2,1)}, bf16[4,4,2,4,2,2,16,128]{7...) custom-call(bf16[3,4,2,2,128,128]{5,4,3,2,1,0:T(8,128)(2,1)} %get-tu, ...), custom_call_target="tpu_custom_call" | custom-call | tf_op jit(solution)/shard_map/tail/pallas_call | solution.py:1452
  366.1 0.0 copy-start.1
  366.1 0.0 copy-start
  366.1 10.6 %widen.1 = (f32[4,2048,128]{2,1,0:T(8,128)}, f32[4,128,2048]{2,1,0:T(8,128)}, f32[2048,128]{1,0:T(8,128)}, f32[128,8192]{1,0:T(8,128)}, f32[8192,128]{1,0:T(8,128)}, /*index=5*/f32[128,2048]{1,0:T(8,128)}) custom-call(bf16[4,2048,128]{2,1,0:T(8,128)(2,1)} %bitcast.20, bf16[2048,128]{1,0:T(8,128)(2,1)} %bitcast.26, ...), custom_call_target="tpu_custom_call" | custom-call | tf_op jit(solution)/shard_map/widen/pallas_call | solution.py:1512
  376.7 0.0 copy-done.1
  376.7 0.8 copy.28
  377.5 0.0 copy-done
  377.5 0.8 copy.29
Async XLA Ops:
  366.1 10.6 %copy-start.1 = (bf16[128,2048]{1,0:T(8,128)(2,1)S(1)}, bf16[128,2048]{1,0:T(8,128)(2,1)}, u32[]{:S(2)}) copy-start(bf16[128,2048]{1,0:T(8,128)(2,1)} %get-tuple-element.74) | copy-start | bytes 1572868
  366.1 11.4 %copy-start = (bf16[128,2048]{1,0:T(8,128)(2,1)S(1)}, bf16[128,2048]{1,0:T(8,128)(2,1)}, u32[]{:S(2)}) copy-start(bf16[128,2048]{1,0:T(8,128)(2,1)} %get-tuple-element.75) | copy-start | bytes 1572868
